TPU v7x, 128 devices: a whole 4x4x4 slice. The times are simulated.
128 devices in a mesh: sx: 16 (over x, y), sy: 8 (over z, core).
Axes of the slice: x: 4, y: 4, z: 4, core: 2. Of those that a mesh axis runs over, the one named last changes fastest.
Arguments:
- panels: bfloat16 [128, 384, 400], P(('sx', 'sy')), may hold values from -0.3125 to 0.3125
- coupling: bfloat16 [1024, 2, 384, 384], P(('sx', 'sy')), may hold values from -6 to 6
- partner: int32 [1024], P(('sx', 'sy')), may hold values from 0 to 23, as said below
- counts: int32 [1024], P(('sx', 'sy')), may hold values from 48 to 384
Outputs:
- pair_blocks: bfloat16 [1024, 2, 400, 400], P(('sx', 'sy'))
- partner_blocks: float32 [128, 2, 400, 400], P(('sx', 'sy'))
Inputs may be any that keep to these rules, and one draw needn't show every extreme that they name: `partner`: A code below 16 names the substructure with that sx index in the first substructure's sy column; a code c of 16 or more names the one with sy index c - 16 in its sx row; a pair never names its own first substructure.
All inputs are finite; a program needn't handle non-finite values.
Results may differ from a plain program's by a relative error of at most 0.014.
Values may be sent and summed in bfloat16 or wider, within the bound.
No kernel may reach another device: no remote copies, remote signals or barrier semaphores. Data moves between devices by JAX's collectives and lax.ppermute only.
A program may use at most 192 MiB of HBM per device.

v0:
```python
import jax
import jax.numpy as jnp
from jax import lax
from jax.experimental import pallas as pl
from jax.experimental.pallas import tpu as pltpu
from jax.sharding import PartitionSpec as P

SIDE = 4
SPAN_X, SPAN_Y = SIDE * SIDE, 2 * SIDE
PARTS = ((0, 4), (4, 4), (8, 2), (10, 2), (12, 4))
CHUNK = 80


def slot_of(d1, d2):
    low = d2 < 2
    return jnp.where(
        d1 == 0, 12 + d2,
        jnp.where(d1 == 1, jnp.where(low, 8 + d2, d2),
                  jnp.where(d1 == 2, jnp.where(low, d2, 2 + d2), jnp.where(low, 6 + d2, 8 + d2))))


def offsets(code):
    me = lax.axis_index("sx")
    dx = (code // SIDE - me // SIDE + SIDE) % SIDE
    dy = (code % SIDE - me % SIDE + SIDE) % SIDE
    swapped = lax.axis_index("sy") % 2 == 1
    return jnp.where(swapped, dy, dx), jnp.where(swapped, dx, dy)


def ring_offset(code):
    me = lax.axis_index("sy")
    other = code - SPAN_X
    return (other // 2 - me // 2 + SIDE) % SIDE, other % 2, me % 2


def left_kernel(partner_hbm, counts_hbm, own_hbm, coupling_hbm, left_hbm, *rest):
    outs = rest[:7]
    partner_ref, counts_ref, own_ref, blocks, lefts, zero, sums = rest[7:14]
    keys, number, seen, at_sum, in_sem, left_sem, out_sem = rest[14:]
    count, pairs = blocks.shape[0], keys.shape[0]
    modes, width = own_ref.shape
    slots = SPAN_X + SPAN_Y

    def load(i):
        return pltpu.make_async_copy(coupling_hbm.at[i // 2, i % 2], blocks.at[i], in_sem.at[i])

    def save(i):
        return pltpu.make_async_copy(lefts.at[i], left_hbm.at[i // 2, i % 2], left_sem.at[i])

    load_partner = pltpu.make_async_copy(partner_hbm, partner_ref, in_sem.at[count + 1])
    load_partner.start()
    load_counts = pltpu.make_async_copy(counts_hbm, counts_ref, in_sem.at[count + 2])
    load_counts.start()
    load_own = pltpu.make_async_copy(own_hbm, own_ref, in_sem.at[count])
    load_own.start()

    @pl.loop(0, count)
    def _(i):
        load(i).start()

    @pl.loop(0, slots)
    def _(k):
        number[k] = 0
        seen[k] = 0

    at_sum[slots] = 0
    load_partner.wait()
    load_counts.wait()

    @pl.loop(0, pairs)
    def _(p):
        code = partner_ref[p]
        d1, d2 = offsets(code)
        dz, core, me = ring_offset(code)
        step = jnp.where((dz == 1) | (dz == 3), jnp.where((dz == 1) == (core == 0), 1, 2), jnp.where(dz == 2, 3, 0))
        key = jnp.where(code < SPAN_X, slot_of(d1, d2), SPAN_X + step + jnp.where(core == me, SIDE, 0))
        keys[p] = key
        number[key] = number[key] + 1

    @pl.loop(0, 2 * (modes // CHUNK))
    def _(r):
        rows = pl.ds(pl.multiple_of(r // 2 * CHUNK, CHUNK), CHUNK)
        zero[r % 2, rows] = jnp.zeros((CHUNK, width), zero.dtype)

    def send(source, key):
        for out, (at, size) in zip(outs, PARTS + ((SPAN_X, SIDE), (SPAN_X + SIDE, SIDE)), strict=True):
            @pl.when((key >= at) & (key < at + size))
            def _():
                pltpu.make_async_copy(source, out.at[key - at], out_sem.at[key]).start()

    @pl.loop(0, slots)
    def _(k):
        @pl.when(number[k] == 0)
        def _():
            send(zero, k)

    load_own.wait()

    @pl.loop(0, count)
    def _(i):
        p = i // 2
        load(i).wait()
        keep = lax.broadcasted_iota(jnp.int32, (1, width), 1) < counts_ref[p]
        own = jnp.where(keep, own_ref[...], jnp.zeros((modes, width), own_ref.dtype))
        product = jnp.dot(own, blocks[i], preferred_element_type=jnp.float32)
        lefts[i] = jnp.where(keep, product, 0.0).astype(jnp.bfloat16)
        save(i).start()
        key = keys[p]
        single = number[key] == 1

        @pl.when((i % 2 == 1) & single)
        def _():
            send(lefts.at[pl.ds(i - 1, 2)], key)

        @pl.when((i % 2 == 1) & jnp.logical_not(single))
        def _():
            fresh = seen[key] == 0

            @pl.when(fresh)
            def _():
                at_sum[key] = at_sum[slots]
                at_sum[slots] = at_sum[slots] + 1

            seen[key] = seen[key] + 1
            place = at_sum[key]

            @pl.loop(0, 2 * (modes // CHUNK))
            def _(r):
                t, rows = r % 2, pl.ds(pl.multiple_of(r // 2 * CHUNK, CHUNK), CHUNK)
                before = jnp.where(fresh, 0.0, sums[place, t, rows].astype(jnp.float32))
                sums[place, t, rows] = (before + lefts[i - 1 + t, rows].astype(jnp.float32)).astype(jnp.bfloat16)

            @pl.when(seen[key] == number[key])
            def _():
                send(sums.at[place], key)

    @pl.loop(0, count)
    def _(i):
        save(i).wait()

    @pl.loop(0, slots)
    def _(k):
        pltpu.make_async_copy(zero, outs[0].at[0], out_sem.at[k]).wait()


def in_hbm(value):
    return pltpu.with_memory_space_constraint(value, pltpu.HBM)


def left_products(own, coupling, partner, counts):
    pairs, blocks, width, _ = coupling.shape
    modes = own.shape[0]
    hbm = pl.BlockSpec(memory_space=pltpu.HBM)
    slots = SPAN_X + SPAN_Y
    sizes = [pairs] + [size for _, size in PARTS] + [SIDE] * 2
    out = pl.pallas_call(
        left_kernel,
        in_specs=[hbm] * 4,
        out_specs=[hbm] * len(sizes),
        out_shape=[pltpu.HBM((n, blocks, modes, width), jnp.bfloat16) for n in sizes],
        scratch_shapes=[
            pltpu.SMEM((pairs,), jnp.int32),
            pltpu.SMEM((pairs,), jnp.int32),
            pltpu.VMEM((modes, width), jnp.bfloat16),
            pltpu.VMEM((pairs * blocks, width, width), jnp.bfloat16),
            pltpu.VMEM((pairs * blocks, modes, width), jnp.bfloat16),
            pltpu.VMEM((blocks, modes, width), jnp.bfloat16),
            pltpu.VMEM((pairs // 2, blocks, modes, width), jnp.bfloat16),
            pltpu.SMEM((pairs,), jnp.int32),
            pltpu.SMEM((slots,), jnp.int32),
            pltpu.SMEM((slots,), jnp.int32),
            pltpu.SMEM((slots + 1,), jnp.int32),
            pltpu.SemaphoreType.DMA((pairs * blocks + 3,)),
            pltpu.SemaphoreType.DMA((pairs * blocks,)),
            pltpu.SemaphoreType.DMA((slots,)),
        ],
        compiler_params=pltpu.CompilerParams(vmem_limit_bytes=20 * 2**20),
        cost_estimate=pl.CostEstimate(flops=2 * pairs * blocks * modes * width * width,
                                      bytes_accessed=25 * 10**6, transcendentals=0),
    )(*map(in_hbm, (partner, counts, own, coupling)))
    return out[0], out[1:6], out[6], out[7]


def nt(a, b):
    return lax.dot_general(a, b, (((1,), (1,)), ((), ())), preferred_element_type=jnp.float32)


def pair_kernel(partner_ref, left_hbm, *rest):
    (kept, near, far, low, high, ring_mine, ring_other), out_hbm = rest[:7], rest[7]
    lefts, panels, outs, left_sem, panel_sem, out_sem = rest[8:]
    pairs, count = panels.shape[0], lefts.shape[0]

    def load(i):
        return pltpu.make_async_copy(left_hbm.at[i // 2, i % 2], lefts.at[i], left_sem.at[i])

    def save(i):
        return pltpu.make_async_copy(outs.at[i], out_hbm.at[i // 2, i % 2], out_sem.at[i])

    @pl.loop(0, pairs)
    def _(q):
        load(2 * q).start()
        load(2 * q + 1).start()
        code = partner_ref[q]
        d1, d2 = offsets(code)
        dz, core, me = ring_offset(code)
        step = jnp.where((dz == 1) | (dz == 3), jnp.where((dz == 3) == (core == 0), 1, 2), jnp.where(dz == 2, 3, 0))
        along = code < SPAN_X
        for ref, index, chosen in (
            (kept, d1, along & (d2 == 0)),
            (near, d1, along & (d2 == 1)),
            (far, d1, along & (d2 == 3)),
            (low, d1, along & (d2 == 2) & (d1 < 2)),
            (high, d1 - 2, along & (d2 == 2) & (d1 >= 2)),
            (ring_mine, step, (code >= SPAN_X) & (core == me)),
            (ring_other, step, (code >= SPAN_X) & (core != me)),
        ):
            @pl.when(chosen)
            def _():
                pltpu.make_async_copy(ref.at[index], panels.at[q], panel_sem.at[q]).start()

    @pl.loop(0, count)
    def _(i):
        p = i // 2

        @pl.when(i % 2 == 0)
        def _():
            pltpu.make_async_copy(kept.at[0], panels.at[p], panel_sem.at[p]).wait()

        load(i).wait()
        outs[i] = nt(lefts[i], panels[p]).astype(jnp.bfloat16)
        save(i).start()

    @pl.loop(0, count)
    def _(i):
        save(i).wait()


def pair_products(left, sources, partner):
    pairs, blocks, modes, width = left.shape
    hbm, smem = pl.BlockSpec(memory_space=pltpu.HBM), pl.BlockSpec(memory_space=pltpu.SMEM)
    return pl.pallas_call(
        pair_kernel,
        in_specs=[smem] + [hbm] * 8,
        out_specs=hbm,
        out_shape=jax.ShapeDtypeStruct((pairs, blocks, modes, modes), jnp.bfloat16),
        scratch_shapes=[
            pltpu.VMEM((pairs * blocks, modes, width), jnp.bfloat16),
            pltpu.VMEM((pairs, modes, width), jnp.bfloat16),
            pltpu.VMEM((pairs * blocks, modes, modes), jnp.bfloat16),
            pltpu.SemaphoreType.DMA((pairs * blocks,)),
            pltpu.SemaphoreType.DMA((pairs,)),
            pltpu.SemaphoreType.DMA((pairs * blocks,)),
        ],
        compiler_params=pltpu.CompilerParams(vmem_limit_bytes=20 * 2**20),
        cost_estimate=pl.CostEstimate(flops=2 * pairs * blocks * modes * width * modes,
                                      bytes_accessed=15 * 10**6, transcendentals=0),
    )(partner, in_hbm(left), *map(in_hbm, sources))


def partner_kernel(own_ref, sum_ref, *rest):
    last, out_ref = rest[:-1], rest[-1]

    @pl.loop(0, out_ref.shape[0])
    def _(t):
        total = sum_ref[t]
        for ref in last:
            total = total + ref[t].astype(jnp.float32)
        out_ref[t] = nt(own_ref[...], total.astype(jnp.bfloat16))


def partner_products(own, start, last):
    modes, _ = own.shape
    blocks = start.shape[0]
    return pl.pallas_call(
        partner_kernel,
        out_shape=jax.ShapeDtypeStruct((blocks, modes, modes), jnp.float32),
        compiler_params=pltpu.CompilerParams(vmem_limit_bytes=16 * 2**20),
    )(own, start, *last)


def permuted(value, move):
    pairs = []
    for n in range(SPAN_X * SPAN_Y):
        here = (n // SPAN_Y // SIDE, n // SPAN_Y % SIDE, n % SPAN_Y // 2, n % 2)
        x, y, z, c = move(*here)
        pairs.append((n, ((x % SIDE) * SIDE + y % SIDE) * SPAN_Y + (z % SIDE) * 2 + c))
    return lax.ppermute(value, ("sx", "sy"), pairs)


def first(value, by):
    return permuted(value, lambda x, y, z, c: (x + by, y, z, c) if c == 0 else (x, y + by, z, c))


def second(value, by):
    return permuted(value, lambda x, y, z, c: (x, y + by, z, c) if c == 0 else (x + by, y, z, c))


def turn(value, by):
    return permuted(value, lambda x, y, z, c: (x, y, z + (by if c == 0 else -by), c))


def swap(value):
    return permuted(value, lambda x, y, z, c: (x, y, z, 1 - c))


def added(*terms):
    return sum(v.astype(jnp.float32) for v in terms)


def rounded(*terms):
    return added(*terms).astype(jnp.bfloat16)


def after(value, *others):
    return lax.optimization_barrier((value,) + others)[0]


def body(panels, coupling, partner, counts):
    own = jnp.swapaxes(panels[0], 0, 1)
    barrier = lax.optimization_barrier

    moved = [first(own, -1), first(own, 2), first(own, 1)]
    kept = jnp.stack([own] + moved)
    left, (up, down, pass_up, pass_down, here), z_other, z_mine = left_products(own, coupling, partner, counts)
    kept, up, down, z_other, own_z = barrier((kept, up, down, z_other, own))

    got = [first(up, 1), first(down, -1)]
    ring = [second(kept, -1), second(kept, 1)]
    ring1 = turn(own_z, 1)
    ring2 = turn(after(own_z, ring1), -1)
    ring3 = turn(after(own_z, ring2), 2)
    ring_mine = jnp.stack([own, ring1, ring2, ring3])
    ring_other = swap(ring_mine)
    got, ring, ring_other, z_other = barrier((got, ring, ring_other, z_other))
    (got_up, got_down), (near, far) = got, ring

    last = [first(rounded(pass_up, got_up[:2]), 1), first(rounded(pass_down, got_down[:2]), -1)]
    relay = [second(near[:2], -1), second(far[2:], 1)]
    pair_sum = swap(z_other)
    w = [rounded(z_mine[k], pair_sum[k]) for k in range(SIDE)]
    z1 = turn(w[1], 1)
    last, relay, w, z1 = barrier((last, relay, w, z1))
    (last_up, last_down), (low, high) = last, relay

    v = [
        rounded(here[0], got_down[2], last_up[0]),
        rounded(here[1], got_down[3], last_up[1]),
        rounded(here[2], got_up[2], last_down[0]),
        rounded(here[3], got_up[3], last_down[1]),
    ]
    ends = [second(v[1], 1), second(v[3], -1), second(v[2], 2)]
    z2, z3 = turn(w[2], -1), turn(w[3], 2)

    sources = [kept, near, far, low, high, ring_mine, ring_other]
    pair_blocks = pair_products(left, sources, after(partner, *v))
    partner_blocks = partner_products(own, added(v[0], w[0], z1, z2, z3), ends)
    return (pair_blocks, partner_blocks[None])


def solution(mesh):
    placed = (
        P(("sx", "sy"), None, None),
        P(("sx", "sy"), None, None, None),
        P(("sx", "sy")),
        P(("sx", "sy")),
    )
    return jax.shard_map(
        body,
        mesh=mesh,
        in_specs=placed,
        out_specs=(P(("sx", "sy"), None, None, None), P(("sx", "sy"), None, None, None)),
        check_vma=False,
    )
```

profile of v0, /device:TPU:0, one launch (start us, length us, event | category | flops | bytes accessed | tf_op | source)
XLA Modules:
  0.0 125.1 jit_solution(12363612286451961055)
XLA Ops:
  0.6 2.9 %collective-permute-start = (bf16[400,384]{1,0:T(8,128)(2,1)}, bf16[400,384]{1,0:T(8,128)(2,1)S(1)}, u32[]{:S(2)}, u32[]{:S(2)}) collective-permute-start(bf16[400,384]{1,0:T(8,128)(2,1)} %bitcast.29), channel_id=1, source_target_pairs={{0,96},{1,25},{2,98},{3,27},{4,100},{5,29},{6,102},{7,31},{8,104},... | collective-permute-start | bytes 921608 | tf_op jit(solution)/shard_map/ppermute | solution.py:287
  3.5 0.8 collective-permute-start.1
  4.4 0.9 collective-permute-start.2
  5.2 9.7 %shard_map.59 = (bf16[8,2,400,384]{3,2,1,0:T(8,128)(2,1)}, bf16[4,2,400,384]{3,2,1,0:T(8,128)(2,1)}, bf16[4,2,400,384]{3,2,1,0:T(8,128)(2,1)}, bf16[2,2,400,384]...) custom-call(s32[8]{0:T(128)} %partner_ref, ...), custom_call_target="tpu_custom_call" | custom-call | flops 1887436800 | bytes 25000000 | tf_op jit(solution)/shard_map/pallas_call | solution.py:156
  14.9 0.0 collective-permute-done
  14.9 0.0 collective-permute-done.1
  15.0 0.5 collective-permute-done.2
  15.4 0.2 fusion.1.rest_0_
  15.6 2.0 %collective-permute-start.3 = (bf16[4,2,400,384]{3,2,1,0:T(8,128)(2,1)}, bf16[4,2,400,384]{3,2,1,0:T(8,128)(2,1)S(1)}, u32[]{:S(2)}, u32[]{:S(2)}) collective-permute-start(bf16[4,2,400,384]{3,2,1,0:T(8,128)(2,1)} %get-tuple-element.36), channel_id=1, source_target_pairs={{0,32},{1,9},{2,34},{3,11},{4,36},{5,13},{6,38},{7,15},{8,40},{9,1... | collective-permute-start | bytes 7372808 | tf_op jit(solution)/shard_map/ppermute | solution.py:287
  17.6 2.3 %collective-permute-start.4 = (bf16[4,2,400,384]{3,2,1,0:T(8,128)(2,1)}, bf16[4,2,400,384]{3,2,1,0:T(8,128)(2,1)S(1)}, u32[]{:S(2)}, u32[]{:S(2)}) collective-permute-start(bf16[4,2,400,384]{3,2,1,0:T(8,128)(2,1)} %get-tuple-element.37), channel_id=1, source_target_pairs={{0,96},{1,25},{2,98},{3,27},{4,100},{5,29},{6,102},{7,31},{8,104},... | collective-permute-start | bytes 7372808 | tf_op jit(solution)/shard_map/ppermute | solution.py:287
  19.9 1.6 %collective-permute-start.7 = (bf16[400,384]{1,0:T(8,128)(2,1)S(1)}, bf16[400,384]{1,0:T(8,128)(2,1)S(1)}, u32[]{:S(2)}, u32[]{:S(2)}) collective-permute-start(bf16[400,384]{1,0:T(8,128)(2,1)S(1)} %bitcast.34), channel_id=1, source_target_pairs={{0,2},{1,7},{2,4},{3,1},{4,6},{5,3},{6,0},{7,5},{8,10},{9,15},{10,... | collective-permute-start | bytes 921608 | tf_op jit(solution)/shard_map/ppermute | solution.py:287
  21.6 6.4 %collective-permute-done.7 = bf16[400,384]{1,0:T(8,128)(2,1)S(1)} collective-permute-done((bf16[400,384]{1,0:T(8,128)(2,1)S(1)}, bf16[400,384]{1,0:T(8,128)(2,1)S(1)}, u32[]{:S(2)}, u32[]{:S(2)}) %collective-permute-start.7) | collective-permute-done | bytes 307232 | tf_op jit(solution)/shard_map/ppermute | solution.py:287
  28.0 1.8 %collective-permute-start.8 = (bf16[400,384]{1,0:T(8,128)(2,1)S(1)}, bf16[400,384]{1,0:T(8,128)(2,1)S(1)}, u32[]{:S(2)}, u32[]{:S(2)}) collective-permute-start(bf16[400,384]{1,0:T(8,128)(2,1)S(1)} %bitcast.35), channel_id=1, source_target_pairs={{0,6},{1,3},{2,0},{3,5},{4,2},{5,7},{6,4},{7,1},{8,14},{9,11},{10,... | collective-permute-start | bytes 921608 | tf_op jit(solution)/shard_map/ppermute | solution.py:287
  29.8 5.0 %collective-permute-done.8 = bf16[400,384]{1,0:T(8,128)(2,1)S(1)} collective-permute-done((bf16[400,384]{1,0:T(8,128)(2,1)S(1)}, bf16[400,384]{1,0:T(8,128)(2,1)S(1)}, u32[]{:S(2)}, u32[]{:S(2)}) %collective-permute-start.8) | collective-permute-done | bytes 307232 | tf_op jit(solution)/shard_map/ppermute | solution.py:287
  34.9 1.9 %collective-permute-start.9 = (bf16[400,384]{1,0:T(8,128)(2,1)S(1)}, bf16[400,384]{1,0:T(8,128)(2,1)S(1)}, u32[]{:S(2)}, u32[]{:S(2)}) collective-permute-start(bf16[400,384]{1,0:T(8,128)(2,1)S(1)} %bitcast.36), channel_id=1, source_target_pairs={{0,4},{1,5},{2,6},{3,7},{4,0},{5,1},{6,2},{7,3},{8,12},{9,13},{10,... | collective-permute-start | bytes 921608 | tf_op jit(solution)/shard_map/ppermute | solution.py:287
  36.8 5.0 %collective-permute-start.5 = (bf16[4,400,384]{2,1,0:T(8,128)(2,1)S(1)}, bf16[4,400,384]{2,1,0:T(8,128)(2,1)S(1)}, u32[]{:S(2)}, u32[]{:S(2)}) collective-permute-start(bf16[4,400,384]{2,1,0:T(8,128)(2,1)S(1)} %fusion.1.rest_0_), channel_id=1, source_target_pairs={{0,24},{1,97},{2,26},{3,99},{4,28},{5,101},{6,30},{7,103},{8,0},{9... | collective-permute-start | bytes 3686408 | tf_op jit(solution)/shard_map/ppermute | solution.py:287
  41.7 0.9 collective-permute-start.6
  42.6 0.9 collective-permute-done.9
  43.5 0.2 fusion.3.rest_5_
  43.7 0.1 collective-permute-start.10
  43.8 15.9 %collective-permute-done.5.rest_1_ = bf16[4,400,384]{2,1,0:T(8,128)(2,1)S(1)} collective-permute-done((bf16[4,400,384]{2,1,0:T(8,128)(2,1)S(1)}, bf16[4,400,384]{2,1,0:T(8,128)(2,1)S(1)}, u32[]{:S(2)}, u32[]{:S(2)}) %collective-permute-start.5) | collective-permute-done | bytes 1228832 | tf_op jit(solution)/shard_map/ppermute | solution.py:287
  59.7 0.0 collective-permute-done.6.rest_2_
  59.7 0.0 collective-permute-done.10.rest_6_
  59.7 0.0 collective-permute-done.3
  59.7 1.3 %collective-permute-start.15 = (bf16[4,2,400,384]{3,2,1,0:T(8,128)(2,1)S(1)}, bf16[4,2,400,384]{3,2,1,0:T(8,128)(2,1)S(1)}, u32[]{:S(2)}, u32[]{:S(2)}) collective-permute-start(bf16[4,2,400,384]{3,2,1,0:T(8,128)(2,1)S(1)} %copy-done.13), channel_id=1, source_target_pairs={{0,1},{1,0},{2,3},{3,2},{4,5},{5,4},{6,7},{7,6},{8,9},{9,8},{10,11... | collective-permute-start | bytes 7372808 | tf_op jit(solution)/shard_map/ppermute | solution.py:287
  61.0 0.3 add_convert_fusion
  61.4 3.4 %collective-permute-start.12 = (bf16[2,2,400,384]{3,2,1,0:T(8,128)(2,1)S(1)}, bf16[2,2,400,384]{3,2,1,0:T(8,128)(2,1)S(1)}, u32[]{:S(2)}, u32[]{:S(2)}) collective-permute-start(bf16[2,2,400,384]{3,2,1,0:T(8,128)(2,1)S(1)} %add_convert_fusion), channel_id=1, source_target_pairs={{0,96},{1,25},{2,98},{3,27},{4,100},{5,29},{6,102},{7,31},{8,104},... | collective-permute-start | bytes 3686408 | tf_op jit(solution)/shard_map/ppermute | solution.py:287
  64.8 0.3 add_convert_fusion.1
  65.2 0.1 collective-permute-start.11
  65.3 0.1 slice.76
  65.3 3.3 %collective-permute-start.13 = (bf16[2,400,384]{2,1,0:T(8,128)(2,1)S(1)}, bf16[2,400,384]{2,1,0:T(8,128)(2,1)S(1)}, u32[]{:S(2)}, u32[]{:S(2)}) collective-permute-start(bf16[2,400,384]{2,1,0:T(8,128)(2,1)S(1)} %slice.76), channel_id=1, source_target_pairs={{0,24},{1,97},{2,26},{3,99},{4,28},{5,101},{6,30},{7,103},{8,0},{9... | collective-permute-start | bytes 1843208 | tf_op jit(solution)/shard_map/ppermute | solution.py:287
  68.6 0.1 slice.77
  68.7 0.1 collective-permute-start.14
  68.8 0.6 fusion.7
  69.4 1.0 collective-permute-start.16
  70.4 12.5 %collective-permute-done.13.rest_3_ = bf16[2,400,384]{2,1,0:T(8,128)(2,1)S(1)} collective-permute-done((bf16[2,400,384]{2,1,0:T(8,128)(2,1)S(1)}, bf16[2,400,384]{2,1,0:T(8,128)(2,1)S(1)}, u32[]{:S(2)}, u32[]{:S(2)}) %collective-permute-start.13) | collective-permute-done | bytes 614432 | tf_op jit(solution)/shard_map/ppermute | solution.py:287
  82.9 3.8 %collective-permute-done.14.rest_4_ = bf16[2,400,384]{2,1,0:T(8,128)(2,1)S(1)} collective-permute-done((bf16[2,400,384]{2,1,0:T(8,128)(2,1)S(1)}, bf16[2,400,384]{2,1,0:T(8,128)(2,1)S(1)}, u32[]{:S(2)}, u32[]{:S(2)}) %collective-permute-start.14) | collective-permute-done | bytes 614432 | tf_op jit(solution)/shard_map/ppermute | solution.py:287
  86.7 3.0 %collective-permute-done.11 = bf16[2,2,400,384]{3,2,1,0:T(8,128)(2,1)S(1)} collective-permute-done((bf16[2,2,400,384]{3,2,1,0:T(8,128)(2,1)S(1)}, bf16[2,2,400,384]{3,2,1,0:T(8,128)(2,1)S(1)}, u32[]{:S(2)}, u32[]{:S(2)}) %collective-permute-start.11) | collective-permute-done | bytes 1228832 | tf_op jit(solution)/shard_map/ppermute | solution.py:287
  89.8 3.0 %collective-permute-start.17 = (bf16[2,400,384]{2,1,0:T(8,128)(2,1)S(1)}, bf16[2,400,384]{2,1,0:T(8,128)(2,1)S(1)}, u32[]{:S(2)}, u32[]{:S(2)}) collective-permute-start(bf16[2,400,384]{2,1,0:T(8,128)(2,1)S(1)} %get-tuple-element.60), channel_id=1, source_target_pairs={{0,6},{1,3},{2,0},{3,5},{4,2},{5,7},{6,4},{7,1},{8,14},{9,11},{10,... | collective-permute-start | bytes 1843208 | tf_op jit(solution)/shard_map/ppermute | solution.py:287
  92.8 0.7 collective-permute-start.18
  93.5 0.7 fusion.11
  94.2 1.8 %collective-permute-start.19 = (bf16[2,400,384]{2,1,0:T(8,128)(2,1)S(1)}, bf16[2,400,384]{2,1,0:T(8,128)(2,1)S(1)}, u32[]{:S(2)}, u32[]{:S(2)}) collective-permute-start(bf16[2,400,384]{2,1,0:T(8,128)(2,1)S(1)} %get-tuple-element.70), channel_id=1, source_target_pairs={{0,8},{1,33},{2,10},{3,35},{4,12},{5,37},{6,14},{7,39},{8,16},{9,4... | collective-permute-start | bytes 1843208 | tf_op jit(solution)/shard_map/ppermute | solution.py:287
  96.0 1.5 %collective-permute-start.20 = (bf16[2,400,384]{2,1,0:T(8,128)(2,1)S(1)}, bf16[2,400,384]{2,1,0:T(8,128)(2,1)S(1)}, u32[]{:S(2)}, u32[]{:S(2)}) collective-permute-start(bf16[2,400,384]{2,1,0:T(8,128)(2,1)S(1)} %get-tuple-element.64), channel_id=1, source_target_pairs={{0,24},{1,97},{2,26},{3,99},{4,28},{5,101},{6,30},{7,103},{8,0},{9... | collective-permute-start | bytes 1843208 | tf_op jit(solution)/shard_map/ppermute | solution.py:287
  97.5 2.1 %collective-permute-start.21 = (bf16[2,400,384]{2,1,0:T(8,128)(2,1)S(1)}, bf16[2,400,384]{2,1,0:T(8,128)(2,1)S(1)}, u32[]{:S(2)}, u32[]{:S(2)}) collective-permute-start(bf16[2,400,384]{2,1,0:T(8,128)(2,1)S(1)} %get-tuple-element.65), channel_id=1, source_target_pairs={{0,16},{1,65},{2,18},{3,67},{4,20},{5,69},{6,22},{7,71},{8,24},{9,... | collective-permute-start | bytes 1843208 | tf_op jit(solution)/shard_map/ppermute | solution.py:287
  99.6 13.7 %collective-permute-done.17 = bf16[2,400,384]{2,1,0:T(8,128)(2,1)S(1)} collective-permute-done((bf16[2,400,384]{2,1,0:T(8,128)(2,1)S(1)}, bf16[2,400,384]{2,1,0:T(8,128)(2,1)S(1)}, u32[]{:S(2)}, u32[]{:S(2)}) %collective-permute-start.17) | collective-permute-done | bytes 614432 | tf_op jit(solution)/shard_map/ppermute | solution.py:287
  113.3 0.5 convert_add_fusion
  113.8 9.2 %shard_map.60 = bf16[8,2,400,400]{3,2,1,0:T(8,128)(2,1)} custom-call(s32[8]{0:T(128)S(1)} %copy-done.1, bf16[8,2,400,384]{3,2,1,0:T(8,128)(2,1)} %get-tuple-element.54.left_hbm, bf16[4,400,384]{2,1,0:T(8,128)(2,1)} %copy-done.2, bf16[4,400,384]{2,1,0:T(8,128)(2,1)} %copy-done.4, bf16[4,400,384]{2,1,0:T(8,128)(2,1)} %copy-done.5, ...), custom_call_target="tpu_custom_call" | custom-call | flops 1966080000 | bytes 15000000 | tf_op jit(solution)/shard_map/pallas_call | solution.py:241
  123.1 2.1 %shard_map.61 = f32[2,400,400]{2,1,0:T(8,128)} custom-call(bf16[400,384]{1,0:T(8,128)(2,1)S(1)} %bitcast.38, f32[2,400,384]{2,1,0:T(8,128)S(1)} %convert_add_fusion, bf16[2,400,384]{2,1,0:T(8,128)(2,1)S(1)} %collective-permute-done.19.rest_0_, bf16[2,400,384]{2,1,0:T(8,128)(2,1)S(1)} %collective-permute-done.20.rest_1_, ...), custom_call_target="tpu_custom_call" | custom-call | tf_op jit(solution)/shard_map/pallas_call | solution.py:274
  (36 shorter events, 0.1 us)
Async XLA Ops:
  0.6 14.8 %copy-start = (bf16[1,384,400]{1,2,0:T(8,128)(2,1)S(1)}, bf16[1,384,400]{1,2,0:T(8,128)(2,1)}, u32[]{:S(2)}) copy-start(bf16[1,384,400]{1,2,0:T(8,128)(2,1)} %param.4) | copy-start | bytes 921604
  0.6 14.3 %collective-permute-start = (bf16[400,384]{1,0:T(8,128)(2,1)}, bf16[400,384]{1,0:T(8,128)(2,1)S(1)}, u32[]{:S(2)}, u32[]{:S(2)}) collective-permute-start(bf16[400,384]{1,0:T(8,128)(2,1)} %bitcast.29), channel_id=1, source_target_pairs={{0,96},{1,25},{2,98},{3,27},{4,100},{5,29},{6,102},{7,31},{8,104},... | collective-permute-start | bytes 921608 | tf_op jit(solution)/shard_map/ppermute | solution.py:287
  3.5 11.4 %collective-permute-start.1 = (bf16[400,384]{1,0:T(8,128)(2,1)}, bf16[400,384]{1,0:T(8,128)(2,1)S(1)}, u32[]{:S(2)}, u32[]{:S(2)}) collective-permute-start(bf16[400,384]{1,0:T(8,128)(2,1)} %bitcast.30), channel_id=1, source_target_pairs={{0,64},{1,17},{2,66},{3,19},{4,68},{5,21},{6,70},{7,23},{8,72},{9,... | collective-permute-start | bytes 921608 | tf_op jit(solution)/shard_map/ppermute | solution.py:287
  4.4 11.1 %collective-permute-start.2 = (bf16[400,384]{1,0:T(8,128)(2,1)}, bf16[400,384]{1,0:T(8,128)(2,1)S(1)}, u32[]{:S(2)}, u32[]{:S(2)}) collective-permute-start(bf16[400,384]{1,0:T(8,128)(2,1)} %bitcast.31), channel_id=1, source_target_pairs={{0,32},{1,9},{2,34},{3,11},{4,36},{5,13},{6,38},{7,15},{8,40},{9,1... | collective-permute-start | bytes 921608 | tf_op jit(solution)/shard_map/ppermute | solution.py:287
  15.4 44.3 %copy-start.13 = (bf16[4,2,400,384]{3,2,1,0:T(8,128)(2,1)S(1)}, bf16[4,2,400,384]{3,2,1,0:T(8,128)(2,1)}, u32[]{:S(2)}) copy-start(bf16[4,2,400,384]{3,2,1,0:T(8,128)(2,1)} %get-tuple-element.50) | copy-start | bytes 7372804
  15.6 28.1 %copy-start.2 = (bf16[4,400,384]{2,1,0:T(8,128)(2,1)}, bf16[4,400,384]{2,1,0:T(8,128)(2,1)S(1)}, u32[]{:S(2)}) copy-start(bf16[4,400,384]{2,1,0:T(8,128)(2,1)S(1)} %fusion.1.rest_0_) | copy-start | bytes 3686404
  15.6 44.1 %collective-permute-start.3 = (bf16[4,2,400,384]{3,2,1,0:T(8,128)(2,1)}, bf16[4,2,400,384]{3,2,1,0:T(8,128)(2,1)S(1)}, u32[]{:S(2)}, u32[]{:S(2)}) collective-permute-start(bf16[4,2,400,384]{3,2,1,0:T(8,128)(2,1)} %get-tuple-element.36), channel_id=1, source_target_pairs={{0,32},{1,9},{2,34},{3,11},{4,36},{5,13},{6,38},{7,15},{8,40},{9,1... | collective-permute-start | bytes 7372808 | tf_op jit(solution)/shard_map/ppermute | solution.py:287
  17.6 42.1 %collective-permute-start.4 = (bf16[4,2,400,384]{3,2,1,0:T(8,128)(2,1)}, bf16[4,2,400,384]{3,2,1,0:T(8,128)(2,1)S(1)}, u32[]{:S(2)}, u32[]{:S(2)}) collective-permute-start(bf16[4,2,400,384]{3,2,1,0:T(8,128)(2,1)} %get-tuple-element.37), channel_id=1, source_target_pairs={{0,96},{1,25},{2,98},{3,27},{4,100},{5,29},{6,102},{7,31},{8,104},... | collective-permute-start | bytes 7372808 | tf_op jit(solution)/shard_map/ppermute | solution.py:287
  19.9 8.1 %collective-permute-start.7 = (bf16[400,384]{1,0:T(8,128)(2,1)S(1)}, bf16[400,384]{1,0:T(8,128)(2,1)S(1)}, u32[]{:S(2)}, u32[]{:S(2)}) collective-permute-start(bf16[400,384]{1,0:T(8,128)(2,1)S(1)} %bitcast.34), channel_id=1, source_target_pairs={{0,2},{1,7},{2,4},{3,1},{4,6},{5,3},{6,0},{7,5},{8,10},{9,15},{10,... | collective-permute-start | bytes 921608 | tf_op jit(solution)/shard_map/ppermute | solution.py:287
  28.0 6.9 %collective-permute-start.8 = (bf16[400,384]{1,0:T(8,128)(2,1)S(1)}, bf16[400,384]{1,0:T(8,128)(2,1)S(1)}, u32[]{:S(2)}, u32[]{:S(2)}) collective-permute-start(bf16[400,384]{1,0:T(8,128)(2,1)S(1)} %bitcast.35), channel_id=1, source_target_pairs={{0,6},{1,3},{2,0},{3,5},{4,2},{5,7},{6,4},{7,1},{8,14},{9,11},{10,... | collective-permute-start | bytes 921608 | tf_op jit(solution)/shard_map/ppermute | solution.py:287
  34.9 8.7 %collective-permute-start.9 = (bf16[400,384]{1,0:T(8,128)(2,1)S(1)}, bf16[400,384]{1,0:T(8,128)(2,1)S(1)}, u32[]{:S(2)}, u32[]{:S(2)}) collective-permute-start(bf16[400,384]{1,0:T(8,128)(2,1)S(1)} %bitcast.36), channel_id=1, source_target_pairs={{0,4},{1,5},{2,6},{3,7},{4,0},{5,1},{6,2},{7,3},{8,12},{9,13},{10,... | collective-permute-start | bytes 921608 | tf_op jit(solution)/shard_map/ppermute | solution.py:287
  36.8 22.9 %collective-permute-start.5 = (bf16[4,400,384]{2,1,0:T(8,128)(2,1)S(1)}, bf16[4,400,384]{2,1,0:T(8,128)(2,1)S(1)}, u32[]{:S(2)}, u32[]{:S(2)}) collective-permute-start(bf16[4,400,384]{2,1,0:T(8,128)(2,1)S(1)} %fusion.1.rest_0_), channel_id=1, source_target_pairs={{0,24},{1,97},{2,26},{3,99},{4,28},{5,101},{6,30},{7,103},{8,0},{9... | collective-permute-start | bytes 3686408 | tf_op jit(solution)/shard_map/ppermute | solution.py:287
  41.7 18.0 %collective-permute-start.6 = (bf16[4,400,384]{2,1,0:T(8,128)(2,1)S(1)}, bf16[4,400,384]{2,1,0:T(8,128)(2,1)S(1)}, u32[]{:S(2)}, u32[]{:S(2)}) collective-permute-start(bf16[4,400,384]{2,1,0:T(8,128)(2,1)S(1)} %fusion.1.rest_0_), channel_id=1, source_target_pairs={{0,8},{1,33},{2,10},{3,35},{4,12},{5,37},{6,14},{7,39},{8,16},{9,4... | collective-permute-start | bytes 3686408 | tf_op jit(solution)/shard_map/ppermute | solution.py:287
  43.5 17.5 %copy-start.9 = (bf16[2,2,400,384]{3,2,1,0:T(8,128)(2,1)S(1)}, bf16[2,2,400,384]{3,2,1,0:T(8,128)(2,1)}, u32[]{:S(2)}) copy-start(bf16[2,2,400,384]{3,2,1,0:T(8,128)(2,1)} %get-tuple-element.46) | copy-start | bytes 3686404
  43.7 17.7 %copy-start.3 = (bf16[4,400,384]{2,1,0:T(8,128)(2,1)}, bf16[4,400,384]{2,1,0:T(8,128)(2,1)S(1)}, u32[]{:S(2)}) copy-start(bf16[4,400,384]{2,1,0:T(8,128)(2,1)S(1)} %fusion.3.rest_5_) | copy-start | bytes 3686404
  43.7 16.0 %collective-permute-start.10 = (bf16[4,400,384]{2,1,0:T(8,128)(2,1)S(1)}, bf16[4,400,384]{2,1,0:T(8,128)(2,1)S(1)}, u32[]{:S(2)}, u32[]{:S(2)}) collective-permute-start(bf16[4,400,384]{2,1,0:T(8,128)(2,1)S(1)} %fusion.3.rest_5_), channel_id=1, source_target_pairs={{0,1},{1,0},{2,3},{3,2},{4,5},{5,4},{6,7},{7,6},{8,9},{9,8},{10,11... | collective-permute-start | bytes 3686408 | tf_op jit(solution)/shard_map/ppermute | solution.py:287
  59.7 5.6 %copy-start.4 = (bf16[4,400,384]{2,1,0:T(8,128)(2,1)}, bf16[4,400,384]{2,1,0:T(8,128)(2,1)S(1)}, u32[]{:S(2)}) copy-start(bf16[4,400,384]{2,1,0:T(8,128)(2,1)S(1)} %collective-permute-done.5.rest_1_) | copy-start | bytes 3686404
  59.7 8.9 %copy-start.5 = (bf16[4,400,384]{2,1,0:T(8,128)(2,1)}, bf16[4,400,384]{2,1,0:T(8,128)(2,1)S(1)}, u32[]{:S(2)}) copy-start(bf16[4,400,384]{2,1,0:T(8,128)(2,1)S(1)} %collective-permute-done.6.rest_2_) | copy-start | bytes 3686404
  59.7 5.4 %copy-start.10 = (bf16[4,400,384]{2,1,0:T(8,128)(2,1)}, bf16[4,400,384]{2,1,0:T(8,128)(2,1)S(1)}, u32[]{:S(2)}) copy-start(bf16[4,400,384]{2,1,0:T(8,128)(2,1)S(1)} %collective-permute-done.10.rest_6_) | copy-start | bytes 3686404
  59.7 9.0 %collective-permute-start.15 = (bf16[4,2,400,384]{3,2,1,0:T(8,128)(2,1)S(1)}, bf16[4,2,400,384]{3,2,1,0:T(8,128)(2,1)S(1)}, u32[]{:S(2)}, u32[]{:S(2)}) collective-permute-start(bf16[4,2,400,384]{3,2,1,0:T(8,128)(2,1)S(1)} %copy-done.13), channel_id=1, source_target_pairs={{0,1},{1,0},{2,3},{3,2},{4,5},{5,4},{6,7},{7,6},{8,9},{9,8},{10,11... | collective-permute-start | bytes 7372808 | tf_op jit(solution)/shard_map/ppermute | solution.py:287
  61.0 3.8 %copy-start.8 = (bf16[2,2,400,384]{3,2,1,0:T(8,128)(2,1)S(1)}, bf16[2,2,400,384]{3,2,1,0:T(8,128)(2,1)}, u32[]{:S(2)}) copy-start(bf16[2,2,400,384]{3,2,1,0:T(8,128)(2,1)} %get-tuple-element.44) | copy-start | bytes 3686404
  61.4 25.3 %collective-permute-start.12 = (bf16[2,2,400,384]{3,2,1,0:T(8,128)(2,1)S(1)}, bf16[2,2,400,384]{3,2,1,0:T(8,128)(2,1)S(1)}, u32[]{:S(2)}, u32[]{:S(2)}) collective-permute-start(bf16[2,2,400,384]{3,2,1,0:T(8,128)(2,1)S(1)} %add_convert_fusion), channel_id=1, source_target_pairs={{0,96},{1,25},{2,98},{3,27},{4,100},{5,29},{6,102},{7,31},{8,104},... | collective-permute-start | bytes 3686408 | tf_op jit(solution)/shard_map/ppermute | solution.py:287
  65.2 3.6 %copy-start.6 = (bf16[4,2,400,384]{3,2,1,0:T(8,128)(2,1)S(1)}, bf16[4,2,400,384]{3,2,1,0:T(8,128)(2,1)}, u32[]{:S(2)}) copy-start(bf16[4,2,400,384]{3,2,1,0:T(8,128)(2,1)} %get-tuple-element.49) | copy-start | bytes 7372804
  65.2 24.6 %collective-permute-start.11 = (bf16[2,2,400,384]{3,2,1,0:T(8,128)(2,1)S(1)}, bf16[2,2,400,384]{3,2,1,0:T(8,128)(2,1)S(1)}, u32[]{:S(2)}, u32[]{:S(2)}) collective-permute-start(bf16[2,2,400,384]{3,2,1,0:T(8,128)(2,1)S(1)} %add_convert_fusion.1), channel_id=1, source_target_pairs={{0,32},{1,9},{2,34},{3,11},{4,36},{5,13},{6,38},{7,15},{8,40},{9,1... | collective-permute-start | bytes 3686408 | tf_op jit(solution)/shard_map/ppermute | solution.py:287
  65.3 17.6 %collective-permute-start.13 = (bf16[2,400,384]{2,1,0:T(8,128)(2,1)S(1)}, bf16[2,400,384]{2,1,0:T(8,128)(2,1)S(1)}, u32[]{:S(2)}, u32[]{:S(2)}) collective-permute-start(bf16[2,400,384]{2,1,0:T(8,128)(2,1)S(1)} %slice.76), channel_id=1, source_target_pairs={{0,24},{1,97},{2,26},{3,99},{4,28},{5,101},{6,30},{7,103},{8,0},{9... | collective-permute-start | bytes 1843208 | tf_op jit(solution)/shard_map/ppermute | solution.py:287
  68.7 18.1 %collective-permute-start.14 = (bf16[2,400,384]{2,1,0:T(8,128)(2,1)S(1)}, bf16[2,400,384]{2,1,0:T(8,128)(2,1)S(1)}, u32[]{:S(2)}, u32[]{:S(2)}) collective-permute-start(bf16[2,400,384]{2,1,0:T(8,128)(2,1)S(1)} %slice.77), channel_id=1, source_target_pairs={{0,8},{1,33},{2,10},{3,35},{4,12},{5,37},{6,14},{7,39},{8,16},{9,4... | collective-permute-start | bytes 1843208 | tf_op jit(solution)/shard_map/ppermute | solution.py:287
  68.8 24.7 %copy-start.7 = (bf16[4,2,400,384]{3,2,1,0:T(8,128)(2,1)S(1)}, bf16[4,2,400,384]{3,2,1,0:T(8,128)(2,1)}, u32[]{:S(2)}) copy-start(bf16[4,2,400,384]{3,2,1,0:T(8,128)(2,1)} %get-tuple-element.32) | copy-start | bytes 7372804
  69.4 20.4 %collective-permute-start.16 = (bf16[2,400,384]{2,1,0:T(8,128)(2,1)S(1)}, bf16[2,400,384]{2,1,0:T(8,128)(2,1)S(1)}, u32[]{:S(2)}, u32[]{:S(2)}) collective-permute-start(bf16[2,400,384]{2,1,0:T(8,128)(2,1)S(1)} %get-tuple-element.68), channel_id=1, source_target_pairs={{0,2},{1,7},{2,4},{3,1},{4,6},{5,3},{6,0},{7,5},{8,10},{9,15},{10,... | collective-permute-start | bytes 1843208 | tf_op jit(solution)/shard_map/ppermute | solution.py:287
  82.9 11.3 %copy-start.11 = (bf16[2,400,384]{2,1,0:T(8,128)(2,1)}, bf16[2,400,384]{2,1,0:T(8,128)(2,1)S(1)}, u32[]{:S(2)}) copy-start(bf16[2,400,384]{2,1,0:T(8,128)(2,1)S(1)} %collective-permute-done.13.rest_3_) | copy-start | bytes 1843204
  86.7 7.5 %copy-start.12 = (bf16[2,400,384]{2,1,0:T(8,128)(2,1)}, bf16[2,400,384]{2,1,0:T(8,128)(2,1)S(1)}, u32[]{:S(2)}) copy-start(bf16[2,400,384]{2,1,0:T(8,128)(2,1)S(1)} %collective-permute-done.14.rest_4_) | copy-start | bytes 1843204
  89.8 23.5 %collective-permute-start.17 = (bf16[2,400,384]{2,1,0:T(8,128)(2,1)S(1)}, bf16[2,400,384]{2,1,0:T(8,128)(2,1)S(1)}, u32[]{:S(2)}, u32[]{:S(2)}) collective-permute-start(bf16[2,400,384]{2,1,0:T(8,128)(2,1)S(1)} %get-tuple-element.60), channel_id=1, source_target_pairs={{0,6},{1,3},{2,0},{3,5},{4,2},{5,7},{6,4},{7,1},{8,14},{9,11},{10,... | collective-permute-start | bytes 1843208 | tf_op jit(solution)/shard_map/ppermute | solution.py:287
  92.8 20.5 %collective-permute-start.18 = (bf16[2,400,384]{2,1,0:T(8,128)(2,1)S(1)}, bf16[2,400,384]{2,1,0:T(8,128)(2,1)S(1)}, u32[]{:S(2)}, u32[]{:S(2)}) collective-permute-start(bf16[2,400,384]{2,1,0:T(8,128)(2,1)S(1)} %get-tuple-element.61), channel_id=1, source_target_pairs={{0,4},{1,5},{2,6},{3,7},{4,0},{5,1},{6,2},{7,3},{8,12},{9,13},{10,... | collective-permute-start | bytes 1843208 | tf_op jit(solution)/shard_map/ppermute | solution.py:287
  94.2 28.8 %collective-permute-start.19 = (bf16[2,400,384]{2,1,0:T(8,128)(2,1)S(1)}, bf16[2,400,384]{2,1,0:T(8,128)(2,1)S(1)}, u32[]{:S(2)}, u32[]{:S(2)}) collective-permute-start(bf16[2,400,384]{2,1,0:T(8,128)(2,1)S(1)} %get-tuple-element.70), channel_id=1, source_target_pairs={{0,8},{1,33},{2,10},{3,35},{4,12},{5,37},{6,14},{7,39},{8,16},{9,4... | collective-permute-start | bytes 1843208 | tf_op jit(solution)/shard_map/ppermute | solution.py:287
  96.0 27.0 %collective-permute-start.20 = (bf16[2,400,384]{2,1,0:T(8,128)(2,1)S(1)}, bf16[2,400,384]{2,1,0:T(8,128)(2,1)S(1)}, u32[]{:S(2)}, u32[]{:S(2)}) collective-permute-start(bf16[2,400,384]{2,1,0:T(8,128)(2,1)S(1)} %get-tuple-element.64), channel_id=1, source_target_pairs={{0,24},{1,97},{2,26},{3,99},{4,28},{5,101},{6,30},{7,103},{8,0},{9... | collective-permute-start | bytes 1843208 | tf_op jit(solution)/shard_map/ppermute | solution.py:287
  97.5 16.3 %copy-start.1 = (s32[8]{0:T(128)S(1)}, s32[8]{0:T(128)}, u32[]{:S(2)}) copy-start(s32[8]{0:T(128)} %partner_ref) | copy-start | bytes 100
  97.5 25.5 %collective-permute-start.21 = (bf16[2,400,384]{2,1,0:T(8,128)(2,1)S(1)}, bf16[2,400,384]{2,1,0:T(8,128)(2,1)S(1)}, u32[]{:S(2)}, u32[]{:S(2)}) collective-permute-start(bf16[2,400,384]{2,1,0:T(8,128)(2,1)S(1)} %get-tuple-element.65), channel_id=1, source_target_pairs={{0,16},{1,65},{2,18},{3,67},{4,20},{5,69},{6,22},{7,71},{8,24},{9,... | collective-permute-start | bytes 1843208 | tf_op jit(solution)/shard_map/ppermute | solution.py:287
where the time goes:
time: 127 us; the launch traced here: 125 us
  waiting for transfers between devices  61.8 us (49%)
  starting transfers between devices  38.3 us (30%)
  Pallas kernels  21 us (17%)
  other arithmetic  2.94 us (2%)
    ppermute x22, waiting for transfers between devices, permuted(): return lax.ppermute(value, ('sx', 'sy'), pairs)  61.8 us
    ppermute x22, starting transfers between devices, permuted(): return lax.ppermute(value, ('sx', 'sy'), pairs)  38.3 us
    pallas_call x1, Pallas kernels, left_products(): pl.pallas_call(left_kernel, in_specs=[hbm] * 4, out_specs=[hbm] * len(siz...  9.69 us
    pallas_call x1, Pallas kernels, pair_products(): pl.pallas_call(pair_kernel, in_specs=[smem] + [hbm] * 8, out_specs=hbm, o...  9.21 us
  transfers between devices with their start and end apart: 22, of which 9 were waited for; matrix products, arithmetic and copies ran while one was open for 2% of the time, Pallas kernels for 15%

commit v1 on v0

--- a/solution.py
+++ b/solution.py
@@ -320,27 +320,26 @@
     barrier = lax.optimization_barrier
 
     moved = [first(own, -1), first(own, 2), first(own, 1)]
+    ring1, ring2 = turn(own, 1), turn(own, -1)
     kept = jnp.stack([own] + moved)
     left, (up, down, pass_up, pass_down, here), z_other, z_mine = left_products(own, coupling, partner, counts)
-    kept, up, down, z_other, own_z = barrier((kept, up, down, z_other, own))
+    kept, ring1, ring2, up, down, z_other, own_z = barrier((kept, ring1, ring2, up, down, z_other, own))
 
     got = [first(up, 1), first(down, -1)]
-    ring = [second(kept, -1), second(kept, 1)]
-    ring1 = turn(own_z, 1)
-    ring2 = turn(after(own_z, ring1), -1)
-    ring3 = turn(after(own_z, ring2), 2)
+    near, far = second(kept, -1), second(kept, 1)
+    ring3 = turn(own_z, 2)
     ring_mine = jnp.stack([own, ring1, ring2, ring3])
+    pair_sum = swap(z_other)
+    got, near, far, ring_mine, pair_sum = barrier((got, near, far, ring_mine, pair_sum))
+    got_up, got_down = got
+
+    last = [first(rounded(pass_up, got_up[:2]), 1), first(rounded(pass_down, got_down[:2]), -1)]
+    low, high = second(near[:2], -1), second(far[2:], 1)
     ring_other = swap(ring_mine)
-    got, ring, ring_other, z_other = barrier((got, ring, ring_other, z_other))
-    (got_up, got_down), (near, far) = got, ring
-
-    last = [first(rounded(pass_up, got_up[:2]), 1), first(rounded(pass_down, got_down[:2]), -1)]
-    relay = [second(near[:2], -1), second(far[2:], 1)]
-    pair_sum = swap(z_other)
     w = [rounded(z_mine[k], pair_sum[k]) for k in range(SIDE)]
     z1 = turn(w[1], 1)
-    last, relay, w, z1 = barrier((last, relay, w, z1))
-    (last_up, last_down), (low, high) = last, relay
+    last, low, high, ring_other, w, z1 = barrier((last, low, high, ring_other, w, z1))
+    last_up, last_down = last
 
     v = [
         rounded(here[0], got_down[2], last_up[0]),
@@ -348,11 +347,13 @@
         rounded(here[2], got_up[2], last_down[0]),
         rounded(here[3], got_up[3], last_down[1]),
     ]
+    v, w = barrier((v, w))
+    z3, z2 = turn(w[3], 2), turn(w[2], -1)
     ends = [second(v[1], 1), second(v[3], -1), second(v[2], 2)]
-    z2, z3 = turn(w[2], -1), turn(w[3], 2)
 
     sources = [kept, near, far, low, high, ring_mine, ring_other]
     pair_blocks = pair_products(left, sources, after(partner, *v))
+    pair_blocks, z2, z3, ends = barrier((pair_blocks, z2, z3, ends))
     partner_blocks = partner_products(own, added(v[0], w[0], z1, z2, z3), ends)
     return (pair_blocks, partner_blocks[None])
 

time: 127 us -> 122 us (0.961)
  starting transfers between devices: 38.3 us -> 33 us
  waiting for transfers between devices: 61.8 us -> 60.1 us
    ppermute x22, starting transfers between devices: 38.3 us -> 33 us  [permuted(): return lax.ppermute(value, ('sx', 'sy'), pairs)]
    ppermute x22, waiting for transfers between devices: 61.8 us -> 60.1 us  [permuted(): return lax.ppermute(value, ('sx', 'sy'), pairs)]
  transfers between devices with their start and end apart: 22 -> 22, of which waited for: 9 -> 11; matrix products, arithmetic and copies ran while one was open for 2% -> 2% of each run, Pallas kernels for 15% -> 16%
where the time goes in v1:
time: 122 us; the launch traced here: 120 us
  waiting for transfers between devices  60.1 us (49%)
  starting transfers between devices  33 us (27%)
  Pallas kernels  21.7 us (18%)
  other arithmetic  3.04 us (2%)
    ppermute x22, waiting for transfers between devices, permuted(): return lax.ppermute(value, ('sx', 'sy'), pairs)  60.1 us
    ppermute x22, starting transfers between devices, permuted(): return lax.ppermute(value, ('sx', 'sy'), pairs)  33 us
    pallas_call x1, Pallas kernels, left_products(): pl.pallas_call(left_kernel, in_specs=[hbm] * 4, out_specs=[hbm] * len(siz...  10.4 us
    pallas_call x1, Pallas kernels, pair_products(): pl.pallas_call(pair_kernel, in_specs=[smem] + [hbm] * 8, out_specs=hbm, o...  9.22 us
  transfers between devices with their start and end apart: 22, of which 11 were waited for; matrix products, arithmetic and copies ran while one was open for 2% of the time, Pallas kernels for 16%

profile of v1, /device:TPU:0, one launch (start us, length us, event | category | flops | bytes accessed | tf_op | source)
XLA Modules:
  0.0 119.7 jit_solution(10165736326528984365)
XLA Ops:
  0.6 1.6 %collective-permute-start.2 = (bf16[400,384]{1,0:T(8,128)(2,1)}, bf16[400,384]{1,0:T(8,128)(2,1)S(1)}, u32[]{:S(2)}, u32[]{:S(2)}) collective-permute-start(bf16[400,384]{1,0:T(8,128)(2,1)} %bitcast.28), channel_id=1, source_target_pairs={{0,32},{1,9},{2,34},{3,11},{4,36},{5,13},{6,38},{7,15},{8,40},{9,1... | collective-permute-start | bytes 921608 | tf_op jit(solution)/shard_map/ppermute | solution.py:287
  2.3 2.7 %collective-permute-start.1 = (bf16[400,384]{1,0:T(8,128)(2,1)}, bf16[400,384]{1,0:T(8,128)(2,1)S(1)}, u32[]{:S(2)}, u32[]{:S(2)}) collective-permute-start(bf16[400,384]{1,0:T(8,128)(2,1)} %bitcast.29), channel_id=1, source_target_pairs={{0,64},{1,17},{2,66},{3,19},{4,68},{5,21},{6,70},{7,23},{8,72},{9,... | collective-permute-start | bytes 921608 | tf_op jit(solution)/shard_map/ppermute | solution.py:287
  5.0 1.4 %collective-permute-start = (bf16[400,384]{1,0:T(8,128)(2,1)}, bf16[400,384]{1,0:T(8,128)(2,1)S(1)}, u32[]{:S(2)}, u32[]{:S(2)}) collective-permute-start(bf16[400,384]{1,0:T(8,128)(2,1)} %bitcast.30), channel_id=1, source_target_pairs={{0,96},{1,25},{2,98},{3,27},{4,100},{5,29},{6,102},{7,31},{8,104},... | collective-permute-start | bytes 921608 | tf_op jit(solution)/shard_map/ppermute | solution.py:287
  6.4 4.0 %collective-permute-start.4 = (bf16[400,384]{1,0:T(8,128)(2,1)}, bf16[400,384]{1,0:T(8,128)(2,1)S(1)}, u32[]{:S(2)}, u32[]{:S(2)}) collective-permute-start(bf16[400,384]{1,0:T(8,128)(2,1)} %bitcast.31), channel_id=1, source_target_pairs={{0,6},{1,3},{2,0},{3,5},{4,2},{5,7},{6,4},{7,1},{8,14},{9,11},{10,... | collective-permute-start | bytes 921608 | tf_op jit(solution)/shard_map/ppermute | solution.py:287
  10.5 10.4 %shard_map.59 = (bf16[8,2,400,384]{3,2,1,0:T(8,128)(2,1)}, bf16[4,2,400,384]{3,2,1,0:T(8,128)(2,1)}, bf16[4,2,400,384]{3,2,1,0:T(8,128)(2,1)}, bf16[2,2,400,384]...) custom-call(s32[8]{0:T(128)} %partner_ref, ...), custom_call_target="tpu_custom_call" | custom-call | flops 1887436800 | bytes 25000000 | tf_op jit(solution)/shard_map/pallas_call | solution.py:156
  20.9 0.0 collective-permute-done.2
  20.9 0.0 collective-permute-done.1
  20.9 0.2 fusion.1.rest_0_
  21.1 0.0 collective-permute-done.3
  21.1 0.1 collective-permute-start.5
  21.2 3.2 %collective-permute-start.6 = (bf16[4,2,400,384]{3,2,1,0:T(8,128)(2,1)}, bf16[4,2,400,384]{3,2,1,0:T(8,128)(2,1)S(1)}, u32[]{:S(2)}, u32[]{:S(2)}) collective-permute-start(bf16[4,2,400,384]{3,2,1,0:T(8,128)(2,1)} %get-tuple-element.51), channel_id=1, source_target_pairs={{0,96},{1,25},{2,98},{3,27},{4,100},{5,29},{6,102},{7,31},{8,104},... | collective-permute-start | bytes 7372808 | tf_op jit(solution)/shard_map/ppermute | solution.py:287
  24.5 1.7 %collective-permute-start.9 = (bf16[400,384]{1,0:T(8,128)(2,1)S(1)}, bf16[400,384]{1,0:T(8,128)(2,1)S(1)}, u32[]{:S(2)}, u32[]{:S(2)}) collective-permute-start(bf16[400,384]{1,0:T(8,128)(2,1)S(1)} %bitcast.35), channel_id=1, source_target_pairs={{0,4},{1,5},{2,6},{3,7},{4,0},{5,1},{6,2},{7,3},{8,12},{9,13},{10,... | collective-permute-start | bytes 921608 | tf_op jit(solution)/shard_map/ppermute | solution.py:287
  26.1 1.1 collective-permute-start.8
  27.2 8.4 %collective-permute-done.9 = bf16[400,384]{1,0:T(8,128)(2,1)S(1)} collective-permute-done((bf16[400,384]{1,0:T(8,128)(2,1)S(1)}, bf16[400,384]{1,0:T(8,128)(2,1)S(1)}, u32[]{:S(2)}, u32[]{:S(2)}) %collective-permute-start.9) | collective-permute-done | bytes 307232 | tf_op jit(solution)/shard_map/ppermute | solution.py:287
  35.6 3.0 %collective-permute-start.7 = (bf16[4,400,384]{2,1,0:T(8,128)(2,1)S(1)}, bf16[4,400,384]{2,1,0:T(8,128)(2,1)S(1)}, u32[]{:S(2)}, u32[]{:S(2)}) collective-permute-start(bf16[4,400,384]{2,1,0:T(8,128)(2,1)S(1)} %fusion.1.rest_0_), channel_id=1, source_target_pairs={{0,24},{1,97},{2,26},{3,99},{4,28},{5,101},{6,30},{7,103},{8,0},{9... | collective-permute-start | bytes 3686408 | tf_op jit(solution)/shard_map/ppermute | solution.py:287
  38.7 0.2 fusion.3.rest_5_
  38.9 0.0 copy-start.9
  38.9 18.4 %collective-permute-done.8.rest_2_ = bf16[4,400,384]{2,1,0:T(8,128)(2,1)S(1)} collective-permute-done((bf16[4,400,384]{2,1,0:T(8,128)(2,1)S(1)}, bf16[4,400,384]{2,1,0:T(8,128)(2,1)S(1)}, u32[]{:S(2)}, u32[]{:S(2)}) %collective-permute-start.8) | collective-permute-done | bytes 1228832 | tf_op jit(solution)/shard_map/ppermute | solution.py:287
  57.3 5.8 %collective-permute-done.7.rest_1_ = bf16[4,400,384]{2,1,0:T(8,128)(2,1)S(1)} collective-permute-done((bf16[4,400,384]{2,1,0:T(8,128)(2,1)S(1)}, bf16[4,400,384]{2,1,0:T(8,128)(2,1)S(1)}, u32[]{:S(2)}, u32[]{:S(2)}) %collective-permute-start.7) | collective-permute-done | bytes 1228832 | tf_op jit(solution)/shard_map/ppermute | solution.py:287
  63.1 2.6 %collective-permute-done.5 = bf16[4,2,400,384]{3,2,1,0:T(8,128)(2,1)S(1)} collective-permute-done((bf16[4,2,400,384]{3,2,1,0:T(8,128)(2,1)}, bf16[4,2,400,384]{3,2,1,0:T(8,128)(2,1)S(1)}, u32[]{:S(2)}, u32[]{:S(2)}) %collective-permute-start.5) | collective-permute-done | bytes 2457632 | tf_op jit(solution)/shard_map/ppermute | solution.py:287
  65.7 0.1 slice.77
  65.8 1.6 %collective-permute-start.14 = (bf16[2,400,384]{2,1,0:T(8,128)(2,1)S(1)}, bf16[2,400,384]{2,1,0:T(8,128)(2,1)S(1)}, u32[]{:S(2)}, u32[]{:S(2)}) collective-permute-start(bf16[2,400,384]{2,1,0:T(8,128)(2,1)S(1)} %slice.77), channel_id=1, source_target_pairs={{0,8},{1,33},{2,10},{3,35},{4,12},{5,37},{6,14},{7,39},{8,16},{9,4... | collective-permute-start | bytes 1843208 | tf_op jit(solution)/shard_map/ppermute | solution.py:287
  67.4 0.3 add_convert_fusion.1
  67.8 0.1 collective-permute-start.11
  67.9 0.9 copy-done.8
  68.7 0.3 add_convert_fusion
  69.0 3.3 %collective-permute-start.12 = (bf16[2,2,400,384]{3,2,1,0:T(8,128)(2,1)S(1)}, bf16[2,2,400,384]{3,2,1,0:T(8,128)(2,1)S(1)}, u32[]{:S(2)}, u32[]{:S(2)}) collective-permute-start(bf16[2,2,400,384]{3,2,1,0:T(8,128)(2,1)S(1)} %add_convert_fusion), channel_id=1, source_target_pairs={{0,96},{1,25},{2,98},{3,27},{4,100},{5,29},{6,102},{7,31},{8,104},... | collective-permute-start | bytes 3686408 | tf_op jit(solution)/shard_map/ppermute | solution.py:287
  72.4 0.1 slice.76
  72.4 1.7 %collective-permute-start.13 = (bf16[2,400,384]{2,1,0:T(8,128)(2,1)S(1)}, bf16[2,400,384]{2,1,0:T(8,128)(2,1)S(1)}, u32[]{:S(2)}, u32[]{:S(2)}) collective-permute-start(bf16[2,400,384]{2,1,0:T(8,128)(2,1)S(1)} %slice.76), channel_id=1, source_target_pairs={{0,24},{1,97},{2,26},{3,99},{4,28},{5,101},{6,30},{7,103},{8,0},{9... | collective-permute-start | bytes 1843208 | tf_op jit(solution)/shard_map/ppermute | solution.py:287
  74.2 0.7 fusion.7
  74.9 8.9 %collective-permute-done.14.rest_4_ = bf16[2,400,384]{2,1,0:T(8,128)(2,1)S(1)} collective-permute-done((bf16[2,400,384]{2,1,0:T(8,128)(2,1)S(1)}, bf16[2,400,384]{2,1,0:T(8,128)(2,1)S(1)}, u32[]{:S(2)}, u32[]{:S(2)}) %collective-permute-start.14) | collective-permute-done | bytes 614432 | tf_op jit(solution)/shard_map/ppermute | solution.py:287
  83.8 5.5 %collective-permute-done.13.rest_3_ = bf16[2,400,384]{2,1,0:T(8,128)(2,1)S(1)} collective-permute-done((bf16[2,400,384]{2,1,0:T(8,128)(2,1)S(1)}, bf16[2,400,384]{2,1,0:T(8,128)(2,1)S(1)}, u32[]{:S(2)}, u32[]{:S(2)}) %collective-permute-start.13) | collective-permute-done | bytes 614432 | tf_op jit(solution)/shard_map/ppermute | solution.py:287
  89.3 5.9 %collective-permute-done.16 = bf16[2,400,384]{2,1,0:T(8,128)(2,1)S(1)} collective-permute-done((bf16[2,400,384]{2,1,0:T(8,128)(2,1)S(1)}, bf16[2,400,384]{2,1,0:T(8,128)(2,1)S(1)}, u32[]{:S(2)}, u32[]{:S(2)}) %collective-permute-start.16) | collective-permute-done | bytes 614432 | tf_op jit(solution)/shard_map/ppermute | solution.py:287
  95.2 0.0 copy-start.10
  95.2 0.0 copy-start.1
  95.2 0.9 fusion.11
  96.2 0.0 copy-done.10
  96.2 2.2 %collective-permute-start.17 = (bf16[2,400,384]{2,1,0:T(8,128)(2,1)S(1)}, bf16[2,400,384]{2,1,0:T(8,128)(2,1)S(1)}, u32[]{:S(2)}, u32[]{:S(2)}) collective-permute-start(bf16[2,400,384]{2,1,0:T(8,128)(2,1)S(1)} %get-tuple-element.80), channel_id=1, source_target_pairs={{0,6},{1,3},{2,0},{3,5},{4,2},{5,7},{6,4},{7,1},{8,14},{9,11},{10,... | collective-permute-start | bytes 1843208 | tf_op jit(solution)/shard_map/ppermute | solution.py:287
  98.5 1.2 %collective-permute-start.19 = (bf16[2,400,384]{2,1,0:T(8,128)(2,1)S(1)}, bf16[2,400,384]{2,1,0:T(8,128)(2,1)S(1)}, u32[]{:S(2)}, u32[]{:S(2)}) collective-permute-start(bf16[2,400,384]{2,1,0:T(8,128)(2,1)S(1)} %get-tuple-element.72), channel_id=1, source_target_pairs={{0,8},{1,33},{2,10},{3,35},{4,12},{5,37},{6,14},{7,39},{8,16},{9,4... | collective-permute-start | bytes 1843208 | tf_op jit(solution)/shard_map/ppermute | solution.py:287
  99.7 1.9 %collective-permute-start.21 = (bf16[2,400,384]{2,1,0:T(8,128)(2,1)S(1)}, bf16[2,400,384]{2,1,0:T(8,128)(2,1)S(1)}, u32[]{:S(2)}, u32[]{:S(2)}) collective-permute-start(bf16[2,400,384]{2,1,0:T(8,128)(2,1)S(1)} %get-tuple-element.73), channel_id=1, source_target_pairs={{0,16},{1,65},{2,18},{3,67},{4,20},{5,69},{6,22},{7,71},{8,24},{9,... | collective-permute-start | bytes 1843208 | tf_op jit(solution)/shard_map/ppermute | solution.py:287
  101.6 1.9 %collective-permute-start.20 = (bf16[2,400,384]{2,1,0:T(8,128)(2,1)S(1)}, bf16[2,400,384]{2,1,0:T(8,128)(2,1)S(1)}, u32[]{:S(2)}, u32[]{:S(2)}) collective-permute-start(bf16[2,400,384]{2,1,0:T(8,128)(2,1)S(1)} %get-tuple-element.74), channel_id=1, source_target_pairs={{0,24},{1,97},{2,26},{3,99},{4,28},{5,101},{6,30},{7,103},{8,0},{9... | collective-permute-start | bytes 1843208 | tf_op jit(solution)/shard_map/ppermute | solution.py:287
  103.5 9.2 %shard_map.60 = bf16[8,2,400,400]{3,2,1,0:T(8,128)(2,1)} custom-call(s32[8]{0:T(128)S(1)} %copy-done.1, bf16[8,2,400,384]{3,2,1,0:T(8,128)(2,1)} %get-tuple-element.76.left_hbm, bf16[4,400,384]{2,1,0:T(8,128)(2,1)} %copy-done.2, bf16[4,400,384]{2,1,0:T(8,128)(2,1)} %copy-done.5, bf16[4,400,384]{2,1,0:T(8,128)(2,1)} %copy-done.4, ...), custom_call_target="tpu_custom_call" | custom-call | flops 1966080000 | bytes 15000000 | tf_op jit(solution)/shard_map/pallas_call | solution.py:241
  112.8 1.9 %collective-permute-done.17 = bf16[2,400,384]{2,1,0:T(8,128)(2,1)S(1)} collective-permute-done((bf16[2,400,384]{2,1,0:T(8,128)(2,1)S(1)}, bf16[2,400,384]{2,1,0:T(8,128)(2,1)S(1)}, u32[]{:S(2)}, u32[]{:S(2)}) %collective-permute-start.17) | collective-permute-done | bytes 614432 | tf_op jit(solution)/shard_map/ppermute | solution.py:287
  114.7 1.5 %collective-permute-done.18 = bf16[2,400,384]{2,1,0:T(8,128)(2,1)S(1)} collective-permute-done((bf16[2,400,384]{2,1,0:T(8,128)(2,1)S(1)}, bf16[2,400,384]{2,1,0:T(8,128)(2,1)S(1)}, u32[]{:S(2)}, u32[]{:S(2)}) %collective-permute-start.18) | collective-permute-done | bytes 614432 | tf_op jit(solution)/shard_map/ppermute | solution.py:287
  116.2 0.2 collective-permute-done.21.rest_2_
  116.4 0.9 collective-permute-done.20.rest_1_
  117.3 0.4 convert_add_fusion.sum_ref
  117.7 2.1 %shard_map.61 = f32[2,400,400]{2,1,0:T(8,128)} custom-call(bf16[400,384]{1,0:T(8,128)(2,1)S(1)} %bitcast.37, f32[2,400,384]{2,1,0:T(8,128)S(1)} %convert_add_fusion.sum_ref, bf16[2,400,384]{2,1,0:T(8,128)(2,1)S(1)} %collective-permute-done.19.rest_0_, bf16[2,400,384]{2,1,0:T(8,128)(2,1)S(1)} %collective-permute-done.20.rest_1_, ...), custom_call_target="tpu_custom_call" | custom-call | tf_op jit(solution)/shard_map/pallas_call | solution.py:274
  (36 shorter events, 0.1 us)
Async XLA Ops:
  0.6 20.3 %copy-start = (bf16[1,384,400]{1,2,0:T(8,128)(2,1)S(1)}, bf16[1,384,400]{1,2,0:T(8,128)(2,1)}, u32[]{:S(2)}) copy-start(bf16[1,384,400]{1,2,0:T(8,128)(2,1)} %param.4) | copy-start | bytes 921604
  0.6 20.2 %collective-permute-start.2 = (bf16[400,384]{1,0:T(8,128)(2,1)}, bf16[400,384]{1,0:T(8,128)(2,1)S(1)}, u32[]{:S(2)}, u32[]{:S(2)}) collective-permute-start(bf16[400,384]{1,0:T(8,128)(2,1)} %bitcast.28), channel_id=1, source_target_pairs={{0,32},{1,9},{2,34},{3,11},{4,36},{5,13},{6,38},{7,15},{8,40},{9,1... | collective-permute-start | bytes 921608 | tf_op jit(solution)/shard_map/ppermute | solution.py:287
  2.3 18.6 %collective-permute-start.1 = (bf16[400,384]{1,0:T(8,128)(2,1)}, bf16[400,384]{1,0:T(8,128)(2,1)S(1)}, u32[]{:S(2)}, u32[]{:S(2)}) collective-permute-start(bf16[400,384]{1,0:T(8,128)(2,1)} %bitcast.29), channel_id=1, source_target_pairs={{0,64},{1,17},{2,66},{3,19},{4,68},{5,21},{6,70},{7,23},{8,72},{9,... | collective-permute-start | bytes 921608 | tf_op jit(solution)/shard_map/ppermute | solution.py:287
  5.0 15.9 %collective-permute-start = (bf16[400,384]{1,0:T(8,128)(2,1)}, bf16[400,384]{1,0:T(8,128)(2,1)S(1)}, u32[]{:S(2)}, u32[]{:S(2)}) collective-permute-start(bf16[400,384]{1,0:T(8,128)(2,1)} %bitcast.30), channel_id=1, source_target_pairs={{0,96},{1,25},{2,98},{3,27},{4,100},{5,29},{6,102},{7,31},{8,104},... | collective-permute-start | bytes 921608 | tf_op jit(solution)/shard_map/ppermute | solution.py:287
  6.4 14.7 %collective-permute-start.4 = (bf16[400,384]{1,0:T(8,128)(2,1)}, bf16[400,384]{1,0:T(8,128)(2,1)S(1)}, u32[]{:S(2)}, u32[]{:S(2)}) collective-permute-start(bf16[400,384]{1,0:T(8,128)(2,1)} %bitcast.31), channel_id=1, source_target_pairs={{0,6},{1,3},{2,0},{3,5},{4,2},{5,7},{6,4},{7,1},{8,14},{9,11},{10,... | collective-permute-start | bytes 921608 | tf_op jit(solution)/shard_map/ppermute | solution.py:287
  10.5 10.7 %collective-permute-start.3 = (bf16[400,384]{1,0:T(8,128)(2,1)}, bf16[400,384]{1,0:T(8,128)(2,1)S(1)}, u32[]{:S(2)}, u32[]{:S(2)}) collective-permute-start(bf16[400,384]{1,0:T(8,128)(2,1)} %bitcast.32), channel_id=1, source_target_pairs={{0,2},{1,7},{2,4},{3,1},{4,6},{5,3},{6,0},{7,5},{8,10},{9,15},{10,... | collective-permute-start | bytes 921608 | tf_op jit(solution)/shard_map/ppermute | solution.py:287
  20.9 3.5 %copy-start.13 = (bf16[4,2,400,384]{3,2,1,0:T(8,128)(2,1)S(1)}, bf16[4,2,400,384]{3,2,1,0:T(8,128)(2,1)}, u32[]{:S(2)}) copy-start(bf16[4,2,400,384]{3,2,1,0:T(8,128)(2,1)} %get-tuple-element.56) | copy-start | bytes 7372804
  21.1 17.7 %copy-start.2 = (bf16[4,400,384]{2,1,0:T(8,128)(2,1)}, bf16[4,400,384]{2,1,0:T(8,128)(2,1)S(1)}, u32[]{:S(2)}) copy-start(bf16[4,400,384]{2,1,0:T(8,128)(2,1)S(1)} %fusion.1.rest_0_) | copy-start | bytes 3686404
  21.1 44.6 %collective-permute-start.5 = (bf16[4,2,400,384]{3,2,1,0:T(8,128)(2,1)}, bf16[4,2,400,384]{3,2,1,0:T(8,128)(2,1)S(1)}, u32[]{:S(2)}, u32[]{:S(2)}) collective-permute-start(bf16[4,2,400,384]{3,2,1,0:T(8,128)(2,1)} %get-tuple-element.50), channel_id=1, source_target_pairs={{0,32},{1,9},{2,34},{3,11},{4,36},{5,13},{6,38},{7,15},{8,40},{9,1... | collective-permute-start | bytes 7372808 | tf_op jit(solution)/shard_map/ppermute | solution.py:287
  21.2 44.5 %collective-permute-start.6 = (bf16[4,2,400,384]{3,2,1,0:T(8,128)(2,1)}, bf16[4,2,400,384]{3,2,1,0:T(8,128)(2,1)S(1)}, u32[]{:S(2)}, u32[]{:S(2)}) collective-permute-start(bf16[4,2,400,384]{3,2,1,0:T(8,128)(2,1)} %get-tuple-element.51), channel_id=1, source_target_pairs={{0,96},{1,25},{2,98},{3,27},{4,100},{5,29},{6,102},{7,31},{8,104},... | collective-permute-start | bytes 7372808 | tf_op jit(solution)/shard_map/ppermute | solution.py:287
  24.5 41.2 %collective-permute-start.10 = (bf16[4,2,400,384]{3,2,1,0:T(8,128)(2,1)S(1)}, bf16[4,2,400,384]{3,2,1,0:T(8,128)(2,1)S(1)}, u32[]{:S(2)}, u32[]{:S(2)}) collective-permute-start(bf16[4,2,400,384]{3,2,1,0:T(8,128)(2,1)S(1)} %copy-done.13), channel_id=1, source_target_pairs={{0,1},{1,0},{2,3},{3,2},{4,5},{5,4},{6,7},{7,6},{8,9},{9,8},{10,11... | collective-permute-start | bytes 7372808 | tf_op jit(solution)/shard_map/ppermute | solution.py:287
  24.5 11.2 %collective-permute-start.9 = (bf16[400,384]{1,0:T(8,128)(2,1)S(1)}, bf16[400,384]{1,0:T(8,128)(2,1)S(1)}, u32[]{:S(2)}, u32[]{:S(2)}) collective-permute-start(bf16[400,384]{1,0:T(8,128)(2,1)S(1)} %bitcast.35), channel_id=1, source_target_pairs={{0,4},{1,5},{2,6},{3,7},{4,0},{5,1},{6,2},{7,3},{8,12},{9,13},{10,... | collective-permute-start | bytes 921608 | tf_op jit(solution)/shard_map/ppermute | solution.py:287
  26.1 31.2 %collective-permute-start.8 = (bf16[4,400,384]{2,1,0:T(8,128)(2,1)S(1)}, bf16[4,400,384]{2,1,0:T(8,128)(2,1)S(1)}, u32[]{:S(2)}, u32[]{:S(2)}) collective-permute-start(bf16[4,400,384]{2,1,0:T(8,128)(2,1)S(1)} %fusion.1.rest_0_), channel_id=1, source_target_pairs={{0,8},{1,33},{2,10},{3,35},{4,12},{5,37},{6,14},{7,39},{8,16},{9,4... | collective-permute-start | bytes 3686408 | tf_op jit(solution)/shard_map/ppermute | solution.py:287
  35.6 27.5 %collective-permute-start.7 = (bf16[4,400,384]{2,1,0:T(8,128)(2,1)S(1)}, bf16[4,400,384]{2,1,0:T(8,128)(2,1)S(1)}, u32[]{:S(2)}, u32[]{:S(2)}) collective-permute-start(bf16[4,400,384]{2,1,0:T(8,128)(2,1)S(1)} %fusion.1.rest_0_), channel_id=1, source_target_pairs={{0,24},{1,97},{2,26},{3,99},{4,28},{5,101},{6,30},{7,103},{8,0},{9... | collective-permute-start | bytes 3686408 | tf_op jit(solution)/shard_map/ppermute | solution.py:287
  38.9 33.5 %copy-start.3 = (bf16[4,400,384]{2,1,0:T(8,128)(2,1)}, bf16[4,400,384]{2,1,0:T(8,128)(2,1)S(1)}, u32[]{:S(2)}) copy-start(bf16[4,400,384]{2,1,0:T(8,128)(2,1)S(1)} %fusion.3.rest_5_) | copy-start | bytes 3686404
  38.9 28.5 %copy-start.9 = (bf16[2,2,400,384]{3,2,1,0:T(8,128)(2,1)S(1)}, bf16[2,2,400,384]{3,2,1,0:T(8,128)(2,1)}, u32[]{:S(2)}) copy-start(bf16[2,2,400,384]{3,2,1,0:T(8,128)(2,1)} %get-tuple-element.58) | copy-start | bytes 3686404
  57.3 10.5 %copy-start.4 = (bf16[4,400,384]{2,1,0:T(8,128)(2,1)}, bf16[4,400,384]{2,1,0:T(8,128)(2,1)S(1)}, u32[]{:S(2)}) copy-start(bf16[4,400,384]{2,1,0:T(8,128)(2,1)S(1)} %collective-permute-done.8.rest_2_) | copy-start | bytes 3686404
  63.1 9.2 %copy-start.5 = (bf16[4,400,384]{2,1,0:T(8,128)(2,1)}, bf16[4,400,384]{2,1,0:T(8,128)(2,1)S(1)}, u32[]{:S(2)}) copy-start(bf16[4,400,384]{2,1,0:T(8,128)(2,1)S(1)} %collective-permute-done.7.rest_1_) | copy-start | bytes 3686404
  65.8 18.0 %collective-permute-start.14 = (bf16[2,400,384]{2,1,0:T(8,128)(2,1)S(1)}, bf16[2,400,384]{2,1,0:T(8,128)(2,1)S(1)}, u32[]{:S(2)}, u32[]{:S(2)}) collective-permute-start(bf16[2,400,384]{2,1,0:T(8,128)(2,1)S(1)} %slice.77), channel_id=1, source_target_pairs={{0,8},{1,33},{2,10},{3,35},{4,12},{5,37},{6,14},{7,39},{8,16},{9,4... | collective-permute-start | bytes 1843208 | tf_op jit(solution)/shard_map/ppermute | solution.py:287
  67.4 1.3 %copy-start.8 = (bf16[2,2,400,384]{3,2,1,0:T(8,128)(2,1)S(1)}, bf16[2,2,400,384]{3,2,1,0:T(8,128)(2,1)}, u32[]{:S(2)}) copy-start(bf16[2,2,400,384]{3,2,1,0:T(8,128)(2,1)} %get-tuple-element.60) | copy-start | bytes 3686404
  67.8 27.4 %collective-permute-start.11 = (bf16[2,2,400,384]{3,2,1,0:T(8,128)(2,1)S(1)}, bf16[2,2,400,384]{3,2,1,0:T(8,128)(2,1)S(1)}, u32[]{:S(2)}, u32[]{:S(2)}) collective-permute-start(bf16[2,2,400,384]{3,2,1,0:T(8,128)(2,1)S(1)} %add_convert_fusion.1), channel_id=1, source_target_pairs={{0,32},{1,9},{2,34},{3,11},{4,36},{5,13},{6,38},{7,15},{8,40},{9,1... | collective-permute-start | bytes 3686408 | tf_op jit(solution)/shard_map/ppermute | solution.py:287
  68.7 5.5 %copy-start.6 = (bf16[4,2,400,384]{3,2,1,0:T(8,128)(2,1)S(1)}, bf16[4,2,400,384]{3,2,1,0:T(8,128)(2,1)}, u32[]{:S(2)}) copy-start(bf16[4,2,400,384]{3,2,1,0:T(8,128)(2,1)} %get-tuple-element.64) | copy-start | bytes 7372804
  69.0 26.1 %collective-permute-start.12 = (bf16[2,2,400,384]{3,2,1,0:T(8,128)(2,1)S(1)}, bf16[2,2,400,384]{3,2,1,0:T(8,128)(2,1)S(1)}, u32[]{:S(2)}, u32[]{:S(2)}) collective-permute-start(bf16[2,2,400,384]{3,2,1,0:T(8,128)(2,1)S(1)} %add_convert_fusion), channel_id=1, source_target_pairs={{0,96},{1,25},{2,98},{3,27},{4,100},{5,29},{6,102},{7,31},{8,104},... | collective-permute-start | bytes 3686408 | tf_op jit(solution)/shard_map/ppermute | solution.py:287
  72.4 22.8 %collective-permute-start.15 = (bf16[4,400,384]{2,1,0:T(8,128)(2,1)S(1)}, bf16[4,400,384]{2,1,0:T(8,128)(2,1)S(1)}, u32[]{:S(2)}, u32[]{:S(2)}) collective-permute-start(bf16[4,400,384]{2,1,0:T(8,128)(2,1)S(1)} %fusion.3.rest_5_), channel_id=1, source_target_pairs={{0,1},{1,0},{2,3},{3,2},{4,5},{5,4},{6,7},{7,6},{8,9},{9,8},{10,11... | collective-permute-start | bytes 3686408 | tf_op jit(solution)/shard_map/ppermute | solution.py:287
  72.4 16.9 %collective-permute-start.13 = (bf16[2,400,384]{2,1,0:T(8,128)(2,1)S(1)}, bf16[2,400,384]{2,1,0:T(8,128)(2,1)S(1)}, u32[]{:S(2)}, u32[]{:S(2)}) collective-permute-start(bf16[2,400,384]{2,1,0:T(8,128)(2,1)S(1)} %slice.76), channel_id=1, source_target_pairs={{0,24},{1,97},{2,26},{3,99},{4,28},{5,101},{6,30},{7,103},{8,0},{9... | collective-permute-start | bytes 1843208 | tf_op jit(solution)/shard_map/ppermute | solution.py:287
  74.2 21.0 %copy-start.7 = (bf16[4,2,400,384]{3,2,1,0:T(8,128)(2,1)S(1)}, bf16[4,2,400,384]{3,2,1,0:T(8,128)(2,1)}, u32[]{:S(2)}) copy-start(bf16[4,2,400,384]{3,2,1,0:T(8,128)(2,1)} %get-tuple-element.46) | copy-start | bytes 7372804
  83.8 12.4 %copy-start.11 = (bf16[2,400,384]{2,1,0:T(8,128)(2,1)}, bf16[2,400,384]{2,1,0:T(8,128)(2,1)S(1)}, u32[]{:S(2)}) copy-start(bf16[2,400,384]{2,1,0:T(8,128)(2,1)S(1)} %collective-permute-done.14.rest_4_) | copy-start | bytes 1843204
  83.8 11.4 %collective-permute-start.16 = (bf16[2,400,384]{2,1,0:T(8,128)(2,1)S(1)}, bf16[2,400,384]{2,1,0:T(8,128)(2,1)S(1)}, u32[]{:S(2)}, u32[]{:S(2)}) collective-permute-start(bf16[2,400,384]{2,1,0:T(8,128)(2,1)S(1)} %get-tuple-element.96), channel_id=1, source_target_pairs={{0,2},{1,7},{2,4},{3,1},{4,6},{5,3},{6,0},{7,5},{8,10},{9,15},{10,... | collective-permute-start | bytes 1843208 | tf_op jit(solution)/shard_map/ppermute | solution.py:287
  89.3 6.9 %copy-start.12 = (bf16[2,400,384]{2,1,0:T(8,128)(2,1)}, bf16[2,400,384]{2,1,0:T(8,128)(2,1)S(1)}, u32[]{:S(2)}) copy-start(bf16[2,400,384]{2,1,0:T(8,128)(2,1)S(1)} %collective-permute-done.13.rest_3_) | copy-start | bytes 1843204
  95.2 1.0 copy-start.10
  95.2 8.3 %copy-start.1 = (s32[8]{0:T(128)S(1)}, s32[8]{0:T(128)}, u32[]{:S(2)}) copy-start(s32[8]{0:T(128)} %partner_ref) | copy-start | bytes 100
  96.2 18.4 %collective-permute-start.17 = (bf16[2,400,384]{2,1,0:T(8,128)(2,1)S(1)}, bf16[2,400,384]{2,1,0:T(8,128)(2,1)S(1)}, u32[]{:S(2)}, u32[]{:S(2)}) collective-permute-start(bf16[2,400,384]{2,1,0:T(8,128)(2,1)S(1)} %get-tuple-element.80), channel_id=1, source_target_pairs={{0,6},{1,3},{2,0},{3,5},{4,2},{5,7},{6,4},{7,1},{8,14},{9,11},{10,... | collective-permute-start | bytes 1843208 | tf_op jit(solution)/shard_map/ppermute | solution.py:287
  98.4 17.7 %collective-permute-start.18 = (bf16[2,400,384]{2,1,0:T(8,128)(2,1)S(1)}, bf16[2,400,384]{2,1,0:T(8,128)(2,1)S(1)}, u32[]{:S(2)}, u32[]{:S(2)}) collective-permute-start(bf16[2,400,384]{2,1,0:T(8,128)(2,1)S(1)} %get-tuple-element.81), channel_id=1, source_target_pairs={{0,4},{1,5},{2,6},{3,7},{4,0},{5,1},{6,2},{7,3},{8,12},{9,13},{10,... | collective-permute-start | bytes 1843208 | tf_op jit(solution)/shard_map/ppermute | solution.py:287
  98.5 17.7 %collective-permute-start.19 = (bf16[2,400,384]{2,1,0:T(8,128)(2,1)S(1)}, bf16[2,400,384]{2,1,0:T(8,128)(2,1)S(1)}, u32[]{:S(2)}, u32[]{:S(2)}) collective-permute-start(bf16[2,400,384]{2,1,0:T(8,128)(2,1)S(1)} %get-tuple-element.72), channel_id=1, source_target_pairs={{0,8},{1,33},{2,10},{3,35},{4,12},{5,37},{6,14},{7,39},{8,16},{9,4... | collective-permute-start | bytes 1843208 | tf_op jit(solution)/shard_map/ppermute | solution.py:287
  99.7 16.7 %collective-permute-start.21 = (bf16[2,400,384]{2,1,0:T(8,128)(2,1)S(1)}, bf16[2,400,384]{2,1,0:T(8,128)(2,1)S(1)}, u32[]{:S(2)}, u32[]{:S(2)}) collective-permute-start(bf16[2,400,384]{2,1,0:T(8,128)(2,1)S(1)} %get-tuple-element.73), channel_id=1, source_target_pairs={{0,16},{1,65},{2,18},{3,67},{4,20},{5,69},{6,22},{7,71},{8,24},{9,... | collective-permute-start | bytes 1843208 | tf_op jit(solution)/shard_map/ppermute | solution.py:287
  101.6 15.7 %collective-permute-start.20 = (bf16[2,400,384]{2,1,0:T(8,128)(2,1)S(1)}, bf16[2,400,384]{2,1,0:T(8,128)(2,1)S(1)}, u32[]{:S(2)}, u32[]{:S(2)}) collective-permute-start(bf16[2,400,384]{2,1,0:T(8,128)(2,1)S(1)} %get-tuple-element.74), channel_id=1, source_target_pairs={{0,24},{1,97},{2,26},{3,99},{4,28},{5,101},{6,30},{7,103},{8,0},{9... | collective-permute-start | bytes 1843208 | tf_op jit(solution)/shard_map/ppermute | solution.py:287

commit v2 on v1

--- a/solution.py
+++ b/solution.py
@@ -330,15 +330,19 @@
     ring3 = turn(own_z, 2)
     ring_mine = jnp.stack([own, ring1, ring2, ring3])
     pair_sum = swap(z_other)
-    got, near, far, ring_mine, pair_sum = barrier((got, near, far, ring_mine, pair_sum))
+    w = [rounded(z_mine[k], pair_sum[k]) for k in range(SIDE)]
+    z1 = turn(w[1], 1)
+    got, near, far, ring_mine, w, z1 = barrier((got, near, far, ring_mine, w, z1))
     got_up, got_down = got
 
-    last = [first(rounded(pass_up, got_up[:2]), 1), first(rounded(pass_down, got_down[:2]), -1)]
+    b_up, b_down = rounded(pass_up, got_up[:2]), rounded(pass_down, got_down[:2])
+    b_up, b_down, near, far, ring_mine, w = barrier((b_up, b_down, near, far, ring_mine, w))
+    last = [first(b_up, 1), first(b_down, -1)]
     low, high = second(near[:2], -1), second(far[2:], 1)
     ring_other = swap(ring_mine)
-    w = [rounded(z_mine[k], pair_sum[k]) for k in range(SIDE)]
-    z1 = turn(w[1], 1)
-    last, low, high, ring_other, w, z1 = barrier((last, low, high, ring_other, w, z1))
+    z2 = turn(w[2], -1)
+    z3 = turn(after(w[3], z2), 2)
+    last, low, high, ring_other, z2, z3 = barrier((last, low, high, ring_other, z2, z3))
     last_up, last_down = last
 
     v = [
@@ -347,13 +351,11 @@
         rounded(here[2], got_up[2], last_down[0]),
         rounded(here[3], got_up[3], last_down[1]),
     ]
-    v, w = barrier((v, w))
-    z3, z2 = turn(w[3], 2), turn(w[2], -1)
     ends = [second(v[1], 1), second(v[3], -1), second(v[2], 2)]
 
     sources = [kept, near, far, low, high, ring_mine, ring_other]
     pair_blocks = pair_products(left, sources, after(partner, *v))
-    pair_blocks, z2, z3, ends = barrier((pair_blocks, z2, z3, ends))
+    pair_blocks, ends = barrier((pair_blocks, ends))
     partner_blocks = partner_products(own, added(v[0], w[0], z1, z2, z3), ends)
     return (pair_blocks, partner_blocks[None])
 

time: 122 us -> 120 us (0.984); the launches traced: 120 us -> 120 us
  transfers between devices with their start and end apart: 22 -> 22, of which waited for: 11 -> 11; matrix products, arithmetic and copies ran while one was open for 2% -> 1% of each run, Pallas kernels for 16% -> 16%
where the time goes in v2:
time: 120 us
  waiting for transfers between devices  60.7 us (51%)
  starting transfers between devices  33 us (28%)
  Pallas kernels  21.6 us (18%)
  other arithmetic  2.95 us (2%)
    ppermute x22, waiting for transfers between devices, permuted(): return lax.ppermute(value, ('sx', 'sy'), pairs)  60.7 us
    ppermute x22, starting transfers between devices, permuted(): return lax.ppermute(value, ('sx', 'sy'), pairs)  33 us
    pallas_call x1, Pallas kernels, left_products(): pl.pallas_call(left_kernel, in_specs=[hbm] * 4, out_specs=[hbm] * len(siz...  10.4 us
    pallas_call x1, Pallas kernels, pair_products(): pl.pallas_call(pair_kernel, in_specs=[smem] + [hbm] * 8, out_specs=hbm, o...  9.21 us
  transfers between devices with their start and end apart: 22, of which 11 were waited for; matrix products, arithmetic and copies ran while one was open for 1% of the time, Pallas kernels for 16%

profile of v2, /device:TPU:0, one launch (start us, length us, event | category | flops | bytes accessed | tf_op | source)
XLA Modules:
  0.0 119.6 jit_solution(12149380836569034232)
XLA Ops:
  0.6 2.9 %collective-permute-start = (bf16[400,384]{1,0:T(8,128)(2,1)}, bf16[400,384]{1,0:T(8,128)(2,1)S(1)}, u32[]{:S(2)}, u32[]{:S(2)}) collective-permute-start(bf16[400,384]{1,0:T(8,128)(2,1)} %bitcast.29), channel_id=1, source_target_pairs={{0,96},{1,25},{2,98},{3,27},{4,100},{5,29},{6,102},{7,31},{8,104},... | collective-permute-start | bytes 921608 | tf_op jit(solution)/shard_map/ppermute | solution.py:287
  3.5 0.8 collective-permute-start.1
  4.4 0.9 collective-permute-start.2
  5.2 1.9 %collective-permute-start.3 = (bf16[400,384]{1,0:T(8,128)(2,1)}, bf16[400,384]{1,0:T(8,128)(2,1)S(1)}, u32[]{:S(2)}, u32[]{:S(2)}) collective-permute-start(bf16[400,384]{1,0:T(8,128)(2,1)} %bitcast.32), channel_id=1, source_target_pairs={{0,2},{1,7},{2,4},{3,1},{4,6},{5,3},{6,0},{7,5},{8,10},{9,15},{10,... | collective-permute-start | bytes 921608 | tf_op jit(solution)/shard_map/ppermute | solution.py:287
  7.2 2.1 %collective-permute-start.4 = (bf16[400,384]{1,0:T(8,128)(2,1)}, bf16[400,384]{1,0:T(8,128)(2,1)S(1)}, u32[]{:S(2)}, u32[]{:S(2)}) collective-permute-start(bf16[400,384]{1,0:T(8,128)(2,1)} %bitcast.33), channel_id=1, source_target_pairs={{0,6},{1,3},{2,0},{3,5},{4,2},{5,7},{6,4},{7,1},{8,14},{9,11},{10,... | collective-permute-start | bytes 921608 | tf_op jit(solution)/shard_map/ppermute | solution.py:287
  9.3 10.4 %shard_map.59 = (bf16[8,2,400,384]{3,2,1,0:T(8,128)(2,1)}, bf16[4,2,400,384]{3,2,1,0:T(8,128)(2,1)}, bf16[4,2,400,384]{3,2,1,0:T(8,128)(2,1)}, bf16[2,2,400,384]...) custom-call(s32[8]{0:T(128)} %partner_ref, ...), custom_call_target="tpu_custom_call" | custom-call | flops 1887436800 | bytes 25000000 | tf_op jit(solution)/shard_map/pallas_call | solution.py:156
  19.7 0.0 collective-permute-done
  19.7 0.0 collective-permute-done.2
  19.7 0.2 fusion.1.rest_0_
  19.9 0.0 collective-permute-done.3
  19.9 0.1 collective-permute-start.10
  20.0 1.7 %collective-permute-start.5 = (bf16[4,2,400,384]{3,2,1,0:T(8,128)(2,1)}, bf16[4,2,400,384]{3,2,1,0:T(8,128)(2,1)S(1)}, u32[]{:S(2)}, u32[]{:S(2)}) collective-permute-start(bf16[4,2,400,384]{3,2,1,0:T(8,128)(2,1)} %get-tuple-element.51), channel_id=1, source_target_pairs={{0,32},{1,9},{2,34},{3,11},{4,36},{5,13},{6,38},{7,15},{8,40},{9,1... | collective-permute-start | bytes 7372808 | tf_op jit(solution)/shard_map/ppermute | solution.py:287
  21.7 1.6 %collective-permute-start.6 = (bf16[4,2,400,384]{3,2,1,0:T(8,128)(2,1)}, bf16[4,2,400,384]{3,2,1,0:T(8,128)(2,1)S(1)}, u32[]{:S(2)}, u32[]{:S(2)}) collective-permute-start(bf16[4,2,400,384]{3,2,1,0:T(8,128)(2,1)} %get-tuple-element.52), channel_id=1, source_target_pairs={{0,96},{1,25},{2,98},{3,27},{4,100},{5,29},{6,102},{7,31},{8,104},... | collective-permute-start | bytes 7372808 | tf_op jit(solution)/shard_map/ppermute | solution.py:287
  23.3 3.4 %collective-permute-start.7 = (bf16[4,400,384]{2,1,0:T(8,128)(2,1)S(1)}, bf16[4,400,384]{2,1,0:T(8,128)(2,1)S(1)}, u32[]{:S(2)}, u32[]{:S(2)}) collective-permute-start(bf16[4,400,384]{2,1,0:T(8,128)(2,1)S(1)} %fusion.1.rest_0_), channel_id=1, source_target_pairs={{0,24},{1,97},{2,26},{3,99},{4,28},{5,101},{6,30},{7,103},{8,0},{9... | collective-permute-start | bytes 3686408 | tf_op jit(solution)/shard_map/ppermute | solution.py:287
  26.7 2.1 %collective-permute-start.9 = (bf16[400,384]{1,0:T(8,128)(2,1)S(1)}, bf16[400,384]{1,0:T(8,128)(2,1)S(1)}, u32[]{:S(2)}, u32[]{:S(2)}) collective-permute-start(bf16[400,384]{1,0:T(8,128)(2,1)S(1)} %bitcast.36), channel_id=1, source_target_pairs={{0,4},{1,5},{2,6},{3,7},{4,0},{5,1},{6,2},{7,3},{8,12},{9,13},{10,... | collective-permute-start | bytes 921608 | tf_op jit(solution)/shard_map/ppermute | solution.py:287
  28.8 0.6 fusion.7
  29.4 7.7 %collective-permute-done.9 = bf16[400,384]{1,0:T(8,128)(2,1)S(1)} collective-permute-done((bf16[400,384]{1,0:T(8,128)(2,1)S(1)}, bf16[400,384]{1,0:T(8,128)(2,1)S(1)}, u32[]{:S(2)}, u32[]{:S(2)}) %collective-permute-start.9) | collective-permute-done | bytes 307232 | tf_op jit(solution)/shard_map/ppermute | solution.py:287
  37.2 0.0 collective-permute-start.11
  37.2 0.2 fusion.3.rest_5_
  37.4 16.8 %collective-permute-done.7.rest_1_ = bf16[4,400,384]{2,1,0:T(8,128)(2,1)S(1)} collective-permute-done((bf16[4,400,384]{2,1,0:T(8,128)(2,1)S(1)}, bf16[4,400,384]{2,1,0:T(8,128)(2,1)S(1)}, u32[]{:S(2)}, u32[]{:S(2)}) %collective-permute-start.7) | collective-permute-done | bytes 1228832 | tf_op jit(solution)/shard_map/ppermute | solution.py:287
  54.2 3.7 %collective-permute-done.8.rest_2_ = bf16[4,400,384]{2,1,0:T(8,128)(2,1)S(1)} collective-permute-done((bf16[4,400,384]{2,1,0:T(8,128)(2,1)S(1)}, bf16[4,400,384]{2,1,0:T(8,128)(2,1)S(1)}, u32[]{:S(2)}, u32[]{:S(2)}) %collective-permute-start.8) | collective-permute-done | bytes 1228832 | tf_op jit(solution)/shard_map/ppermute | solution.py:287
  57.9 6.7 %collective-permute-done.5 = bf16[4,2,400,384]{3,2,1,0:T(8,128)(2,1)S(1)} collective-permute-done((bf16[4,2,400,384]{3,2,1,0:T(8,128)(2,1)}, bf16[4,2,400,384]{3,2,1,0:T(8,128)(2,1)S(1)}, u32[]{:S(2)}, u32[]{:S(2)}) %collective-permute-start.5) | collective-permute-done | bytes 2457632 | tf_op jit(solution)/shard_map/ppermute | solution.py:287
  64.6 0.4 collective-permute-done.6
  65.0 0.7 add_convert_fusion
  65.7 2.4 %collective-permute-start.17 = (bf16[2,400,384]{2,1,0:T(8,128)(2,1)S(1)}, bf16[2,400,384]{2,1,0:T(8,128)(2,1)S(1)}, u32[]{:S(2)}, u32[]{:S(2)}) collective-permute-start(bf16[2,400,384]{2,1,0:T(8,128)(2,1)S(1)} %get-tuple-element.74), channel_id=1, source_target_pairs={{0,6},{1,3},{2,0},{3,5},{4,2},{5,7},{6,4},{7,1},{8,14},{9,11},{10,... | collective-permute-start | bytes 1843208 | tf_op jit(solution)/shard_map/ppermute | solution.py:287
  68.1 0.1 slice.84
  68.2 2.6 %collective-permute-start.14 = (bf16[2,400,384]{2,1,0:T(8,128)(2,1)S(1)}, bf16[2,400,384]{2,1,0:T(8,128)(2,1)S(1)}, u32[]{:S(2)}, u32[]{:S(2)}) collective-permute-start(bf16[2,400,384]{2,1,0:T(8,128)(2,1)S(1)} %slice.84), channel_id=1, source_target_pairs={{0,24},{1,97},{2,26},{3,99},{4,28},{5,101},{6,30},{7,103},{8,0},{9... | collective-permute-start | bytes 1843208 | tf_op jit(solution)/shard_map/ppermute | solution.py:287
  70.8 1.1 collective-permute-start.12
  71.9 2.1 %collective-permute-start.13 = (bf16[2,2,400,384]{3,2,1,0:T(8,128)(2,1)S(1)}, bf16[2,2,400,384]{3,2,1,0:T(8,128)(2,1)S(1)}, u32[]{:S(2)}, u32[]{:S(2)}) collective-permute-start(bf16[2,2,400,384]{3,2,1,0:T(8,128)(2,1)S(1)} %get-tuple-element.70), channel_id=1, source_target_pairs={{0,96},{1,25},{2,98},{3,27},{4,100},{5,29},{6,102},{7,31},{8,104},... | collective-permute-start | bytes 3686408 | tf_op jit(solution)/shard_map/ppermute | solution.py:287
  74.0 0.0 collective-permute-start.16
  74.0 0.1 slice.85
  74.1 1.8 %collective-permute-done.17 = bf16[2,400,384]{2,1,0:T(8,128)(2,1)S(1)} collective-permute-done((bf16[2,400,384]{2,1,0:T(8,128)(2,1)S(1)}, bf16[2,400,384]{2,1,0:T(8,128)(2,1)S(1)}, u32[]{:S(2)}, u32[]{:S(2)}) %collective-permute-start.17) | collective-permute-done | bytes 614432 | tf_op jit(solution)/shard_map/ppermute | solution.py:287
  75.9 1.4 %collective-permute-start.15 = (bf16[2,400,384]{2,1,0:T(8,128)(2,1)S(1)}, bf16[2,400,384]{2,1,0:T(8,128)(2,1)S(1)}, u32[]{:S(2)}, u32[]{:S(2)}) collective-permute-start(bf16[2,400,384]{2,1,0:T(8,128)(2,1)S(1)} %slice.85), channel_id=1, source_target_pairs={{0,8},{1,33},{2,10},{3,35},{4,12},{5,37},{6,14},{7,39},{8,16},{9,4... | collective-permute-start | bytes 1843208 | tf_op jit(solution)/shard_map/ppermute | solution.py:287
  77.3 7.6 %collective-permute-done.14.rest_3_ = bf16[2,400,384]{2,1,0:T(8,128)(2,1)S(1)} collective-permute-done((bf16[2,400,384]{2,1,0:T(8,128)(2,1)S(1)}, bf16[2,400,384]{2,1,0:T(8,128)(2,1)S(1)}, u32[]{:S(2)}, u32[]{:S(2)}) %collective-permute-start.14) | collective-permute-done | bytes 614432 | tf_op jit(solution)/shard_map/ppermute | solution.py:287
  85.0 7.0 %collective-permute-done.15.rest_4_ = bf16[2,400,384]{2,1,0:T(8,128)(2,1)S(1)} collective-permute-done((bf16[2,400,384]{2,1,0:T(8,128)(2,1)S(1)}, bf16[2,400,384]{2,1,0:T(8,128)(2,1)S(1)}, u32[]{:S(2)}, u32[]{:S(2)}) %collective-permute-start.15) | collective-permute-done | bytes 614432 | tf_op jit(solution)/shard_map/ppermute | solution.py:287
  91.9 4.7 %collective-permute-done.18 = bf16[2,400,384]{2,1,0:T(8,128)(2,1)S(1)} collective-permute-done((bf16[2,400,384]{2,1,0:T(8,128)(2,1)S(1)}, bf16[2,400,384]{2,1,0:T(8,128)(2,1)S(1)}, u32[]{:S(2)}, u32[]{:S(2)}) %collective-permute-start.18) | collective-permute-done | bytes 614432 | tf_op jit(solution)/shard_map/ppermute | solution.py:287
  96.6 0.0 copy-start.10
  96.6 0.7 fusion.11
  97.4 0.3 copy-done.10
  97.7 1.4 %collective-permute-start.19 = (bf16[2,400,384]{2,1,0:T(8,128)(2,1)S(1)}, bf16[2,400,384]{2,1,0:T(8,128)(2,1)S(1)}, u32[]{:S(2)}, u32[]{:S(2)}) collective-permute-start(bf16[2,400,384]{2,1,0:T(8,128)(2,1)S(1)} %get-tuple-element.100), channel_id=1, source_target_pairs={{0,8},{1,33},{2,10},{3,35},{4,12},{5,37},{6,14},{7,39},{8,16},{9,4... | collective-permute-start | bytes 1843208 | tf_op jit(solution)/shard_map/ppermute | solution.py:287
  99.1 2.2 %collective-permute-start.20 = (bf16[2,400,384]{2,1,0:T(8,128)(2,1)S(1)}, bf16[2,400,384]{2,1,0:T(8,128)(2,1)S(1)}, u32[]{:S(2)}, u32[]{:S(2)}) collective-permute-start(bf16[2,400,384]{2,1,0:T(8,128)(2,1)S(1)} %get-tuple-element.94), channel_id=1, source_target_pairs={{0,24},{1,97},{2,26},{3,99},{4,28},{5,101},{6,30},{7,103},{8,0},{9... | collective-permute-start | bytes 1843208 | tf_op jit(solution)/shard_map/ppermute | solution.py:287
  101.3 2.1 %collective-permute-start.21 = (bf16[2,400,384]{2,1,0:T(8,128)(2,1)S(1)}, bf16[2,400,384]{2,1,0:T(8,128)(2,1)S(1)}, u32[]{:S(2)}, u32[]{:S(2)}) collective-permute-start(bf16[2,400,384]{2,1,0:T(8,128)(2,1)S(1)} %get-tuple-element.95), channel_id=1, source_target_pairs={{0,16},{1,65},{2,18},{3,67},{4,20},{5,69},{6,22},{7,71},{8,24},{9,... | collective-permute-start | bytes 1843208 | tf_op jit(solution)/shard_map/ppermute | solution.py:287
  103.5 0.5 convert_add_fusion
  104.0 9.2 %shard_map.60 = bf16[8,2,400,400]{3,2,1,0:T(8,128)(2,1)} custom-call(s32[8]{0:T(128)S(1)} %copy-done.1, bf16[8,2,400,384]{3,2,1,0:T(8,128)(2,1)} %get-tuple-element.80.left_hbm, bf16[4,400,384]{2,1,0:T(8,128)(2,1)} %copy-done.2, bf16[4,400,384]{2,1,0:T(8,128)(2,1)} %copy-done.4, bf16[4,400,384]{2,1,0:T(8,128)(2,1)} %copy-done.5, ...), custom_call_target="tpu_custom_call" | custom-call | flops 1966080000 | bytes 15000000 | tf_op jit(solution)/shard_map/pallas_call | solution.py:241
  113.2 0.0 collective-permute-done.19.rest_0_
  113.2 2.4 %collective-permute-done.20.rest_1_ = bf16[2,400,384]{2,1,0:T(8,128)(2,1)S(1)} collective-permute-done((bf16[2,400,384]{2,1,0:T(8,128)(2,1)S(1)}, bf16[2,400,384]{2,1,0:T(8,128)(2,1)S(1)}, u32[]{:S(2)}, u32[]{:S(2)}) %collective-permute-start.20) | collective-permute-done | bytes 614432 | tf_op jit(solution)/shard_map/ppermute | solution.py:287
  115.6 1.9 %collective-permute-done.21.rest_2_ = bf16[2,400,384]{2,1,0:T(8,128)(2,1)S(1)} collective-permute-done((bf16[2,400,384]{2,1,0:T(8,128)(2,1)S(1)}, bf16[2,400,384]{2,1,0:T(8,128)(2,1)S(1)}, u32[]{:S(2)}, u32[]{:S(2)}) %collective-permute-start.21) | collective-permute-done | bytes 614432 | tf_op jit(solution)/shard_map/ppermute | solution.py:287
  117.5 2.1 %shard_map.61 = f32[2,400,400]{2,1,0:T(8,128)} custom-call(bf16[400,384]{1,0:T(8,128)(2,1)S(1)} %bitcast.38, f32[2,400,384]{2,1,0:T(8,128)S(1)} %convert_add_fusion, bf16[2,400,384]{2,1,0:T(8,128)(2,1)S(1)} %collective-permute-done.19.rest_0_, bf16[2,400,384]{2,1,0:T(8,128)(2,1)S(1)} %collective-permute-done.20.rest_1_, ...), custom_call_target="tpu_custom_call" | custom-call | tf_op jit(solution)/shard_map/pallas_call | solution.py:274
  (33 shorter events, 0.1 us)
Async XLA Ops:
  0.6 19.1 %copy-start = (bf16[1,384,400]{1,2,0:T(8,128)(2,1)S(1)}, bf16[1,384,400]{1,2,0:T(8,128)(2,1)}, u32[]{:S(2)}) copy-start(bf16[1,384,400]{1,2,0:T(8,128)(2,1)} %param.4) | copy-start | bytes 921604
  0.6 19.0 %collective-permute-start = (bf16[400,384]{1,0:T(8,128)(2,1)}, bf16[400,384]{1,0:T(8,128)(2,1)S(1)}, u32[]{:S(2)}, u32[]{:S(2)}) collective-permute-start(bf16[400,384]{1,0:T(8,128)(2,1)} %bitcast.29), channel_id=1, source_target_pairs={{0,96},{1,25},{2,98},{3,27},{4,100},{5,29},{6,102},{7,31},{8,104},... | collective-permute-start | bytes 921608 | tf_op jit(solution)/shard_map/ppermute | solution.py:287
  3.5 16.1 %collective-permute-start.1 = (bf16[400,384]{1,0:T(8,128)(2,1)}, bf16[400,384]{1,0:T(8,128)(2,1)S(1)}, u32[]{:S(2)}, u32[]{:S(2)}) collective-permute-start(bf16[400,384]{1,0:T(8,128)(2,1)} %bitcast.30), channel_id=1, source_target_pairs={{0,64},{1,17},{2,66},{3,19},{4,68},{5,21},{6,70},{7,23},{8,72},{9,... | collective-permute-start | bytes 921608 | tf_op jit(solution)/shard_map/ppermute | solution.py:287
  4.4 15.3 %collective-permute-start.2 = (bf16[400,384]{1,0:T(8,128)(2,1)}, bf16[400,384]{1,0:T(8,128)(2,1)S(1)}, u32[]{:S(2)}, u32[]{:S(2)}) collective-permute-start(bf16[400,384]{1,0:T(8,128)(2,1)} %bitcast.31), channel_id=1, source_target_pairs={{0,32},{1,9},{2,34},{3,11},{4,36},{5,13},{6,38},{7,15},{8,40},{9,1... | collective-permute-start | bytes 921608 | tf_op jit(solution)/shard_map/ppermute | solution.py:287
  5.2 14.7 %collective-permute-start.3 = (bf16[400,384]{1,0:T(8,128)(2,1)}, bf16[400,384]{1,0:T(8,128)(2,1)S(1)}, u32[]{:S(2)}, u32[]{:S(2)}) collective-permute-start(bf16[400,384]{1,0:T(8,128)(2,1)} %bitcast.32), channel_id=1, source_target_pairs={{0,2},{1,7},{2,4},{3,1},{4,6},{5,3},{6,0},{7,5},{8,10},{9,15},{10,... | collective-permute-start | bytes 921608 | tf_op jit(solution)/shard_map/ppermute | solution.py:287
  7.2 12.8 %collective-permute-start.4 = (bf16[400,384]{1,0:T(8,128)(2,1)}, bf16[400,384]{1,0:T(8,128)(2,1)S(1)}, u32[]{:S(2)}, u32[]{:S(2)}) collective-permute-start(bf16[400,384]{1,0:T(8,128)(2,1)} %bitcast.33), channel_id=1, source_target_pairs={{0,6},{1,3},{2,0},{3,5},{4,2},{5,7},{6,4},{7,1},{8,14},{9,11},{10,... | collective-permute-start | bytes 921608 | tf_op jit(solution)/shard_map/ppermute | solution.py:287
  19.7 9.1 %copy-start.6 = (bf16[4,2,400,384]{3,2,1,0:T(8,128)(2,1)S(1)}, bf16[4,2,400,384]{3,2,1,0:T(8,128)(2,1)}, u32[]{:S(2)}) copy-start(bf16[4,2,400,384]{3,2,1,0:T(8,128)(2,1)} %get-tuple-element.57) | copy-start | bytes 7372804
  19.9 9.5 %copy-start.2 = (bf16[4,400,384]{2,1,0:T(8,128)(2,1)}, bf16[4,400,384]{2,1,0:T(8,128)(2,1)S(1)}, u32[]{:S(2)}) copy-start(bf16[4,400,384]{2,1,0:T(8,128)(2,1)S(1)} %fusion.1.rest_0_) | copy-start | bytes 3686404
  19.9 6.8 %collective-permute-start.10 = (bf16[4,2,400,384]{3,2,1,0:T(8,128)(2,1)}, bf16[4,2,400,384]{3,2,1,0:T(8,128)(2,1)S(1)}, u32[]{:S(2)}, u32[]{:S(2)}) collective-permute-start(bf16[4,2,400,384]{3,2,1,0:T(8,128)(2,1)} %get-tuple-element.58), channel_id=1, source_target_pairs={{0,1},{1,0},{2,3},{3,2},{4,5},{5,4},{6,7},{7,6},{8,9},{9,8},{10,11... | collective-permute-start | bytes 7372808 | tf_op jit(solution)/shard_map/ppermute | solution.py:287
  20.0 44.6 %collective-permute-start.5 = (bf16[4,2,400,384]{3,2,1,0:T(8,128)(2,1)}, bf16[4,2,400,384]{3,2,1,0:T(8,128)(2,1)S(1)}, u32[]{:S(2)}, u32[]{:S(2)}) collective-permute-start(bf16[4,2,400,384]{3,2,1,0:T(8,128)(2,1)} %get-tuple-element.51), channel_id=1, source_target_pairs={{0,32},{1,9},{2,34},{3,11},{4,36},{5,13},{6,38},{7,15},{8,40},{9,1... | collective-permute-start | bytes 7372808 | tf_op jit(solution)/shard_map/ppermute | solution.py:287
  21.7 43.3 %collective-permute-start.6 = (bf16[4,2,400,384]{3,2,1,0:T(8,128)(2,1)}, bf16[4,2,400,384]{3,2,1,0:T(8,128)(2,1)S(1)}, u32[]{:S(2)}, u32[]{:S(2)}) collective-permute-start(bf16[4,2,400,384]{3,2,1,0:T(8,128)(2,1)} %get-tuple-element.52), channel_id=1, source_target_pairs={{0,96},{1,25},{2,98},{3,27},{4,100},{5,29},{6,102},{7,31},{8,104},... | collective-permute-start | bytes 7372808 | tf_op jit(solution)/shard_map/ppermute | solution.py:287
  23.3 30.8 %collective-permute-start.7 = (bf16[4,400,384]{2,1,0:T(8,128)(2,1)S(1)}, bf16[4,400,384]{2,1,0:T(8,128)(2,1)S(1)}, u32[]{:S(2)}, u32[]{:S(2)}) collective-permute-start(bf16[4,400,384]{2,1,0:T(8,128)(2,1)S(1)} %fusion.1.rest_0_), channel_id=1, source_target_pairs={{0,24},{1,97},{2,26},{3,99},{4,28},{5,101},{6,30},{7,103},{8,0},{9... | collective-permute-start | bytes 3686408 | tf_op jit(solution)/shard_map/ppermute | solution.py:287
  26.7 31.2 %collective-permute-start.8 = (bf16[4,400,384]{2,1,0:T(8,128)(2,1)S(1)}, bf16[4,400,384]{2,1,0:T(8,128)(2,1)S(1)}, u32[]{:S(2)}, u32[]{:S(2)}) collective-permute-start(bf16[4,400,384]{2,1,0:T(8,128)(2,1)S(1)} %fusion.1.rest_0_), channel_id=1, source_target_pairs={{0,8},{1,33},{2,10},{3,35},{4,12},{5,37},{6,14},{7,39},{8,16},{9,4... | collective-permute-start | bytes 3686408 | tf_op jit(solution)/shard_map/ppermute | solution.py:287
  26.7 10.5 %collective-permute-start.9 = (bf16[400,384]{1,0:T(8,128)(2,1)S(1)}, bf16[400,384]{1,0:T(8,128)(2,1)S(1)}, u32[]{:S(2)}, u32[]{:S(2)}) collective-permute-start(bf16[400,384]{1,0:T(8,128)(2,1)S(1)} %bitcast.36), channel_id=1, source_target_pairs={{0,4},{1,5},{2,6},{3,7},{4,0},{5,1},{6,2},{7,3},{8,12},{9,13},{10,... | collective-permute-start | bytes 921608 | tf_op jit(solution)/shard_map/ppermute | solution.py:287
  37.2 27.8 %collective-permute-start.11 = (bf16[2,400,384]{2,1,0:T(8,128)(2,1)S(1)}, bf16[2,400,384]{2,1,0:T(8,128)(2,1)S(1)}, u32[]{:S(2)}, u32[]{:S(2)}) collective-permute-start(bf16[2,400,384]{2,1,0:T(8,128)(2,1)S(1)} %get-tuple-element.98), channel_id=1, source_target_pairs={{0,2},{1,7},{2,4},{3,1},{4,6},{5,3},{6,0},{7,5},{8,10},{9,15},{10,... | collective-permute-start | bytes 1843208 | tf_op jit(solution)/shard_map/ppermute | solution.py:287
  37.2 27.8 %copy-start.8 = (bf16[2,2,400,384]{3,2,1,0:T(8,128)(2,1)S(1)}, bf16[2,2,400,384]{3,2,1,0:T(8,128)(2,1)}, u32[]{:S(2)}) copy-start(bf16[2,2,400,384]{3,2,1,0:T(8,128)(2,1)} %get-tuple-element.60) | copy-start | bytes 3686404
  37.2 27.8 %copy-start.9 = (bf16[2,2,400,384]{3,2,1,0:T(8,128)(2,1)S(1)}, bf16[2,2,400,384]{3,2,1,0:T(8,128)(2,1)}, u32[]{:S(2)}) copy-start(bf16[2,2,400,384]{3,2,1,0:T(8,128)(2,1)} %get-tuple-element.62) | copy-start | bytes 3686404
  37.4 36.6 %copy-start.3 = (bf16[4,400,384]{2,1,0:T(8,128)(2,1)}, bf16[4,400,384]{2,1,0:T(8,128)(2,1)S(1)}, u32[]{:S(2)}) copy-start(bf16[4,400,384]{2,1,0:T(8,128)(2,1)S(1)} %fusion.3.rest_5_) | copy-start | bytes 3686404
  54.2 13.9 %copy-start.4 = (bf16[4,400,384]{2,1,0:T(8,128)(2,1)}, bf16[4,400,384]{2,1,0:T(8,128)(2,1)S(1)}, u32[]{:S(2)}) copy-start(bf16[4,400,384]{2,1,0:T(8,128)(2,1)S(1)} %collective-permute-done.7.rest_1_) | copy-start | bytes 3686404
  57.9 16.2 %copy-start.5 = (bf16[4,400,384]{2,1,0:T(8,128)(2,1)}, bf16[4,400,384]{2,1,0:T(8,128)(2,1)S(1)}, u32[]{:S(2)}) copy-start(bf16[4,400,384]{2,1,0:T(8,128)(2,1)S(1)} %collective-permute-done.8.rest_2_) | copy-start | bytes 3686404
  65.7 31.0 %copy-start.7 = (bf16[4,2,400,384]{3,2,1,0:T(8,128)(2,1)S(1)}, bf16[4,2,400,384]{3,2,1,0:T(8,128)(2,1)}, u32[]{:S(2)}) copy-start(bf16[4,2,400,384]{3,2,1,0:T(8,128)(2,1)} %get-tuple-element.47) | copy-start | bytes 7372804
  65.7 10.2 %collective-permute-start.17 = (bf16[2,400,384]{2,1,0:T(8,128)(2,1)S(1)}, bf16[2,400,384]{2,1,0:T(8,128)(2,1)S(1)}, u32[]{:S(2)}, u32[]{:S(2)}) collective-permute-start(bf16[2,400,384]{2,1,0:T(8,128)(2,1)S(1)} %get-tuple-element.74), channel_id=1, source_target_pairs={{0,6},{1,3},{2,0},{3,5},{4,2},{5,7},{6,4},{7,1},{8,14},{9,11},{10,... | collective-permute-start | bytes 1843208 | tf_op jit(solution)/shard_map/ppermute | solution.py:287
  68.2 16.8 %collective-permute-start.14 = (bf16[2,400,384]{2,1,0:T(8,128)(2,1)S(1)}, bf16[2,400,384]{2,1,0:T(8,128)(2,1)S(1)}, u32[]{:S(2)}, u32[]{:S(2)}) collective-permute-start(bf16[2,400,384]{2,1,0:T(8,128)(2,1)S(1)} %slice.84), channel_id=1, source_target_pairs={{0,24},{1,97},{2,26},{3,99},{4,28},{5,101},{6,30},{7,103},{8,0},{9... | collective-permute-start | bytes 1843208 | tf_op jit(solution)/shard_map/ppermute | solution.py:287
  70.8 25.8 %collective-permute-start.12 = (bf16[2,2,400,384]{3,2,1,0:T(8,128)(2,1)S(1)}, bf16[2,2,400,384]{3,2,1,0:T(8,128)(2,1)S(1)}, u32[]{:S(2)}, u32[]{:S(2)}) collective-permute-start(bf16[2,2,400,384]{3,2,1,0:T(8,128)(2,1)S(1)} %get-tuple-element.69), channel_id=1, source_target_pairs={{0,32},{1,9},{2,34},{3,11},{4,36},{5,13},{6,38},{7,15},{8,40},{9,1... | collective-permute-start | bytes 3686408 | tf_op jit(solution)/shard_map/ppermute | solution.py:287
  71.9 24.7 %collective-permute-start.13 = (bf16[2,2,400,384]{3,2,1,0:T(8,128)(2,1)S(1)}, bf16[2,2,400,384]{3,2,1,0:T(8,128)(2,1)S(1)}, u32[]{:S(2)}, u32[]{:S(2)}) collective-permute-start(bf16[2,2,400,384]{3,2,1,0:T(8,128)(2,1)S(1)} %get-tuple-element.70), channel_id=1, source_target_pairs={{0,96},{1,25},{2,98},{3,27},{4,100},{5,29},{6,102},{7,31},{8,104},... | collective-permute-start | bytes 3686408 | tf_op jit(solution)/shard_map/ppermute | solution.py:287
  74.0 22.6 %collective-permute-start.16 = (bf16[4,400,384]{2,1,0:T(8,128)(2,1)S(1)}, bf16[4,400,384]{2,1,0:T(8,128)(2,1)S(1)}, u32[]{:S(2)}, u32[]{:S(2)}) collective-permute-start(bf16[4,400,384]{2,1,0:T(8,128)(2,1)S(1)} %fusion.3.rest_5_), channel_id=1, source_target_pairs={{0,1},{1,0},{2,3},{3,2},{4,5},{5,4},{6,7},{7,6},{8,9},{9,8},{10,11... | collective-permute-start | bytes 3686408 | tf_op jit(solution)/shard_map/ppermute | solution.py:287
  75.9 16.0 %collective-permute-start.15 = (bf16[2,400,384]{2,1,0:T(8,128)(2,1)S(1)}, bf16[2,400,384]{2,1,0:T(8,128)(2,1)S(1)}, u32[]{:S(2)}, u32[]{:S(2)}) collective-permute-start(bf16[2,400,384]{2,1,0:T(8,128)(2,1)S(1)} %slice.85), channel_id=1, source_target_pairs={{0,8},{1,33},{2,10},{3,35},{4,12},{5,37},{6,14},{7,39},{8,16},{9,4... | collective-permute-start | bytes 1843208 | tf_op jit(solution)/shard_map/ppermute | solution.py:287
  85.0 12.4 %copy-start.11 = (bf16[2,400,384]{2,1,0:T(8,128)(2,1)}, bf16[2,400,384]{2,1,0:T(8,128)(2,1)S(1)}, u32[]{:S(2)}) copy-start(bf16[2,400,384]{2,1,0:T(8,128)(2,1)S(1)} %collective-permute-done.14.rest_3_) | copy-start | bytes 1843204
  85.0 11.7 %collective-permute-start.18 = (bf16[2,400,384]{2,1,0:T(8,128)(2,1)S(1)}, bf16[2,400,384]{2,1,0:T(8,128)(2,1)S(1)}, u32[]{:S(2)}, u32[]{:S(2)}) collective-permute-start(bf16[2,400,384]{2,1,0:T(8,128)(2,1)S(1)} %get-tuple-element.76), channel_id=1, source_target_pairs={{0,4},{1,5},{2,6},{3,7},{4,0},{5,1},{6,2},{7,3},{8,12},{9,13},{10,... | collective-permute-start | bytes 1843208 | tf_op jit(solution)/shard_map/ppermute | solution.py:287
  91.9 5.5 %copy-start.12 = (bf16[2,400,384]{2,1,0:T(8,128)(2,1)}, bf16[2,400,384]{2,1,0:T(8,128)(2,1)S(1)}, u32[]{:S(2)}) copy-start(bf16[2,400,384]{2,1,0:T(8,128)(2,1)S(1)} %collective-permute-done.15.rest_4_) | copy-start | bytes 1843204
  96.6 1.0 copy-start.10
  97.7 15.6 %collective-permute-start.19 = (bf16[2,400,384]{2,1,0:T(8,128)(2,1)S(1)}, bf16[2,400,384]{2,1,0:T(8,128)(2,1)S(1)}, u32[]{:S(2)}, u32[]{:S(2)}) collective-permute-start(bf16[2,400,384]{2,1,0:T(8,128)(2,1)S(1)} %get-tuple-element.100), channel_id=1, source_target_pairs={{0,8},{1,33},{2,10},{3,35},{4,12},{5,37},{6,14},{7,39},{8,16},{9,4... | collective-permute-start | bytes 1843208 | tf_op jit(solution)/shard_map/ppermute | solution.py:287
  99.1 16.5 %collective-permute-start.20 = (bf16[2,400,384]{2,1,0:T(8,128)(2,1)S(1)}, bf16[2,400,384]{2,1,0:T(8,128)(2,1)S(1)}, u32[]{:S(2)}, u32[]{:S(2)}) collective-permute-start(bf16[2,400,384]{2,1,0:T(8,128)(2,1)S(1)} %get-tuple-element.94), channel_id=1, source_target_pairs={{0,24},{1,97},{2,26},{3,99},{4,28},{5,101},{6,30},{7,103},{8,0},{9... | collective-permute-start | bytes 1843208 | tf_op jit(solution)/shard_map/ppermute | solution.py:287
  101.3 2.7 %copy-start.1 = (s32[8]{0:T(128)S(1)}, s32[8]{0:T(128)}, u32[]{:S(2)}) copy-start(s32[8]{0:T(128)} %partner_ref) | copy-start | bytes 100
  101.3 16.2 %collective-permute-start.21 = (bf16[2,400,384]{2,1,0:T(8,128)(2,1)S(1)}, bf16[2,400,384]{2,1,0:T(8,128)(2,1)S(1)}, u32[]{:S(2)}, u32[]{:S(2)}) collective-permute-start(bf16[2,400,384]{2,1,0:T(8,128)(2,1)S(1)} %get-tuple-element.95), channel_id=1, source_target_pairs={{0,16},{1,65},{2,18},{3,67},{4,20},{5,69},{6,22},{7,71},{8,24},{9,... | collective-permute-start | bytes 1843208 | tf_op jit(solution)/shard_map/ppermute | solution.py:287

commit v3 on v2

--- a/solution.py
+++ b/solution.py
@@ -33,19 +33,16 @@
     return (other // 2 - me // 2 + SIDE) % SIDE, other % 2, me % 2
 
 
-def left_kernel(partner_hbm, counts_hbm, own_hbm, coupling_hbm, left_hbm, *rest):
+def left_kernel(partner_hbm, counts_hbm, own_hbm, coupling_hbm, left_ref, *rest):
     outs = rest[:7]
-    partner_ref, counts_ref, own_ref, blocks, lefts, zero, sums = rest[7:14]
-    keys, number, seen, at_sum, in_sem, left_sem, out_sem = rest[14:]
-    count, pairs = blocks.shape[0], keys.shape[0]
+    partner_ref, counts_ref, own_ref, blocks, used, in_sem = rest[7:]
+    count, pairs = blocks.shape[0], left_ref.shape[0]
     modes, width = own_ref.shape
-    slots = SPAN_X + SPAN_Y
+    places = PARTS + ((SPAN_X, SIDE), (SPAN_X + SIDE, SIDE))
+    chunks = modes // CHUNK
 
     def load(i):
         return pltpu.make_async_copy(coupling_hbm.at[i // 2, i % 2], blocks.at[i], in_sem.at[i])
-
-    def save(i):
-        return pltpu.make_async_copy(lefts.at[i], left_hbm.at[i // 2, i % 2], left_sem.at[i])
 
     load_partner = pltpu.make_async_copy(partner_hbm, partner_ref, in_sem.at[count + 1])
     load_partner.start()
@@ -58,89 +55,65 @@
     def _(i):
         load(i).start()
 
-    @pl.loop(0, slots)
+    @pl.loop(0, SPAN_X + SPAN_Y)
     def _(k):
-        number[k] = 0
-        seen[k] = 0
-
-    at_sum[slots] = 0
-    load_partner.wait()
-    load_counts.wait()
-
-    @pl.loop(0, pairs)
-    def _(p):
+        used[k] = 0
+
+    def key_of(p):
         code = partner_ref[p]
         d1, d2 = offsets(code)
         dz, core, me = ring_offset(code)
         step = jnp.where((dz == 1) | (dz == 3), jnp.where((dz == 1) == (core == 0), 1, 2), jnp.where(dz == 2, 3, 0))
-        key = jnp.where(code < SPAN_X, slot_of(d1, d2), SPAN_X + step + jnp.where(core == me, SIDE, 0))
-        keys[p] = key
-        number[key] = number[key] + 1
-
-    @pl.loop(0, 2 * (modes // CHUNK))
-    def _(r):
-        rows = pl.ds(pl.multiple_of(r // 2 * CHUNK, CHUNK), CHUNK)
-        zero[r % 2, rows] = jnp.zeros((CHUNK, width), zero.dtype)
-
-    def send(source, key):
-        for out, (at, size) in zip(outs, PARTS + ((SPAN_X, SIDE), (SPAN_X + SIDE, SIDE)), strict=True):
-            @pl.when((key >= at) & (key < at + size))
-            def _():
-                pltpu.make_async_copy(source, out.at[key - at], out_sem.at[key]).start()
-
-    @pl.loop(0, slots)
-    def _(k):
-        @pl.when(number[k] == 0)
-        def _():
-            send(zero, k)
-
+        return jnp.where(code < SPAN_X, slot_of(d1, d2), SPAN_X + step + jnp.where(core == me, SIDE, 0))
+
+    def rows(r):
+        return r % 2, pl.ds(pl.multiple_of(r // 2 * CHUNK, CHUNK), CHUNK)
+
+    load_partner.wait()
+    load_counts.wait()
     load_own.wait()
 
     @pl.loop(0, count)
     def _(i):
-        p = i // 2
+        p, t = i // 2, i % 2
         load(i).wait()
         keep = lax.broadcasted_iota(jnp.int32, (1, width), 1) < counts_ref[p]
         own = jnp.where(keep, own_ref[...], jnp.zeros((modes, width), own_ref.dtype))
         product = jnp.dot(own, blocks[i], preferred_element_type=jnp.float32)
-        lefts[i] = jnp.where(keep, product, 0.0).astype(jnp.bfloat16)
-        save(i).start()
-        key = keys[p]
-        single = number[key] == 1
-
-        @pl.when((i % 2 == 1) & single)
+        left_ref[p, t] = jnp.where(keep, product, 0.0).astype(jnp.bfloat16)
+
+        @pl.when(t == 1)
         def _():
-            send(lefts.at[pl.ds(i - 1, 2)], key)
-
-        @pl.when((i % 2 == 1) & jnp.logical_not(single))
-        def _():
-            fresh = seen[key] == 0
-
-            @pl.when(fresh)
+            key = key_of(p)
+            fresh = used[key] == 0
+            used[key] = 1
+            for out, (at, size) in zip(outs, places, strict=True):
+                here = (key >= at) & (key < at + size)
+
+                @pl.when(here & fresh)
+                def _():
+                    @pl.loop(0, 2 * chunks)
+                    def _(r):
+                        b, some = rows(r)
+                        out[key - at, b, some] = left_ref[p, b, some]
+
+                @pl.when(here & jnp.logical_not(fresh))
+                def _():
+                    @pl.loop(0, 2 * chunks)
+                    def _(r):
+                        b, some = rows(r)
+                        total = out[key - at, b, some].astype(jnp.float32) + left_ref[p, b, some].astype(jnp.float32)
+                        out[key - at, b, some] = total.astype(jnp.bfloat16)
+
+    for out, (at, size) in zip(outs, places, strict=True):
+        @pl.loop(0, size)
+        def _(k):
+            @pl.when(used[at + k] == 0)
             def _():
-                at_sum[key] = at_sum[slots]
-                at_sum[slots] = at_sum[slots] + 1
-
-            seen[key] = seen[key] + 1
-            place = at_sum[key]
-
-            @pl.loop(0, 2 * (modes // CHUNK))
-            def _(r):
-                t, rows = r % 2, pl.ds(pl.multiple_of(r // 2 * CHUNK, CHUNK), CHUNK)
-                before = jnp.where(fresh, 0.0, sums[place, t, rows].astype(jnp.float32))
-                sums[place, t, rows] = (before + lefts[i - 1 + t, rows].astype(jnp.float32)).astype(jnp.bfloat16)
-
-            @pl.when(seen[key] == number[key])
-            def _():
-                send(sums.at[place], key)
-
-    @pl.loop(0, count)
-    def _(i):
-        save(i).wait()
-
-    @pl.loop(0, slots)
-    def _(k):
-        pltpu.make_async_copy(zero, outs[0].at[0], out_sem.at[k]).wait()
+                @pl.loop(0, 2 * chunks)
+                def _(r):
+                    b, some = rows(r)
+                    out[k, b, some] = jnp.zeros((CHUNK, width), out.dtype)
 
 
 def in_hbm(value):
@@ -150,31 +123,22 @@
 def left_products(own, coupling, partner, counts):
     pairs, blocks, width, _ = coupling.shape
     modes = own.shape[0]
-    hbm = pl.BlockSpec(memory_space=pltpu.HBM)
     slots = SPAN_X + SPAN_Y
     sizes = [pairs] + [size for _, size in PARTS] + [SIDE] * 2
     out = pl.pallas_call(
         left_kernel,
-        in_specs=[hbm] * 4,
-        out_specs=[hbm] * len(sizes),
-        out_shape=[pltpu.HBM((n, blocks, modes, width), jnp.bfloat16) for n in sizes],
+        in_specs=[pl.BlockSpec(memory_space=pltpu.HBM)] * 4,
+        out_specs=[pl.BlockSpec(memory_space=pltpu.VMEM)] * len(sizes),
+        out_shape=[pltpu.VMEM((n, blocks, modes, width), jnp.bfloat16) for n in sizes],
         scratch_shapes=[
             pltpu.SMEM((pairs,), jnp.int32),
             pltpu.SMEM((pairs,), jnp.int32),
             pltpu.VMEM((modes, width), jnp.bfloat16),
             pltpu.VMEM((pairs * blocks, width, width), jnp.bfloat16),
-            pltpu.VMEM((pairs * blocks, modes, width), jnp.bfloat16),
-            pltpu.VMEM((blocks, modes, width), jnp.bfloat16),
-            pltpu.VMEM((pairs // 2, blocks, modes, width), jnp.bfloat16),
-            pltpu.SMEM((pairs,), jnp.int32),
             pltpu.SMEM((slots,), jnp.int32),
-            pltpu.SMEM((slots,), jnp.int32),
-            pltpu.SMEM((slots + 1,), jnp.int32),
             pltpu.SemaphoreType.DMA((pairs * blocks + 3,)),
-            pltpu.SemaphoreType.DMA((pairs * blocks,)),
-            pltpu.SemaphoreType.DMA((slots,)),
         ],
-        compiler_params=pltpu.CompilerParams(vmem_limit_bytes=20 * 2**20),
+        compiler_params=pltpu.CompilerParams(vmem_limit_bytes=8 * 2**20),
         cost_estimate=pl.CostEstimate(flops=2 * pairs * blocks * modes * width * width,
                                       bytes_accessed=25 * 10**6, transcendentals=0),
     )(*map(in_hbm, (partner, counts, own, coupling)))
@@ -185,21 +149,16 @@
     return lax.dot_general(a, b, (((1,), (1,)), ((), ())), preferred_element_type=jnp.float32)
 
 
-def pair_kernel(partner_ref, left_hbm, *rest):
+def pair_kernel(partner_ref, left_ref, *rest):
     (kept, near, far, low, high, ring_mine, ring_other), out_hbm = rest[:7], rest[7]
-    lefts, panels, outs, left_sem, panel_sem, out_sem = rest[8:]
-    pairs, count = panels.shape[0], lefts.shape[0]
-
-    def load(i):
-        return pltpu.make_async_copy(left_hbm.at[i // 2, i % 2], lefts.at[i], left_sem.at[i])
+    panels, outs, panel_sem, out_sem = rest[8:]
+    pairs, count = panels.shape[0], outs.shape[0]
 
     def save(i):
         return pltpu.make_async_copy(outs.at[i], out_hbm.at[i // 2, i % 2], out_sem.at[i])
 
     @pl.loop(0, pairs)
     def _(q):
-        load(2 * q).start()
-        load(2 * q + 1).start()
         code = partner_ref[q]
         d1, d2 = offsets(code)
         dz, core, me = ring_offset(code)
@@ -226,8 +185,7 @@
         def _():
             pltpu.make_async_copy(kept.at[0], panels.at[p], panel_sem.at[p]).wait()
 
-        load(i).wait()
-        outs[i] = nt(lefts[i], panels[p]).astype(jnp.bfloat16)
+        outs[i] = nt(left_ref[p, i % 2], panels[p]).astype(jnp.bfloat16)
         save(i).start()
 
     @pl.loop(0, count)
@@ -240,21 +198,19 @@
     hbm, smem = pl.BlockSpec(memory_space=pltpu.HBM), pl.BlockSpec(memory_space=pltpu.SMEM)
     return pl.pallas_call(
         pair_kernel,
-        in_specs=[smem] + [hbm] * 8,
+        in_specs=[smem, pl.BlockSpec(memory_space=pltpu.VMEM)] + [pl.BlockSpec(memory_space=pl.ANY)] * 7,
         out_specs=hbm,
         out_shape=jax.ShapeDtypeStruct((pairs, blocks, modes, modes), jnp.bfloat16),
         scratch_shapes=[
-            pltpu.VMEM((pairs * blocks, modes, width), jnp.bfloat16),
             pltpu.VMEM((pairs, modes, width), jnp.bfloat16),
             pltpu.VMEM((pairs * blocks, modes, modes), jnp.bfloat16),
-            pltpu.SemaphoreType.DMA((pairs * blocks,)),
             pltpu.SemaphoreType.DMA((pairs,)),
             pltpu.SemaphoreType.DMA((pairs * blocks,)),
         ],
-        compiler_params=pltpu.CompilerParams(vmem_limit_bytes=20 * 2**20),
+        compiler_params=pltpu.CompilerParams(vmem_limit_bytes=14 * 2**20),
         cost_estimate=pl.CostEstimate(flops=2 * pairs * blocks * modes * width * modes,
                                       bytes_accessed=15 * 10**6, transcendentals=0),
-    )(partner, in_hbm(left), *map(in_hbm, sources))
+    )(partner, left, *sources)
 
 
 def partner_kernel(own_ref, sum_ref, *rest):
@@ -331,18 +287,16 @@
     ring_mine = jnp.stack([own, ring1, ring2, ring3])
     pair_sum = swap(z_other)
     w = [rounded(z_mine[k], pair_sum[k]) for k in range(SIDE)]
-    z1 = turn(w[1], 1)
-    got, near, far, ring_mine, w, z1 = barrier((got, near, far, ring_mine, w, z1))
+    z1, z2, z3 = turn(w[1], 1), turn(w[2], -1), turn(w[3], 2)
+    got, near, far, ring_mine, w, z1, z2, z3 = barrier((got, near, far, ring_mine, w, z1, z2, z3))
     got_up, got_down = got
 
     b_up, b_down = rounded(pass_up, got_up[:2]), rounded(pass_down, got_down[:2])
-    b_up, b_down, near, far, ring_mine, w = barrier((b_up, b_down, near, far, ring_mine, w))
-    last = [first(b_up, 1), first(b_down, -1)]
+    b_up, b_down, near, far, ring_mine = barrier((b_up, b_down, near, far, ring_mine))
     low, high = second(near[:2], -1), second(far[2:], 1)
     ring_other = swap(ring_mine)
-    z2 = turn(w[2], -1)
-    z3 = turn(after(w[3], z2), 2)
-    last, low, high, ring_other, z2, z3 = barrier((last, low, high, ring_other, z2, z3))
+    last = [first(b_up, 1), first(b_down, -1)]
+    last, low, high, ring_other = barrier((last, low, high, ring_other))
     last_up, last_down = last
 
     v = [

time: 120 us -> 127 us (1.058)
  waiting for transfers between devices: 60.7 us -> 66.3 us
  Pallas kernels: 21.6 us -> 24.5 us
  starting transfers between devices: 33 us -> 31 us
    ppermute x22, waiting for transfers between devices: 60.7 us -> 66.3 us  [permuted(): return lax.ppermute(value, ('sx', 'sy'), pairs)]
    pallas_call x2, Pallas kernels: 19.6 us -> 22.4 us  [the longest x1 13.2 us: left_products(): pl.pallas_call(left_kernel, in_specs=[pl.BlockSpec(memory_space=pltpu.HBM...]
    ppermute x22, starting transfers between devices: 33 us -> 31 us  [permuted(): return lax.ppermute(value, ('sx', 'sy'), pairs)]
  transfers between devices with their start and end apart: 22 -> 22, of which waited for: 11 -> 10; matrix products, arithmetic and copies ran while one was open for 1% -> 1% of each run, Pallas kernels for 16% -> 18%
where the time goes in v3:
time: 127 us; the launch traced here: 126 us
  waiting for transfers between devices  66.3 us (52%)
  starting transfers between devices  31 us (24%)
  Pallas kernels  24.5 us (19%)
  other arithmetic  2.92 us (2%)
    ppermute x22, waiting for transfers between devices, permuted(): return lax.ppermute(value, ('sx', 'sy'), pairs)  66.3 us
    ppermute x22, starting transfers between devices, permuted(): return lax.ppermute(value, ('sx', 'sy'), pairs)  31 us
    pallas_call x1, Pallas kernels, left_products(): pl.pallas_call(left_kernel, in_specs=[pl.BlockSpec(memory_space=pltpu.HBM...  13.2 us
    pallas_call x1, Pallas kernels, pair_products(): pl.pallas_call(pair_kernel, in_specs=[smem, pl.BlockSpec(memory_space=plt...  9.28 us
  transfers between devices with their start and end apart: 22, of which 10 were waited for; matrix products, arithmetic and copies ran while one was open for 1% of the time, Pallas kernels for 18%

profile of v3, /device:TPU:0, one launch (start us, length us, event | category | flops | bytes accessed | tf_op | source)
XLA Modules:
  0.0 125.6 jit_solution(7263017299438445416)
XLA Ops:
  0.6 2.9 %collective-permute-start = (bf16[400,384]{1,0:T(8,128)(2,1)}, bf16[400,384]{1,0:T(8,128)(2,1)S(1)}, u32[]{:S(2)}, u32[]{:S(2)}) collective-permute-start(bf16[400,384]{1,0:T(8,128)(2,1)} %bitcast.29), channel_id=1, source_target_pairs={{0,96},{1,25},{2,98},{3,27},{4,100},{5,29},{6,102},{7,31},{8,104},... | collective-permute-start | bytes 921608 | tf_op jit(solution)/shard_map/ppermute | solution.py:243
  3.5 0.8 collective-permute-start.1
  4.4 0.9 collective-permute-start.2
  5.2 1.9 %collective-permute-start.3 = (bf16[400,384]{1,0:T(8,128)(2,1)}, bf16[400,384]{1,0:T(8,128)(2,1)S(1)}, u32[]{:S(2)}, u32[]{:S(2)}) collective-permute-start(bf16[400,384]{1,0:T(8,128)(2,1)} %bitcast.32), channel_id=1, source_target_pairs={{0,2},{1,7},{2,4},{3,1},{4,6},{5,3},{6,0},{7,5},{8,10},{9,15},{10,... | collective-permute-start | bytes 921608 | tf_op jit(solution)/shard_map/ppermute | solution.py:243
  7.2 2.1 %collective-permute-start.4 = (bf16[400,384]{1,0:T(8,128)(2,1)}, bf16[400,384]{1,0:T(8,128)(2,1)S(1)}, u32[]{:S(2)}, u32[]{:S(2)}) collective-permute-start(bf16[400,384]{1,0:T(8,128)(2,1)} %bitcast.33), channel_id=1, source_target_pairs={{0,6},{1,3},{2,0},{3,5},{4,2},{5,7},{6,4},{7,1},{8,14},{9,11},{10,... | collective-permute-start | bytes 921608 | tf_op jit(solution)/shard_map/ppermute | solution.py:243
  9.3 13.2 %shard_map.59 = (bf16[8,2,400,384]{3,2,1,0:T(8,128)(2,1)S(1)}, bf16[4,2,400,384]{3,2,1,0:T(8,128)(2,1)S(1)}, bf16[4,2,400,384]{3,2,1,0:T(8,128)(2,1)S(1)}, bf16[...) custom-call(s32[8]{0:T(128)} %partner_ref, ...), custom_call_target="tpu_custom_call" | custom-call | flops 1887436800 | bytes 25000000 | tf_op jit(solution)/shard_map/pallas_call | solution.py:128
  22.4 0.0 collective-permute-done
  22.4 0.0 collective-permute-done.1
  22.5 0.0 collective-permute-done.2
  22.5 0.2 fusion.1.rest_0_
  22.7 0.0 collective-permute-done.3
  22.7 0.0 collective-permute-done.4
  22.7 0.1 collective-permute-start.10
  22.8 1.9 %collective-permute-start.5 = (bf16[4,2,400,384]{3,2,1,0:T(8,128)(2,1)S(1)}, bf16[4,2,400,384]{3,2,1,0:T(8,128)(2,1)S(1)}, u32[]{:S(2)}, u32[]{:S(2)}) collective-permute-start(bf16[4,2,400,384]{3,2,1,0:T(8,128)(2,1)S(1)} %get-tuple-element.45), channel_id=1, source_target_pairs={{0,32},{1,9},{2,34},{3,11},{4,36},{5,13},{6,38},{7,15},{8,40},{9,1... | collective-permute-start | bytes 7372808 | tf_op jit(solution)/shard_map/ppermute | solution.py:243
  24.7 1.4 %collective-permute-start.6 = (bf16[4,2,400,384]{3,2,1,0:T(8,128)(2,1)S(1)}, bf16[4,2,400,384]{3,2,1,0:T(8,128)(2,1)S(1)}, u32[]{:S(2)}, u32[]{:S(2)}) collective-permute-start(bf16[4,2,400,384]{3,2,1,0:T(8,128)(2,1)S(1)} %get-tuple-element.46), channel_id=1, source_target_pairs={{0,96},{1,25},{2,98},{3,27},{4,100},{5,29},{6,102},{7,31},{8,104},... | collective-permute-start | bytes 7372808 | tf_op jit(solution)/shard_map/ppermute | solution.py:243
  26.1 3.2 %collective-permute-start.7 = (bf16[4,400,384]{2,1,0:T(8,128)(2,1)S(1)}, bf16[4,400,384]{2,1,0:T(8,128)(2,1)S(1)}, u32[]{:S(2)}, u32[]{:S(2)}) collective-permute-start(bf16[4,400,384]{2,1,0:T(8,128)(2,1)S(1)} %fusion.1.rest_0_), channel_id=1, source_target_pairs={{0,24},{1,97},{2,26},{3,99},{4,28},{5,101},{6,30},{7,103},{8,0},{9... | collective-permute-start | bytes 3686408 | tf_op jit(solution)/shard_map/ppermute | solution.py:243
  29.3 0.0 collective-permute-start.8
  29.4 1.9 %collective-permute-start.9 = (bf16[400,384]{1,0:T(8,128)(2,1)S(1)}, bf16[400,384]{1,0:T(8,128)(2,1)S(1)}, u32[]{:S(2)}, u32[]{:S(2)}) collective-permute-start(bf16[400,384]{1,0:T(8,128)(2,1)S(1)} %bitcast.36), channel_id=1, source_target_pairs={{0,4},{1,5},{2,6},{3,7},{4,0},{5,1},{6,2},{7,3},{8,12},{9,13},{10,... | collective-permute-start | bytes 921608 | tf_op jit(solution)/shard_map/ppermute | solution.py:243
  31.2 0.6 fusion.7
  31.9 6.9 %collective-permute-done.9 = bf16[400,384]{1,0:T(8,128)(2,1)S(1)} collective-permute-done((bf16[400,384]{1,0:T(8,128)(2,1)S(1)}, bf16[400,384]{1,0:T(8,128)(2,1)S(1)}, u32[]{:S(2)}, u32[]{:S(2)}) %collective-permute-start.9) | collective-permute-done | bytes 307232 | tf_op jit(solution)/shard_map/ppermute | solution.py:243
  38.8 0.2 collective-permute-start.11
  38.9 17.9 %collective-permute-done.7.rest_1_ = bf16[4,400,384]{2,1,0:T(8,128)(2,1)S(1)} collective-permute-done((bf16[4,400,384]{2,1,0:T(8,128)(2,1)S(1)}, bf16[4,400,384]{2,1,0:T(8,128)(2,1)S(1)}, u32[]{:S(2)}, u32[]{:S(2)}) %collective-permute-start.7) | collective-permute-done | bytes 1228832 | tf_op jit(solution)/shard_map/ppermute | solution.py:243
  56.8 1.8 %collective-permute-start.12 = (bf16[2,400,384]{2,1,0:T(8,128)(2,1)S(1)}, bf16[2,400,384]{2,1,0:T(8,128)(2,1)S(1)}, u32[]{:S(2)}, u32[]{:S(2)}) collective-permute-start(bf16[2,400,384]{2,1,0:T(8,128)(2,1)S(1)} %get-tuple-element.85), channel_id=1, source_target_pairs={{0,6},{1,3},{2,0},{3,5},{4,2},{5,7},{6,4},{7,1},{8,14},{9,11},{10,... | collective-permute-start | bytes 1843208 | tf_op jit(solution)/shard_map/ppermute | solution.py:243
  58.6 1.9 %collective-permute-done.8.rest_2_ = bf16[4,400,384]{2,1,0:T(8,128)(2,1)S(1)} collective-permute-done((bf16[4,400,384]{2,1,0:T(8,128)(2,1)S(1)}, bf16[4,400,384]{2,1,0:T(8,128)(2,1)S(1)}, u32[]{:S(2)}, u32[]{:S(2)}) %collective-permute-start.8) | collective-permute-done | bytes 1228832 | tf_op jit(solution)/shard_map/ppermute | solution.py:243
  60.5 1.9 %collective-permute-start.13 = (bf16[2,400,384]{2,1,0:T(8,128)(2,1)S(1)}, bf16[2,400,384]{2,1,0:T(8,128)(2,1)S(1)}, u32[]{:S(2)}, u32[]{:S(2)}) collective-permute-start(bf16[2,400,384]{2,1,0:T(8,128)(2,1)S(1)} %get-tuple-element.84), channel_id=1, source_target_pairs={{0,4},{1,5},{2,6},{3,7},{4,0},{5,1},{6,2},{7,3},{8,12},{9,13},{10,... | collective-permute-start | bytes 1843208 | tf_op jit(solution)/shard_map/ppermute | solution.py:243
  62.4 0.2 fusion.3.rest_5_
  62.6 4.6 %collective-permute-done.5 = bf16[4,2,400,384]{3,2,1,0:T(8,128)(2,1)S(1)} collective-permute-done((bf16[4,2,400,384]{3,2,1,0:T(8,128)(2,1)S(1)}, bf16[4,2,400,384]{3,2,1,0:T(8,128)(2,1)S(1)}, u32[]{:S(2)}, u32[]{:S(2)}) %collective-permute-start.5) | collective-permute-done | bytes 2457632 | tf_op jit(solution)/shard_map/ppermute | solution.py:243
  67.1 0.6 collective-permute-done.6
  67.7 11.7 %collective-permute-done.12 = bf16[2,400,384]{2,1,0:T(8,128)(2,1)S(1)} collective-permute-done((bf16[2,400,384]{2,1,0:T(8,128)(2,1)S(1)}, bf16[2,400,384]{2,1,0:T(8,128)(2,1)S(1)}, u32[]{:S(2)}, u32[]{:S(2)}) %collective-permute-start.12) | collective-permute-done | bytes 614432 | tf_op jit(solution)/shard_map/ppermute | solution.py:243
  79.5 0.7 add_convert_fusion
  80.2 0.7 collective-permute-start.14
  80.8 2.6 %collective-permute-start.15 = (bf16[2,2,400,384]{3,2,1,0:T(8,128)(2,1)S(1)}, bf16[2,2,400,384]{3,2,1,0:T(8,128)(2,1)S(1)}, u32[]{:S(2)}, u32[]{:S(2)}) collective-permute-start(bf16[2,2,400,384]{3,2,1,0:T(8,128)(2,1)S(1)} %get-tuple-element.61), channel_id=1, source_target_pairs={{0,96},{1,25},{2,98},{3,27},{4,100},{5,29},{6,102},{7,31},{8,104},... | collective-permute-start | bytes 3686408 | tf_op jit(solution)/shard_map/ppermute | solution.py:243
  83.5 0.1 slice.84
  83.5 1.2 collective-permute-start.16
  84.7 0.1 slice.85
  84.8 1.0 collective-permute-start.17
  85.8 14.6 %collective-permute-done.16.rest_3_ = bf16[2,400,384]{2,1,0:T(8,128)(2,1)S(1)} collective-permute-done((bf16[2,400,384]{2,1,0:T(8,128)(2,1)S(1)}, bf16[2,400,384]{2,1,0:T(8,128)(2,1)S(1)}, u32[]{:S(2)}, u32[]{:S(2)}) %collective-permute-start.16) | collective-permute-done | bytes 614432 | tf_op jit(solution)/shard_map/ppermute | solution.py:243
  100.4 2.5 %collective-permute-done.17.rest_4_ = bf16[2,400,384]{2,1,0:T(8,128)(2,1)S(1)} collective-permute-done((bf16[2,400,384]{2,1,0:T(8,128)(2,1)S(1)}, bf16[2,400,384]{2,1,0:T(8,128)(2,1)S(1)}, u32[]{:S(2)}, u32[]{:S(2)}) %collective-permute-start.17) | collective-permute-done | bytes 614432 | tf_op jit(solution)/shard_map/ppermute | solution.py:243
  102.9 1.9 %collective-permute-done.14 = bf16[2,2,400,384]{3,2,1,0:T(8,128)(2,1)S(1)} collective-permute-done((bf16[2,2,400,384]{3,2,1,0:T(8,128)(2,1)S(1)}, bf16[2,2,400,384]{3,2,1,0:T(8,128)(2,1)S(1)}, u32[]{:S(2)}, u32[]{:S(2)}) %collective-permute-start.14) | collective-permute-done | bytes 1228832 | tf_op jit(solution)/shard_map/ppermute | solution.py:243
  104.7 0.0 collective-permute-done.15
  104.7 0.7 fusion.11
  105.5 1.4 %collective-permute-start.19 = (bf16[2,400,384]{2,1,0:T(8,128)(2,1)S(1)}, bf16[2,400,384]{2,1,0:T(8,128)(2,1)S(1)}, u32[]{:S(2)}, u32[]{:S(2)}) collective-permute-start(bf16[2,400,384]{2,1,0:T(8,128)(2,1)S(1)} %get-tuple-element.88), channel_id=1, source_target_pairs={{0,8},{1,33},{2,10},{3,35},{4,12},{5,37},{6,14},{7,39},{8,16},{9,4... | collective-permute-start | bytes 1843208 | tf_op jit(solution)/shard_map/ppermute | solution.py:243
  106.9 1.9 %collective-permute-start.20 = (bf16[2,400,384]{2,1,0:T(8,128)(2,1)S(1)}, bf16[2,400,384]{2,1,0:T(8,128)(2,1)S(1)}, u32[]{:S(2)}, u32[]{:S(2)}) collective-permute-start(bf16[2,400,384]{2,1,0:T(8,128)(2,1)S(1)} %get-tuple-element.82), channel_id=1, source_target_pairs={{0,24},{1,97},{2,26},{3,99},{4,28},{5,101},{6,30},{7,103},{8,0},{9... | collective-permute-start | bytes 1843208 | tf_op jit(solution)/shard_map/ppermute | solution.py:243
  108.8 1.2 collective-permute-start.21
  110.0 0.5 convert_add_fusion
  110.5 9.3 %shard_map.60 = bf16[8,2,400,400]{3,2,1,0:T(8,128)(2,1)} custom-call(s32[8]{0:T(128)S(1)} %copy-done.1, bf16[8,2,400,384]{3,2,1,0:T(8,128)(2,1)S(1)} %get-tuple-element.68.left_ref, bf16[4,400,384]{2,1,0:T(8,128)(2,1)S(1)} %fusion.1.rest_0_, bf16[4,400,384]{2,1,0:T(8,128)(2,1)S(1)} %collective-permute-done.7.rest_1_, ...), custom_call_target="tpu_custom_call" | custom-call | flops 1966080000 | bytes 15000000 | tf_op jit(solution)/shard_map/pallas_call | solution.py:199
  119.8 3.7 %collective-permute-done.19.rest_0_ = bf16[2,400,384]{2,1,0:T(8,128)(2,1)S(1)} collective-permute-done((bf16[2,400,384]{2,1,0:T(8,128)(2,1)S(1)}, bf16[2,400,384]{2,1,0:T(8,128)(2,1)S(1)}, u32[]{:S(2)}, u32[]{:S(2)}) %collective-permute-start.19) | collective-permute-done | bytes 614432 | tf_op jit(solution)/shard_map/ppermute | solution.py:243
  123.5 2.1 %shard_map.61 = f32[2,400,400]{2,1,0:T(8,128)} custom-call(bf16[400,384]{1,0:T(8,128)(2,1)S(1)} %bitcast.38, f32[2,400,384]{2,1,0:T(8,128)S(1)} %convert_add_fusion, bf16[2,400,384]{2,1,0:T(8,128)(2,1)S(1)} %collective-permute-done.19.rest_0_, bf16[2,400,384]{2,1,0:T(8,128)(2,1)S(1)} %collective-permute-done.20.rest_1_, ...), custom_call_target="tpu_custom_call" | custom-call | tf_op jit(solution)/shard_map/pallas_call | solution.py:230
  (11 shorter events, 0.0 us)
Async XLA Ops:
  0.6 21.8 %copy-start = (bf16[1,384,400]{1,2,0:T(8,128)(2,1)S(1)}, bf16[1,384,400]{1,2,0:T(8,128)(2,1)}, u32[]{:S(2)}) copy-start(bf16[1,384,400]{1,2,0:T(8,128)(2,1)} %param.4) | copy-start | bytes 921604
  0.6 21.8 %collective-permute-start = (bf16[400,384]{1,0:T(8,128)(2,1)}, bf16[400,384]{1,0:T(8,128)(2,1)S(1)}, u32[]{:S(2)}, u32[]{:S(2)}) collective-permute-start(bf16[400,384]{1,0:T(8,128)(2,1)} %bitcast.29), channel_id=1, source_target_pairs={{0,96},{1,25},{2,98},{3,27},{4,100},{5,29},{6,102},{7,31},{8,104},... | collective-permute-start | bytes 921608 | tf_op jit(solution)/shard_map/ppermute | solution.py:243
  3.5 18.9 %collective-permute-start.1 = (bf16[400,384]{1,0:T(8,128)(2,1)}, bf16[400,384]{1,0:T(8,128)(2,1)S(1)}, u32[]{:S(2)}, u32[]{:S(2)}) collective-permute-start(bf16[400,384]{1,0:T(8,128)(2,1)} %bitcast.30), channel_id=1, source_target_pairs={{0,64},{1,17},{2,66},{3,19},{4,68},{5,21},{6,70},{7,23},{8,72},{9,... | collective-permute-start | bytes 921608 | tf_op jit(solution)/shard_map/ppermute | solution.py:243
  4.4 18.1 %collective-permute-start.2 = (bf16[400,384]{1,0:T(8,128)(2,1)}, bf16[400,384]{1,0:T(8,128)(2,1)S(1)}, u32[]{:S(2)}, u32[]{:S(2)}) collective-permute-start(bf16[400,384]{1,0:T(8,128)(2,1)} %bitcast.31), channel_id=1, source_target_pairs={{0,32},{1,9},{2,34},{3,11},{4,36},{5,13},{6,38},{7,15},{8,40},{9,1... | collective-permute-start | bytes 921608 | tf_op jit(solution)/shard_map/ppermute | solution.py:243
  5.2 17.4 %collective-permute-start.3 = (bf16[400,384]{1,0:T(8,128)(2,1)}, bf16[400,384]{1,0:T(8,128)(2,1)S(1)}, u32[]{:S(2)}, u32[]{:S(2)}) collective-permute-start(bf16[400,384]{1,0:T(8,128)(2,1)} %bitcast.32), channel_id=1, source_target_pairs={{0,2},{1,7},{2,4},{3,1},{4,6},{5,3},{6,0},{7,5},{8,10},{9,15},{10,... | collective-permute-start | bytes 921608 | tf_op jit(solution)/shard_map/ppermute | solution.py:243
  7.2 15.5 %collective-permute-start.4 = (bf16[400,384]{1,0:T(8,128)(2,1)}, bf16[400,384]{1,0:T(8,128)(2,1)S(1)}, u32[]{:S(2)}, u32[]{:S(2)}) collective-permute-start(bf16[400,384]{1,0:T(8,128)(2,1)} %bitcast.33), channel_id=1, source_target_pairs={{0,6},{1,3},{2,0},{3,5},{4,2},{5,7},{6,4},{7,1},{8,14},{9,11},{10,... | collective-permute-start | bytes 921608 | tf_op jit(solution)/shard_map/ppermute | solution.py:243
  22.7 6.7 %collective-permute-start.10 = (bf16[4,2,400,384]{3,2,1,0:T(8,128)(2,1)S(1)}, bf16[4,2,400,384]{3,2,1,0:T(8,128)(2,1)S(1)}, u32[]{:S(2)}, u32[]{:S(2)}) collective-permute-start(bf16[4,2,400,384]{3,2,1,0:T(8,128)(2,1)S(1)} %get-tuple-element.52), channel_id=1, source_target_pairs={{0,1},{1,0},{2,3},{3,2},{4,5},{5,4},{6,7},{7,6},{8,9},{9,8},{10,11... | collective-permute-start | bytes 7372808 | tf_op jit(solution)/shard_map/ppermute | solution.py:243
  22.8 44.3 %collective-permute-start.5 = (bf16[4,2,400,384]{3,2,1,0:T(8,128)(2,1)S(1)}, bf16[4,2,400,384]{3,2,1,0:T(8,128)(2,1)S(1)}, u32[]{:S(2)}, u32[]{:S(2)}) collective-permute-start(bf16[4,2,400,384]{3,2,1,0:T(8,128)(2,1)S(1)} %get-tuple-element.45), channel_id=1, source_target_pairs={{0,32},{1,9},{2,34},{3,11},{4,36},{5,13},{6,38},{7,15},{8,40},{9,1... | collective-permute-start | bytes 7372808 | tf_op jit(solution)/shard_map/ppermute | solution.py:243
  24.7 43.1 %collective-permute-start.6 = (bf16[4,2,400,384]{3,2,1,0:T(8,128)(2,1)S(1)}, bf16[4,2,400,384]{3,2,1,0:T(8,128)(2,1)S(1)}, u32[]{:S(2)}, u32[]{:S(2)}) collective-permute-start(bf16[4,2,400,384]{3,2,1,0:T(8,128)(2,1)S(1)} %get-tuple-element.46), channel_id=1, source_target_pairs={{0,96},{1,25},{2,98},{3,27},{4,100},{5,29},{6,102},{7,31},{8,104},... | collective-permute-start | bytes 7372808 | tf_op jit(solution)/shard_map/ppermute | solution.py:243
  26.1 30.7 %collective-permute-start.7 = (bf16[4,400,384]{2,1,0:T(8,128)(2,1)S(1)}, bf16[4,400,384]{2,1,0:T(8,128)(2,1)S(1)}, u32[]{:S(2)}, u32[]{:S(2)}) collective-permute-start(bf16[4,400,384]{2,1,0:T(8,128)(2,1)S(1)} %fusion.1.rest_0_), channel_id=1, source_target_pairs={{0,24},{1,97},{2,26},{3,99},{4,28},{5,101},{6,30},{7,103},{8,0},{9... | collective-permute-start | bytes 3686408 | tf_op jit(solution)/shard_map/ppermute | solution.py:243
  29.3 31.2 %collective-permute-start.8 = (bf16[4,400,384]{2,1,0:T(8,128)(2,1)S(1)}, bf16[4,400,384]{2,1,0:T(8,128)(2,1)S(1)}, u32[]{:S(2)}, u32[]{:S(2)}) collective-permute-start(bf16[4,400,384]{2,1,0:T(8,128)(2,1)S(1)} %fusion.1.rest_0_), channel_id=1, source_target_pairs={{0,8},{1,33},{2,10},{3,35},{4,12},{5,37},{6,14},{7,39},{8,16},{9,4... | collective-permute-start | bytes 3686408 | tf_op jit(solution)/shard_map/ppermute | solution.py:243
  29.4 9.4 %collective-permute-start.9 = (bf16[400,384]{1,0:T(8,128)(2,1)S(1)}, bf16[400,384]{1,0:T(8,128)(2,1)S(1)}, u32[]{:S(2)}, u32[]{:S(2)}) collective-permute-start(bf16[400,384]{1,0:T(8,128)(2,1)S(1)} %bitcast.36), channel_id=1, source_target_pairs={{0,4},{1,5},{2,6},{3,7},{4,0},{5,1},{6,2},{7,3},{8,12},{9,13},{10,... | collective-permute-start | bytes 921608 | tf_op jit(solution)/shard_map/ppermute | solution.py:243
  38.8 29.0 %collective-permute-start.11 = (bf16[2,400,384]{2,1,0:T(8,128)(2,1)S(1)}, bf16[2,400,384]{2,1,0:T(8,128)(2,1)S(1)}, u32[]{:S(2)}, u32[]{:S(2)}) collective-permute-start(bf16[2,400,384]{2,1,0:T(8,128)(2,1)S(1)} %get-tuple-element.86), channel_id=1, source_target_pairs={{0,2},{1,7},{2,4},{3,1},{4,6},{5,3},{6,0},{7,5},{8,10},{9,15},{10,... | collective-permute-start | bytes 1843208 | tf_op jit(solution)/shard_map/ppermute | solution.py:243
  56.8 22.6 %collective-permute-start.12 = (bf16[2,400,384]{2,1,0:T(8,128)(2,1)S(1)}, bf16[2,400,384]{2,1,0:T(8,128)(2,1)S(1)}, u32[]{:S(2)}, u32[]{:S(2)}) collective-permute-start(bf16[2,400,384]{2,1,0:T(8,128)(2,1)S(1)} %get-tuple-element.85), channel_id=1, source_target_pairs={{0,6},{1,3},{2,0},{3,5},{4,2},{5,7},{6,4},{7,1},{8,14},{9,11},{10,... | collective-permute-start | bytes 1843208 | tf_op jit(solution)/shard_map/ppermute | solution.py:243
  60.5 19.0 %collective-permute-start.13 = (bf16[2,400,384]{2,1,0:T(8,128)(2,1)S(1)}, bf16[2,400,384]{2,1,0:T(8,128)(2,1)S(1)}, u32[]{:S(2)}, u32[]{:S(2)}) collective-permute-start(bf16[2,400,384]{2,1,0:T(8,128)(2,1)S(1)} %get-tuple-element.84), channel_id=1, source_target_pairs={{0,4},{1,5},{2,6},{3,7},{4,0},{5,1},{6,2},{7,3},{8,12},{9,13},{10,... | collective-permute-start | bytes 1843208 | tf_op jit(solution)/shard_map/ppermute | solution.py:243
  80.2 24.6 %collective-permute-start.14 = (bf16[2,2,400,384]{3,2,1,0:T(8,128)(2,1)S(1)}, bf16[2,2,400,384]{3,2,1,0:T(8,128)(2,1)S(1)}, u32[]{:S(2)}, u32[]{:S(2)}) collective-permute-start(bf16[2,2,400,384]{3,2,1,0:T(8,128)(2,1)S(1)} %get-tuple-element.60), channel_id=1, source_target_pairs={{0,32},{1,9},{2,34},{3,11},{4,36},{5,13},{6,38},{7,15},{8,40},{9,1... | collective-permute-start | bytes 3686408 | tf_op jit(solution)/shard_map/ppermute | solution.py:243
  80.8 23.9 %collective-permute-start.15 = (bf16[2,2,400,384]{3,2,1,0:T(8,128)(2,1)S(1)}, bf16[2,2,400,384]{3,2,1,0:T(8,128)(2,1)S(1)}, u32[]{:S(2)}, u32[]{:S(2)}) collective-permute-start(bf16[2,2,400,384]{3,2,1,0:T(8,128)(2,1)S(1)} %get-tuple-element.61), channel_id=1, source_target_pairs={{0,96},{1,25},{2,98},{3,27},{4,100},{5,29},{6,102},{7,31},{8,104},... | collective-permute-start | bytes 3686408 | tf_op jit(solution)/shard_map/ppermute | solution.py:243
  83.5 21.3 %collective-permute-start.18 = (bf16[4,400,384]{2,1,0:T(8,128)(2,1)S(1)}, bf16[4,400,384]{2,1,0:T(8,128)(2,1)S(1)}, u32[]{:S(2)}, u32[]{:S(2)}) collective-permute-start(bf16[4,400,384]{2,1,0:T(8,128)(2,1)S(1)} %fusion.3.rest_5_), channel_id=1, source_target_pairs={{0,1},{1,0},{2,3},{3,2},{4,5},{5,4},{6,7},{7,6},{8,9},{9,8},{10,11... | collective-permute-start | bytes 3686408 | tf_op jit(solution)/shard_map/ppermute | solution.py:243
  83.5 16.9 %collective-permute-start.16 = (bf16[2,400,384]{2,1,0:T(8,128)(2,1)S(1)}, bf16[2,400,384]{2,1,0:T(8,128)(2,1)S(1)}, u32[]{:S(2)}, u32[]{:S(2)}) collective-permute-start(bf16[2,400,384]{2,1,0:T(8,128)(2,1)S(1)} %slice.84), channel_id=1, source_target_pairs={{0,24},{1,97},{2,26},{3,99},{4,28},{5,101},{6,30},{7,103},{8,0},{9... | collective-permute-start | bytes 1843208 | tf_op jit(solution)/shard_map/ppermute | solution.py:243
  84.8 18.1 %collective-permute-start.17 = (bf16[2,400,384]{2,1,0:T(8,128)(2,1)S(1)}, bf16[2,400,384]{2,1,0:T(8,128)(2,1)S(1)}, u32[]{:S(2)}, u32[]{:S(2)}) collective-permute-start(bf16[2,400,384]{2,1,0:T(8,128)(2,1)S(1)} %slice.85), channel_id=1, source_target_pairs={{0,8},{1,33},{2,10},{3,35},{4,12},{5,37},{6,14},{7,39},{8,16},{9,4... | collective-permute-start | bytes 1843208 | tf_op jit(solution)/shard_map/ppermute | solution.py:243
  105.5 18.0 %collective-permute-start.19 = (bf16[2,400,384]{2,1,0:T(8,128)(2,1)S(1)}, bf16[2,400,384]{2,1,0:T(8,128)(2,1)S(1)}, u32[]{:S(2)}, u32[]{:S(2)}) collective-permute-start(bf16[2,400,384]{2,1,0:T(8,128)(2,1)S(1)} %get-tuple-element.88), channel_id=1, source_target_pairs={{0,8},{1,33},{2,10},{3,35},{4,12},{5,37},{6,14},{7,39},{8,16},{9,4... | collective-permute-start | bytes 1843208 | tf_op jit(solution)/shard_map/ppermute | solution.py:243
  106.9 16.6 %collective-permute-start.20 = (bf16[2,400,384]{2,1,0:T(8,128)(2,1)S(1)}, bf16[2,400,384]{2,1,0:T(8,128)(2,1)S(1)}, u32[]{:S(2)}, u32[]{:S(2)}) collective-permute-start(bf16[2,400,384]{2,1,0:T(8,128)(2,1)S(1)} %get-tuple-element.82), channel_id=1, source_target_pairs={{0,24},{1,97},{2,26},{3,99},{4,28},{5,101},{6,30},{7,103},{8,0},{9... | collective-permute-start | bytes 1843208 | tf_op jit(solution)/shard_map/ppermute | solution.py:243
  108.8 1.7 %copy-start.1 = (s32[8]{0:T(128)S(1)}, s32[8]{0:T(128)}, u32[]{:S(2)}) copy-start(s32[8]{0:T(128)} %partner_ref) | copy-start | bytes 100
  108.8 14.7 %collective-permute-start.21 = (bf16[2,400,384]{2,1,0:T(8,128)(2,1)S(1)}, bf16[2,400,384]{2,1,0:T(8,128)(2,1)S(1)}, u32[]{:S(2)}, u32[]{:S(2)}) collective-permute-start(bf16[2,400,384]{2,1,0:T(8,128)(2,1)S(1)} %get-tuple-element.83), channel_id=1, source_target_pairs={{0,16},{1,65},{2,18},{3,67},{4,20},{5,69},{6,22},{7,71},{8,24},{9,... | collective-permute-start | bytes 1843208 | tf_op jit(solution)/shard_map/ppermute | solution.py:243

commit v4 on v2

--- a/solution.py
+++ b/solution.py
@@ -33,19 +33,16 @@
     return (other // 2 - me // 2 + SIDE) % SIDE, other % 2, me % 2
 
 
-def left_kernel(partner_hbm, counts_hbm, own_hbm, coupling_hbm, left_hbm, *rest):
+def left_kernel(partner_hbm, counts_hbm, own_hbm, coupling_hbm, left_ref, *rest):
     outs = rest[:7]
-    partner_ref, counts_ref, own_ref, blocks, lefts, zero, sums = rest[7:14]
-    keys, number, seen, at_sum, in_sem, left_sem, out_sem = rest[14:]
+    partner_ref, counts_ref, own_ref, blocks, zero, sums = rest[7:13]
+    keys, number, seen, at_sum, in_sem, out_sem = rest[13:]
     count, pairs = blocks.shape[0], keys.shape[0]
     modes, width = own_ref.shape
     slots = SPAN_X + SPAN_Y
 
     def load(i):
         return pltpu.make_async_copy(coupling_hbm.at[i // 2, i % 2], blocks.at[i], in_sem.at[i])
-
-    def save(i):
-        return pltpu.make_async_copy(lefts.at[i], left_hbm.at[i // 2, i % 2], left_sem.at[i])
 
     load_partner = pltpu.make_async_copy(partner_hbm, partner_ref, in_sem.at[count + 1])
     load_partner.start()
@@ -103,14 +100,13 @@
         keep = lax.broadcasted_iota(jnp.int32, (1, width), 1) < counts_ref[p]
         own = jnp.where(keep, own_ref[...], jnp.zeros((modes, width), own_ref.dtype))
         product = jnp.dot(own, blocks[i], preferred_element_type=jnp.float32)
-        lefts[i] = jnp.where(keep, product, 0.0).astype(jnp.bfloat16)
-        save(i).start()
+        left_ref[p, i % 2] = jnp.where(keep, product, 0.0).astype(jnp.bfloat16)
         key = keys[p]
         single = number[key] == 1
 
         @pl.when((i % 2 == 1) & single)
         def _():
-            send(lefts.at[pl.ds(i - 1, 2)], key)
+            send(left_ref.at[p], key)
 
         @pl.when((i % 2 == 1) & jnp.logical_not(single))
         def _():
@@ -128,16 +124,12 @@
             def _(r):
                 t, rows = r % 2, pl.ds(pl.multiple_of(r // 2 * CHUNK, CHUNK), CHUNK)
                 before = jnp.where(fresh, 0.0, sums[place, t, rows].astype(jnp.float32))
-                sums[place, t, rows] = (before + lefts[i - 1 + t, rows].astype(jnp.float32)).astype(jnp.bfloat16)
+                sums[place, t, rows] = (before + left_ref[p, t, rows].astype(jnp.float32)).astype(jnp.bfloat16)
 
             @pl.when(seen[key] == number[key])
             def _():
                 send(sums.at[place], key)
 
-    @pl.loop(0, count)
-    def _(i):
-        save(i).wait()
-
     @pl.loop(0, slots)
     def _(k):
         pltpu.make_async_copy(zero, outs[0].at[0], out_sem.at[k]).wait()
@@ -150,20 +142,18 @@
 def left_products(own, coupling, partner, counts):
     pairs, blocks, width, _ = coupling.shape
     modes = own.shape[0]
-    hbm = pl.BlockSpec(memory_space=pltpu.HBM)
     slots = SPAN_X + SPAN_Y
     sizes = [pairs] + [size for _, size in PARTS] + [SIDE] * 2
     out = pl.pallas_call(
         left_kernel,
-        in_specs=[hbm] * 4,
-        out_specs=[hbm] * len(sizes),
-        out_shape=[pltpu.HBM((n, blocks, modes, width), jnp.bfloat16) for n in sizes],
+        in_specs=[pl.BlockSpec(memory_space=pltpu.HBM)] * 4,
+        out_specs=[pl.BlockSpec(memory_space=pltpu.VMEM)] * len(sizes),
+        out_shape=[pltpu.VMEM((n, blocks, modes, width), jnp.bfloat16) for n in sizes],
         scratch_shapes=[
             pltpu.SMEM((pairs,), jnp.int32),
             pltpu.SMEM((pairs,), jnp.int32),
             pltpu.VMEM((modes, width), jnp.bfloat16),
             pltpu.VMEM((pairs * blocks, width, width), jnp.bfloat16),
-            pltpu.VMEM((pairs * blocks, modes, width), jnp.bfloat16),
             pltpu.VMEM((blocks, modes, width), jnp.bfloat16),
             pltpu.VMEM((pairs // 2, blocks, modes, width), jnp.bfloat16),
             pltpu.SMEM((pairs,), jnp.int32),
@@ -171,10 +161,9 @@
             pltpu.SMEM((slots,), jnp.int32),
             pltpu.SMEM((slots + 1,), jnp.int32),
             pltpu.SemaphoreType.DMA((pairs * blocks + 3,)),
-            pltpu.SemaphoreType.DMA((pairs * blocks,)),
             pltpu.SemaphoreType.DMA((slots,)),
         ],
-        compiler_params=pltpu.CompilerParams(vmem_limit_bytes=20 * 2**20),
+        compiler_params=pltpu.CompilerParams(vmem_limit_bytes=12 * 2**20),
         cost_estimate=pl.CostEstimate(flops=2 * pairs * blocks * modes * width * width,
                                       bytes_accessed=25 * 10**6, transcendentals=0),
     )(*map(in_hbm, (partner, counts, own, coupling)))
@@ -185,21 +174,16 @@
     return lax.dot_general(a, b, (((1,), (1,)), ((), ())), preferred_element_type=jnp.float32)
 
 
-def pair_kernel(partner_ref, left_hbm, *rest):
-    (kept, near, far, low, high, ring_mine, ring_other), out_hbm = rest[:7], rest[7]
-    lefts, panels, outs, left_sem, panel_sem, out_sem = rest[8:]
-    pairs, count = panels.shape[0], lefts.shape[0]
-
-    def load(i):
-        return pltpu.make_async_copy(left_hbm.at[i // 2, i % 2], lefts.at[i], left_sem.at[i])
+def pair_kernel(partner_ref, left_ref, *rest):
+    (kept, near, far, low, high, ring_mine, ring_other, across), out_hbm = rest[:8], rest[8]
+    panels, outs, panel_sem, out_sem = rest[9:]
+    pairs, count = panels.shape[0], outs.shape[0]
 
     def save(i):
         return pltpu.make_async_copy(outs.at[i], out_hbm.at[i // 2, i % 2], out_sem.at[i])
 
     @pl.loop(0, pairs)
     def _(q):
-        load(2 * q).start()
-        load(2 * q + 1).start()
         code = partner_ref[q]
         d1, d2 = offsets(code)
         dz, core, me = ring_offset(code)
@@ -211,8 +195,9 @@
             (far, d1, along & (d2 == 3)),
             (low, d1, along & (d2 == 2) & (d1 < 2)),
             (high, d1 - 2, along & (d2 == 2) & (d1 >= 2)),
-            (ring_mine, step, (code >= SPAN_X) & (core == me)),
-            (ring_other, step, (code >= SPAN_X) & (core != me)),
+            (ring_mine, step, (code >= SPAN_X) & (dz != 2) & (core == me)),
+            (ring_other, step, (code >= SPAN_X) & (dz != 2) & (core != me)),
+            (across, jnp.where(core == me, 0, 1), (code >= SPAN_X) & (dz == 2)),
         ):
             @pl.when(chosen)
             def _():
@@ -226,8 +211,7 @@
         def _():
             pltpu.make_async_copy(kept.at[0], panels.at[p], panel_sem.at[p]).wait()
 
-        load(i).wait()
-        outs[i] = nt(lefts[i], panels[p]).astype(jnp.bfloat16)
+        outs[i] = nt(left_ref[p, i % 2], panels[p]).astype(jnp.bfloat16)
         save(i).start()
 
     @pl.loop(0, count)
@@ -240,21 +224,19 @@
     hbm, smem = pl.BlockSpec(memory_space=pltpu.HBM), pl.BlockSpec(memory_space=pltpu.SMEM)
     return pl.pallas_call(
         pair_kernel,
-        in_specs=[smem] + [hbm] * 8,
+        in_specs=[smem, pl.BlockSpec(memory_space=pltpu.VMEM)] + [pl.BlockSpec(memory_space=pl.ANY)] * 8,
         out_specs=hbm,
         out_shape=jax.ShapeDtypeStruct((pairs, blocks, modes, modes), jnp.bfloat16),
         scratch_shapes=[
-            pltpu.VMEM((pairs * blocks, modes, width), jnp.bfloat16),
             pltpu.VMEM((pairs, modes, width), jnp.bfloat16),
             pltpu.VMEM((pairs * blocks, modes, modes), jnp.bfloat16),
-            pltpu.SemaphoreType.DMA((pairs * blocks,)),
             pltpu.SemaphoreType.DMA((pairs,)),
             pltpu.SemaphoreType.DMA((pairs * blocks,)),
         ],
-        compiler_params=pltpu.CompilerParams(vmem_limit_bytes=20 * 2**20),
+        compiler_params=pltpu.CompilerParams(vmem_limit_bytes=14 * 2**20),
         cost_estimate=pl.CostEstimate(flops=2 * pairs * blocks * modes * width * modes,
                                       bytes_accessed=15 * 10**6, transcendentals=0),
-    )(partner, in_hbm(left), *map(in_hbm, sources))
+    )(partner, left, *sources)
 
 
 def partner_kernel(own_ref, sum_ref, *rest):
@@ -327,22 +309,24 @@
 
     got = [first(up, 1), first(down, -1)]
     near, far = second(kept, -1), second(kept, 1)
-    ring3 = turn(own_z, 2)
-    ring_mine = jnp.stack([own, ring1, ring2, ring3])
+    ring_mine = jnp.stack([own, ring1, ring2])
     pair_sum = swap(z_other)
     w = [rounded(z_mine[k], pair_sum[k]) for k in range(SIDE)]
-    z1 = turn(w[1], 1)
-    got, near, far, ring_mine, w, z1 = barrier((got, near, far, ring_mine, w, z1))
+    ring_other = swap(after(ring_mine, w))
+    opposite, back = turn(after(w[3], ring_other), 1), turn(w[2], -1)
+    got, near, far, ring_mine, ring_other, w, opposite, back = barrier(
+        (got, near, far, ring_mine, ring_other, w, opposite, back)
+    )
     got_up, got_down = got
 
     b_up, b_down = rounded(pass_up, got_up[:2]), rounded(pass_down, got_down[:2])
-    b_up, b_down, near, far, ring_mine, w = barrier((b_up, b_down, near, far, ring_mine, w))
+    across = jnp.stack([ring_mine[2], ring_other[1]])
+    z_pass = rounded(w[1], opposite)
+    b_up, b_down, near, far, across, z_pass = barrier((b_up, b_down, near, far, across, z_pass))
+    low, high = second(near[:2], -1), second(far[2:], 1)
+    across = turn(across, -1)
     last = [first(b_up, 1), first(b_down, -1)]
-    low, high = second(near[:2], -1), second(far[2:], 1)
-    ring_other = swap(ring_mine)
-    z2 = turn(w[2], -1)
-    z3 = turn(after(w[3], z2), 2)
-    last, low, high, ring_other, z2, z3 = barrier((last, low, high, ring_other, z2, z3))
+    last, low, high, across, z_pass = barrier((last, low, high, across, z_pass))
     last_up, last_down = last
 
     v = [
@@ -351,12 +335,14 @@
         rounded(here[2], got_up[2], last_down[0]),
         rounded(here[3], got_up[3], last_down[1]),
     ]
+    v, z_pass = barrier((v, z_pass))
+    z_last = turn(z_pass, 1)
     ends = [second(v[1], 1), second(v[3], -1), second(v[2], 2)]
 
-    sources = [kept, near, far, low, high, ring_mine, ring_other]
+    sources = [kept, near, far, low, high, ring_mine, ring_other, across]
     pair_blocks = pair_products(left, sources, after(partner, *v))
-    pair_blocks, ends = barrier((pair_blocks, ends))
-    partner_blocks = partner_products(own, added(v[0], w[0], z1, z2, z3), ends)
+    pair_blocks, ends, z_last = barrier((pair_blocks, ends, z_last))
+    partner_blocks = partner_products(own, added(v[0], w[0], back, z_last), ends)
     return (pair_blocks, partner_blocks[None])
 
 

time: 120 us -> 117 us (0.975)
  waiting for transfers between devices: 60.7 us -> 56 us
  Pallas kernels: 21.6 us -> 25 us
    ppermute x22, waiting for transfers between devices: 60.7 us -> 56 us  [permuted(): return lax.ppermute(value, ('sx', 'sy'), pairs)]
    pallas_call x2, Pallas kernels: 19.6 us -> 23 us  [the longest x1 13.6 us: left_products(): pl.pallas_call(left_kernel, in_specs=[pl.BlockSpec(memory_space=pltpu.HBM...]
    convert_element_type x3 -> x4, other arithmetic: 2.05 us -> 2.43 us  [rounded(): return added(*terms).astype(jnp.bfloat16)]
  transfers between devices with their start and end apart: 22 -> 22, of which waited for: 11 -> 11; matrix products, arithmetic and copies ran while one was open for 1% -> 1% of each run, Pallas kernels for 16% -> 20%
where the time goes in v4:
time: 117 us; the launch traced here: 118 us
  waiting for transfers between devices  56 us (48%)
  starting transfers between devices  32.4 us (28%)
  Pallas kernels  25 us (21%)
  other arithmetic  3.1 us (3%)
    ppermute x22, waiting for transfers between devices, permuted(): return lax.ppermute(value, ('sx', 'sy'), pairs)  56 us
    ppermute x22, starting transfers between devices, permuted(): return lax.ppermute(value, ('sx', 'sy'), pairs)  32.4 us
    pallas_call x1, Pallas kernels, left_products(): pl.pallas_call(left_kernel, in_specs=[pl.BlockSpec(memory_space=pltpu.HBM...  13.6 us
    pallas_call x1, Pallas kernels, pair_products(): pl.pallas_call(pair_kernel, in_specs=[smem, pl.BlockSpec(memory_space=plt...  9.34 us
    convert_element_type x4, other arithmetic, rounded(): return added(*terms).astype(jnp.bfloat16)  2.43 us
  transfers between devices with their start and end apart: 22, of which 11 were waited for; matrix products, arithmetic and copies ran while one was open for 1% of the time, Pallas kernels for 20%

profile of v4, /device:TPU:0, one launch (start us, length us, event | category | flops | bytes accessed | tf_op | source)
XLA Modules:
  0.0 117.6 jit_solution(984137909672096437)
XLA Ops:
  0.6 2.9 %collective-permute-start = (bf16[400,384]{1,0:T(8,128)(2,1)}, bf16[400,384]{1,0:T(8,128)(2,1)S(1)}, u32[]{:S(2)}, u32[]{:S(2)}) collective-permute-start(bf16[400,384]{1,0:T(8,128)(2,1)} %bitcast.27), channel_id=1, source_target_pairs={{0,96},{1,25},{2,98},{3,27},{4,100},{5,29},{6,102},{7,31},{8,104},... | collective-permute-start | bytes 921608 | tf_op jit(solution)/shard_map/ppermute | solution.py:269
  3.5 0.8 collective-permute-start.1
  4.4 0.9 collective-permute-start.2
  5.2 1.9 %collective-permute-start.3 = (bf16[400,384]{1,0:T(8,128)(2,1)}, bf16[400,384]{1,0:T(8,128)(2,1)S(1)}, u32[]{:S(2)}, u32[]{:S(2)}) collective-permute-start(bf16[400,384]{1,0:T(8,128)(2,1)} %bitcast.30), channel_id=1, source_target_pairs={{0,2},{1,7},{2,4},{3,1},{4,6},{5,3},{6,0},{7,5},{8,10},{9,15},{10,... | collective-permute-start | bytes 921608 | tf_op jit(solution)/shard_map/ppermute | solution.py:269
  7.2 2.1 %collective-permute-start.4 = (bf16[400,384]{1,0:T(8,128)(2,1)}, bf16[400,384]{1,0:T(8,128)(2,1)S(1)}, u32[]{:S(2)}, u32[]{:S(2)}) collective-permute-start(bf16[400,384]{1,0:T(8,128)(2,1)} %bitcast.31), channel_id=1, source_target_pairs={{0,6},{1,3},{2,0},{3,5},{4,2},{5,7},{6,4},{7,1},{8,14},{9,11},{10,... | collective-permute-start | bytes 921608 | tf_op jit(solution)/shard_map/ppermute | solution.py:269
  9.3 13.6 %shard_map.59 = (bf16[8,2,400,384]{3,2,1,0:T(8,128)(2,1)S(1)}, bf16[4,2,400,384]{3,2,1,0:T(8,128)(2,1)S(1)}, bf16[4,2,400,384]{3,2,1,0:T(8,128)(2,1)S(1)}, bf16[...) custom-call(s32[8]{0:T(128)} %partner_ref, ...), custom_call_target="tpu_custom_call" | custom-call | flops 1887436800 | bytes 25000000 | tf_op jit(solution)/shard_map/pallas_call | solution.py:147
  22.9 0.0 collective-permute-done
  22.9 0.2 pad_maximum_fusion.rest_0_
  23.2 0.0 collective-permute-done.4
  23.2 0.1 collective-permute-start.9
  23.3 1.9 %collective-permute-start.5 = (bf16[4,2,400,384]{3,2,1,0:T(8,128)(2,1)S(1)}, bf16[4,2,400,384]{3,2,1,0:T(8,128)(2,1)S(1)}, u32[]{:S(2)}, u32[]{:S(2)}) collective-permute-start(bf16[4,2,400,384]{3,2,1,0:T(8,128)(2,1)S(1)} %get-tuple-element.55), channel_id=1, source_target_pairs={{0,32},{1,9},{2,34},{3,11},{4,36},{5,13},{6,38},{7,15},{8,40},{9,1... | collective-permute-start | bytes 7372808 | tf_op jit(solution)/shard_map/ppermute | solution.py:269
  25.1 1.7 %collective-permute-start.6 = (bf16[4,2,400,384]{3,2,1,0:T(8,128)(2,1)S(1)}, bf16[4,2,400,384]{3,2,1,0:T(8,128)(2,1)S(1)}, u32[]{:S(2)}, u32[]{:S(2)}) collective-permute-start(bf16[4,2,400,384]{3,2,1,0:T(8,128)(2,1)S(1)} %get-tuple-element.56), channel_id=1, source_target_pairs={{0,96},{1,25},{2,98},{3,27},{4,100},{5,29},{6,102},{7,31},{8,104},... | collective-permute-start | bytes 7372808 | tf_op jit(solution)/shard_map/ppermute | solution.py:269
  26.8 3.1 %collective-permute-start.7 = (bf16[4,400,384]{2,1,0:T(8,128)(2,1)S(1)}, bf16[4,400,384]{2,1,0:T(8,128)(2,1)S(1)}, u32[]{:S(2)}, u32[]{:S(2)}) collective-permute-start(bf16[4,400,384]{2,1,0:T(8,128)(2,1)S(1)} %pad_maximum_fusion.rest_0_), channel_id=1, source_target_pairs={{0,24},{1,97},{2,26},{3,99},{4,28},{5,101},{6,30},{7,103},{8,0},{9... | collective-permute-start | bytes 3686408 | tf_op jit(solution)/shard_map/ppermute | solution.py:269
  29.9 0.1 pad_maximum_fusion.1.rest_5_
  30.1 0.7 fusion.3
  30.7 0.1 collective-permute-start.10
  30.8 0.1 collective-permute-start.8
  30.9 2.4 %collective-permute-done.10.rest_6_ = bf16[3,400,384]{2,1,0:T(8,128)(2,1)S(1)} collective-permute-done((bf16[3,400,384]{2,1,0:T(8,128)(2,1)S(1)}, bf16[3,400,384]{2,1,0:T(8,128)(2,1)S(1)}, u32[]{:S(2)}, u32[]{:S(2)}) %collective-permute-start.10) | collective-permute-done | bytes 921632 | tf_op jit(solution)/shard_map/ppermute | solution.py:269
  33.3 2.7 %collective-permute-start.12 = (bf16[2,400,384]{2,1,0:T(8,128)(2,1)S(1)}, bf16[2,400,384]{2,1,0:T(8,128)(2,1)S(1)}, u32[]{:S(2)}, u32[]{:S(2)}) collective-permute-start(bf16[2,400,384]{2,1,0:T(8,128)(2,1)S(1)} %get-tuple-element.105), channel_id=1, source_target_pairs={{0,6},{1,3},{2,0},{3,5},{4,2},{5,7},{6,4},{7,1},{8,14},{9,11},{10,... | collective-permute-start | bytes 1843208 | tf_op jit(solution)/shard_map/ppermute | solution.py:269
  36.0 21.4 %collective-permute-done.7.rest_1_ = bf16[4,400,384]{2,1,0:T(8,128)(2,1)S(1)} collective-permute-done((bf16[4,400,384]{2,1,0:T(8,128)(2,1)S(1)}, bf16[4,400,384]{2,1,0:T(8,128)(2,1)S(1)}, u32[]{:S(2)}, u32[]{:S(2)}) %collective-permute-start.7) | collective-permute-done | bytes 1228832 | tf_op jit(solution)/shard_map/ppermute | solution.py:269
  57.4 0.2 collective-permute-start.11
  57.7 4.4 %collective-permute-done.8.rest_2_ = bf16[4,400,384]{2,1,0:T(8,128)(2,1)S(1)} collective-permute-done((bf16[4,400,384]{2,1,0:T(8,128)(2,1)S(1)}, bf16[4,400,384]{2,1,0:T(8,128)(2,1)S(1)}, u32[]{:S(2)}, u32[]{:S(2)}) %collective-permute-start.8) | collective-permute-done | bytes 1228832 | tf_op jit(solution)/shard_map/ppermute | solution.py:269
  62.1 5.7 %collective-permute-done.5 = bf16[4,2,400,384]{3,2,1,0:T(8,128)(2,1)S(1)} collective-permute-done((bf16[4,2,400,384]{3,2,1,0:T(8,128)(2,1)S(1)}, bf16[4,2,400,384]{3,2,1,0:T(8,128)(2,1)S(1)}, u32[]{:S(2)}, u32[]{:S(2)}) %collective-permute-start.5) | collective-permute-done | bytes 2457632 | tf_op jit(solution)/shard_map/ppermute | solution.py:269
  67.8 0.4 collective-permute-done.6
  68.2 0.6 collective-permute-done.11
  68.8 0.2 add_convert_fusion.6
  69.0 0.1 pad_maximum_fusion.2
  69.1 0.7 add_convert_fusion
  69.8 1.0 collective-permute-start.13
  70.8 2.3 %collective-permute-start.14 = (bf16[2,2,400,384]{3,2,1,0:T(8,128)(2,1)S(1)}, bf16[2,2,400,384]{3,2,1,0:T(8,128)(2,1)S(1)}, u32[]{:S(2)}, u32[]{:S(2)}) collective-permute-start(bf16[2,2,400,384]{3,2,1,0:T(8,128)(2,1)S(1)} %get-tuple-element.75), channel_id=1, source_target_pairs={{0,96},{1,25},{2,98},{3,27},{4,100},{5,29},{6,102},{7,31},{8,104},... | collective-permute-start | bytes 3686408 | tf_op jit(solution)/shard_map/ppermute | solution.py:269
  73.1 0.1 slice.92
  73.1 3.8 %collective-permute-start.15 = (bf16[2,400,384]{2,1,0:T(8,128)(2,1)S(1)}, bf16[2,400,384]{2,1,0:T(8,128)(2,1)S(1)}, u32[]{:S(2)}, u32[]{:S(2)}) collective-permute-start(bf16[2,400,384]{2,1,0:T(8,128)(2,1)S(1)} %slice.92), channel_id=1, source_target_pairs={{0,24},{1,97},{2,26},{3,99},{4,28},{5,101},{6,30},{7,103},{8,0},{9... | collective-permute-start | bytes 1843208 | tf_op jit(solution)/shard_map/ppermute | solution.py:269
  76.9 0.1 slice.93
  77.0 0.1 collective-permute-start.16
  77.0 1.6 %collective-permute-start.17 = (bf16[2,400,384]{2,1,0:T(8,128)(2,1)S(1)}, bf16[2,400,384]{2,1,0:T(8,128)(2,1)S(1)}, u32[]{:S(2)}, u32[]{:S(2)}) collective-permute-start(bf16[2,400,384]{2,1,0:T(8,128)(2,1)S(1)} %pad_maximum_fusion.2), channel_id=1, source_target_pairs={{0,6},{1,3},{2,0},{3,5},{4,2},{5,7},{6,4},{7,1},{8,14},{9,11},{10,... | collective-permute-start | bytes 1843208 | tf_op jit(solution)/shard_map/ppermute | solution.py:269
  78.6 12.6 %collective-permute-done.15.rest_3_ = bf16[2,400,384]{2,1,0:T(8,128)(2,1)S(1)} collective-permute-done((bf16[2,400,384]{2,1,0:T(8,128)(2,1)S(1)}, bf16[2,400,384]{2,1,0:T(8,128)(2,1)S(1)}, u32[]{:S(2)}, u32[]{:S(2)}) %collective-permute-start.15) | collective-permute-done | bytes 614432 | tf_op jit(solution)/shard_map/ppermute | solution.py:269
  91.2 1.0 collective-permute-done.16.rest_4_
  92.2 0.0 collective-permute-done.17.rest_7_
  92.2 2.1 %collective-permute-done.13 = bf16[2,2,400,384]{3,2,1,0:T(8,128)(2,1)S(1)} collective-permute-done((bf16[2,2,400,384]{3,2,1,0:T(8,128)(2,1)S(1)}, bf16[2,2,400,384]{3,2,1,0:T(8,128)(2,1)S(1)}, u32[]{:S(2)}, u32[]{:S(2)}) %collective-permute-start.13) | collective-permute-done | bytes 1228832 | tf_op jit(solution)/shard_map/ppermute | solution.py:269
  94.4 0.9 fusion.7
  95.3 1.0 collective-permute-start.18
  96.3 2.9 %collective-permute-start.19 = (bf16[2,400,384]{2,1,0:T(8,128)(2,1)S(1)}, bf16[2,400,384]{2,1,0:T(8,128)(2,1)S(1)}, u32[]{:S(2)}, u32[]{:S(2)}) collective-permute-start(bf16[2,400,384]{2,1,0:T(8,128)(2,1)S(1)} %get-tuple-element.86), channel_id=1, source_target_pairs={{0,24},{1,97},{2,26},{3,99},{4,28},{5,101},{6,30},{7,103},{8,0},{9... | collective-permute-start | bytes 1843208 | tf_op jit(solution)/shard_map/ppermute | solution.py:269
  99.1 1.4 %collective-permute-start.20 = (bf16[2,400,384]{2,1,0:T(8,128)(2,1)S(1)}, bf16[2,400,384]{2,1,0:T(8,128)(2,1)S(1)}, u32[]{:S(2)}, u32[]{:S(2)}) collective-permute-start(bf16[2,400,384]{2,1,0:T(8,128)(2,1)S(1)} %get-tuple-element.85), channel_id=1, source_target_pairs={{0,16},{1,65},{2,18},{3,67},{4,20},{5,69},{6,22},{7,71},{8,24},{9,... | collective-permute-start | bytes 1843208 | tf_op jit(solution)/shard_map/ppermute | solution.py:269
  100.5 9.3 %shard_map.60 = bf16[8,2,400,400]{3,2,1,0:T(8,128)(2,1)} custom-call(s32[8]{0:T(128)S(1)} %copy-done.1, bf16[8,2,400,384]{3,2,1,0:T(8,128)(2,1)S(1)} %get-tuple-element.88.left_ref, bf16[4,400,384]{2,1,0:T(8,128)(2,1)S(1)} %pad_maximum_fusion.rest_0_, bf16[4,400,384]{2,1,0:T(8,128)(2,1)S(1)} %collective-permute-done.7.rest_1_, ...), custom_call_target="tpu_custom_call" | custom-call | flops 1966080000 | bytes 15000000 | tf_op jit(solution)/shard_map/pallas_call | solution.py:225
  109.9 3.5 %collective-permute-done.19.rest_1_ = bf16[2,400,384]{2,1,0:T(8,128)(2,1)S(1)} collective-permute-done((bf16[2,400,384]{2,1,0:T(8,128)(2,1)S(1)}, bf16[2,400,384]{2,1,0:T(8,128)(2,1)S(1)}, u32[]{:S(2)}, u32[]{:S(2)}) %collective-permute-start.19) | collective-permute-done | bytes 614432 | tf_op jit(solution)/shard_map/ppermute | solution.py:269
  113.4 1.8 %collective-permute-done.20.rest_2_ = bf16[2,400,384]{2,1,0:T(8,128)(2,1)S(1)} collective-permute-done((bf16[2,400,384]{2,1,0:T(8,128)(2,1)S(1)}, bf16[2,400,384]{2,1,0:T(8,128)(2,1)S(1)}, u32[]{:S(2)}, u32[]{:S(2)}) %collective-permute-start.20) | collective-permute-done | bytes 614432 | tf_op jit(solution)/shard_map/ppermute | solution.py:269
  115.2 0.3 convert_add_fusion.sum_ref
  115.5 2.1 %shard_map.61 = f32[2,400,400]{2,1,0:T(8,128)} custom-call(bf16[400,384]{1,0:T(8,128)(2,1)S(1)} %bitcast.35, f32[2,400,384]{2,1,0:T(8,128)S(1)} %convert_add_fusion.sum_ref, bf16[2,400,384]{2,1,0:T(8,128)(2,1)S(1)} %collective-permute-done.18.rest_0_, bf16[2,400,384]{2,1,0:T(8,128)(2,1)S(1)} %collective-permute-done.19.rest_1_, ...), custom_call_target="tpu_custom_call" | custom-call | tf_op jit(solution)/shard_map/pallas_call | solution.py:256
  (15 shorter events, 0.1 us)
Async XLA Ops:
  0.6 22.3 %copy-start = (bf16[1,384,400]{1,2,0:T(8,128)(2,1)S(1)}, bf16[1,384,400]{1,2,0:T(8,128)(2,1)}, u32[]{:S(2)}) copy-start(bf16[1,384,400]{1,2,0:T(8,128)(2,1)} %param.4) | copy-start | bytes 921604
  0.6 22.3 %collective-permute-start = (bf16[400,384]{1,0:T(8,128)(2,1)}, bf16[400,384]{1,0:T(8,128)(2,1)S(1)}, u32[]{:S(2)}, u32[]{:S(2)}) collective-permute-start(bf16[400,384]{1,0:T(8,128)(2,1)} %bitcast.27), channel_id=1, source_target_pairs={{0,96},{1,25},{2,98},{3,27},{4,100},{5,29},{6,102},{7,31},{8,104},... | collective-permute-start | bytes 921608 | tf_op jit(solution)/shard_map/ppermute | solution.py:269
  3.5 19.4 %collective-permute-start.1 = (bf16[400,384]{1,0:T(8,128)(2,1)}, bf16[400,384]{1,0:T(8,128)(2,1)S(1)}, u32[]{:S(2)}, u32[]{:S(2)}) collective-permute-start(bf16[400,384]{1,0:T(8,128)(2,1)} %bitcast.28), channel_id=1, source_target_pairs={{0,64},{1,17},{2,66},{3,19},{4,68},{5,21},{6,70},{7,23},{8,72},{9,... | collective-permute-start | bytes 921608 | tf_op jit(solution)/shard_map/ppermute | solution.py:269
  4.4 18.6 %collective-permute-start.2 = (bf16[400,384]{1,0:T(8,128)(2,1)}, bf16[400,384]{1,0:T(8,128)(2,1)S(1)}, u32[]{:S(2)}, u32[]{:S(2)}) collective-permute-start(bf16[400,384]{1,0:T(8,128)(2,1)} %bitcast.29), channel_id=1, source_target_pairs={{0,32},{1,9},{2,34},{3,11},{4,36},{5,13},{6,38},{7,15},{8,40},{9,1... | collective-permute-start | bytes 921608 | tf_op jit(solution)/shard_map/ppermute | solution.py:269
  5.2 17.9 %collective-permute-start.3 = (bf16[400,384]{1,0:T(8,128)(2,1)}, bf16[400,384]{1,0:T(8,128)(2,1)S(1)}, u32[]{:S(2)}, u32[]{:S(2)}) collective-permute-start(bf16[400,384]{1,0:T(8,128)(2,1)} %bitcast.30), channel_id=1, source_target_pairs={{0,2},{1,7},{2,4},{3,1},{4,6},{5,3},{6,0},{7,5},{8,10},{9,15},{10,... | collective-permute-start | bytes 921608 | tf_op jit(solution)/shard_map/ppermute | solution.py:269
  7.2 16.0 %collective-permute-start.4 = (bf16[400,384]{1,0:T(8,128)(2,1)}, bf16[400,384]{1,0:T(8,128)(2,1)S(1)}, u32[]{:S(2)}, u32[]{:S(2)}) collective-permute-start(bf16[400,384]{1,0:T(8,128)(2,1)} %bitcast.31), channel_id=1, source_target_pairs={{0,6},{1,3},{2,0},{3,5},{4,2},{5,7},{6,4},{7,1},{8,14},{9,11},{10,... | collective-permute-start | bytes 921608 | tf_op jit(solution)/shard_map/ppermute | solution.py:269
  23.2 6.9 %collective-permute-start.9 = (bf16[4,2,400,384]{3,2,1,0:T(8,128)(2,1)S(1)}, bf16[4,2,400,384]{3,2,1,0:T(8,128)(2,1)S(1)}, u32[]{:S(2)}, u32[]{:S(2)}) collective-permute-start(bf16[4,2,400,384]{3,2,1,0:T(8,128)(2,1)S(1)} %get-tuple-element.61), channel_id=1, source_target_pairs={{0,1},{1,0},{2,3},{3,2},{4,5},{5,4},{6,7},{7,6},{8,9},{9,8},{10,11... | collective-permute-start | bytes 7372808 | tf_op jit(solution)/shard_map/ppermute | solution.py:269
  23.3 44.5 %collective-permute-start.5 = (bf16[4,2,400,384]{3,2,1,0:T(8,128)(2,1)S(1)}, bf16[4,2,400,384]{3,2,1,0:T(8,128)(2,1)S(1)}, u32[]{:S(2)}, u32[]{:S(2)}) collective-permute-start(bf16[4,2,400,384]{3,2,1,0:T(8,128)(2,1)S(1)} %get-tuple-element.55), channel_id=1, source_target_pairs={{0,32},{1,9},{2,34},{3,11},{4,36},{5,13},{6,38},{7,15},{8,40},{9,1... | collective-permute-start | bytes 7372808 | tf_op jit(solution)/shard_map/ppermute | solution.py:269
  25.1 43.1 %collective-permute-start.6 = (bf16[4,2,400,384]{3,2,1,0:T(8,128)(2,1)S(1)}, bf16[4,2,400,384]{3,2,1,0:T(8,128)(2,1)S(1)}, u32[]{:S(2)}, u32[]{:S(2)}) collective-permute-start(bf16[4,2,400,384]{3,2,1,0:T(8,128)(2,1)S(1)} %get-tuple-element.56), channel_id=1, source_target_pairs={{0,96},{1,25},{2,98},{3,27},{4,100},{5,29},{6,102},{7,31},{8,104},... | collective-permute-start | bytes 7372808 | tf_op jit(solution)/shard_map/ppermute | solution.py:269
  26.8 30.6 %collective-permute-start.7 = (bf16[4,400,384]{2,1,0:T(8,128)(2,1)S(1)}, bf16[4,400,384]{2,1,0:T(8,128)(2,1)S(1)}, u32[]{:S(2)}, u32[]{:S(2)}) collective-permute-start(bf16[4,400,384]{2,1,0:T(8,128)(2,1)S(1)} %pad_maximum_fusion.rest_0_), channel_id=1, source_target_pairs={{0,24},{1,97},{2,26},{3,99},{4,28},{5,101},{6,30},{7,103},{8,0},{9... | collective-permute-start | bytes 3686408 | tf_op jit(solution)/shard_map/ppermute | solution.py:269
  30.7 2.6 %collective-permute-start.10 = (bf16[3,400,384]{2,1,0:T(8,128)(2,1)S(1)}, bf16[3,400,384]{2,1,0:T(8,128)(2,1)S(1)}, u32[]{:S(2)}, u32[]{:S(2)}) collective-permute-start(bf16[3,400,384]{2,1,0:T(8,128)(2,1)S(1)} %pad_maximum_fusion.1.rest_5_), channel_id=1, source_target_pairs={{0,1},{1,0},{2,3},{3,2},{4,5},{5,4},{6,7},{7,6},{8,9},{9,8},{10,11... | collective-permute-start | bytes 2764808 | tf_op jit(solution)/shard_map/ppermute | solution.py:269
  30.8 31.2 %collective-permute-start.8 = (bf16[4,400,384]{2,1,0:T(8,128)(2,1)S(1)}, bf16[4,400,384]{2,1,0:T(8,128)(2,1)S(1)}, u32[]{:S(2)}, u32[]{:S(2)}) collective-permute-start(bf16[4,400,384]{2,1,0:T(8,128)(2,1)S(1)} %pad_maximum_fusion.rest_0_), channel_id=1, source_target_pairs={{0,8},{1,33},{2,10},{3,35},{4,12},{5,37},{6,14},{7,39},{8,16},{9,4... | collective-permute-start | bytes 3686408 | tf_op jit(solution)/shard_map/ppermute | solution.py:269
  33.3 34.9 %collective-permute-start.12 = (bf16[2,400,384]{2,1,0:T(8,128)(2,1)S(1)}, bf16[2,400,384]{2,1,0:T(8,128)(2,1)S(1)}, u32[]{:S(2)}, u32[]{:S(2)}) collective-permute-start(bf16[2,400,384]{2,1,0:T(8,128)(2,1)S(1)} %get-tuple-element.105), channel_id=1, source_target_pairs={{0,6},{1,3},{2,0},{3,5},{4,2},{5,7},{6,4},{7,1},{8,14},{9,11},{10,... | collective-permute-start | bytes 1843208 | tf_op jit(solution)/shard_map/ppermute | solution.py:269
  57.4 11.4 %collective-permute-start.11 = (bf16[2,400,384]{2,1,0:T(8,128)(2,1)S(1)}, bf16[2,400,384]{2,1,0:T(8,128)(2,1)S(1)}, u32[]{:S(2)}, u32[]{:S(2)}) collective-permute-start(bf16[2,400,384]{2,1,0:T(8,128)(2,1)S(1)} %get-tuple-element.63), channel_id=1, source_target_pairs={{0,2},{1,7},{2,4},{3,1},{4,6},{5,3},{6,0},{7,5},{8,10},{9,15},{10,... | collective-permute-start | bytes 1843208 | tf_op jit(solution)/shard_map/ppermute | solution.py:269
  69.8 24.6 %collective-permute-start.13 = (bf16[2,2,400,384]{3,2,1,0:T(8,128)(2,1)S(1)}, bf16[2,2,400,384]{3,2,1,0:T(8,128)(2,1)S(1)}, u32[]{:S(2)}, u32[]{:S(2)}) collective-permute-start(bf16[2,2,400,384]{3,2,1,0:T(8,128)(2,1)S(1)} %get-tuple-element.74), channel_id=1, source_target_pairs={{0,32},{1,9},{2,34},{3,11},{4,36},{5,13},{6,38},{7,15},{8,40},{9,1... | collective-permute-start | bytes 3686408 | tf_op jit(solution)/shard_map/ppermute | solution.py:269
  70.8 23.6 %collective-permute-start.14 = (bf16[2,2,400,384]{3,2,1,0:T(8,128)(2,1)S(1)}, bf16[2,2,400,384]{3,2,1,0:T(8,128)(2,1)S(1)}, u32[]{:S(2)}, u32[]{:S(2)}) collective-permute-start(bf16[2,2,400,384]{3,2,1,0:T(8,128)(2,1)S(1)} %get-tuple-element.75), channel_id=1, source_target_pairs={{0,96},{1,25},{2,98},{3,27},{4,100},{5,29},{6,102},{7,31},{8,104},... | collective-permute-start | bytes 3686408 | tf_op jit(solution)/shard_map/ppermute | solution.py:269
  73.1 18.1 %collective-permute-start.15 = (bf16[2,400,384]{2,1,0:T(8,128)(2,1)S(1)}, bf16[2,400,384]{2,1,0:T(8,128)(2,1)S(1)}, u32[]{:S(2)}, u32[]{:S(2)}) collective-permute-start(bf16[2,400,384]{2,1,0:T(8,128)(2,1)S(1)} %slice.92), channel_id=1, source_target_pairs={{0,24},{1,97},{2,26},{3,99},{4,28},{5,101},{6,30},{7,103},{8,0},{9... | collective-permute-start | bytes 1843208 | tf_op jit(solution)/shard_map/ppermute | solution.py:269
  77.0 15.3 %collective-permute-start.16 = (bf16[2,400,384]{2,1,0:T(8,128)(2,1)S(1)}, bf16[2,400,384]{2,1,0:T(8,128)(2,1)S(1)}, u32[]{:S(2)}, u32[]{:S(2)}) collective-permute-start(bf16[2,400,384]{2,1,0:T(8,128)(2,1)S(1)} %slice.93), channel_id=1, source_target_pairs={{0,8},{1,33},{2,10},{3,35},{4,12},{5,37},{6,14},{7,39},{8,16},{9,4... | collective-permute-start | bytes 1843208 | tf_op jit(solution)/shard_map/ppermute | solution.py:269
  77.0 15.2 %collective-permute-start.17 = (bf16[2,400,384]{2,1,0:T(8,128)(2,1)S(1)}, bf16[2,400,384]{2,1,0:T(8,128)(2,1)S(1)}, u32[]{:S(2)}, u32[]{:S(2)}) collective-permute-start(bf16[2,400,384]{2,1,0:T(8,128)(2,1)S(1)} %pad_maximum_fusion.2), channel_id=1, source_target_pairs={{0,6},{1,3},{2,0},{3,5},{4,2},{5,7},{6,4},{7,1},{8,14},{9,11},{10,... | collective-permute-start | bytes 1843208 | tf_op jit(solution)/shard_map/ppermute | solution.py:269
  94.3 6.2 %copy-start.1 = (s32[8]{0:T(128)S(1)}, s32[8]{0:T(128)}, u32[]{:S(2)}) copy-start(s32[8]{0:T(128)} %partner_ref) | copy-start | bytes 100
  95.3 14.6 %collective-permute-start.18 = (bf16[2,400,384]{2,1,0:T(8,128)(2,1)S(1)}, bf16[2,400,384]{2,1,0:T(8,128)(2,1)S(1)}, u32[]{:S(2)}, u32[]{:S(2)}) collective-permute-start(bf16[2,400,384]{2,1,0:T(8,128)(2,1)S(1)} %get-tuple-element.84), channel_id=1, source_target_pairs={{0,8},{1,33},{2,10},{3,35},{4,12},{5,37},{6,14},{7,39},{8,16},{9,4... | collective-permute-start | bytes 1843208 | tf_op jit(solution)/shard_map/ppermute | solution.py:269
  96.3 17.1 %collective-permute-start.19 = (bf16[2,400,384]{2,1,0:T(8,128)(2,1)S(1)}, bf16[2,400,384]{2,1,0:T(8,128)(2,1)S(1)}, u32[]{:S(2)}, u32[]{:S(2)}) collective-permute-start(bf16[2,400,384]{2,1,0:T(8,128)(2,1)S(1)} %get-tuple-element.86), channel_id=1, source_target_pairs={{0,24},{1,97},{2,26},{3,99},{4,28},{5,101},{6,30},{7,103},{8,0},{9... | collective-permute-start | bytes 1843208 | tf_op jit(solution)/shard_map/ppermute | solution.py:269
  99.1 16.1 %collective-permute-start.20 = (bf16[2,400,384]{2,1,0:T(8,128)(2,1)S(1)}, bf16[2,400,384]{2,1,0:T(8,128)(2,1)S(1)}, u32[]{:S(2)}, u32[]{:S(2)}) collective-permute-start(bf16[2,400,384]{2,1,0:T(8,128)(2,1)S(1)} %get-tuple-element.85), channel_id=1, source_target_pairs={{0,16},{1,65},{2,18},{3,67},{4,20},{5,69},{6,22},{7,71},{8,24},{9,... | collective-permute-start | bytes 1843208 | tf_op jit(solution)/shard_map/ppermute | solution.py:269
  100.5 14.7 %collective-permute-start.21 = (bf16[2,400,384]{2,1,0:T(8,128)(2,1)S(1)}, bf16[2,400,384]{2,1,0:T(8,128)(2,1)S(1)}, u32[]{:S(2)}, u32[]{:S(2)}) collective-permute-start(bf16[2,400,384]{2,1,0:T(8,128)(2,1)S(1)} %add_convert_fusion.6), channel_id=1, source_target_pairs={{0,2},{1,7},{2,4},{3,1},{4,6},{5,3},{6,0},{7,5},{8,10},{9,15},{10,... | collective-permute-start | bytes 1843208 | tf_op jit(solution)/shard_map/ppermute | solution.py:269

commit v5 on v4

--- a/solution.py
+++ b/solution.py
@@ -37,12 +37,13 @@
     outs = rest[:7]
     partner_ref, counts_ref, own_ref, blocks, zero, sums = rest[7:13]
     keys, number, seen, at_sum, in_sem, out_sem = rest[13:]
-    count, pairs = blocks.shape[0], keys.shape[0]
-    modes, width = own_ref.shape
+    pairs, width = blocks.shape[0], blocks.shape[1]
+    count, modes = 2 * pairs, own_ref.shape[0]
     slots = SPAN_X + SPAN_Y
 
     def load(i):
-        return pltpu.make_async_copy(coupling_hbm.at[i // 2, i % 2], blocks.at[i], in_sem.at[i])
+        return pltpu.make_async_copy(coupling_hbm.at[i // 2, i % 2],
+                                     blocks.at[i // 2, :, pl.ds(pl.multiple_of(i % 2 * width, width), width)], in_sem.at[i])
 
     load_partner = pltpu.make_async_copy(partner_hbm, partner_ref, in_sem.at[count + 1])
     load_partner.start()
@@ -93,22 +94,23 @@
 
     load_own.wait()
 
-    @pl.loop(0, count)
-    def _(i):
-        p = i // 2
-        load(i).wait()
+    @pl.loop(0, pairs)
+    def _(p):
+        load(2 * p).wait()
+        load(2 * p + 1).wait()
         keep = lax.broadcasted_iota(jnp.int32, (1, width), 1) < counts_ref[p]
         own = jnp.where(keep, own_ref[...], jnp.zeros((modes, width), own_ref.dtype))
-        product = jnp.dot(own, blocks[i], preferred_element_type=jnp.float32)
-        left_ref[p, i % 2] = jnp.where(keep, product, 0.0).astype(jnp.bfloat16)
+        product = jnp.dot(own, blocks[p], preferred_element_type=jnp.float32)
+        for t in range(2):
+            left_ref[p, t] = jnp.where(keep, product[:, t * width:(t + 1) * width], 0.0).astype(jnp.bfloat16)
         key = keys[p]
         single = number[key] == 1
 
-        @pl.when((i % 2 == 1) & single)
+        @pl.when(single)
         def _():
             send(left_ref.at[p], key)
 
-        @pl.when((i % 2 == 1) & jnp.logical_not(single))
+        @pl.when(jnp.logical_not(single))
         def _():
             fresh = seen[key] == 0
 
@@ -144,16 +146,18 @@
     modes = own.shape[0]
     slots = SPAN_X + SPAN_Y
     sizes = [pairs] + [size for _, size in PARTS] + [SIDE] * 2
+    hbm, vmem = pltpu.HBM, pltpu.VMEM
+    spaces = [vmem, hbm, hbm, vmem, vmem, hbm, hbm, hbm]
     out = pl.pallas_call(
         left_kernel,
         in_specs=[pl.BlockSpec(memory_space=pltpu.HBM)] * 4,
-        out_specs=[pl.BlockSpec(memory_space=pltpu.VMEM)] * len(sizes),
-        out_shape=[pltpu.VMEM((n, blocks, modes, width), jnp.bfloat16) for n in sizes],
+        out_specs=[pl.BlockSpec(memory_space=space) for space in spaces],
+        out_shape=[space((n, blocks, modes, width), jnp.bfloat16) for n, space in zip(sizes, spaces, strict=True)],
         scratch_shapes=[
             pltpu.SMEM((pairs,), jnp.int32),
             pltpu.SMEM((pairs,), jnp.int32),
             pltpu.VMEM((modes, width), jnp.bfloat16),
-            pltpu.VMEM((pairs * blocks, width, width), jnp.bfloat16),
+            pltpu.VMEM((pairs, width, blocks * width), jnp.bfloat16),
             pltpu.VMEM((blocks, modes, width), jnp.bfloat16),
             pltpu.VMEM((pairs // 2, blocks, modes, width), jnp.bfloat16),
             pltpu.SMEM((pairs,), jnp.int32),

time: 117 us -> 113 us (0.966)
  Pallas kernels: 25 us -> 20.3 us
    pallas_call x1, Pallas kernels: 13.6 us -> 8.84 us  [left_products(): pl.pallas_call(left_kernel, in_specs=[pl.BlockSpec(memory_space=pltpu.HBM...]
  transfers between devices with their start and end apart: 22 -> 22, of which waited for: 11 -> 10; matrix products, arithmetic and copies ran while one was open for 1% -> 1% of each run, Pallas kernels for 20% -> 16%
where the time goes in v5:
time: 113 us
  waiting for transfers between devices  55.8 us (49%)
  starting transfers between devices  32.4 us (29%)
  Pallas kernels  20.3 us (18%)
  other arithmetic  3.08 us (3%)
    ppermute x22, waiting for transfers between devices, permuted(): return lax.ppermute(value, ('sx', 'sy'), pairs)  55.8 us
    ppermute x22, starting transfers between devices, permuted(): return lax.ppermute(value, ('sx', 'sy'), pairs)  32.4 us
    pallas_call x1, Pallas kernels, pair_products(): pl.pallas_call(pair_kernel, in_specs=[smem, pl.BlockSpec(memory_space=plt...  9.35 us
    pallas_call x1, Pallas kernels, left_products(): pl.pallas_call(left_kernel, in_specs=[pl.BlockSpec(memory_space=pltpu.HBM...  8.84 us
    convert_element_type x4, other arithmetic, rounded(): return added(*terms).astype(jnp.bfloat16)  2.41 us
  transfers between devices with their start and end apart: 22, of which 10 were waited for; matrix products, arithmetic and copies ran while one was open for 1% of the time, Pallas kernels for 16%

profile of v5, /device:TPU:0, one launch (start us, length us, event | category | flops | bytes accessed | tf_op | source)
XLA Modules:
  0.0 112.7 jit_solution(5779828019486252801)
XLA Ops:
  0.6 2.9 %collective-permute-start = (bf16[400,384]{1,0:T(8,128)(2,1)}, bf16[400,384]{1,0:T(8,128)(2,1)S(1)}, u32[]{:S(2)}, u32[]{:S(2)}) collective-permute-start(bf16[400,384]{1,0:T(8,128)(2,1)} %bitcast.27), channel_id=1, source_target_pairs={{0,96},{1,25},{2,98},{3,27},{4,100},{5,29},{6,102},{7,31},{8,104},... | collective-permute-start | bytes 921608 | tf_op jit(solution)/shard_map/ppermute | solution.py:273
  3.5 0.8 collective-permute-start.1
  4.4 0.9 collective-permute-start.2
  5.2 1.9 %collective-permute-start.3 = (bf16[400,384]{1,0:T(8,128)(2,1)}, bf16[400,384]{1,0:T(8,128)(2,1)S(1)}, u32[]{:S(2)}, u32[]{:S(2)}) collective-permute-start(bf16[400,384]{1,0:T(8,128)(2,1)} %bitcast.30), channel_id=1, source_target_pairs={{0,2},{1,7},{2,4},{3,1},{4,6},{5,3},{6,0},{7,5},{8,10},{9,15},{10,... | collective-permute-start | bytes 921608 | tf_op jit(solution)/shard_map/ppermute | solution.py:273
  7.2 2.1 %collective-permute-start.4 = (bf16[400,384]{1,0:T(8,128)(2,1)}, bf16[400,384]{1,0:T(8,128)(2,1)S(1)}, u32[]{:S(2)}, u32[]{:S(2)}) collective-permute-start(bf16[400,384]{1,0:T(8,128)(2,1)} %bitcast.31), channel_id=1, source_target_pairs={{0,6},{1,3},{2,0},{3,5},{4,2},{5,7},{6,4},{7,1},{8,14},{9,11},{10,... | collective-permute-start | bytes 921608 | tf_op jit(solution)/shard_map/ppermute | solution.py:273
  9.3 8.8 %shard_map.59 = (bf16[8,2,400,384]{3,2,1,0:T(8,128)(2,1)S(1)}, bf16[4,2,400,384]{3,2,1,0:T(8,128)(2,1)}, bf16[4,2,400,384]{3,2,1,0:T(8,128)(2,1)}, bf16[2,2,400,...) custom-call(s32[8]{0:T(128)} %partner_ref, ...), custom_call_target="tpu_custom_call" | custom-call | flops 1887436800 | bytes 25000000 | tf_op jit(solution)/shard_map/pallas_call | solution.py:151
  18.1 0.0 collective-permute-done
  18.1 0.0 collective-permute-done.2
  18.2 0.2 pad_maximum_fusion.rest_0_
  18.4 0.0 collective-permute-done.3
  18.4 0.0 collective-permute-done.4
  18.4 0.1 collective-permute-start.9
  18.5 2.6 %collective-permute-start.5 = (bf16[4,2,400,384]{3,2,1,0:T(8,128)(2,1)}, bf16[4,2,400,384]{3,2,1,0:T(8,128)(2,1)S(1)}, u32[]{:S(2)}, u32[]{:S(2)}) collective-permute-start(bf16[4,2,400,384]{3,2,1,0:T(8,128)(2,1)} %get-tuple-element.55), channel_id=1, source_target_pairs={{0,32},{1,9},{2,34},{3,11},{4,36},{5,13},{6,38},{7,15},{8,40},{9,1... | collective-permute-start | bytes 7372808 | tf_op jit(solution)/shard_map/ppermute | solution.py:273
  21.1 0.7 collective-permute-start.6
  21.8 2.9 %collective-permute-start.7 = (bf16[4,400,384]{2,1,0:T(8,128)(2,1)S(1)}, bf16[4,400,384]{2,1,0:T(8,128)(2,1)S(1)}, u32[]{:S(2)}, u32[]{:S(2)}) collective-permute-start(bf16[4,400,384]{2,1,0:T(8,128)(2,1)S(1)} %pad_maximum_fusion.rest_0_), channel_id=1, source_target_pairs={{0,24},{1,97},{2,26},{3,99},{4,28},{5,101},{6,30},{7,103},{8,0},{9... | collective-permute-start | bytes 3686408 | tf_op jit(solution)/shard_map/ppermute | solution.py:273
  24.7 0.1 pad_maximum_fusion.1.rest_5_
  24.9 0.6 fusion.3
  25.5 0.1 collective-permute-start.10
  25.6 0.1 collective-permute-start.8
  25.7 2.4 %collective-permute-done.10.rest_6_ = bf16[3,400,384]{2,1,0:T(8,128)(2,1)S(1)} collective-permute-done((bf16[3,400,384]{2,1,0:T(8,128)(2,1)S(1)}, bf16[3,400,384]{2,1,0:T(8,128)(2,1)S(1)}, u32[]{:S(2)}, u32[]{:S(2)}) %collective-permute-start.10) | collective-permute-done | bytes 921632 | tf_op jit(solution)/shard_map/ppermute | solution.py:273
  28.1 3.5 %collective-permute-start.12 = (bf16[2,400,384]{2,1,0:T(8,128)(2,1)S(1)}, bf16[2,400,384]{2,1,0:T(8,128)(2,1)S(1)}, u32[]{:S(2)}, u32[]{:S(2)}) collective-permute-start(bf16[2,400,384]{2,1,0:T(8,128)(2,1)S(1)} %get-tuple-element.105), channel_id=1, source_target_pairs={{0,6},{1,3},{2,0},{3,5},{4,2},{5,7},{6,4},{7,1},{8,14},{9,11},{10,... | collective-permute-start | bytes 1843208 | tf_op jit(solution)/shard_map/ppermute | solution.py:273
  31.6 20.6 %collective-permute-done.7.rest_1_ = bf16[4,400,384]{2,1,0:T(8,128)(2,1)S(1)} collective-permute-done((bf16[4,400,384]{2,1,0:T(8,128)(2,1)S(1)}, bf16[4,400,384]{2,1,0:T(8,128)(2,1)S(1)}, u32[]{:S(2)}, u32[]{:S(2)}) %collective-permute-start.7) | collective-permute-done | bytes 1228832 | tf_op jit(solution)/shard_map/ppermute | solution.py:273
  52.2 0.3 collective-permute-start.11
  52.6 4.3 %collective-permute-done.8.rest_2_ = bf16[4,400,384]{2,1,0:T(8,128)(2,1)S(1)} collective-permute-done((bf16[4,400,384]{2,1,0:T(8,128)(2,1)S(1)}, bf16[4,400,384]{2,1,0:T(8,128)(2,1)S(1)}, u32[]{:S(2)}, u32[]{:S(2)}) %collective-permute-start.8) | collective-permute-done | bytes 1228832 | tf_op jit(solution)/shard_map/ppermute | solution.py:273
  56.8 6.2 %collective-permute-done.5 = bf16[4,2,400,384]{3,2,1,0:T(8,128)(2,1)S(1)} collective-permute-done((bf16[4,2,400,384]{3,2,1,0:T(8,128)(2,1)}, bf16[4,2,400,384]{3,2,1,0:T(8,128)(2,1)S(1)}, u32[]{:S(2)}, u32[]{:S(2)}) %collective-permute-start.5) | collective-permute-done | bytes 2457632 | tf_op jit(solution)/shard_map/ppermute | solution.py:273
  63.0 1.3 %collective-permute-done.6 = bf16[4,2,400,384]{3,2,1,0:T(8,128)(2,1)S(1)} collective-permute-done((bf16[4,2,400,384]{3,2,1,0:T(8,128)(2,1)}, bf16[4,2,400,384]{3,2,1,0:T(8,128)(2,1)S(1)}, u32[]{:S(2)}, u32[]{:S(2)}) %collective-permute-start.6) | collective-permute-done | bytes 2457632 | tf_op jit(solution)/shard_map/ppermute | solution.py:273
  64.4 0.2 add_convert_fusion.6
  64.6 0.1 pad_maximum_fusion.2
  64.7 0.7 add_convert_fusion
  65.4 0.2 collective-permute-start.13
  65.5 3.2 %collective-permute-start.14 = (bf16[2,2,400,384]{3,2,1,0:T(8,128)(2,1)S(1)}, bf16[2,2,400,384]{3,2,1,0:T(8,128)(2,1)S(1)}, u32[]{:S(2)}, u32[]{:S(2)}) collective-permute-start(bf16[2,2,400,384]{3,2,1,0:T(8,128)(2,1)S(1)} %get-tuple-element.75), channel_id=1, source_target_pairs={{0,96},{1,25},{2,98},{3,27},{4,100},{5,29},{6,102},{7,31},{8,104},... | collective-permute-start | bytes 3686408 | tf_op jit(solution)/shard_map/ppermute | solution.py:273
  68.7 0.1 slice.92
  68.7 3.3 %collective-permute-start.15 = (bf16[2,400,384]{2,1,0:T(8,128)(2,1)S(1)}, bf16[2,400,384]{2,1,0:T(8,128)(2,1)S(1)}, u32[]{:S(2)}, u32[]{:S(2)}) collective-permute-start(bf16[2,400,384]{2,1,0:T(8,128)(2,1)S(1)} %slice.92), channel_id=1, source_target_pairs={{0,24},{1,97},{2,26},{3,99},{4,28},{5,101},{6,30},{7,103},{8,0},{9... | collective-permute-start | bytes 1843208 | tf_op jit(solution)/shard_map/ppermute | solution.py:273
  72.0 0.1 slice.93
  72.1 0.1 collective-permute-start.16
  72.1 2.1 %collective-permute-start.17 = (bf16[2,400,384]{2,1,0:T(8,128)(2,1)S(1)}, bf16[2,400,384]{2,1,0:T(8,128)(2,1)S(1)}, u32[]{:S(2)}, u32[]{:S(2)}) collective-permute-start(bf16[2,400,384]{2,1,0:T(8,128)(2,1)S(1)} %pad_maximum_fusion.2), channel_id=1, source_target_pairs={{0,6},{1,3},{2,0},{3,5},{4,2},{5,7},{6,4},{7,1},{8,14},{9,11},{10,... | collective-permute-start | bytes 1843208 | tf_op jit(solution)/shard_map/ppermute | solution.py:273
  74.2 12.1 %collective-permute-done.15.rest_3_ = bf16[2,400,384]{2,1,0:T(8,128)(2,1)S(1)} collective-permute-done((bf16[2,400,384]{2,1,0:T(8,128)(2,1)S(1)}, bf16[2,400,384]{2,1,0:T(8,128)(2,1)S(1)}, u32[]{:S(2)}, u32[]{:S(2)}) %collective-permute-start.15) | collective-permute-done | bytes 614432 | tf_op jit(solution)/shard_map/ppermute | solution.py:273
  86.3 1.0 collective-permute-done.16.rest_4_
  87.3 2.7 %collective-permute-done.13 = bf16[2,2,400,384]{3,2,1,0:T(8,128)(2,1)S(1)} collective-permute-done((bf16[2,2,400,384]{3,2,1,0:T(8,128)(2,1)S(1)}, bf16[2,2,400,384]{3,2,1,0:T(8,128)(2,1)S(1)}, u32[]{:S(2)}, u32[]{:S(2)}) %collective-permute-start.13) | collective-permute-done | bytes 1228832 | tf_op jit(solution)/shard_map/ppermute | solution.py:273
  90.0 0.9 fusion.7
  90.9 0.2 collective-permute-start.18
  91.1 3.1 %collective-permute-start.19 = (bf16[2,400,384]{2,1,0:T(8,128)(2,1)S(1)}, bf16[2,400,384]{2,1,0:T(8,128)(2,1)S(1)}, u32[]{:S(2)}, u32[]{:S(2)}) collective-permute-start(bf16[2,400,384]{2,1,0:T(8,128)(2,1)S(1)} %get-tuple-element.86), channel_id=1, source_target_pairs={{0,24},{1,97},{2,26},{3,99},{4,28},{5,101},{6,30},{7,103},{8,0},{9... | collective-permute-start | bytes 1843208 | tf_op jit(solution)/shard_map/ppermute | solution.py:273
  94.2 1.4 %collective-permute-start.20 = (bf16[2,400,384]{2,1,0:T(8,128)(2,1)S(1)}, bf16[2,400,384]{2,1,0:T(8,128)(2,1)S(1)}, u32[]{:S(2)}, u32[]{:S(2)}) collective-permute-start(bf16[2,400,384]{2,1,0:T(8,128)(2,1)S(1)} %get-tuple-element.85), channel_id=1, source_target_pairs={{0,16},{1,65},{2,18},{3,67},{4,20},{5,69},{6,22},{7,71},{8,24},{9,... | collective-permute-start | bytes 1843208 | tf_op jit(solution)/shard_map/ppermute | solution.py:273
  95.6 9.4 %shard_map.60 = bf16[8,2,400,400]{3,2,1,0:T(8,128)(2,1)} custom-call(s32[8]{0:T(128)S(1)} %copy-done.1, bf16[8,2,400,384]{3,2,1,0:T(8,128)(2,1)S(1)} %get-tuple-element.88.left_ref, bf16[4,400,384]{2,1,0:T(8,128)(2,1)S(1)} %pad_maximum_fusion.rest_0_, bf16[4,400,384]{2,1,0:T(8,128)(2,1)S(1)} %collective-permute-done.7.rest_1_, ...), custom_call_target="tpu_custom_call" | custom-call | flops 1966080000 | bytes 15000000 | tf_op jit(solution)/shard_map/pallas_call | solution.py:229
  105.0 3.5 %collective-permute-done.19.rest_1_ = bf16[2,400,384]{2,1,0:T(8,128)(2,1)S(1)} collective-permute-done((bf16[2,400,384]{2,1,0:T(8,128)(2,1)S(1)}, bf16[2,400,384]{2,1,0:T(8,128)(2,1)S(1)}, u32[]{:S(2)}, u32[]{:S(2)}) %collective-permute-start.19) | collective-permute-done | bytes 614432 | tf_op jit(solution)/shard_map/ppermute | solution.py:273
  108.5 1.8 %collective-permute-done.20.rest_2_ = bf16[2,400,384]{2,1,0:T(8,128)(2,1)S(1)} collective-permute-done((bf16[2,400,384]{2,1,0:T(8,128)(2,1)S(1)}, bf16[2,400,384]{2,1,0:T(8,128)(2,1)S(1)}, u32[]{:S(2)}, u32[]{:S(2)}) %collective-permute-start.20) | collective-permute-done | bytes 614432 | tf_op jit(solution)/shard_map/ppermute | solution.py:273
  110.3 0.3 convert_add_fusion.sum_ref
  110.6 2.1 %shard_map.61 = f32[2,400,400]{2,1,0:T(8,128)} custom-call(bf16[400,384]{1,0:T(8,128)(2,1)S(1)} %bitcast.35, f32[2,400,384]{2,1,0:T(8,128)S(1)} %convert_add_fusion.sum_ref, bf16[2,400,384]{2,1,0:T(8,128)(2,1)S(1)} %collective-permute-done.18.rest_0_, bf16[2,400,384]{2,1,0:T(8,128)(2,1)S(1)} %collective-permute-done.19.rest_1_, ...), custom_call_target="tpu_custom_call" | custom-call | tf_op jit(solution)/shard_map/pallas_call | solution.py:260
  (19 shorter events, 0.1 us)
Async XLA Ops:
  0.6 17.5 %copy-start = (bf16[1,384,400]{1,2,0:T(8,128)(2,1)S(1)}, bf16[1,384,400]{1,2,0:T(8,128)(2,1)}, u32[]{:S(2)}) copy-start(bf16[1,384,400]{1,2,0:T(8,128)(2,1)} %param.4) | copy-start | bytes 921604
  0.6 17.5 %collective-permute-start = (bf16[400,384]{1,0:T(8,128)(2,1)}, bf16[400,384]{1,0:T(8,128)(2,1)S(1)}, u32[]{:S(2)}, u32[]{:S(2)}) collective-permute-start(bf16[400,384]{1,0:T(8,128)(2,1)} %bitcast.27), channel_id=1, source_target_pairs={{0,96},{1,25},{2,98},{3,27},{4,100},{5,29},{6,102},{7,31},{8,104},... | collective-permute-start | bytes 921608 | tf_op jit(solution)/shard_map/ppermute | solution.py:273
  3.5 14.6 %collective-permute-start.1 = (bf16[400,384]{1,0:T(8,128)(2,1)}, bf16[400,384]{1,0:T(8,128)(2,1)S(1)}, u32[]{:S(2)}, u32[]{:S(2)}) collective-permute-start(bf16[400,384]{1,0:T(8,128)(2,1)} %bitcast.28), channel_id=1, source_target_pairs={{0,64},{1,17},{2,66},{3,19},{4,68},{5,21},{6,70},{7,23},{8,72},{9,... | collective-permute-start | bytes 921608 | tf_op jit(solution)/shard_map/ppermute | solution.py:273
  4.4 13.8 %collective-permute-start.2 = (bf16[400,384]{1,0:T(8,128)(2,1)}, bf16[400,384]{1,0:T(8,128)(2,1)S(1)}, u32[]{:S(2)}, u32[]{:S(2)}) collective-permute-start(bf16[400,384]{1,0:T(8,128)(2,1)} %bitcast.29), channel_id=1, source_target_pairs={{0,32},{1,9},{2,34},{3,11},{4,36},{5,13},{6,38},{7,15},{8,40},{9,1... | collective-permute-start | bytes 921608 | tf_op jit(solution)/shard_map/ppermute | solution.py:273
  5.2 13.1 %collective-permute-start.3 = (bf16[400,384]{1,0:T(8,128)(2,1)}, bf16[400,384]{1,0:T(8,128)(2,1)S(1)}, u32[]{:S(2)}, u32[]{:S(2)}) collective-permute-start(bf16[400,384]{1,0:T(8,128)(2,1)} %bitcast.30), channel_id=1, source_target_pairs={{0,2},{1,7},{2,4},{3,1},{4,6},{5,3},{6,0},{7,5},{8,10},{9,15},{10,... | collective-permute-start | bytes 921608 | tf_op jit(solution)/shard_map/ppermute | solution.py:273
  7.2 11.2 %collective-permute-start.4 = (bf16[400,384]{1,0:T(8,128)(2,1)}, bf16[400,384]{1,0:T(8,128)(2,1)S(1)}, u32[]{:S(2)}, u32[]{:S(2)}) collective-permute-start(bf16[400,384]{1,0:T(8,128)(2,1)} %bitcast.31), channel_id=1, source_target_pairs={{0,6},{1,3},{2,0},{3,5},{4,2},{5,7},{6,4},{7,1},{8,14},{9,11},{10,... | collective-permute-start | bytes 921608 | tf_op jit(solution)/shard_map/ppermute | solution.py:273
  18.2 6.7 %copy-start.2 = (bf16[4,2,400,384]{3,2,1,0:T(8,128)(2,1)S(1)}, bf16[4,2,400,384]{3,2,1,0:T(8,128)(2,1)}, u32[]{:S(2)}) copy-start(bf16[4,2,400,384]{3,2,1,0:T(8,128)(2,1)} %get-tuple-element.60) | copy-start | bytes 7372804
  18.4 6.5 %collective-permute-start.9 = (bf16[4,2,400,384]{3,2,1,0:T(8,128)(2,1)}, bf16[4,2,400,384]{3,2,1,0:T(8,128)(2,1)S(1)}, u32[]{:S(2)}, u32[]{:S(2)}) collective-permute-start(bf16[4,2,400,384]{3,2,1,0:T(8,128)(2,1)} %get-tuple-element.61), channel_id=1, source_target_pairs={{0,1},{1,0},{2,3},{3,2},{4,5},{5,4},{6,7},{7,6},{8,9},{9,8},{10,11... | collective-permute-start | bytes 7372808 | tf_op jit(solution)/shard_map/ppermute | solution.py:273
  18.5 44.6 %collective-permute-start.5 = (bf16[4,2,400,384]{3,2,1,0:T(8,128)(2,1)}, bf16[4,2,400,384]{3,2,1,0:T(8,128)(2,1)S(1)}, u32[]{:S(2)}, u32[]{:S(2)}) collective-permute-start(bf16[4,2,400,384]{3,2,1,0:T(8,128)(2,1)} %get-tuple-element.55), channel_id=1, source_target_pairs={{0,32},{1,9},{2,34},{3,11},{4,36},{5,13},{6,38},{7,15},{8,40},{9,1... | collective-permute-start | bytes 7372808 | tf_op jit(solution)/shard_map/ppermute | solution.py:273
  21.1 43.3 %collective-permute-start.6 = (bf16[4,2,400,384]{3,2,1,0:T(8,128)(2,1)}, bf16[4,2,400,384]{3,2,1,0:T(8,128)(2,1)S(1)}, u32[]{:S(2)}, u32[]{:S(2)}) collective-permute-start(bf16[4,2,400,384]{3,2,1,0:T(8,128)(2,1)} %get-tuple-element.56), channel_id=1, source_target_pairs={{0,96},{1,25},{2,98},{3,27},{4,100},{5,29},{6,102},{7,31},{8,104},... | collective-permute-start | bytes 7372808 | tf_op jit(solution)/shard_map/ppermute | solution.py:273
  21.8 30.4 %collective-permute-start.7 = (bf16[4,400,384]{2,1,0:T(8,128)(2,1)S(1)}, bf16[4,400,384]{2,1,0:T(8,128)(2,1)S(1)}, u32[]{:S(2)}, u32[]{:S(2)}) collective-permute-start(bf16[4,400,384]{2,1,0:T(8,128)(2,1)S(1)} %pad_maximum_fusion.rest_0_), channel_id=1, source_target_pairs={{0,24},{1,97},{2,26},{3,99},{4,28},{5,101},{6,30},{7,103},{8,0},{9... | collective-permute-start | bytes 3686408 | tf_op jit(solution)/shard_map/ppermute | solution.py:273
  25.5 2.6 %collective-permute-start.10 = (bf16[3,400,384]{2,1,0:T(8,128)(2,1)S(1)}, bf16[3,400,384]{2,1,0:T(8,128)(2,1)S(1)}, u32[]{:S(2)}, u32[]{:S(2)}) collective-permute-start(bf16[3,400,384]{2,1,0:T(8,128)(2,1)S(1)} %pad_maximum_fusion.1.rest_5_), channel_id=1, source_target_pairs={{0,1},{1,0},{2,3},{3,2},{4,5},{5,4},{6,7},{7,6},{8,9},{9,8},{10,11... | collective-permute-start | bytes 2764808 | tf_op jit(solution)/shard_map/ppermute | solution.py:273
  25.6 31.2 %collective-permute-start.8 = (bf16[4,400,384]{2,1,0:T(8,128)(2,1)S(1)}, bf16[4,400,384]{2,1,0:T(8,128)(2,1)S(1)}, u32[]{:S(2)}, u32[]{:S(2)}) collective-permute-start(bf16[4,400,384]{2,1,0:T(8,128)(2,1)S(1)} %pad_maximum_fusion.rest_0_), channel_id=1, source_target_pairs={{0,8},{1,33},{2,10},{3,35},{4,12},{5,37},{6,14},{7,39},{8,16},{9,4... | collective-permute-start | bytes 3686408 | tf_op jit(solution)/shard_map/ppermute | solution.py:273
  28.1 36.3 %collective-permute-start.12 = (bf16[2,400,384]{2,1,0:T(8,128)(2,1)S(1)}, bf16[2,400,384]{2,1,0:T(8,128)(2,1)S(1)}, u32[]{:S(2)}, u32[]{:S(2)}) collective-permute-start(bf16[2,400,384]{2,1,0:T(8,128)(2,1)S(1)} %get-tuple-element.105), channel_id=1, source_target_pairs={{0,6},{1,3},{2,0},{3,5},{4,2},{5,7},{6,4},{7,1},{8,14},{9,11},{10,... | collective-permute-start | bytes 1843208 | tf_op jit(solution)/shard_map/ppermute | solution.py:273
  52.2 12.1 %collective-permute-start.11 = (bf16[2,400,384]{2,1,0:T(8,128)(2,1)S(1)}, bf16[2,400,384]{2,1,0:T(8,128)(2,1)S(1)}, u32[]{:S(2)}, u32[]{:S(2)}) collective-permute-start(bf16[2,400,384]{2,1,0:T(8,128)(2,1)S(1)} %get-tuple-element.63), channel_id=1, source_target_pairs={{0,2},{1,7},{2,4},{3,1},{4,6},{5,3},{6,0},{7,5},{8,10},{9,15},{10,... | collective-permute-start | bytes 1843208 | tf_op jit(solution)/shard_map/ppermute | solution.py:273
  65.3 24.6 %copy-start.3 = (bf16[4,2,400,384]{3,2,1,0:T(8,128)(2,1)S(1)}, bf16[4,2,400,384]{3,2,1,0:T(8,128)(2,1)}, u32[]{:S(2)}) copy-start(bf16[4,2,400,384]{3,2,1,0:T(8,128)(2,1)} %get-tuple-element.51) | copy-start | bytes 7372804
  65.4 24.6 %collective-permute-start.13 = (bf16[2,2,400,384]{3,2,1,0:T(8,128)(2,1)S(1)}, bf16[2,2,400,384]{3,2,1,0:T(8,128)(2,1)S(1)}, u32[]{:S(2)}, u32[]{:S(2)}) collective-permute-start(bf16[2,2,400,384]{3,2,1,0:T(8,128)(2,1)S(1)} %get-tuple-element.74), channel_id=1, source_target_pairs={{0,32},{1,9},{2,34},{3,11},{4,36},{5,13},{6,38},{7,15},{8,40},{9,1... | collective-permute-start | bytes 3686408 | tf_op jit(solution)/shard_map/ppermute | solution.py:273
  65.5 24.4 %collective-permute-start.14 = (bf16[2,2,400,384]{3,2,1,0:T(8,128)(2,1)S(1)}, bf16[2,2,400,384]{3,2,1,0:T(8,128)(2,1)S(1)}, u32[]{:S(2)}, u32[]{:S(2)}) collective-permute-start(bf16[2,2,400,384]{3,2,1,0:T(8,128)(2,1)S(1)} %get-tuple-element.75), channel_id=1, source_target_pairs={{0,96},{1,25},{2,98},{3,27},{4,100},{5,29},{6,102},{7,31},{8,104},... | collective-permute-start | bytes 3686408 | tf_op jit(solution)/shard_map/ppermute | solution.py:273
  68.7 17.6 %collective-permute-start.15 = (bf16[2,400,384]{2,1,0:T(8,128)(2,1)S(1)}, bf16[2,400,384]{2,1,0:T(8,128)(2,1)S(1)}, u32[]{:S(2)}, u32[]{:S(2)}) collective-permute-start(bf16[2,400,384]{2,1,0:T(8,128)(2,1)S(1)} %slice.92), channel_id=1, source_target_pairs={{0,24},{1,97},{2,26},{3,99},{4,28},{5,101},{6,30},{7,103},{8,0},{9... | collective-permute-start | bytes 1843208 | tf_op jit(solution)/shard_map/ppermute | solution.py:273
  72.1 15.2 %collective-permute-start.16 = (bf16[2,400,384]{2,1,0:T(8,128)(2,1)S(1)}, bf16[2,400,384]{2,1,0:T(8,128)(2,1)S(1)}, u32[]{:S(2)}, u32[]{:S(2)}) collective-permute-start(bf16[2,400,384]{2,1,0:T(8,128)(2,1)S(1)} %slice.93), channel_id=1, source_target_pairs={{0,8},{1,33},{2,10},{3,35},{4,12},{5,37},{6,14},{7,39},{8,16},{9,4... | collective-permute-start | bytes 1843208 | tf_op jit(solution)/shard_map/ppermute | solution.py:273
  72.1 15.1 %collective-permute-start.17 = (bf16[2,400,384]{2,1,0:T(8,128)(2,1)S(1)}, bf16[2,400,384]{2,1,0:T(8,128)(2,1)S(1)}, u32[]{:S(2)}, u32[]{:S(2)}) collective-permute-start(bf16[2,400,384]{2,1,0:T(8,128)(2,1)S(1)} %pad_maximum_fusion.2), channel_id=1, source_target_pairs={{0,6},{1,3},{2,0},{3,5},{4,2},{5,7},{6,4},{7,1},{8,14},{9,11},{10,... | collective-permute-start | bytes 1843208 | tf_op jit(solution)/shard_map/ppermute | solution.py:273
  90.0 5.7 %copy-start.1 = (s32[8]{0:T(128)S(1)}, s32[8]{0:T(128)}, u32[]{:S(2)}) copy-start(s32[8]{0:T(128)} %partner_ref) | copy-start | bytes 100
  90.9 14.1 %collective-permute-start.18 = (bf16[2,400,384]{2,1,0:T(8,128)(2,1)S(1)}, bf16[2,400,384]{2,1,0:T(8,128)(2,1)S(1)}, u32[]{:S(2)}, u32[]{:S(2)}) collective-permute-start(bf16[2,400,384]{2,1,0:T(8,128)(2,1)S(1)} %get-tuple-element.84), channel_id=1, source_target_pairs={{0,8},{1,33},{2,10},{3,35},{4,12},{5,37},{6,14},{7,39},{8,16},{9,4... | collective-permute-start | bytes 1843208 | tf_op jit(solution)/shard_map/ppermute | solution.py:273
  91.1 17.4 %collective-permute-start.19 = (bf16[2,400,384]{2,1,0:T(8,128)(2,1)S(1)}, bf16[2,400,384]{2,1,0:T(8,128)(2,1)S(1)}, u32[]{:S(2)}, u32[]{:S(2)}) collective-permute-start(bf16[2,400,384]{2,1,0:T(8,128)(2,1)S(1)} %get-tuple-element.86), channel_id=1, source_target_pairs={{0,24},{1,97},{2,26},{3,99},{4,28},{5,101},{6,30},{7,103},{8,0},{9... | collective-permute-start | bytes 1843208 | tf_op jit(solution)/shard_map/ppermute | solution.py:273
  94.2 16.1 %collective-permute-start.20 = (bf16[2,400,384]{2,1,0:T(8,128)(2,1)S(1)}, bf16[2,400,384]{2,1,0:T(8,128)(2,1)S(1)}, u32[]{:S(2)}, u32[]{:S(2)}) collective-permute-start(bf16[2,400,384]{2,1,0:T(8,128)(2,1)S(1)} %get-tuple-element.85), channel_id=1, source_target_pairs={{0,16},{1,65},{2,18},{3,67},{4,20},{5,69},{6,22},{7,71},{8,24},{9,... | collective-permute-start | bytes 1843208 | tf_op jit(solution)/shard_map/ppermute | solution.py:273
  95.6 14.7 %collective-permute-start.21 = (bf16[2,400,384]{2,1,0:T(8,128)(2,1)S(1)}, bf16[2,400,384]{2,1,0:T(8,128)(2,1)S(1)}, u32[]{:S(2)}, u32[]{:S(2)}) collective-permute-start(bf16[2,400,384]{2,1,0:T(8,128)(2,1)S(1)} %add_convert_fusion.6), channel_id=1, source_target_pairs={{0,2},{1,7},{2,4},{3,1},{4,6},{5,3},{6,0},{7,5},{8,10},{9,15},{10,... | collective-permute-start | bytes 1843208 | tf_op jit(solution)/shard_map/ppermute | solution.py:273

commit v6 on v5

--- a/solution.py
+++ b/solution.py
@@ -308,29 +308,27 @@
     moved = [first(own, -1), first(own, 2), first(own, 1)]
     ring1, ring2 = turn(own, 1), turn(own, -1)
     kept = jnp.stack([own] + moved)
-    left, (up, down, pass_up, pass_down, here), z_other, z_mine = left_products(own, coupling, partner, counts)
-    kept, ring1, ring2, up, down, z_other, own_z = barrier((kept, ring1, ring2, up, down, z_other, own))
-
-    got = [first(up, 1), first(down, -1)]
+    kept, ring1, ring2 = barrier((kept, ring1, ring2))
     near, far = second(kept, -1), second(kept, 1)
+    left, (up, down, pass_up, pass_down, here), z_other, z_mine = left_products(
+        own, coupling, partner, after(counts, kept)
+    )
+
+    got_up, got_down = first(up, 1), first(down, -1)
     ring_mine = jnp.stack([own, ring1, ring2])
-    pair_sum = swap(z_other)
+    ring_other = swap(after(ring_mine, up))
+    across = turn(jnp.stack([ring2, ring_other[1]]), -1)
+    pair_sum = swap(after(z_other, near, far))
+    b_up, b_down = rounded(pass_up, got_up[:2]), rounded(pass_down, got_down[:2])
+    b_up, b_down, near, far, ring_mine, ring_other, across, pair_sum = barrier(
+        (b_up, b_down, near, far, ring_mine, ring_other, across, pair_sum)
+    )
+
     w = [rounded(z_mine[k], pair_sum[k]) for k in range(SIDE)]
-    ring_other = swap(after(ring_mine, w))
-    opposite, back = turn(after(w[3], ring_other), 1), turn(w[2], -1)
-    got, near, far, ring_mine, ring_other, w, opposite, back = barrier(
-        (got, near, far, ring_mine, ring_other, w, opposite, back)
-    )
-    got_up, got_down = got
-
-    b_up, b_down = rounded(pass_up, got_up[:2]), rounded(pass_down, got_down[:2])
-    across = jnp.stack([ring_mine[2], ring_other[1]])
-    z_pass = rounded(w[1], opposite)
-    b_up, b_down, near, far, across, z_pass = barrier((b_up, b_down, near, far, across, z_pass))
     low, high = second(near[:2], -1), second(far[2:], 1)
-    across = turn(across, -1)
+    opposite = turn(w[3], 1)
     last = [first(b_up, 1), first(b_down, -1)]
-    last, low, high, across, z_pass = barrier((last, low, high, across, z_pass))
+    last, low, high, opposite = barrier((last, low, high, opposite))
     last_up, last_down = last
 
     v = [
@@ -339,13 +337,14 @@
         rounded(here[2], got_up[2], last_down[0]),
         rounded(here[3], got_up[3], last_down[1]),
     ]
-    v, z_pass = barrier((v, z_pass))
-    z_last = turn(z_pass, 1)
+    z_pass = rounded(w[1], opposite)
+    v, z_pass, z_back = barrier((v, z_pass, w[2]))
     ends = [second(v[1], 1), second(v[3], -1), second(v[2], 2)]
+    z_last, back = turn(z_pass, 1), turn(z_back, -1)
 
     sources = [kept, near, far, low, high, ring_mine, ring_other, across]
     pair_blocks = pair_products(left, sources, after(partner, *v))
-    pair_blocks, ends, z_last = barrier((pair_blocks, ends, z_last))
+    pair_blocks, ends = barrier((pair_blocks, ends))
     partner_blocks = partner_products(own, added(v[0], w[0], back, z_last), ends)
     return (pair_blocks, partner_blocks[None])
 

time: 113 us -> 112 us (level)
  starting transfers between devices: 32.4 us -> 28.7 us
  waiting for transfers between devices: 55.8 us -> 57.3 us
    ppermute x22, starting transfers between devices: 32.4 us -> 28.7 us  [permuted(): return lax.ppermute(value, ('sx', 'sy'), pairs)]
    ppermute x22, waiting for transfers between devices: 55.8 us -> 57.3 us  [permuted(): return lax.ppermute(value, ('sx', 'sy'), pairs)]
    convert_element_type x4 -> x5, other arithmetic: 2.41 us -> 2.19 us  [rounded(): return added(*terms).astype(jnp.bfloat16)]
  transfers between devices with their start and end apart: 22 -> 22, of which waited for: 10 -> 13; matrix products, arithmetic and copies ran while one was open for 1% -> 2% of each run, Pallas kernels for 16% -> 17%
where the time goes in v6:
time: 112 us; the launch traced here: 111 us
  waiting for transfers between devices  57.3 us (51%)
  starting transfers between devices  28.7 us (26%)
  Pallas kernels  20.6 us (18%)
  other arithmetic  3.9 us (3%)
    ppermute x22, waiting for transfers between devices, permuted(): return lax.ppermute(value, ('sx', 'sy'), pairs)  57.3 us
    ppermute x22, starting transfers between devices, permuted(): return lax.ppermute(value, ('sx', 'sy'), pairs)  28.7 us
    pallas_call x1, Pallas kernels, pair_products(): pl.pallas_call(pair_kernel, in_specs=[smem, pl.BlockSpec(memory_space=plt...  9.33 us
    pallas_call x1, Pallas kernels, left_products(): pl.pallas_call(left_kernel, in_specs=[pl.BlockSpec(memory_space=pltpu.HBM...  9.14 us
  transfers between devices with their start and end apart: 22, of which 13 were waited for; matrix products, arithmetic and copies ran while one was open for 2% of the time, Pallas kernels for 17%

profile of v6, /device:TPU:0, one launch (start us, length us, event | category | flops | bytes accessed | tf_op | source)
XLA Modules:
  0.0 111.4 jit_solution(16812542215533319026)
XLA Ops:
  0.6 1.6 %collective-permute-start.2 = (bf16[400,384]{1,0:T(8,128)(2,1)}, bf16[400,384]{1,0:T(8,128)(2,1)S(1)}, u32[]{:S(2)}, u32[]{:S(2)}) collective-permute-start(bf16[400,384]{1,0:T(8,128)(2,1)} %bitcast.33), channel_id=1, source_target_pairs={{0,32},{1,9},{2,34},{3,11},{4,36},{5,13},{6,38},{7,15},{8,40},{9,1... | collective-permute-start | bytes 921608 | tf_op jit(solution)/shard_map/ppermute | solution.py:273
  2.3 2.7 %collective-permute-start.1 = (bf16[400,384]{1,0:T(8,128)(2,1)}, bf16[400,384]{1,0:T(8,128)(2,1)S(1)}, u32[]{:S(2)}, u32[]{:S(2)}) collective-permute-start(bf16[400,384]{1,0:T(8,128)(2,1)} %bitcast.34), channel_id=1, source_target_pairs={{0,64},{1,17},{2,66},{3,19},{4,68},{5,21},{6,70},{7,23},{8,72},{9,... | collective-permute-start | bytes 921608 | tf_op jit(solution)/shard_map/ppermute | solution.py:273
  5.0 1.4 %collective-permute-start = (bf16[400,384]{1,0:T(8,128)(2,1)}, bf16[400,384]{1,0:T(8,128)(2,1)S(1)}, u32[]{:S(2)}, u32[]{:S(2)}) collective-permute-start(bf16[400,384]{1,0:T(8,128)(2,1)} %bitcast.35), channel_id=1, source_target_pairs={{0,96},{1,25},{2,98},{3,27},{4,100},{5,29},{6,102},{7,31},{8,104},... | collective-permute-start | bytes 921608 | tf_op jit(solution)/shard_map/ppermute | solution.py:273
  6.4 4.0 %collective-permute-start.4 = (bf16[400,384]{1,0:T(8,128)(2,1)}, bf16[400,384]{1,0:T(8,128)(2,1)S(1)}, u32[]{:S(2)}, u32[]{:S(2)}) collective-permute-start(bf16[400,384]{1,0:T(8,128)(2,1)} %bitcast.36), channel_id=1, source_target_pairs={{0,6},{1,3},{2,0},{3,5},{4,2},{5,7},{6,4},{7,1},{8,14},{9,11},{10,... | collective-permute-start | bytes 921608 | tf_op jit(solution)/shard_map/ppermute | solution.py:273
  10.5 2.9 %collective-permute-done.1 = bf16[400,384]{1,0:T(8,128)(2,1)S(1)} collective-permute-done((bf16[400,384]{1,0:T(8,128)(2,1)}, bf16[400,384]{1,0:T(8,128)(2,1)S(1)}, u32[]{:S(2)}, u32[]{:S(2)}) %collective-permute-start.1) | collective-permute-done | bytes 307232 | tf_op jit(solution)/shard_map/ppermute | solution.py:273
  13.3 1.2 %pad_maximum_fusion.rest_0_ = bf16[4,400,384]{2,1,0:T(8,128)(2,1)S(1)} fusion(bf16[1,400,384]{2,1,0:T(8,128)(2,1)S(1)} %bitcast.46, bf16[1,400,384]{2,1,0:T(8,128)(2,1)S(1)} %bitcast.47, bf16[1,400,384]{2,1,0:T(8,128)(2,1)S(1)} %bitcast.48, bf16[1,400,384]{2,1,0:T(8,128)(2,1)} %bitcast.38), kind=kLoop, calls=%fused_computation.2 | loop fusion | flops 1843200 | bytes 2457600 | tf_op jit(solution)/shard_map/stack | solution.py:310
  14.5 0.0 copy-start
  14.5 2.2 %collective-permute-done.4 = bf16[400,384]{1,0:T(8,128)(2,1)S(1)} collective-permute-done((bf16[400,384]{1,0:T(8,128)(2,1)}, bf16[400,384]{1,0:T(8,128)(2,1)S(1)}, u32[]{:S(2)}, u32[]{:S(2)}) %collective-permute-start.4) | collective-permute-done | bytes 307232 | tf_op jit(solution)/shard_map/ppermute | solution.py:273
  16.8 2.0 %collective-permute-done.3 = bf16[400,384]{1,0:T(8,128)(2,1)S(1)} collective-permute-done((bf16[400,384]{1,0:T(8,128)(2,1)}, bf16[400,384]{1,0:T(8,128)(2,1)S(1)}, u32[]{:S(2)}, u32[]{:S(2)}) %collective-permute-start.3) | collective-permute-done | bytes 307232 | tf_op jit(solution)/shard_map/ppermute | solution.py:273
  18.8 1.6 %collective-permute-start.8 = (bf16[4,400,384]{2,1,0:T(8,128)(2,1)S(1)}, bf16[4,400,384]{2,1,0:T(8,128)(2,1)S(1)}, u32[]{:S(2)}, u32[]{:S(2)}) collective-permute-start(bf16[4,400,384]{2,1,0:T(8,128)(2,1)S(1)} %pad_maximum_fusion.rest_0_), channel_id=1, source_target_pairs={{0,8},{1,33},{2,10},{3,35},{4,12},{5,37},{6,14},{7,39},{8,16},{9,4... | collective-permute-start | bytes 3686408 | tf_op jit(solution)/shard_map/ppermute | solution.py:273
  20.3 1.7 %collective-permute-start.7 = (bf16[4,400,384]{2,1,0:T(8,128)(2,1)S(1)}, bf16[4,400,384]{2,1,0:T(8,128)(2,1)S(1)}, u32[]{:S(2)}, u32[]{:S(2)}) collective-permute-start(bf16[4,400,384]{2,1,0:T(8,128)(2,1)S(1)} %pad_maximum_fusion.rest_0_), channel_id=1, source_target_pairs={{0,24},{1,97},{2,26},{3,99},{4,28},{5,101},{6,30},{7,103},{8,0},{9... | collective-permute-start | bytes 3686408 | tf_op jit(solution)/shard_map/ppermute | solution.py:273
  22.0 9.1 %shard_map.59 = (bf16[8,2,400,384]{3,2,1,0:T(8,128)(2,1)S(1)}, bf16[4,2,400,384]{3,2,1,0:T(8,128)(2,1)}, bf16[4,2,400,384]{3,2,1,0:T(8,128)(2,1)}, bf16[2,2,400,...) custom-call(s32[8]{0:T(128)} %partner_ref, ...), custom_call_target="tpu_custom_call" | custom-call | flops 1887436800 | bytes 25000000 | tf_op jit(solution)/shard_map/pallas_call | solution.py:151
  31.1 0.8 collective-permute-start.5
  31.9 1.3 %collective-permute-start.6 = (bf16[4,2,400,384]{3,2,1,0:T(8,128)(2,1)}, bf16[4,2,400,384]{3,2,1,0:T(8,128)(2,1)S(1)}, u32[]{:S(2)}, u32[]{:S(2)}) collective-permute-start(bf16[4,2,400,384]{3,2,1,0:T(8,128)(2,1)} %get-tuple-element.45), channel_id=1, source_target_pairs={{0,32},{1,9},{2,34},{3,11},{4,36},{5,13},{6,38},{7,15},{8,40},{9,1... | collective-permute-start | bytes 7372808 | tf_op jit(solution)/shard_map/ppermute | solution.py:273
  33.2 7.8 %collective-permute-done.8.rest_2_ = bf16[4,400,384]{2,1,0:T(8,128)(2,1)S(1)} collective-permute-done((bf16[4,400,384]{2,1,0:T(8,128)(2,1)S(1)}, bf16[4,400,384]{2,1,0:T(8,128)(2,1)S(1)}, u32[]{:S(2)}, u32[]{:S(2)}) %collective-permute-start.8) | collective-permute-done | bytes 1228832 | tf_op jit(solution)/shard_map/ppermute | solution.py:273
  41.0 2.6 %collective-permute-done.7.rest_1_ = bf16[4,400,384]{2,1,0:T(8,128)(2,1)S(1)} collective-permute-done((bf16[4,400,384]{2,1,0:T(8,128)(2,1)S(1)}, bf16[4,400,384]{2,1,0:T(8,128)(2,1)S(1)}, u32[]{:S(2)}, u32[]{:S(2)}) %collective-permute-start.7) | collective-permute-done | bytes 1228832 | tf_op jit(solution)/shard_map/ppermute | solution.py:273
  43.6 0.1 pad_maximum_fusion.1.rest_5_
  43.8 0.6 collective-permute-start.9
  44.3 5.2 %collective-permute-done.9.rest_6_ = bf16[3,400,384]{2,1,0:T(8,128)(2,1)S(1)} collective-permute-done((bf16[3,400,384]{2,1,0:T(8,128)(2,1)S(1)}, bf16[3,400,384]{2,1,0:T(8,128)(2,1)S(1)}, u32[]{:S(2)}, u32[]{:S(2)}) %collective-permute-start.9) | collective-permute-done | bytes 921632 | tf_op jit(solution)/shard_map/ppermute | solution.py:273
  49.6 0.1 pad_maximum_fusion.2
  49.7 0.1 collective-permute-start.10
  49.8 11.5 %collective-permute-done.5 = bf16[4,2,400,384]{3,2,1,0:T(8,128)(2,1)S(1)} collective-permute-done((bf16[4,2,400,384]{3,2,1,0:T(8,128)(2,1)}, bf16[4,2,400,384]{3,2,1,0:T(8,128)(2,1)S(1)}, u32[]{:S(2)}, u32[]{:S(2)}) %collective-permute-start.5) | collective-permute-done | bytes 2457632 | tf_op jit(solution)/shard_map/ppermute | solution.py:273
  61.3 0.3 add_convert_fusion
  61.7 1.6 %collective-permute-done.6 = bf16[4,2,400,384]{3,2,1,0:T(8,128)(2,1)S(1)} collective-permute-done((bf16[4,2,400,384]{3,2,1,0:T(8,128)(2,1)}, bf16[4,2,400,384]{3,2,1,0:T(8,128)(2,1)S(1)}, u32[]{:S(2)}, u32[]{:S(2)}) %collective-permute-start.6) | collective-permute-done | bytes 2457632 | tf_op jit(solution)/shard_map/ppermute | solution.py:273
  63.2 0.3 add_convert_fusion.1
  63.6 0.2 collective-permute-start.12
  63.8 3.1 %collective-permute-start.13 = (bf16[2,2,400,384]{3,2,1,0:T(8,128)(2,1)S(1)}, bf16[2,2,400,384]{3,2,1,0:T(8,128)(2,1)S(1)}, u32[]{:S(2)}, u32[]{:S(2)}) collective-permute-start(bf16[2,2,400,384]{3,2,1,0:T(8,128)(2,1)S(1)} %add_convert_fusion), channel_id=1, source_target_pairs={{0,96},{1,25},{2,98},{3,27},{4,100},{5,29},{6,102},{7,31},{8,104},... | collective-permute-start | bytes 3686408 | tf_op jit(solution)/shard_map/ppermute | solution.py:273
  66.9 0.1 slice.80
  67.0 0.1 slice.81
  67.0 0.1 collective-permute-start.15
  67.1 3.2 %collective-permute-start.14 = (bf16[2,400,384]{2,1,0:T(8,128)(2,1)S(1)}, bf16[2,400,384]{2,1,0:T(8,128)(2,1)S(1)}, u32[]{:S(2)}, u32[]{:S(2)}) collective-permute-start(bf16[2,400,384]{2,1,0:T(8,128)(2,1)S(1)} %slice.80), channel_id=1, source_target_pairs={{0,24},{1,97},{2,26},{3,99},{4,28},{5,101},{6,30},{7,103},{8,0},{9... | collective-permute-start | bytes 1843208 | tf_op jit(solution)/shard_map/ppermute | solution.py:273
  70.3 0.3 fusion.9
  70.7 0.1 collective-permute-start.16
  70.8 14.3 %collective-permute-done.15.rest_4_ = bf16[2,400,384]{2,1,0:T(8,128)(2,1)S(1)} collective-permute-done((bf16[2,400,384]{2,1,0:T(8,128)(2,1)S(1)}, bf16[2,400,384]{2,1,0:T(8,128)(2,1)S(1)}, u32[]{:S(2)}, u32[]{:S(2)}) %collective-permute-start.15) | collective-permute-done | bytes 614432 | tf_op jit(solution)/shard_map/ppermute | solution.py:273
  85.1 3.1 %collective-permute-done.12 = bf16[2,2,400,384]{3,2,1,0:T(8,128)(2,1)S(1)} collective-permute-done((bf16[2,2,400,384]{3,2,1,0:T(8,128)(2,1)S(1)}, bf16[2,2,400,384]{3,2,1,0:T(8,128)(2,1)S(1)}, u32[]{:S(2)}, u32[]{:S(2)}) %collective-permute-start.12) | collective-permute-done | bytes 1228832 | tf_op jit(solution)/shard_map/ppermute | solution.py:273
  88.2 0.2 fusion.2
  88.4 0.9 fusion.7
  89.4 0.1 collective-permute-start.17
  89.5 2.7 %collective-permute-start.19 = (bf16[2,400,384]{2,1,0:T(8,128)(2,1)S(1)}, bf16[2,400,384]{2,1,0:T(8,128)(2,1)S(1)}, u32[]{:S(2)}, u32[]{:S(2)}) collective-permute-start(bf16[2,400,384]{2,1,0:T(8,128)(2,1)S(1)} %get-tuple-element.63), channel_id=1, source_target_pairs={{0,16},{1,65},{2,18},{3,67},{4,20},{5,69},{6,22},{7,71},{8,24},{9,... | collective-permute-start | bytes 1843208 | tf_op jit(solution)/shard_map/ppermute | solution.py:273
  92.1 1.4 %collective-permute-start.18 = (bf16[2,400,384]{2,1,0:T(8,128)(2,1)S(1)}, bf16[2,400,384]{2,1,0:T(8,128)(2,1)S(1)}, u32[]{:S(2)}, u32[]{:S(2)}) collective-permute-start(bf16[2,400,384]{2,1,0:T(8,128)(2,1)S(1)} %get-tuple-element.64), channel_id=1, source_target_pairs={{0,24},{1,97},{2,26},{3,99},{4,28},{5,101},{6,30},{7,103},{8,0},{9... | collective-permute-start | bytes 1843208 | tf_op jit(solution)/shard_map/ppermute | solution.py:273
  93.5 1.7 %collective-permute-start.20 = (bf16[2,400,384]{2,1,0:T(8,128)(2,1)S(1)}, bf16[2,400,384]{2,1,0:T(8,128)(2,1)S(1)}, u32[]{:S(2)}, u32[]{:S(2)}) collective-permute-start(bf16[2,400,384]{2,1,0:T(8,128)(2,1)S(1)} %get-tuple-element.73), channel_id=1, source_target_pairs={{0,6},{1,3},{2,0},{3,5},{4,2},{5,7},{6,4},{7,1},{8,14},{9,11},{10,... | collective-permute-start | bytes 1843208 | tf_op jit(solution)/shard_map/ppermute | solution.py:273
  95.2 0.3 collective-permute-start.21
  95.5 9.3 %shard_map.60 = bf16[8,2,400,400]{3,2,1,0:T(8,128)(2,1)} custom-call(s32[8]{0:T(128)S(1)} %copy-done.1, bf16[8,2,400,384]{3,2,1,0:T(8,128)(2,1)S(1)} %get-tuple-element.66.left_ref, bf16[4,400,384]{2,1,0:T(8,128)(2,1)S(1)} %pad_maximum_fusion.rest_0_, bf16[4,400,384]{2,1,0:T(8,128)(2,1)S(1)} %collective-permute-done.7.rest_1_, ...), custom_call_target="tpu_custom_call" | custom-call | flops 1966080000 | bytes 15000000 | tf_op jit(solution)/shard_map/pallas_call | solution.py:229
  104.9 2.5 %collective-permute-done.17.rest_0_ = bf16[2,400,384]{2,1,0:T(8,128)(2,1)S(1)} collective-permute-done((bf16[2,400,384]{2,1,0:T(8,128)(2,1)S(1)}, bf16[2,400,384]{2,1,0:T(8,128)(2,1)S(1)}, u32[]{:S(2)}, u32[]{:S(2)}) %collective-permute-start.17) | collective-permute-done | bytes 614432 | tf_op jit(solution)/shard_map/ppermute | solution.py:273
  107.4 0.9 collective-permute-done.18.rest_1_
  108.3 0.6 collective-permute-done.21
  108.9 0.4 fusion.1.sum_ref
  109.3 2.1 %shard_map.61 = f32[2,400,400]{2,1,0:T(8,128)} custom-call(bf16[400,384]{1,0:T(8,128)(2,1)S(1)} %bitcast.41, f32[2,400,384]{2,1,0:T(8,128)S(1)} %fusion.1.sum_ref, bf16[2,400,384]{2,1,0:T(8,128)(2,1)S(1)} %collective-permute-done.17.rest_0_, bf16[2,400,384]{2,1,0:T(8,128)(2,1)S(1)} %collective-permute-done.18.rest_1_, ...), custom_call_target="tpu_custom_call" | custom-call | tf_op jit(solution)/shard_map/pallas_call | solution.py:260
  (19 shorter events, 0.1 us)
Async XLA Ops:
  0.6 9.9 %collective-permute-start.2 = (bf16[400,384]{1,0:T(8,128)(2,1)}, bf16[400,384]{1,0:T(8,128)(2,1)S(1)}, u32[]{:S(2)}, u32[]{:S(2)}) collective-permute-start(bf16[400,384]{1,0:T(8,128)(2,1)} %bitcast.33), channel_id=1, source_target_pairs={{0,32},{1,9},{2,34},{3,11},{4,36},{5,13},{6,38},{7,15},{8,40},{9,1... | collective-permute-start | bytes 921608 | tf_op jit(solution)/shard_map/ppermute | solution.py:273
  2.3 11.1 %collective-permute-start.1 = (bf16[400,384]{1,0:T(8,128)(2,1)}, bf16[400,384]{1,0:T(8,128)(2,1)S(1)}, u32[]{:S(2)}, u32[]{:S(2)}) collective-permute-start(bf16[400,384]{1,0:T(8,128)(2,1)} %bitcast.34), channel_id=1, source_target_pairs={{0,64},{1,17},{2,66},{3,19},{4,68},{5,21},{6,70},{7,23},{8,72},{9,... | collective-permute-start | bytes 921608 | tf_op jit(solution)/shard_map/ppermute | solution.py:273
  5.0 8.3 %collective-permute-start = (bf16[400,384]{1,0:T(8,128)(2,1)}, bf16[400,384]{1,0:T(8,128)(2,1)S(1)}, u32[]{:S(2)}, u32[]{:S(2)}) collective-permute-start(bf16[400,384]{1,0:T(8,128)(2,1)} %bitcast.35), channel_id=1, source_target_pairs={{0,96},{1,25},{2,98},{3,27},{4,100},{5,29},{6,102},{7,31},{8,104},... | collective-permute-start | bytes 921608 | tf_op jit(solution)/shard_map/ppermute | solution.py:273
  6.4 10.3 %collective-permute-start.4 = (bf16[400,384]{1,0:T(8,128)(2,1)}, bf16[400,384]{1,0:T(8,128)(2,1)S(1)}, u32[]{:S(2)}, u32[]{:S(2)}) collective-permute-start(bf16[400,384]{1,0:T(8,128)(2,1)} %bitcast.36), channel_id=1, source_target_pairs={{0,6},{1,3},{2,0},{3,5},{4,2},{5,7},{6,4},{7,1},{8,14},{9,11},{10,... | collective-permute-start | bytes 921608 | tf_op jit(solution)/shard_map/ppermute | solution.py:273
  10.5 8.3 %collective-permute-start.3 = (bf16[400,384]{1,0:T(8,128)(2,1)}, bf16[400,384]{1,0:T(8,128)(2,1)S(1)}, u32[]{:S(2)}, u32[]{:S(2)}) collective-permute-start(bf16[400,384]{1,0:T(8,128)(2,1)} %bitcast.37), channel_id=1, source_target_pairs={{0,2},{1,7},{2,4},{3,1},{4,6},{5,3},{6,0},{7,5},{8,10},{9,15},{10,... | collective-permute-start | bytes 921608 | tf_op jit(solution)/shard_map/ppermute | solution.py:273
  14.5 29.1 %copy-start = (bf16[1,384,400]{1,2,0:T(8,128)(2,1)S(1)}, bf16[1,384,400]{1,2,0:T(8,128)(2,1)}, u32[]{:S(2)}) copy-start(bf16[1,384,400]{1,2,0:T(8,128)(2,1)} %param.4) | copy-start | bytes 921604
  18.8 22.3 %collective-permute-start.8 = (bf16[4,400,384]{2,1,0:T(8,128)(2,1)S(1)}, bf16[4,400,384]{2,1,0:T(8,128)(2,1)S(1)}, u32[]{:S(2)}, u32[]{:S(2)}) collective-permute-start(bf16[4,400,384]{2,1,0:T(8,128)(2,1)S(1)} %pad_maximum_fusion.rest_0_), channel_id=1, source_target_pairs={{0,8},{1,33},{2,10},{3,35},{4,12},{5,37},{6,14},{7,39},{8,16},{9,4... | collective-permute-start | bytes 3686408 | tf_op jit(solution)/shard_map/ppermute | solution.py:273
  20.3 23.3 %collective-permute-start.7 = (bf16[4,400,384]{2,1,0:T(8,128)(2,1)S(1)}, bf16[4,400,384]{2,1,0:T(8,128)(2,1)S(1)}, u32[]{:S(2)}, u32[]{:S(2)}) collective-permute-start(bf16[4,400,384]{2,1,0:T(8,128)(2,1)S(1)} %pad_maximum_fusion.rest_0_), channel_id=1, source_target_pairs={{0,24},{1,97},{2,26},{3,99},{4,28},{5,101},{6,30},{7,103},{8,0},{9... | collective-permute-start | bytes 3686408 | tf_op jit(solution)/shard_map/ppermute | solution.py:273
  31.1 30.2 %collective-permute-start.5 = (bf16[4,2,400,384]{3,2,1,0:T(8,128)(2,1)}, bf16[4,2,400,384]{3,2,1,0:T(8,128)(2,1)S(1)}, u32[]{:S(2)}, u32[]{:S(2)}) collective-permute-start(bf16[4,2,400,384]{3,2,1,0:T(8,128)(2,1)} %get-tuple-element.43), channel_id=1, source_target_pairs={{0,96},{1,25},{2,98},{3,27},{4,100},{5,29},{6,102},{7,31},{8,104},... | collective-permute-start | bytes 7372808 | tf_op jit(solution)/shard_map/ppermute | solution.py:273
  31.9 31.3 %collective-permute-start.6 = (bf16[4,2,400,384]{3,2,1,0:T(8,128)(2,1)}, bf16[4,2,400,384]{3,2,1,0:T(8,128)(2,1)S(1)}, u32[]{:S(2)}, u32[]{:S(2)}) collective-permute-start(bf16[4,2,400,384]{3,2,1,0:T(8,128)(2,1)} %get-tuple-element.45), channel_id=1, source_target_pairs={{0,32},{1,9},{2,34},{3,11},{4,36},{5,13},{6,38},{7,15},{8,40},{9,1... | collective-permute-start | bytes 7372808 | tf_op jit(solution)/shard_map/ppermute | solution.py:273
  43.6 19.9 %collective-permute-start.11 = (bf16[4,2,400,384]{3,2,1,0:T(8,128)(2,1)}, bf16[4,2,400,384]{3,2,1,0:T(8,128)(2,1)S(1)}, u32[]{:S(2)}, u32[]{:S(2)}) collective-permute-start(bf16[4,2,400,384]{3,2,1,0:T(8,128)(2,1)} %get-tuple-element.51), channel_id=1, source_target_pairs={{0,1},{1,0},{2,3},{3,2},{4,5},{5,4},{6,7},{7,6},{8,9},{9,8},{10,11... | collective-permute-start | bytes 7372808 | tf_op jit(solution)/shard_map/ppermute | solution.py:273
  43.8 5.8 %collective-permute-start.9 = (bf16[3,400,384]{2,1,0:T(8,128)(2,1)S(1)}, bf16[3,400,384]{2,1,0:T(8,128)(2,1)S(1)}, u32[]{:S(2)}, u32[]{:S(2)}) collective-permute-start(bf16[3,400,384]{2,1,0:T(8,128)(2,1)S(1)} %pad_maximum_fusion.1.rest_5_), channel_id=1, source_target_pairs={{0,1},{1,0},{2,3},{3,2},{4,5},{5,4},{6,7},{7,6},{8,9},{9,8},{10,11... | collective-permute-start | bytes 2764808 | tf_op jit(solution)/shard_map/ppermute | solution.py:273
  49.7 13.9 %collective-permute-start.10 = (bf16[2,400,384]{2,1,0:T(8,128)(2,1)S(1)}, bf16[2,400,384]{2,1,0:T(8,128)(2,1)S(1)}, u32[]{:S(2)}, u32[]{:S(2)}) collective-permute-start(bf16[2,400,384]{2,1,0:T(8,128)(2,1)S(1)} %pad_maximum_fusion.2), channel_id=1, source_target_pairs={{0,6},{1,3},{2,0},{3,5},{4,2},{5,7},{6,4},{7,1},{8,14},{9,11},{10,... | collective-permute-start | bytes 1843208 | tf_op jit(solution)/shard_map/ppermute | solution.py:273
  63.5 6.8 %copy-start.3 = (bf16[4,2,400,384]{3,2,1,0:T(8,128)(2,1)S(1)}, bf16[4,2,400,384]{3,2,1,0:T(8,128)(2,1)}, u32[]{:S(2)}) copy-start(bf16[4,2,400,384]{3,2,1,0:T(8,128)(2,1)} %get-tuple-element.56) | copy-start | bytes 7372804
  63.6 24.6 %collective-permute-start.12 = (bf16[2,2,400,384]{3,2,1,0:T(8,128)(2,1)S(1)}, bf16[2,2,400,384]{3,2,1,0:T(8,128)(2,1)S(1)}, u32[]{:S(2)}, u32[]{:S(2)}) collective-permute-start(bf16[2,2,400,384]{3,2,1,0:T(8,128)(2,1)S(1)} %add_convert_fusion.1), channel_id=1, source_target_pairs={{0,32},{1,9},{2,34},{3,11},{4,36},{5,13},{6,38},{7,15},{8,40},{9,1... | collective-permute-start | bytes 3686408 | tf_op jit(solution)/shard_map/ppermute | solution.py:273
  63.8 24.4 %collective-permute-start.13 = (bf16[2,2,400,384]{3,2,1,0:T(8,128)(2,1)S(1)}, bf16[2,2,400,384]{3,2,1,0:T(8,128)(2,1)S(1)}, u32[]{:S(2)}, u32[]{:S(2)}) collective-permute-start(bf16[2,2,400,384]{3,2,1,0:T(8,128)(2,1)S(1)} %add_convert_fusion), channel_id=1, source_target_pairs={{0,96},{1,25},{2,98},{3,27},{4,100},{5,29},{6,102},{7,31},{8,104},... | collective-permute-start | bytes 3686408 | tf_op jit(solution)/shard_map/ppermute | solution.py:273
  67.0 18.1 %collective-permute-start.15 = (bf16[2,400,384]{2,1,0:T(8,128)(2,1)S(1)}, bf16[2,400,384]{2,1,0:T(8,128)(2,1)S(1)}, u32[]{:S(2)}, u32[]{:S(2)}) collective-permute-start(bf16[2,400,384]{2,1,0:T(8,128)(2,1)S(1)} %slice.81), channel_id=1, source_target_pairs={{0,8},{1,33},{2,10},{3,35},{4,12},{5,37},{6,14},{7,39},{8,16},{9,4... | collective-permute-start | bytes 1843208 | tf_op jit(solution)/shard_map/ppermute | solution.py:273
  67.1 18.0 %collective-permute-start.14 = (bf16[2,400,384]{2,1,0:T(8,128)(2,1)S(1)}, bf16[2,400,384]{2,1,0:T(8,128)(2,1)S(1)}, u32[]{:S(2)}, u32[]{:S(2)}) collective-permute-start(bf16[2,400,384]{2,1,0:T(8,128)(2,1)S(1)} %slice.80), channel_id=1, source_target_pairs={{0,24},{1,97},{2,26},{3,99},{4,28},{5,101},{6,30},{7,103},{8,0},{9... | collective-permute-start | bytes 1843208 | tf_op jit(solution)/shard_map/ppermute | solution.py:273
  70.7 17.7 %copy-start.2 = (bf16[4,2,400,384]{3,2,1,0:T(8,128)(2,1)S(1)}, bf16[4,2,400,384]{3,2,1,0:T(8,128)(2,1)}, u32[]{:S(2)}) copy-start(bf16[4,2,400,384]{3,2,1,0:T(8,128)(2,1)} %get-tuple-element.42) | copy-start | bytes 7372804
  70.7 14.4 %collective-permute-start.16 = (bf16[2,400,384]{2,1,0:T(8,128)(2,1)S(1)}, bf16[2,400,384]{2,1,0:T(8,128)(2,1)S(1)}, u32[]{:S(2)}, u32[]{:S(2)}) collective-permute-start(bf16[2,400,384]{2,1,0:T(8,128)(2,1)S(1)} %get-tuple-element.83), channel_id=1, source_target_pairs={{0,2},{1,7},{2,4},{3,1},{4,6},{5,3},{6,0},{7,5},{8,10},{9,15},{10,... | collective-permute-start | bytes 1843208 | tf_op jit(solution)/shard_map/ppermute | solution.py:273
  88.4 7.1 %copy-start.1 = (s32[8]{0:T(128)S(1)}, s32[8]{0:T(128)}, u32[]{:S(2)}) copy-start(s32[8]{0:T(128)} %partner_ref) | copy-start | bytes 100
  89.4 18.0 %collective-permute-start.17 = (bf16[2,400,384]{2,1,0:T(8,128)(2,1)S(1)}, bf16[2,400,384]{2,1,0:T(8,128)(2,1)S(1)}, u32[]{:S(2)}, u32[]{:S(2)}) collective-permute-start(bf16[2,400,384]{2,1,0:T(8,128)(2,1)S(1)} %get-tuple-element.62), channel_id=1, source_target_pairs={{0,8},{1,33},{2,10},{3,35},{4,12},{5,37},{6,14},{7,39},{8,16},{9,4... | collective-permute-start | bytes 1843208 | tf_op jit(solution)/shard_map/ppermute | solution.py:273
  89.5 17.9 %collective-permute-start.19 = (bf16[2,400,384]{2,1,0:T(8,128)(2,1)S(1)}, bf16[2,400,384]{2,1,0:T(8,128)(2,1)S(1)}, u32[]{:S(2)}, u32[]{:S(2)}) collective-permute-start(bf16[2,400,384]{2,1,0:T(8,128)(2,1)S(1)} %get-tuple-element.63), channel_id=1, source_target_pairs={{0,16},{1,65},{2,18},{3,67},{4,20},{5,69},{6,22},{7,71},{8,24},{9,... | collective-permute-start | bytes 1843208 | tf_op jit(solution)/shard_map/ppermute | solution.py:273
  92.1 16.2 %collective-permute-start.18 = (bf16[2,400,384]{2,1,0:T(8,128)(2,1)S(1)}, bf16[2,400,384]{2,1,0:T(8,128)(2,1)S(1)}, u32[]{:S(2)}, u32[]{:S(2)}) collective-permute-start(bf16[2,400,384]{2,1,0:T(8,128)(2,1)S(1)} %get-tuple-element.64), channel_id=1, source_target_pairs={{0,24},{1,97},{2,26},{3,99},{4,28},{5,101},{6,30},{7,103},{8,0},{9... | collective-permute-start | bytes 1843208 | tf_op jit(solution)/shard_map/ppermute | solution.py:273
  93.5 14.8 %collective-permute-start.20 = (bf16[2,400,384]{2,1,0:T(8,128)(2,1)S(1)}, bf16[2,400,384]{2,1,0:T(8,128)(2,1)S(1)}, u32[]{:S(2)}, u32[]{:S(2)}) collective-permute-start(bf16[2,400,384]{2,1,0:T(8,128)(2,1)S(1)} %get-tuple-element.73), channel_id=1, source_target_pairs={{0,6},{1,3},{2,0},{3,5},{4,2},{5,7},{6,4},{7,1},{8,14},{9,11},{10,... | collective-permute-start | bytes 1843208 | tf_op jit(solution)/shard_map/ppermute | solution.py:273
  95.2 13.7 %collective-permute-start.21 = (bf16[2,400,384]{2,1,0:T(8,128)(2,1)S(1)}, bf16[2,400,384]{2,1,0:T(8,128)(2,1)S(1)}, u32[]{:S(2)}, u32[]{:S(2)}) collective-permute-start(bf16[2,400,384]{2,1,0:T(8,128)(2,1)S(1)} %fusion.2), channel_id=1, source_target_pairs={{0,2},{1,7},{2,4},{3,1},{4,6},{5,3},{6,0},{7,5},{8,10},{9,15},{10,... | collective-permute-start | bytes 1843208 | tf_op jit(solution)/shard_map/ppermute | solution.py:273

commit v7 on v6

--- a/solution.py
+++ b/solution.py
@@ -7,7 +7,8 @@
 
 SIDE = 4
 SPAN_X, SPAN_Y = SIDE * SIDE, 2 * SIDE
-PARTS = ((0, 4), (4, 4), (8, 2), (10, 2), (12, 4))
+PARTS = ((0, 2), (2, 2), (4, 2), (6, 2), (8, 2), (10, 2), (12, 4))
+RINGS = ((16, 2), (18, 2), (20, 4))
 CHUNK = 80
 
 
@@ -34,9 +35,9 @@
 
 
 def left_kernel(partner_hbm, counts_hbm, own_hbm, coupling_hbm, left_ref, *rest):
-    outs = rest[:7]
-    partner_ref, counts_ref, own_ref, blocks, zero, sums = rest[7:13]
-    keys, number, seen, at_sum, in_sem, out_sem = rest[13:]
+    outs = rest[:10]
+    partner_ref, counts_ref, own_ref, blocks, zero, sums = rest[10:16]
+    keys, number, seen, at_sum, in_sem, out_sem = rest[16:]
     pairs, width = blocks.shape[0], blocks.shape[1]
     count, modes = 2 * pairs, own_ref.shape[0]
     slots = SPAN_X + SPAN_Y
@@ -81,7 +82,7 @@
         zero[r % 2, rows] = jnp.zeros((CHUNK, width), zero.dtype)
 
     def send(source, key):
-        for out, (at, size) in zip(outs, PARTS + ((SPAN_X, SIDE), (SPAN_X + SIDE, SIDE)), strict=True):
+        for out, (at, size) in zip(outs, PARTS + RINGS, strict=True):
             @pl.when((key >= at) & (key < at + size))
             def _():
                 pltpu.make_async_copy(source, out.at[key - at], out_sem.at[key]).start()
@@ -145,9 +146,9 @@
     pairs, blocks, width, _ = coupling.shape
     modes = own.shape[0]
     slots = SPAN_X + SPAN_Y
-    sizes = [pairs] + [size for _, size in PARTS] + [SIDE] * 2
+    sizes = [pairs] + [size for _, size in PARTS + RINGS]
     hbm, vmem = pltpu.HBM, pltpu.VMEM
-    spaces = [vmem, hbm, hbm, vmem, vmem, hbm, hbm, hbm]
+    spaces = [vmem] + [hbm] * 4 + [vmem] * 2 + [hbm] * 4
     out = pl.pallas_call(
         left_kernel,
         in_specs=[pl.BlockSpec(memory_space=pltpu.HBM)] * 4,
@@ -171,7 +172,7 @@
         cost_estimate=pl.CostEstimate(flops=2 * pairs * blocks * modes * width * width,
                                       bytes_accessed=25 * 10**6, transcendentals=0),
     )(*map(in_hbm, (partner, counts, own, coupling)))
-    return out[0], out[1:6], out[6], out[7]
+    return out[0], out[1:8], out[8:11]
 
 
 def nt(a, b):
@@ -310,32 +311,34 @@
     kept = jnp.stack([own] + moved)
     kept, ring1, ring2 = barrier((kept, ring1, ring2))
     near, far = second(kept, -1), second(kept, 1)
-    left, (up, down, pass_up, pass_down, here), z_other, z_mine = left_products(
+    left, (up, up_end, down, down_end, pass_up, pass_down, here), (z_near, z_far, z_mine) = left_products(
         own, coupling, partner, after(counts, kept)
     )
 
     got_up, got_down = first(up, 1), first(down, -1)
+    up_end, down_end, z_far, near, far = barrier((up_end, down_end, z_far, near, far))
+    end_up, end_down = first(up_end, 1), first(down_end, -1)
+    last_up, last_down = first(rounded(pass_up, got_up), 1), first(rounded(pass_down, got_down), -1)
+
     ring_mine = jnp.stack([own, ring1, ring2])
     ring_other = swap(after(ring_mine, up))
+    far_sum = swap(z_far)
     across = turn(jnp.stack([ring2, ring_other[1]]), -1)
-    pair_sum = swap(after(z_other, near, far))
-    b_up, b_down = rounded(pass_up, got_up[:2]), rounded(pass_down, got_down[:2])
-    b_up, b_down, near, far, ring_mine, ring_other, across, pair_sum = barrier(
-        (b_up, b_down, near, far, ring_mine, ring_other, across, pair_sum)
+    near_sum = swap(after(z_near, ring_other))
+    w = [rounded(z_mine[k], (near_sum, far_sum)[k // 2][k % 2]) for k in range(SIDE)]
+
+    near, far, w3, end_up, end_down = barrier((near, far, w[3], end_up, end_down))
+    low, high = second(near[:2], -1), second(far[2:], 1)
+    opposite = turn(w3, 1)
+    last_up, last_down, low, high, opposite, across, ring_other, w = barrier(
+        (last_up, last_down, low, high, opposite, across, ring_other, w)
     )
 
-    w = [rounded(z_mine[k], pair_sum[k]) for k in range(SIDE)]
-    low, high = second(near[:2], -1), second(far[2:], 1)
-    opposite = turn(w[3], 1)
-    last = [first(b_up, 1), first(b_down, -1)]
-    last, low, high, opposite = barrier((last, low, high, opposite))
-    last_up, last_down = last
-
     v = [
-        rounded(here[0], got_down[2], last_up[0]),
-        rounded(here[1], got_down[3], last_up[1]),
-        rounded(here[2], got_up[2], last_down[0]),
-        rounded(here[3], got_up[3], last_down[1]),
+        rounded(here[0], end_down[0], last_up[0]),
+        rounded(here[1], end_down[1], last_up[1]),
+        rounded(here[2], end_up[0], last_down[0]),
+        rounded(here[3], end_up[1], last_down[1]),
     ]
     z_pass = rounded(w[1], opposite)
     v, z_pass, z_back = barrier((v, z_pass, w[2]))

time: 112 us -> 113 us (level); the launches traced: 111 us -> 111 us
  waiting for transfers between devices: 57.3 us -> 51.8 us
  starting transfers between devices: 28.7 us -> 33.7 us
    ppermute x22 -> x25, waiting for transfers between devices: 57.3 us -> 51.8 us  [permuted(): return lax.ppermute(value, ('sx', 'sy'), pairs)]
    ppermute x22 -> x25, starting transfers between devices: 28.7 us -> 33.7 us  [permuted(): return lax.ppermute(value, ('sx', 'sy'), pairs)]
  transfers between devices with their start and end apart: 22 -> 25, of which waited for: 13 -> 12; matrix products, arithmetic and copies ran while one was open for 2% -> 3% of each run, Pallas kernels for 17% -> 17%
where the time goes in v7:
time: 113 us; the launch traced here: 111 us
  waiting for transfers between devices  51.8 us (46%)
  starting transfers between devices  33.7 us (30%)
  Pallas kernels  20.8 us (18%)
  other arithmetic  3.97 us (4%)
    ppermute x25, waiting for transfers between devices, permuted(): return lax.ppermute(value, ('sx', 'sy'), pairs)  51.8 us
    ppermute x25, starting transfers between devices, permuted(): return lax.ppermute(value, ('sx', 'sy'), pairs)  33.7 us
    pallas_call x1, Pallas kernels, left_products(): pl.pallas_call(left_kernel, in_specs=[pl.BlockSpec(memory_space=pltpu.HBM...  9.37 us
    pallas_call x1, Pallas kernels, pair_products(): pl.pallas_call(pair_kernel, in_specs=[smem, pl.BlockSpec(memory_space=plt...  9.33 us
    convert_element_type x5, other arithmetic, rounded(): return added(*terms).astype(jnp.bfloat16)  2.27 us
  transfers between devices with their start and end apart: 25, of which 12 were waited for; matrix products, arithmetic and copies ran while one was open for 3% of the time, Pallas kernels for 17%

profile of v7, /device:TPU:0, one launch (start us, length us, event | category | flops | bytes accessed | tf_op | source)
XLA Modules:
  0.0 111.2 jit_solution(14589737728720439152)
XLA Ops:
  0.6 1.6 %collective-permute-start.2 = (bf16[400,384]{1,0:T(8,128)(2,1)}, bf16[400,384]{1,0:T(8,128)(2,1)S(1)}, u32[]{:S(2)}, u32[]{:S(2)}) collective-permute-start(bf16[400,384]{1,0:T(8,128)(2,1)} %bitcast.27), channel_id=1, source_target_pairs={{0,32},{1,9},{2,34},{3,11},{4,36},{5,13},{6,38},{7,15},{8,40},{9,1... | collective-permute-start | bytes 921608 | tf_op jit(solution)/shard_map/ppermute | solution.py:274
  2.3 2.7 %collective-permute-start.1 = (bf16[400,384]{1,0:T(8,128)(2,1)}, bf16[400,384]{1,0:T(8,128)(2,1)S(1)}, u32[]{:S(2)}, u32[]{:S(2)}) collective-permute-start(bf16[400,384]{1,0:T(8,128)(2,1)} %bitcast.28), channel_id=1, source_target_pairs={{0,64},{1,17},{2,66},{3,19},{4,68},{5,21},{6,70},{7,23},{8,72},{9,... | collective-permute-start | bytes 921608 | tf_op jit(solution)/shard_map/ppermute | solution.py:274
  5.0 1.4 %collective-permute-start = (bf16[400,384]{1,0:T(8,128)(2,1)}, bf16[400,384]{1,0:T(8,128)(2,1)S(1)}, u32[]{:S(2)}, u32[]{:S(2)}) collective-permute-start(bf16[400,384]{1,0:T(8,128)(2,1)} %bitcast.29), channel_id=1, source_target_pairs={{0,96},{1,25},{2,98},{3,27},{4,100},{5,29},{6,102},{7,31},{8,104},... | collective-permute-start | bytes 921608 | tf_op jit(solution)/shard_map/ppermute | solution.py:274
  6.4 1.9 %collective-permute-start.3 = (bf16[400,384]{1,0:T(8,128)(2,1)}, bf16[400,384]{1,0:T(8,128)(2,1)S(1)}, u32[]{:S(2)}, u32[]{:S(2)}) collective-permute-start(bf16[400,384]{1,0:T(8,128)(2,1)} %bitcast.30), channel_id=1, source_target_pairs={{0,2},{1,7},{2,4},{3,1},{4,6},{5,3},{6,0},{7,5},{8,10},{9,15},{10,... | collective-permute-start | bytes 921608 | tf_op jit(solution)/shard_map/ppermute | solution.py:274
  8.4 2.1 %collective-permute-start.4 = (bf16[400,384]{1,0:T(8,128)(2,1)}, bf16[400,384]{1,0:T(8,128)(2,1)S(1)}, u32[]{:S(2)}, u32[]{:S(2)}) collective-permute-start(bf16[400,384]{1,0:T(8,128)(2,1)} %bitcast.31), channel_id=1, source_target_pairs={{0,6},{1,3},{2,0},{3,5},{4,2},{5,7},{6,4},{7,1},{8,14},{9,11},{10,... | collective-permute-start | bytes 921608 | tf_op jit(solution)/shard_map/ppermute | solution.py:274
  10.5 2.9 %collective-permute-done.1 = bf16[400,384]{1,0:T(8,128)(2,1)S(1)} collective-permute-done((bf16[400,384]{1,0:T(8,128)(2,1)}, bf16[400,384]{1,0:T(8,128)(2,1)S(1)}, u32[]{:S(2)}, u32[]{:S(2)}) %collective-permute-start.1) | collective-permute-done | bytes 307232 | tf_op jit(solution)/shard_map/ppermute | solution.py:274
  13.3 1.2 %pad_maximum_fusion.rest_0_ = bf16[4,400,384]{2,1,0:T(8,128)(2,1)S(1)} fusion(bf16[1,400,384]{2,1,0:T(8,128)(2,1)S(1)} %bitcast.40, bf16[1,400,384]{2,1,0:T(8,128)(2,1)S(1)} %bitcast.41, bf16[1,400,384]{2,1,0:T(8,128)(2,1)S(1)} %bitcast.42, bf16[1,400,384]{2,1,0:T(8,128)(2,1)} %bitcast.32), kind=kLoop, calls=%fused_computation.2 | loop fusion | flops 1843200 | bytes 2457600 | tf_op jit(solution)/shard_map/stack | solution.py:311
  14.6 3.1 %collective-permute-done.3 = bf16[400,384]{1,0:T(8,128)(2,1)S(1)} collective-permute-done((bf16[400,384]{1,0:T(8,128)(2,1)}, bf16[400,384]{1,0:T(8,128)(2,1)S(1)}, u32[]{:S(2)}, u32[]{:S(2)}) %collective-permute-start.3) | collective-permute-done | bytes 307232 | tf_op jit(solution)/shard_map/ppermute | solution.py:274
  17.7 2.5 %collective-permute-start.5 = (bf16[4,400,384]{2,1,0:T(8,128)(2,1)S(1)}, bf16[4,400,384]{2,1,0:T(8,128)(2,1)S(1)}, u32[]{:S(2)}, u32[]{:S(2)}) collective-permute-start(bf16[4,400,384]{2,1,0:T(8,128)(2,1)S(1)} %pad_maximum_fusion.rest_0_), channel_id=1, source_target_pairs={{0,24},{1,97},{2,26},{3,99},{4,28},{5,101},{6,30},{7,103},{8,0},{9... | collective-permute-start | bytes 3686408 | tf_op jit(solution)/shard_map/ppermute | solution.py:274
  20.3 0.1 pad_maximum_fusion.1.rest_5_
  20.4 9.4 %shard_map.59 = (bf16[8,2,400,384]{3,2,1,0:T(8,128)(2,1)S(1)}, bf16[2,2,400,384]{3,2,1,0:T(8,128)(2,1)}, bf16[2,2,400,384]{3,2,1,0:T(8,128)(2,1)}, bf16[2,2,400,...) custom-call(s32[8]{0:T(128)} %partner_ref, ...), custom_call_target="tpu_custom_call" | custom-call | flops 1887436800 | bytes 25000000 | tf_op jit(solution)/shard_map/pallas_call | solution.py:152
  29.8 0.1 collective-permute-start.17
  29.9 1.9 %collective-permute-start.10 = (bf16[2,2,400,384]{3,2,1,0:T(8,128)(2,1)}, bf16[2,2,400,384]{3,2,1,0:T(8,128)(2,1)S(1)}, u32[]{:S(2)}, u32[]{:S(2)}) collective-permute-start(bf16[2,2,400,384]{3,2,1,0:T(8,128)(2,1)} %get-tuple-element.64), channel_id=1, source_target_pairs={{0,32},{1,9},{2,34},{3,11},{4,36},{5,13},{6,38},{7,15},{8,40},{9,1... | collective-permute-start | bytes 3686408 | tf_op jit(solution)/shard_map/ppermute | solution.py:274
  31.8 1.4 %collective-permute-start.12 = (bf16[2,2,400,384]{3,2,1,0:T(8,128)(2,1)}, bf16[2,2,400,384]{3,2,1,0:T(8,128)(2,1)S(1)}, u32[]{:S(2)}, u32[]{:S(2)}) collective-permute-start(bf16[2,2,400,384]{3,2,1,0:T(8,128)(2,1)} %get-tuple-element.66), channel_id=1, source_target_pairs={{0,96},{1,25},{2,98},{3,27},{4,100},{5,29},{6,102},{7,31},{8,104},... | collective-permute-start | bytes 3686408 | tf_op jit(solution)/shard_map/ppermute | solution.py:274
  33.2 2.1 %collective-permute-done.5.rest_1_ = bf16[4,400,384]{2,1,0:T(8,128)(2,1)S(1)} collective-permute-done((bf16[4,400,384]{2,1,0:T(8,128)(2,1)S(1)}, bf16[4,400,384]{2,1,0:T(8,128)(2,1)S(1)}, u32[]{:S(2)}, u32[]{:S(2)}) %collective-permute-start.5) | collective-permute-done | bytes 1228832 | tf_op jit(solution)/shard_map/ppermute | solution.py:274
  35.3 6.6 %collective-permute-done.6.rest_2_ = bf16[4,400,384]{2,1,0:T(8,128)(2,1)S(1)} collective-permute-done((bf16[4,400,384]{2,1,0:T(8,128)(2,1)S(1)}, bf16[4,400,384]{2,1,0:T(8,128)(2,1)S(1)}, u32[]{:S(2)}, u32[]{:S(2)}) %collective-permute-start.6) | collective-permute-done | bytes 1228832 | tf_op jit(solution)/shard_map/ppermute | solution.py:274
  42.0 0.1 pad_maximum_fusion.2
  42.1 1.2 %collective-permute-start.8 = (bf16[2,2,400,384]{3,2,1,0:T(8,128)(2,1)}, bf16[2,2,400,384]{3,2,1,0:T(8,128)(2,1)S(1)}, u32[]{:S(2)}, u32[]{:S(2)}) collective-permute-start(bf16[2,2,400,384]{3,2,1,0:T(8,128)(2,1)} %get-tuple-element.60), channel_id=1, source_target_pairs={{0,32},{1,9},{2,34},{3,11},{4,36},{5,13},{6,38},{7,15},{8,40},{9,1... | collective-permute-start | bytes 3686408 | tf_op jit(solution)/shard_map/ppermute | solution.py:274
  43.3 5.8 %collective-permute-done.10 = bf16[2,2,400,384]{3,2,1,0:T(8,128)(2,1)S(1)} collective-permute-done((bf16[2,2,400,384]{3,2,1,0:T(8,128)(2,1)}, bf16[2,2,400,384]{3,2,1,0:T(8,128)(2,1)S(1)}, u32[]{:S(2)}, u32[]{:S(2)}) %collective-permute-start.10) | collective-permute-done | bytes 1228832 | tf_op jit(solution)/shard_map/ppermute | solution.py:274
  49.1 0.3 add_convert_fusion.1
  49.4 2.1 %collective-permute-start.11 = (bf16[2,2,400,384]{3,2,1,0:T(8,128)(2,1)S(1)}, bf16[2,2,400,384]{3,2,1,0:T(8,128)(2,1)S(1)}, u32[]{:S(2)}, u32[]{:S(2)}) collective-permute-start(bf16[2,2,400,384]{3,2,1,0:T(8,128)(2,1)S(1)} %add_convert_fusion.1), channel_id=1, source_target_pairs={{0,32},{1,9},{2,34},{3,11},{4,36},{5,13},{6,38},{7,15},{8,40},{9,1... | collective-permute-start | bytes 3686408 | tf_op jit(solution)/shard_map/ppermute | solution.py:274
  51.5 0.3 add_convert_fusion
  51.9 1.3 %collective-permute-start.13 = (bf16[2,2,400,384]{3,2,1,0:T(8,128)(2,1)S(1)}, bf16[2,2,400,384]{3,2,1,0:T(8,128)(2,1)S(1)}, u32[]{:S(2)}, u32[]{:S(2)}) collective-permute-start(bf16[2,2,400,384]{3,2,1,0:T(8,128)(2,1)S(1)} %add_convert_fusion), channel_id=1, source_target_pairs={{0,96},{1,25},{2,98},{3,27},{4,100},{5,29},{6,102},{7,31},{8,104},... | collective-permute-start | bytes 3686408 | tf_op jit(solution)/shard_map/ppermute | solution.py:274
  53.1 2.6 %collective-permute-start.18 = (bf16[2,400,384]{2,1,0:T(8,128)(2,1)S(1)}, bf16[2,400,384]{2,1,0:T(8,128)(2,1)S(1)}, u32[]{:S(2)}, u32[]{:S(2)}) collective-permute-start(bf16[2,400,384]{2,1,0:T(8,128)(2,1)S(1)} %pad_maximum_fusion.2), channel_id=1, source_target_pairs={{0,6},{1,3},{2,0},{3,5},{4,2},{5,7},{6,4},{7,1},{8,14},{9,11},{10,... | collective-permute-start | bytes 1843208 | tf_op jit(solution)/shard_map/ppermute | solution.py:274
  55.8 0.6 fusion.3
  56.4 5.9 %collective-permute-done.8 = bf16[2,2,400,384]{3,2,1,0:T(8,128)(2,1)S(1)} collective-permute-done((bf16[2,2,400,384]{3,2,1,0:T(8,128)(2,1)}, bf16[2,2,400,384]{3,2,1,0:T(8,128)(2,1)S(1)}, u32[]{:S(2)}, u32[]{:S(2)}) %collective-permute-start.8) | collective-permute-done | bytes 1228832 | tf_op jit(solution)/shard_map/ppermute | solution.py:274
  62.3 3.6 %collective-permute-done.9 = bf16[2,2,400,384]{3,2,1,0:T(8,128)(2,1)S(1)} collective-permute-done((bf16[2,2,400,384]{3,2,1,0:T(8,128)(2,1)S(1)}, bf16[2,2,400,384]{3,2,1,0:T(8,128)(2,1)S(1)}, u32[]{:S(2)}, u32[]{:S(2)}) %collective-permute-start.9) | collective-permute-done | bytes 1228832 | tf_op jit(solution)/shard_map/ppermute | solution.py:274
  65.8 0.1 slice.73
  65.9 2.5 %collective-permute-start.14 = (bf16[2,400,384]{2,1,0:T(8,128)(2,1)S(1)}, bf16[2,400,384]{2,1,0:T(8,128)(2,1)S(1)}, u32[]{:S(2)}, u32[]{:S(2)}) collective-permute-start(bf16[2,400,384]{2,1,0:T(8,128)(2,1)S(1)} %slice.73), channel_id=1, source_target_pairs={{0,24},{1,97},{2,26},{3,99},{4,28},{5,101},{6,30},{7,103},{8,0},{9... | collective-permute-start | bytes 1843208 | tf_op jit(solution)/shard_map/ppermute | solution.py:274
  68.4 0.1 slice.74
  68.5 0.1 collective-permute-start.15
  68.6 0.1 collective-permute-start.16
  68.7 10.7 %collective-permute-done.11 = bf16[2,2,400,384]{3,2,1,0:T(8,128)(2,1)S(1)} collective-permute-done((bf16[2,2,400,384]{3,2,1,0:T(8,128)(2,1)S(1)}, bf16[2,2,400,384]{3,2,1,0:T(8,128)(2,1)S(1)}, u32[]{:S(2)}, u32[]{:S(2)}) %collective-permute-start.11) | collective-permute-done | bytes 1228832 | tf_op jit(solution)/shard_map/ppermute | solution.py:274
  79.4 6.2 %collective-permute-done.13 = bf16[2,2,400,384]{3,2,1,0:T(8,128)(2,1)S(1)} collective-permute-done((bf16[2,2,400,384]{3,2,1,0:T(8,128)(2,1)S(1)}, bf16[2,2,400,384]{3,2,1,0:T(8,128)(2,1)S(1)}, u32[]{:S(2)}, u32[]{:S(2)}) %collective-permute-start.13) | collective-permute-done | bytes 1228832 | tf_op jit(solution)/shard_map/ppermute | solution.py:274
  85.6 0.2 add_convert_fusion.2
  85.8 0.0 copy-start.2
  85.8 0.9 fusion.7
  86.7 1.4 %collective-permute-start.20 = (bf16[2,400,384]{2,1,0:T(8,128)(2,1)S(1)}, bf16[2,400,384]{2,1,0:T(8,128)(2,1)S(1)}, u32[]{:S(2)}, u32[]{:S(2)}) collective-permute-start(bf16[2,400,384]{2,1,0:T(8,128)(2,1)S(1)} %get-tuple-element.82), channel_id=1, source_target_pairs={{0,8},{1,33},{2,10},{3,35},{4,12},{5,37},{6,14},{7,39},{8,16},{9,4... | collective-permute-start | bytes 1843208 | tf_op jit(solution)/shard_map/ppermute | solution.py:274
  88.1 1.9 %collective-permute-start.21 = (bf16[2,400,384]{2,1,0:T(8,128)(2,1)S(1)}, bf16[2,400,384]{2,1,0:T(8,128)(2,1)S(1)}, u32[]{:S(2)}, u32[]{:S(2)}) collective-permute-start(bf16[2,400,384]{2,1,0:T(8,128)(2,1)S(1)} %get-tuple-element.84), channel_id=1, source_target_pairs={{0,24},{1,97},{2,26},{3,99},{4,28},{5,101},{6,30},{7,103},{8,0},{9... | collective-permute-start | bytes 1843208 | tf_op jit(solution)/shard_map/ppermute | solution.py:274
  90.0 1.4 %collective-permute-start.22 = (bf16[2,400,384]{2,1,0:T(8,128)(2,1)S(1)}, bf16[2,400,384]{2,1,0:T(8,128)(2,1)S(1)}, u32[]{:S(2)}, u32[]{:S(2)}) collective-permute-start(bf16[2,400,384]{2,1,0:T(8,128)(2,1)S(1)} %get-tuple-element.83), channel_id=1, source_target_pairs={{0,16},{1,65},{2,18},{3,67},{4,20},{5,69},{6,22},{7,71},{8,24},{9,... | collective-permute-start | bytes 1843208 | tf_op jit(solution)/shard_map/ppermute | solution.py:274
  91.4 3.2 %collective-permute-start.23 = (bf16[2,400,384]{2,1,0:T(8,128)(2,1)S(1)}, bf16[2,400,384]{2,1,0:T(8,128)(2,1)S(1)}, u32[]{:S(2)}, u32[]{:S(2)}) collective-permute-start(bf16[2,400,384]{2,1,0:T(8,128)(2,1)S(1)} %get-tuple-element.93), channel_id=1, source_target_pairs={{0,6},{1,3},{2,0},{3,5},{4,2},{5,7},{6,4},{7,1},{8,14},{9,11},{10,... | collective-permute-start | bytes 1843208 | tf_op jit(solution)/shard_map/ppermute | solution.py:274
  94.7 9.3 %shard_map.60 = bf16[8,2,400,400]{3,2,1,0:T(8,128)(2,1)} custom-call(s32[8]{0:T(128)S(1)} %copy-done.2, bf16[8,2,400,384]{3,2,1,0:T(8,128)(2,1)S(1)} %get-tuple-element.86.left_ref, bf16[4,400,384]{2,1,0:T(8,128)(2,1)S(1)} %pad_maximum_fusion.rest_0_, bf16[4,400,384]{2,1,0:T(8,128)(2,1)S(1)} %collective-permute-done.5.rest_1_, ...), custom_call_target="tpu_custom_call" | custom-call | flops 1966080000 | bytes 15000000 | tf_op jit(solution)/shard_map/pallas_call | solution.py:230
  104.0 0.0 copy-start.1
  104.0 0.2 collective-permute-done.21.rest_1_
  104.3 1.1 %collective-permute-done.22.rest_2_ = bf16[2,400,384]{2,1,0:T(8,128)(2,1)S(1)} collective-permute-done((bf16[2,400,384]{2,1,0:T(8,128)(2,1)S(1)}, bf16[2,400,384]{2,1,0:T(8,128)(2,1)S(1)}, u32[]{:S(2)}, u32[]{:S(2)}) %collective-permute-start.22) | collective-permute-done | bytes 614432 | tf_op jit(solution)/shard_map/ppermute | solution.py:274
  105.4 3.4 %collective-permute-done.24 = bf16[2,400,384]{2,1,0:T(8,128)(2,1)S(1)} collective-permute-done((bf16[2,400,384]{2,1,0:T(8,128)(2,1)S(1)}, bf16[2,400,384]{2,1,0:T(8,128)(2,1)S(1)}, u32[]{:S(2)}, u32[]{:S(2)}) %collective-permute-start.24) | collective-permute-done | bytes 614432 | tf_op jit(solution)/shard_map/ppermute | solution.py:274
  108.8 0.3 convert_add_fusion.sum_ref
  109.1 2.1 %shard_map.61 = f32[2,400,400]{2,1,0:T(8,128)} custom-call(bf16[400,384]{1,0:T(8,128)(2,1)S(1)} %bitcast.35, f32[2,400,384]{2,1,0:T(8,128)S(1)} %convert_add_fusion.sum_ref, bf16[2,400,384]{2,1,0:T(8,128)(2,1)S(1)} %collective-permute-done.20.rest_0_, bf16[2,400,384]{2,1,0:T(8,128)(2,1)S(1)} %collective-permute-done.21.rest_1_, ...), custom_call_target="tpu_custom_call" | custom-call | tf_op jit(solution)/shard_map/pallas_call | solution.py:261
  (29 shorter events, 0.1 us)
Async XLA Ops:
  0.6 9.9 %collective-permute-start.2 = (bf16[400,384]{1,0:T(8,128)(2,1)}, bf16[400,384]{1,0:T(8,128)(2,1)S(1)}, u32[]{:S(2)}, u32[]{:S(2)}) collective-permute-start(bf16[400,384]{1,0:T(8,128)(2,1)} %bitcast.27), channel_id=1, source_target_pairs={{0,32},{1,9},{2,34},{3,11},{4,36},{5,13},{6,38},{7,15},{8,40},{9,1... | collective-permute-start | bytes 921608 | tf_op jit(solution)/shard_map/ppermute | solution.py:274
  2.3 11.1 %collective-permute-start.1 = (bf16[400,384]{1,0:T(8,128)(2,1)}, bf16[400,384]{1,0:T(8,128)(2,1)S(1)}, u32[]{:S(2)}, u32[]{:S(2)}) collective-permute-start(bf16[400,384]{1,0:T(8,128)(2,1)} %bitcast.28), channel_id=1, source_target_pairs={{0,64},{1,17},{2,66},{3,19},{4,68},{5,21},{6,70},{7,23},{8,72},{9,... | collective-permute-start | bytes 921608 | tf_op jit(solution)/shard_map/ppermute | solution.py:274
  5.0 8.3 %collective-permute-start = (bf16[400,384]{1,0:T(8,128)(2,1)}, bf16[400,384]{1,0:T(8,128)(2,1)S(1)}, u32[]{:S(2)}, u32[]{:S(2)}) collective-permute-start(bf16[400,384]{1,0:T(8,128)(2,1)} %bitcast.29), channel_id=1, source_target_pairs={{0,96},{1,25},{2,98},{3,27},{4,100},{5,29},{6,102},{7,31},{8,104},... | collective-permute-start | bytes 921608 | tf_op jit(solution)/shard_map/ppermute | solution.py:274
  6.4 11.3 %collective-permute-start.3 = (bf16[400,384]{1,0:T(8,128)(2,1)}, bf16[400,384]{1,0:T(8,128)(2,1)S(1)}, u32[]{:S(2)}, u32[]{:S(2)}) collective-permute-start(bf16[400,384]{1,0:T(8,128)(2,1)} %bitcast.30), channel_id=1, source_target_pairs={{0,2},{1,7},{2,4},{3,1},{4,6},{5,3},{6,0},{7,5},{8,10},{9,15},{10,... | collective-permute-start | bytes 921608 | tf_op jit(solution)/shard_map/ppermute | solution.py:274
  8.4 9.4 %collective-permute-start.4 = (bf16[400,384]{1,0:T(8,128)(2,1)}, bf16[400,384]{1,0:T(8,128)(2,1)S(1)}, u32[]{:S(2)}, u32[]{:S(2)}) collective-permute-start(bf16[400,384]{1,0:T(8,128)(2,1)} %bitcast.31), channel_id=1, source_target_pairs={{0,6},{1,3},{2,0},{3,5},{4,2},{5,7},{6,4},{7,1},{8,14},{9,11},{10,... | collective-permute-start | bytes 921608 | tf_op jit(solution)/shard_map/ppermute | solution.py:274
  13.3 6.9 %copy-start = (bf16[1,384,400]{1,2,0:T(8,128)(2,1)S(1)}, bf16[1,384,400]{1,2,0:T(8,128)(2,1)}, u32[]{:S(2)}) copy-start(bf16[1,384,400]{1,2,0:T(8,128)(2,1)} %param.4) | copy-start | bytes 921604
  17.7 17.6 %collective-permute-start.5 = (bf16[4,400,384]{2,1,0:T(8,128)(2,1)S(1)}, bf16[4,400,384]{2,1,0:T(8,128)(2,1)S(1)}, u32[]{:S(2)}, u32[]{:S(2)}) collective-permute-start(bf16[4,400,384]{2,1,0:T(8,128)(2,1)S(1)} %pad_maximum_fusion.rest_0_), channel_id=1, source_target_pairs={{0,24},{1,97},{2,26},{3,99},{4,28},{5,101},{6,30},{7,103},{8,0},{9... | collective-permute-start | bytes 3686408 | tf_op jit(solution)/shard_map/ppermute | solution.py:274
  20.2 21.7 %collective-permute-start.6 = (bf16[4,400,384]{2,1,0:T(8,128)(2,1)S(1)}, bf16[4,400,384]{2,1,0:T(8,128)(2,1)S(1)}, u32[]{:S(2)}, u32[]{:S(2)}) collective-permute-start(bf16[4,400,384]{2,1,0:T(8,128)(2,1)S(1)} %pad_maximum_fusion.rest_0_), channel_id=1, source_target_pairs={{0,8},{1,33},{2,10},{3,35},{4,12},{5,37},{6,14},{7,39},{8,16},{9,4... | collective-permute-start | bytes 3686408 | tf_op jit(solution)/shard_map/ppermute | solution.py:274
  29.8 19.4 %copy-start.5 = (bf16[2,2,400,384]{3,2,1,0:T(8,128)(2,1)S(1)}, bf16[2,2,400,384]{3,2,1,0:T(8,128)(2,1)}, u32[]{:S(2)}) copy-start(bf16[2,2,400,384]{3,2,1,0:T(8,128)(2,1)} %get-tuple-element.61) | copy-start | bytes 3686404
  29.8 3.4 %collective-permute-start.17 = (bf16[3,400,384]{2,1,0:T(8,128)(2,1)S(1)}, bf16[3,400,384]{2,1,0:T(8,128)(2,1)S(1)}, u32[]{:S(2)}, u32[]{:S(2)}) collective-permute-start(bf16[3,400,384]{2,1,0:T(8,128)(2,1)S(1)} %pad_maximum_fusion.1.rest_5_), channel_id=1, source_target_pairs={{0,1},{1,0},{2,3},{3,2},{4,5},{5,4},{6,7},{7,6},{8,9},{9,8},{10,11... | collective-permute-start | bytes 2764808 | tf_op jit(solution)/shard_map/ppermute | solution.py:274
  29.9 19.2 %collective-permute-start.10 = (bf16[2,2,400,384]{3,2,1,0:T(8,128)(2,1)}, bf16[2,2,400,384]{3,2,1,0:T(8,128)(2,1)S(1)}, u32[]{:S(2)}, u32[]{:S(2)}) collective-permute-start(bf16[2,2,400,384]{3,2,1,0:T(8,128)(2,1)} %get-tuple-element.64), channel_id=1, source_target_pairs={{0,32},{1,9},{2,34},{3,11},{4,36},{5,13},{6,38},{7,15},{8,40},{9,1... | collective-permute-start | bytes 3686408 | tf_op jit(solution)/shard_map/ppermute | solution.py:274
  31.8 17.7 %collective-permute-start.12 = (bf16[2,2,400,384]{3,2,1,0:T(8,128)(2,1)}, bf16[2,2,400,384]{3,2,1,0:T(8,128)(2,1)S(1)}, u32[]{:S(2)}, u32[]{:S(2)}) collective-permute-start(bf16[2,2,400,384]{3,2,1,0:T(8,128)(2,1)} %get-tuple-element.66), channel_id=1, source_target_pairs={{0,96},{1,25},{2,98},{3,27},{4,100},{5,29},{6,102},{7,31},{8,104},... | collective-permute-start | bytes 3686408 | tf_op jit(solution)/shard_map/ppermute | solution.py:274
  33.2 18.7 %collective-permute-start.19 = (bf16[2,2,400,384]{3,2,1,0:T(8,128)(2,1)}, bf16[2,2,400,384]{3,2,1,0:T(8,128)(2,1)S(1)}, u32[]{:S(2)}, u32[]{:S(2)}) collective-permute-start(bf16[2,2,400,384]{3,2,1,0:T(8,128)(2,1)} %get-tuple-element.74), channel_id=1, source_target_pairs={{0,1},{1,0},{2,3},{3,2},{4,5},{5,4},{6,7},{7,6},{8,9},{9,8},{10,11... | collective-permute-start | bytes 3686408 | tf_op jit(solution)/shard_map/ppermute | solution.py:274
  41.9 11.2 %collective-permute-start.7 = (bf16[2,2,400,384]{3,2,1,0:T(8,128)(2,1)}, bf16[2,2,400,384]{3,2,1,0:T(8,128)(2,1)S(1)}, u32[]{:S(2)}, u32[]{:S(2)}) collective-permute-start(bf16[2,2,400,384]{3,2,1,0:T(8,128)(2,1)} %get-tuple-element.59), channel_id=1, source_target_pairs={{0,1},{1,0},{2,3},{3,2},{4,5},{5,4},{6,7},{7,6},{8,9},{9,8},{10,11... | collective-permute-start | bytes 3686408 | tf_op jit(solution)/shard_map/ppermute | solution.py:274
  42.1 20.2 %collective-permute-start.8 = (bf16[2,2,400,384]{3,2,1,0:T(8,128)(2,1)}, bf16[2,2,400,384]{3,2,1,0:T(8,128)(2,1)S(1)}, u32[]{:S(2)}, u32[]{:S(2)}) collective-permute-start(bf16[2,2,400,384]{3,2,1,0:T(8,128)(2,1)} %get-tuple-element.60), channel_id=1, source_target_pairs={{0,32},{1,9},{2,34},{3,11},{4,36},{5,13},{6,38},{7,15},{8,40},{9,1... | collective-permute-start | bytes 3686408 | tf_op jit(solution)/shard_map/ppermute | solution.py:274
  49.1 16.7 %collective-permute-start.9 = (bf16[2,2,400,384]{3,2,1,0:T(8,128)(2,1)S(1)}, bf16[2,2,400,384]{3,2,1,0:T(8,128)(2,1)S(1)}, u32[]{:S(2)}, u32[]{:S(2)}) collective-permute-start(bf16[2,2,400,384]{3,2,1,0:T(8,128)(2,1)S(1)} %copy-done.5), channel_id=1, source_target_pairs={{0,96},{1,25},{2,98},{3,27},{4,100},{5,29},{6,102},{7,31},{8,104},... | collective-permute-start | bytes 3686408 | tf_op jit(solution)/shard_map/ppermute | solution.py:274
  49.4 29.9 %collective-permute-start.11 = (bf16[2,2,400,384]{3,2,1,0:T(8,128)(2,1)S(1)}, bf16[2,2,400,384]{3,2,1,0:T(8,128)(2,1)S(1)}, u32[]{:S(2)}, u32[]{:S(2)}) collective-permute-start(bf16[2,2,400,384]{3,2,1,0:T(8,128)(2,1)S(1)} %add_convert_fusion.1), channel_id=1, source_target_pairs={{0,32},{1,9},{2,34},{3,11},{4,36},{5,13},{6,38},{7,15},{8,40},{9,1... | collective-permute-start | bytes 3686408 | tf_op jit(solution)/shard_map/ppermute | solution.py:274
  51.5 4.2 %copy-start.3 = (bf16[4,2,400,384]{3,2,1,0:T(8,128)(2,1)S(1)}, bf16[4,2,400,384]{3,2,1,0:T(8,128)(2,1)}, u32[]{:S(2)}) copy-start(bf16[4,2,400,384]{3,2,1,0:T(8,128)(2,1)} %get-tuple-element.58) | copy-start | bytes 7372804
  51.9 33.7 %collective-permute-start.13 = (bf16[2,2,400,384]{3,2,1,0:T(8,128)(2,1)S(1)}, bf16[2,2,400,384]{3,2,1,0:T(8,128)(2,1)S(1)}, u32[]{:S(2)}, u32[]{:S(2)}) collective-permute-start(bf16[2,2,400,384]{3,2,1,0:T(8,128)(2,1)S(1)} %add_convert_fusion), channel_id=1, source_target_pairs={{0,96},{1,25},{2,98},{3,27},{4,100},{5,29},{6,102},{7,31},{8,104},... | collective-permute-start | bytes 3686408 | tf_op jit(solution)/shard_map/ppermute | solution.py:274
  53.1 15.4 %collective-permute-start.18 = (bf16[2,400,384]{2,1,0:T(8,128)(2,1)S(1)}, bf16[2,400,384]{2,1,0:T(8,128)(2,1)S(1)}, u32[]{:S(2)}, u32[]{:S(2)}) collective-permute-start(bf16[2,400,384]{2,1,0:T(8,128)(2,1)S(1)} %pad_maximum_fusion.2), channel_id=1, source_target_pairs={{0,6},{1,3},{2,0},{3,5},{4,2},{5,7},{6,4},{7,1},{8,14},{9,11},{10,... | collective-permute-start | bytes 1843208 | tf_op jit(solution)/shard_map/ppermute | solution.py:274
  65.9 19.7 %collective-permute-start.14 = (bf16[2,400,384]{2,1,0:T(8,128)(2,1)S(1)}, bf16[2,400,384]{2,1,0:T(8,128)(2,1)S(1)}, u32[]{:S(2)}, u32[]{:S(2)}) collective-permute-start(bf16[2,400,384]{2,1,0:T(8,128)(2,1)S(1)} %slice.73), channel_id=1, source_target_pairs={{0,24},{1,97},{2,26},{3,99},{4,28},{5,101},{6,30},{7,103},{8,0},{9... | collective-permute-start | bytes 1843208 | tf_op jit(solution)/shard_map/ppermute | solution.py:274
  68.4 17.3 %copy-start.4 = (bf16[4,2,400,384]{3,2,1,0:T(8,128)(2,1)S(1)}, bf16[4,2,400,384]{3,2,1,0:T(8,128)(2,1)}, u32[]{:S(2)}) copy-start(bf16[4,2,400,384]{3,2,1,0:T(8,128)(2,1)} %get-tuple-element.52) | copy-start | bytes 7372804
  68.5 17.1 %collective-permute-start.15 = (bf16[2,400,384]{2,1,0:T(8,128)(2,1)S(1)}, bf16[2,400,384]{2,1,0:T(8,128)(2,1)S(1)}, u32[]{:S(2)}, u32[]{:S(2)}) collective-permute-start(bf16[2,400,384]{2,1,0:T(8,128)(2,1)S(1)} %slice.74), channel_id=1, source_target_pairs={{0,8},{1,33},{2,10},{3,35},{4,12},{5,37},{6,14},{7,39},{8,16},{9,4... | collective-permute-start | bytes 1843208 | tf_op jit(solution)/shard_map/ppermute | solution.py:274
  68.6 17.0 %collective-permute-start.16 = (bf16[2,400,384]{2,1,0:T(8,128)(2,1)S(1)}, bf16[2,400,384]{2,1,0:T(8,128)(2,1)S(1)}, u32[]{:S(2)}, u32[]{:S(2)}) collective-permute-start(bf16[2,400,384]{2,1,0:T(8,128)(2,1)S(1)} %get-tuple-element.69), channel_id=1, source_target_pairs={{0,2},{1,7},{2,4},{3,1},{4,6},{5,3},{6,0},{7,5},{8,10},{9,15},{10,... | collective-permute-start | bytes 1843208 | tf_op jit(solution)/shard_map/ppermute | solution.py:274
  85.8 8.9 %copy-start.2 = (s32[8]{0:T(128)S(1)}, s32[8]{0:T(128)}, u32[]{:S(2)}) copy-start(s32[8]{0:T(128)} %partner_ref) | copy-start | bytes 100
  86.7 17.3 %collective-permute-start.20 = (bf16[2,400,384]{2,1,0:T(8,128)(2,1)S(1)}, bf16[2,400,384]{2,1,0:T(8,128)(2,1)S(1)}, u32[]{:S(2)}, u32[]{:S(2)}) collective-permute-start(bf16[2,400,384]{2,1,0:T(8,128)(2,1)S(1)} %get-tuple-element.82), channel_id=1, source_target_pairs={{0,8},{1,33},{2,10},{3,35},{4,12},{5,37},{6,14},{7,39},{8,16},{9,4... | collective-permute-start | bytes 1843208 | tf_op jit(solution)/shard_map/ppermute | solution.py:274
  88.1 16.2 %collective-permute-start.21 = (bf16[2,400,384]{2,1,0:T(8,128)(2,1)S(1)}, bf16[2,400,384]{2,1,0:T(8,128)(2,1)S(1)}, u32[]{:S(2)}, u32[]{:S(2)}) collective-permute-start(bf16[2,400,384]{2,1,0:T(8,128)(2,1)S(1)} %get-tuple-element.84), channel_id=1, source_target_pairs={{0,24},{1,97},{2,26},{3,99},{4,28},{5,101},{6,30},{7,103},{8,0},{9... | collective-permute-start | bytes 1843208 | tf_op jit(solution)/shard_map/ppermute | solution.py:274
  90.0 15.4 %collective-permute-start.22 = (bf16[2,400,384]{2,1,0:T(8,128)(2,1)S(1)}, bf16[2,400,384]{2,1,0:T(8,128)(2,1)S(1)}, u32[]{:S(2)}, u32[]{:S(2)}) collective-permute-start(bf16[2,400,384]{2,1,0:T(8,128)(2,1)S(1)} %get-tuple-element.83), channel_id=1, source_target_pairs={{0,16},{1,65},{2,18},{3,67},{4,20},{5,69},{6,22},{7,71},{8,24},{9,... | collective-permute-start | bytes 1843208 | tf_op jit(solution)/shard_map/ppermute | solution.py:274
  91.4 17.4 %collective-permute-start.24 = (bf16[2,400,384]{2,1,0:T(8,128)(2,1)S(1)}, bf16[2,400,384]{2,1,0:T(8,128)(2,1)S(1)}, u32[]{:S(2)}, u32[]{:S(2)}) collective-permute-start(bf16[2,400,384]{2,1,0:T(8,128)(2,1)S(1)} %add_convert_fusion.2), channel_id=1, source_target_pairs={{0,2},{1,7},{2,4},{3,1},{4,6},{5,3},{6,0},{7,5},{8,10},{9,15},{10,... | collective-permute-start | bytes 1843208 | tf_op jit(solution)/shard_map/ppermute | solution.py:274
  91.4 17.4 %collective-permute-start.23 = (bf16[2,400,384]{2,1,0:T(8,128)(2,1)S(1)}, bf16[2,400,384]{2,1,0:T(8,128)(2,1)S(1)}, u32[]{:S(2)}, u32[]{:S(2)}) collective-permute-start(bf16[2,400,384]{2,1,0:T(8,128)(2,1)S(1)} %get-tuple-element.93), channel_id=1, source_target_pairs={{0,6},{1,3},{2,0},{3,5},{4,2},{5,7},{6,4},{7,1},{8,14},{9,11},{10,... | collective-permute-start | bytes 1843208 | tf_op jit(solution)/shard_map/ppermute | solution.py:274
  104.0 5.1 %copy-start.1 = (bf16[1,384,400]{1,2,0:T(8,128)(2,1)S(1)}, bf16[1,384,400]{1,2,0:T(8,128)(2,1)}, u32[]{:S(2)}) copy-start(bf16[1,384,400]{1,2,0:T(8,128)(2,1)} %param.4) | copy-start | bytes 921604

commit v8 on v7

--- a/solution.py
+++ b/solution.py
@@ -309,7 +309,7 @@
     moved = [first(own, -1), first(own, 2), first(own, 1)]
     ring1, ring2 = turn(own, 1), turn(own, -1)
     kept = jnp.stack([own] + moved)
-    kept, ring1, ring2 = barrier((kept, ring1, ring2))
+    kept = barrier(kept)
     near, far = second(kept, -1), second(kept, 1)
     left, (up, up_end, down, down_end, pass_up, pass_down, here), (z_near, z_far, z_mine) = left_products(
         own, coupling, partner, after(counts, kept)
@@ -330,9 +330,8 @@
     near, far, w3, end_up, end_down = barrier((near, far, w[3], end_up, end_down))
     low, high = second(near[:2], -1), second(far[2:], 1)
     opposite = turn(w3, 1)
-    last_up, last_down, low, high, opposite, across, ring_other, w = barrier(
-        (last_up, last_down, low, high, opposite, across, ring_other, w)
-    )
+    low, high, opposite, across, ring_other, w = barrier((low, high, opposite, across, ring_other, w))
+    z_last, back = turn(rounded(w[1], opposite), 1), turn(w[2], -1)
 
     v = [
         rounded(here[0], end_down[0], last_up[0]),
@@ -340,13 +339,10 @@
         rounded(here[2], end_up[0], last_down[0]),
         rounded(here[3], end_up[1], last_down[1]),
     ]
-    z_pass = rounded(w[1], opposite)
-    v, z_pass, z_back = barrier((v, z_pass, w[2]))
     ends = [second(v[1], 1), second(v[3], -1), second(v[2], 2)]
-    z_last, back = turn(z_pass, 1), turn(z_back, -1)
 
     sources = [kept, near, far, low, high, ring_mine, ring_other, across]
-    pair_blocks = pair_products(left, sources, after(partner, *v))
+    pair_blocks = pair_products(left, sources, after(partner, *v, z_last, back))
     pair_blocks, ends = barrier((pair_blocks, ends))
     partner_blocks = partner_products(own, added(v[0], w[0], back, z_last), ends)
     return (pair_blocks, partner_blocks[None])

time: 113 us -> 116 us (1.027)
  the two profiles are of different devices: /device:TPU:0 before, /device:TPU:1 now
where the time goes in v8:
time: 116 us
  waiting for transfers between devices  50.5 us (44%)
  starting transfers between devices  39.3 us (34%)
  Pallas kernels  20.8 us (18%)
  other arithmetic  4.06 us (3%)
    ppermute x25, waiting for transfers between devices, permuted(): return lax.ppermute(value, ('sx', 'sy'), pairs)  50.5 us
    ppermute x25, starting transfers between devices, permuted(): return lax.ppermute(value, ('sx', 'sy'), pairs)  39.3 us
    pallas_call x1, Pallas kernels, left_products(): pl.pallas_call(left_kernel, in_specs=[pl.BlockSpec(memory_space=pltpu.HBM...  9.41 us
    pallas_call x1, Pallas kernels, pair_products(): pl.pallas_call(pair_kernel, in_specs=[smem, pl.BlockSpec(memory_space=plt...  9.34 us
  transfers between devices with their start and end apart: 25, of which 10 were waited for; matrix products, arithmetic and copies ran while one was open for 4% of the time, Pallas kernels for 16%

profile of v8, /device:TPU:1, one launch (start us, length us, event | category | flops | bytes accessed | tf_op | source)
XLA Modules:
  0.0 115.7 jit_solution(7880334086950635915)
XLA Ops:
  0.6 3.6 %collective-permute-start = (bf16[400,384]{1,0:T(8,128)(2,1)}, bf16[400,384]{1,0:T(8,128)(2,1)S(1)}, u32[]{:S(2)}, u32[]{:S(2)}) collective-permute-start(bf16[400,384]{1,0:T(8,128)(2,1)} %bitcast.28), channel_id=1, source_target_pairs={{0,96},{1,25},{2,98},{3,27},{4,100},{5,29},{6,102},{7,31},{8,104},... | collective-permute-start | bytes 921608 | tf_op jit(solution)/shard_map/ppermute | solution.py:274
  4.3 0.3 collective-permute-start.1
  4.6 0.7 collective-permute-start.2
  5.3 1.6 %collective-permute-start.15 = (bf16[400,384]{1,0:T(8,128)(2,1)}, bf16[400,384]{1,0:T(8,128)(2,1)S(1)}, u32[]{:S(2)}, u32[]{:S(2)}) collective-permute-start(bf16[400,384]{1,0:T(8,128)(2,1)} %bitcast.31), channel_id=1, source_target_pairs={{0,6},{1,3},{2,0},{3,5},{4,2},{5,7},{6,4},{7,1},{8,14},{9,11},{10,... | collective-permute-start | bytes 921608 | tf_op jit(solution)/shard_map/ppermute | solution.py:274
  6.9 2.1 %collective-permute-start.16 = (bf16[400,384]{1,0:T(8,128)(2,1)}, bf16[400,384]{1,0:T(8,128)(2,1)S(1)}, u32[]{:S(2)}, u32[]{:S(2)}) collective-permute-start(bf16[400,384]{1,0:T(8,128)(2,1)} %bitcast.32), channel_id=1, source_target_pairs={{0,2},{1,7},{2,4},{3,1},{4,6},{5,3},{6,0},{7,5},{8,10},{9,15},{10,... | collective-permute-start | bytes 921608 | tf_op jit(solution)/shard_map/ppermute | solution.py:274
  9.1 2.6 %collective-permute-done = bf16[400,384]{1,0:T(8,128)(2,1)S(1)} collective-permute-done((bf16[400,384]{1,0:T(8,128)(2,1)}, bf16[400,384]{1,0:T(8,128)(2,1)S(1)}, u32[]{:S(2)}, u32[]{:S(2)}) %collective-permute-start) | collective-permute-done | bytes 307232 | tf_op jit(solution)/shard_map/ppermute | solution.py:274
  11.7 0.4 collective-permute-done.1
  12.0 3.2 %collective-permute-done.2 = bf16[400,384]{1,0:T(8,128)(2,1)S(1)} collective-permute-done((bf16[400,384]{1,0:T(8,128)(2,1)}, bf16[400,384]{1,0:T(8,128)(2,1)S(1)}, u32[]{:S(2)}, u32[]{:S(2)}) %collective-permute-start.2) | collective-permute-done | bytes 307232 | tf_op jit(solution)/shard_map/ppermute | solution.py:274
  15.3 1.2 %pad_maximum_fusion.rest_0_ = bf16[4,400,384]{2,1,0:T(8,128)(2,1)S(1)} fusion(bf16[1,400,384]{2,1,0:T(8,128)(2,1)S(1)} %bitcast.43, bf16[1,400,384]{2,1,0:T(8,128)(2,1)S(1)} %bitcast.42, bf16[1,400,384]{2,1,0:T(8,128)(2,1)S(1)} %bitcast.41, bf16[1,400,384]{2,1,0:T(8,128)(2,1)} %bitcast.33), kind=kLoop, calls=%fused_computation.2 | loop fusion | flops 1843200 | bytes 2457600 | tf_op jit(solution)/shard_map/stack | solution.py:311
  16.5 2.5 %collective-permute-start.3 = (bf16[4,400,384]{2,1,0:T(8,128)(2,1)S(1)}, bf16[4,400,384]{2,1,0:T(8,128)(2,1)S(1)}, u32[]{:S(2)}, u32[]{:S(2)}) collective-permute-start(bf16[4,400,384]{2,1,0:T(8,128)(2,1)S(1)} %pad_maximum_fusion.rest_0_), channel_id=1, source_target_pairs={{0,24},{1,97},{2,26},{3,99},{4,28},{5,101},{6,30},{7,103},{8,0},{9... | collective-permute-start | bytes 3686408 | tf_op jit(solution)/shard_map/ppermute | solution.py:274
  19.0 0.0 collective-permute-start.4
  19.1 0.0 collective-permute-done.15
  19.1 0.0 collective-permute-done.16
  19.1 0.1 pad_maximum_fusion.1.rest_5_
  19.2 9.4 %shard_map.59 = (bf16[8,2,400,384]{3,2,1,0:T(8,128)(2,1)S(1)}, bf16[2,2,400,384]{3,2,1,0:T(8,128)(2,1)}, bf16[2,2,400,384]{3,2,1,0:T(8,128)(2,1)}, bf16[2,2,400,...) custom-call(s32[8]{0:T(128)} %partner_ref, ...), custom_call_target="tpu_custom_call" | custom-call | flops 1887436800 | bytes 25000000 | tf_op jit(solution)/shard_map/pallas_call | solution.py:152
  28.6 2.5 %collective-permute-start.17 = (bf16[3,400,384]{2,1,0:T(8,128)(2,1)S(1)}, bf16[3,400,384]{2,1,0:T(8,128)(2,1)S(1)}, u32[]{:S(2)}, u32[]{:S(2)}) collective-permute-start(bf16[3,400,384]{2,1,0:T(8,128)(2,1)S(1)} %pad_maximum_fusion.1.rest_5_), channel_id=1, source_target_pairs={{0,1},{1,0},{2,3},{3,2},{4,5},{5,4},{6,7},{7,6},{8,9},{9,8},{10,11... | collective-permute-start | bytes 2764808 | tf_op jit(solution)/shard_map/ppermute | solution.py:274
  31.1 2.7 %collective-permute-start.10 = (bf16[2,2,400,384]{3,2,1,0:T(8,128)(2,1)}, bf16[2,2,400,384]{3,2,1,0:T(8,128)(2,1)S(1)}, u32[]{:S(2)}, u32[]{:S(2)}) collective-permute-start(bf16[2,2,400,384]{3,2,1,0:T(8,128)(2,1)} %get-tuple-element.55), channel_id=1, source_target_pairs={{0,96},{1,25},{2,98},{3,27},{4,100},{5,29},{6,102},{7,31},{8,104},... | collective-permute-start | bytes 3686408 | tf_op jit(solution)/shard_map/ppermute | solution.py:274
  33.8 0.6 collective-permute-start.19
  34.4 2.0 %collective-permute-done.4.rest_2_ = bf16[4,400,384]{2,1,0:T(8,128)(2,1)S(1)} collective-permute-done((bf16[4,400,384]{2,1,0:T(8,128)(2,1)S(1)}, bf16[4,400,384]{2,1,0:T(8,128)(2,1)S(1)}, u32[]{:S(2)}, u32[]{:S(2)}) %collective-permute-start.4) | collective-permute-done | bytes 1228832 | tf_op jit(solution)/shard_map/ppermute | solution.py:274
  36.4 6.0 %collective-permute-start.5 = (bf16[2,2,400,384]{3,2,1,0:T(8,128)(2,1)}, bf16[2,2,400,384]{3,2,1,0:T(8,128)(2,1)S(1)}, u32[]{:S(2)}, u32[]{:S(2)}) collective-permute-start(bf16[2,2,400,384]{3,2,1,0:T(8,128)(2,1)} %get-tuple-element.47), channel_id=1, source_target_pairs={{0,1},{1,0},{2,3},{3,2},{4,5},{5,4},{6,7},{7,6},{8,9},{9,8},{10,11... | collective-permute-start | bytes 3686408 | tf_op jit(solution)/shard_map/ppermute | solution.py:274
  42.5 9.4 %collective-permute-done.8 = bf16[2,2,400,384]{3,2,1,0:T(8,128)(2,1)S(1)} collective-permute-done((bf16[2,2,400,384]{3,2,1,0:T(8,128)(2,1)}, bf16[2,2,400,384]{3,2,1,0:T(8,128)(2,1)S(1)}, u32[]{:S(2)}, u32[]{:S(2)}) %collective-permute-start.8) | collective-permute-done | bytes 1228832 | tf_op jit(solution)/shard_map/ppermute | solution.py:274
  51.9 0.1 pad_maximum_fusion.2
  52.0 0.3 add_convert_fusion.1
  52.3 1.7 %collective-permute-start.18 = (bf16[2,400,384]{2,1,0:T(8,128)(2,1)S(1)}, bf16[2,400,384]{2,1,0:T(8,128)(2,1)S(1)}, u32[]{:S(2)}, u32[]{:S(2)}) collective-permute-start(bf16[2,400,384]{2,1,0:T(8,128)(2,1)S(1)} %pad_maximum_fusion.2), channel_id=1, source_target_pairs={{0,6},{1,3},{2,0},{3,5},{4,2},{5,7},{6,4},{7,1},{8,14},{9,11},{10,... | collective-permute-start | bytes 1843208 | tf_op jit(solution)/shard_map/ppermute | solution.py:274
  54.0 0.3 add_convert_fusion
  54.4 1.5 %collective-permute-start.9 = (bf16[2,2,400,384]{3,2,1,0:T(8,128)(2,1)S(1)}, bf16[2,2,400,384]{3,2,1,0:T(8,128)(2,1)S(1)}, u32[]{:S(2)}, u32[]{:S(2)}) collective-permute-start(bf16[2,2,400,384]{3,2,1,0:T(8,128)(2,1)S(1)} %add_convert_fusion.1), channel_id=1, source_target_pairs={{0,32},{1,9},{2,34},{3,11},{4,36},{5,13},{6,38},{7,15},{8,40},{9,1... | collective-permute-start | bytes 3686408 | tf_op jit(solution)/shard_map/ppermute | solution.py:274
  55.9 1.2 %collective-permute-start.11 = (bf16[2,2,400,384]{3,2,1,0:T(8,128)(2,1)S(1)}, bf16[2,2,400,384]{3,2,1,0:T(8,128)(2,1)S(1)}, u32[]{:S(2)}, u32[]{:S(2)}) collective-permute-start(bf16[2,2,400,384]{3,2,1,0:T(8,128)(2,1)S(1)} %add_convert_fusion), channel_id=1, source_target_pairs={{0,96},{1,25},{2,98},{3,27},{4,100},{5,29},{6,102},{7,31},{8,104},... | collective-permute-start | bytes 3686408 | tf_op jit(solution)/shard_map/ppermute | solution.py:274
  57.1 0.6 fusion.7
  57.8 7.2 %collective-permute-done.6 = bf16[2,2,400,384]{3,2,1,0:T(8,128)(2,1)S(1)} collective-permute-done((bf16[2,2,400,384]{3,2,1,0:T(8,128)(2,1)}, bf16[2,2,400,384]{3,2,1,0:T(8,128)(2,1)S(1)}, u32[]{:S(2)}, u32[]{:S(2)}) %collective-permute-start.6) | collective-permute-done | bytes 1228832 | tf_op jit(solution)/shard_map/ppermute | solution.py:274
  65.0 2.9 %collective-permute-done.7 = bf16[2,2,400,384]{3,2,1,0:T(8,128)(2,1)S(1)} collective-permute-done((bf16[2,2,400,384]{3,2,1,0:T(8,128)(2,1)}, bf16[2,2,400,384]{3,2,1,0:T(8,128)(2,1)S(1)}, u32[]{:S(2)}, u32[]{:S(2)}) %collective-permute-start.7) | collective-permute-done | bytes 1228832 | tf_op jit(solution)/shard_map/ppermute | solution.py:274
  67.9 0.1 slice.83
  68.0 0.1 collective-permute-start.12
  68.1 0.1 slice.84
  68.2 1.5 %collective-permute-start.13 = (bf16[2,400,384]{2,1,0:T(8,128)(2,1)S(1)}, bf16[2,400,384]{2,1,0:T(8,128)(2,1)S(1)}, u32[]{:S(2)}, u32[]{:S(2)}) collective-permute-start(bf16[2,400,384]{2,1,0:T(8,128)(2,1)S(1)} %slice.84), channel_id=1, source_target_pairs={{0,8},{1,33},{2,10},{3,35},{4,12},{5,37},{6,14},{7,39},{8,16},{9,4... | collective-permute-start | bytes 1843208 | tf_op jit(solution)/shard_map/ppermute | solution.py:274
  69.7 3.8 %collective-permute-start.14 = (bf16[2,400,384]{2,1,0:T(8,128)(2,1)S(1)}, bf16[2,400,384]{2,1,0:T(8,128)(2,1)S(1)}, u32[]{:S(2)}, u32[]{:S(2)}) collective-permute-start(bf16[2,400,384]{2,1,0:T(8,128)(2,1)S(1)} %get-tuple-element.58), channel_id=1, source_target_pairs={{0,2},{1,7},{2,4},{3,1},{4,6},{5,3},{6,0},{7,5},{8,10},{9,15},{10,... | collective-permute-start | bytes 1843208 | tf_op jit(solution)/shard_map/ppermute | solution.py:274
  73.4 10.6 %collective-permute-done.12.rest_3_ = bf16[2,400,384]{2,1,0:T(8,128)(2,1)S(1)} collective-permute-done((bf16[2,400,384]{2,1,0:T(8,128)(2,1)S(1)}, bf16[2,400,384]{2,1,0:T(8,128)(2,1)S(1)}, u32[]{:S(2)}, u32[]{:S(2)}) %collective-permute-start.12) | collective-permute-done | bytes 614432 | tf_op jit(solution)/shard_map/ppermute | solution.py:274
  84.0 0.2 add_convert_fusion.2
  84.2 3.8 %collective-permute-start.20 = (bf16[2,400,384]{2,1,0:T(8,128)(2,1)S(1)}, bf16[2,400,384]{2,1,0:T(8,128)(2,1)S(1)}, u32[]{:S(2)}, u32[]{:S(2)}) collective-permute-start(bf16[2,400,384]{2,1,0:T(8,128)(2,1)S(1)} %add_convert_fusion.2), channel_id=1, source_target_pairs={{0,2},{1,7},{2,4},{3,1},{4,6},{5,3},{6,0},{7,5},{8,10},{9,15},{10,... | collective-permute-start | bytes 1843208 | tf_op jit(solution)/shard_map/ppermute | solution.py:274
  88.0 0.7 fusion.4
  88.8 0.1 collective-permute-start.22
  88.8 2.7 %collective-permute-start.23 = (bf16[2,400,384]{2,1,0:T(8,128)(2,1)S(1)}, bf16[2,400,384]{2,1,0:T(8,128)(2,1)S(1)}, u32[]{:S(2)}, u32[]{:S(2)}) collective-permute-start(bf16[2,400,384]{2,1,0:T(8,128)(2,1)S(1)} %get-tuple-element.78), channel_id=1, source_target_pairs={{0,24},{1,97},{2,26},{3,99},{4,28},{5,101},{6,30},{7,103},{8,0},{9... | collective-permute-start | bytes 1843208 | tf_op jit(solution)/shard_map/ppermute | solution.py:274
  91.5 0.0 collective-permute-start.24
  91.6 8.4 %collective-permute-done.20 = bf16[2,400,384]{2,1,0:T(8,128)(2,1)S(1)} collective-permute-done((bf16[2,400,384]{2,1,0:T(8,128)(2,1)S(1)}, bf16[2,400,384]{2,1,0:T(8,128)(2,1)S(1)}, u32[]{:S(2)}, u32[]{:S(2)}) %collective-permute-start.20) | collective-permute-done | bytes 614432 | tf_op jit(solution)/shard_map/ppermute | solution.py:274
  99.9 3.8 %collective-permute-done.21 = bf16[2,400,384]{2,1,0:T(8,128)(2,1)S(1)} collective-permute-done((bf16[2,400,384]{2,1,0:T(8,128)(2,1)S(1)}, bf16[2,400,384]{2,1,0:T(8,128)(2,1)S(1)}, u32[]{:S(2)}, u32[]{:S(2)}) %collective-permute-start.21) | collective-permute-done | bytes 614432 | tf_op jit(solution)/shard_map/ppermute | solution.py:274
  103.7 0.4 convert_add_fusion
  104.2 0.0 copy-start.1
  104.2 9.3 %shard_map.60 = bf16[8,2,400,400]{3,2,1,0:T(8,128)(2,1)} custom-call(s32[8]{0:T(128)S(1)} %copy-done.2, bf16[8,2,400,384]{3,2,1,0:T(8,128)(2,1)S(1)} %get-tuple-element.66.left_ref, bf16[4,400,384]{2,1,0:T(8,128)(2,1)S(1)} %pad_maximum_fusion.rest_0_, bf16[4,400,384]{2,1,0:T(8,128)(2,1)S(1)} %collective-permute-done.3.rest_1_, ...), custom_call_target="tpu_custom_call" | custom-call | flops 1966080000 | bytes 15000000 | tf_op jit(solution)/shard_map/pallas_call | solution.py:230
  113.6 2.1 %shard_map.61 = f32[2,400,400]{2,1,0:T(8,128)} custom-call(bf16[400,384]{1,0:T(8,128)(2,1)S(1)} %bitcast.36, f32[2,400,384]{2,1,0:T(8,128)S(1)} %convert_add_fusion, bf16[2,400,384]{2,1,0:T(8,128)(2,1)S(1)} %collective-permute-done.22.rest_0_, bf16[2,400,384]{2,1,0:T(8,128)(2,1)S(1)} %collective-permute-done.23.rest_1_, ...), custom_call_target="tpu_custom_call" | custom-call | tf_op jit(solution)/shard_map/pallas_call | solution.py:261
  (27 shorter events, 0.1 us)
Async XLA Ops:
  0.6 11.0 %collective-permute-start = (bf16[400,384]{1,0:T(8,128)(2,1)}, bf16[400,384]{1,0:T(8,128)(2,1)S(1)}, u32[]{:S(2)}, u32[]{:S(2)}) collective-permute-start(bf16[400,384]{1,0:T(8,128)(2,1)} %bitcast.28), channel_id=1, source_target_pairs={{0,96},{1,25},{2,98},{3,27},{4,100},{5,29},{6,102},{7,31},{8,104},... | collective-permute-start | bytes 921608 | tf_op jit(solution)/shard_map/ppermute | solution.py:274
  4.3 7.8 %collective-permute-start.1 = (bf16[400,384]{1,0:T(8,128)(2,1)}, bf16[400,384]{1,0:T(8,128)(2,1)S(1)}, u32[]{:S(2)}, u32[]{:S(2)}) collective-permute-start(bf16[400,384]{1,0:T(8,128)(2,1)} %bitcast.29), channel_id=1, source_target_pairs={{0,64},{1,17},{2,66},{3,19},{4,68},{5,21},{6,70},{7,23},{8,72},{9,... | collective-permute-start | bytes 921608 | tf_op jit(solution)/shard_map/ppermute | solution.py:274
  4.6 10.7 %collective-permute-start.2 = (bf16[400,384]{1,0:T(8,128)(2,1)}, bf16[400,384]{1,0:T(8,128)(2,1)S(1)}, u32[]{:S(2)}, u32[]{:S(2)}) collective-permute-start(bf16[400,384]{1,0:T(8,128)(2,1)} %bitcast.30), channel_id=1, source_target_pairs={{0,32},{1,9},{2,34},{3,11},{4,36},{5,13},{6,38},{7,15},{8,40},{9,1... | collective-permute-start | bytes 921608 | tf_op jit(solution)/shard_map/ppermute | solution.py:274
  5.3 13.8 %collective-permute-start.15 = (bf16[400,384]{1,0:T(8,128)(2,1)}, bf16[400,384]{1,0:T(8,128)(2,1)S(1)}, u32[]{:S(2)}, u32[]{:S(2)}) collective-permute-start(bf16[400,384]{1,0:T(8,128)(2,1)} %bitcast.31), channel_id=1, source_target_pairs={{0,6},{1,3},{2,0},{3,5},{4,2},{5,7},{6,4},{7,1},{8,14},{9,11},{10,... | collective-permute-start | bytes 921608 | tf_op jit(solution)/shard_map/ppermute | solution.py:274
  6.9 12.1 %collective-permute-start.16 = (bf16[400,384]{1,0:T(8,128)(2,1)}, bf16[400,384]{1,0:T(8,128)(2,1)S(1)}, u32[]{:S(2)}, u32[]{:S(2)}) collective-permute-start(bf16[400,384]{1,0:T(8,128)(2,1)} %bitcast.32), channel_id=1, source_target_pairs={{0,2},{1,7},{2,4},{3,1},{4,6},{5,3},{6,0},{7,5},{8,10},{9,15},{10,... | collective-permute-start | bytes 921608 | tf_op jit(solution)/shard_map/ppermute | solution.py:274
  15.3 3.8 %copy-start = (bf16[1,384,400]{1,2,0:T(8,128)(2,1)S(1)}, bf16[1,384,400]{1,2,0:T(8,128)(2,1)}, u32[]{:S(2)}) copy-start(bf16[1,384,400]{1,2,0:T(8,128)(2,1)} %param.4) | copy-start | bytes 921604
  16.5 17.9 %collective-permute-start.3 = (bf16[4,400,384]{2,1,0:T(8,128)(2,1)S(1)}, bf16[4,400,384]{2,1,0:T(8,128)(2,1)S(1)}, u32[]{:S(2)}, u32[]{:S(2)}) collective-permute-start(bf16[4,400,384]{2,1,0:T(8,128)(2,1)S(1)} %pad_maximum_fusion.rest_0_), channel_id=1, source_target_pairs={{0,24},{1,97},{2,26},{3,99},{4,28},{5,101},{6,30},{7,103},{8,0},{9... | collective-permute-start | bytes 3686408 | tf_op jit(solution)/shard_map/ppermute | solution.py:274
  19.0 17.4 %collective-permute-start.4 = (bf16[4,400,384]{2,1,0:T(8,128)(2,1)S(1)}, bf16[4,400,384]{2,1,0:T(8,128)(2,1)S(1)}, u32[]{:S(2)}, u32[]{:S(2)}) collective-permute-start(bf16[4,400,384]{2,1,0:T(8,128)(2,1)S(1)} %pad_maximum_fusion.rest_0_), channel_id=1, source_target_pairs={{0,8},{1,33},{2,10},{3,35},{4,12},{5,37},{6,14},{7,39},{8,16},{9,4... | collective-permute-start | bytes 3686408 | tf_op jit(solution)/shard_map/ppermute | solution.py:274
  28.6 5.2 %collective-permute-start.17 = (bf16[3,400,384]{2,1,0:T(8,128)(2,1)S(1)}, bf16[3,400,384]{2,1,0:T(8,128)(2,1)S(1)}, u32[]{:S(2)}, u32[]{:S(2)}) collective-permute-start(bf16[3,400,384]{2,1,0:T(8,128)(2,1)S(1)} %pad_maximum_fusion.1.rest_5_), channel_id=1, source_target_pairs={{0,1},{1,0},{2,3},{3,2},{4,5},{5,4},{6,7},{7,6},{8,9},{9,8},{10,11... | collective-permute-start | bytes 2764808 | tf_op jit(solution)/shard_map/ppermute | solution.py:274
  31.1 20.7 %collective-permute-start.8 = (bf16[2,2,400,384]{3,2,1,0:T(8,128)(2,1)}, bf16[2,2,400,384]{3,2,1,0:T(8,128)(2,1)S(1)}, u32[]{:S(2)}, u32[]{:S(2)}) collective-permute-start(bf16[2,2,400,384]{3,2,1,0:T(8,128)(2,1)} %get-tuple-element.52), channel_id=1, source_target_pairs={{0,32},{1,9},{2,34},{3,11},{4,36},{5,13},{6,38},{7,15},{8,40},{9,1... | collective-permute-start | bytes 3686408 | tf_op jit(solution)/shard_map/ppermute | solution.py:274
  31.1 21.2 %collective-permute-start.10 = (bf16[2,2,400,384]{3,2,1,0:T(8,128)(2,1)}, bf16[2,2,400,384]{3,2,1,0:T(8,128)(2,1)S(1)}, u32[]{:S(2)}, u32[]{:S(2)}) collective-permute-start(bf16[2,2,400,384]{3,2,1,0:T(8,128)(2,1)} %get-tuple-element.55), channel_id=1, source_target_pairs={{0,96},{1,25},{2,98},{3,27},{4,100},{5,29},{6,102},{7,31},{8,104},... | collective-permute-start | bytes 3686408 | tf_op jit(solution)/shard_map/ppermute | solution.py:274
  33.8 20.6 %collective-permute-start.19 = (bf16[2,2,400,384]{3,2,1,0:T(8,128)(2,1)}, bf16[2,2,400,384]{3,2,1,0:T(8,128)(2,1)S(1)}, u32[]{:S(2)}, u32[]{:S(2)}) collective-permute-start(bf16[2,2,400,384]{3,2,1,0:T(8,128)(2,1)} %get-tuple-element.61), channel_id=1, source_target_pairs={{0,1},{1,0},{2,3},{3,2},{4,5},{5,4},{6,7},{7,6},{8,9},{9,8},{10,11... | collective-permute-start | bytes 3686408 | tf_op jit(solution)/shard_map/ppermute | solution.py:274
  36.4 19.5 %collective-permute-start.5 = (bf16[2,2,400,384]{3,2,1,0:T(8,128)(2,1)}, bf16[2,2,400,384]{3,2,1,0:T(8,128)(2,1)S(1)}, u32[]{:S(2)}, u32[]{:S(2)}) collective-permute-start(bf16[2,2,400,384]{3,2,1,0:T(8,128)(2,1)} %get-tuple-element.47), channel_id=1, source_target_pairs={{0,1},{1,0},{2,3},{3,2},{4,5},{5,4},{6,7},{7,6},{8,9},{9,8},{10,11... | collective-permute-start | bytes 3686408 | tf_op jit(solution)/shard_map/ppermute | solution.py:274
  42.4 22.6 %collective-permute-start.6 = (bf16[2,2,400,384]{3,2,1,0:T(8,128)(2,1)}, bf16[2,2,400,384]{3,2,1,0:T(8,128)(2,1)S(1)}, u32[]{:S(2)}, u32[]{:S(2)}) collective-permute-start(bf16[2,2,400,384]{3,2,1,0:T(8,128)(2,1)} %get-tuple-element.48), channel_id=1, source_target_pairs={{0,32},{1,9},{2,34},{3,11},{4,36},{5,13},{6,38},{7,15},{8,40},{9,1... | collective-permute-start | bytes 3686408 | tf_op jit(solution)/shard_map/ppermute | solution.py:274
  51.9 16.1 %collective-permute-start.7 = (bf16[2,2,400,384]{3,2,1,0:T(8,128)(2,1)}, bf16[2,2,400,384]{3,2,1,0:T(8,128)(2,1)S(1)}, u32[]{:S(2)}, u32[]{:S(2)}) collective-permute-start(bf16[2,2,400,384]{3,2,1,0:T(8,128)(2,1)} %get-tuple-element.49), channel_id=1, source_target_pairs={{0,96},{1,25},{2,98},{3,27},{4,100},{5,29},{6,102},{7,31},{8,104},... | collective-permute-start | bytes 3686408 | tf_op jit(solution)/shard_map/ppermute | solution.py:274
  52.3 17.4 %collective-permute-start.18 = (bf16[2,400,384]{2,1,0:T(8,128)(2,1)S(1)}, bf16[2,400,384]{2,1,0:T(8,128)(2,1)S(1)}, u32[]{:S(2)}, u32[]{:S(2)}) collective-permute-start(bf16[2,400,384]{2,1,0:T(8,128)(2,1)S(1)} %pad_maximum_fusion.2), channel_id=1, source_target_pairs={{0,6},{1,3},{2,0},{3,5},{4,2},{5,7},{6,4},{7,1},{8,14},{9,11},{10,... | collective-permute-start | bytes 1843208 | tf_op jit(solution)/shard_map/ppermute | solution.py:274
  54.0 3.1 %copy-start.4 = (bf16[4,2,400,384]{3,2,1,0:T(8,128)(2,1)S(1)}, bf16[4,2,400,384]{3,2,1,0:T(8,128)(2,1)}, u32[]{:S(2)}) copy-start(bf16[4,2,400,384]{3,2,1,0:T(8,128)(2,1)} %get-tuple-element.46) | copy-start | bytes 7372804
  54.4 33.6 %collective-permute-start.9 = (bf16[2,2,400,384]{3,2,1,0:T(8,128)(2,1)S(1)}, bf16[2,2,400,384]{3,2,1,0:T(8,128)(2,1)S(1)}, u32[]{:S(2)}, u32[]{:S(2)}) collective-permute-start(bf16[2,2,400,384]{3,2,1,0:T(8,128)(2,1)S(1)} %add_convert_fusion.1), channel_id=1, source_target_pairs={{0,32},{1,9},{2,34},{3,11},{4,36},{5,13},{6,38},{7,15},{8,40},{9,1... | collective-permute-start | bytes 3686408 | tf_op jit(solution)/shard_map/ppermute | solution.py:274
  55.9 32.1 %collective-permute-start.11 = (bf16[2,2,400,384]{3,2,1,0:T(8,128)(2,1)S(1)}, bf16[2,2,400,384]{3,2,1,0:T(8,128)(2,1)S(1)}, u32[]{:S(2)}, u32[]{:S(2)}) collective-permute-start(bf16[2,2,400,384]{3,2,1,0:T(8,128)(2,1)S(1)} %add_convert_fusion), channel_id=1, source_target_pairs={{0,96},{1,25},{2,98},{3,27},{4,100},{5,29},{6,102},{7,31},{8,104},... | collective-permute-start | bytes 3686408 | tf_op jit(solution)/shard_map/ppermute | solution.py:274
  68.0 16.0 %collective-permute-start.12 = (bf16[2,400,384]{2,1,0:T(8,128)(2,1)S(1)}, bf16[2,400,384]{2,1,0:T(8,128)(2,1)S(1)}, u32[]{:S(2)}, u32[]{:S(2)}) collective-permute-start(bf16[2,400,384]{2,1,0:T(8,128)(2,1)S(1)} %slice.83), channel_id=1, source_target_pairs={{0,24},{1,97},{2,26},{3,99},{4,28},{5,101},{6,30},{7,103},{8,0},{9... | collective-permute-start | bytes 1843208 | tf_op jit(solution)/shard_map/ppermute | solution.py:274
  68.1 19.9 %copy-start.3 = (bf16[4,2,400,384]{3,2,1,0:T(8,128)(2,1)S(1)}, bf16[4,2,400,384]{3,2,1,0:T(8,128)(2,1)}, u32[]{:S(2)}) copy-start(bf16[4,2,400,384]{3,2,1,0:T(8,128)(2,1)} %get-tuple-element.40) | copy-start | bytes 7372804
  68.2 15.8 %collective-permute-start.13 = (bf16[2,400,384]{2,1,0:T(8,128)(2,1)S(1)}, bf16[2,400,384]{2,1,0:T(8,128)(2,1)S(1)}, u32[]{:S(2)}, u32[]{:S(2)}) collective-permute-start(bf16[2,400,384]{2,1,0:T(8,128)(2,1)S(1)} %slice.84), channel_id=1, source_target_pairs={{0,8},{1,33},{2,10},{3,35},{4,12},{5,37},{6,14},{7,39},{8,16},{9,4... | collective-permute-start | bytes 1843208 | tf_op jit(solution)/shard_map/ppermute | solution.py:274
  69.7 14.3 %collective-permute-start.14 = (bf16[2,400,384]{2,1,0:T(8,128)(2,1)S(1)}, bf16[2,400,384]{2,1,0:T(8,128)(2,1)S(1)}, u32[]{:S(2)}, u32[]{:S(2)}) collective-permute-start(bf16[2,400,384]{2,1,0:T(8,128)(2,1)S(1)} %get-tuple-element.58), channel_id=1, source_target_pairs={{0,2},{1,7},{2,4},{3,1},{4,6},{5,3},{6,0},{7,5},{8,10},{9,15},{10,... | collective-permute-start | bytes 1843208 | tf_op jit(solution)/shard_map/ppermute | solution.py:274
  84.2 15.7 %collective-permute-start.20 = (bf16[2,400,384]{2,1,0:T(8,128)(2,1)S(1)}, bf16[2,400,384]{2,1,0:T(8,128)(2,1)S(1)}, u32[]{:S(2)}, u32[]{:S(2)}) collective-permute-start(bf16[2,400,384]{2,1,0:T(8,128)(2,1)S(1)} %add_convert_fusion.2), channel_id=1, source_target_pairs={{0,2},{1,7},{2,4},{3,1},{4,6},{5,3},{6,0},{7,5},{8,10},{9,15},{10,... | collective-permute-start | bytes 1843208 | tf_op jit(solution)/shard_map/ppermute | solution.py:274
  88.0 15.7 %collective-permute-start.21 = (bf16[2,400,384]{2,1,0:T(8,128)(2,1)S(1)}, bf16[2,400,384]{2,1,0:T(8,128)(2,1)S(1)}, u32[]{:S(2)}, u32[]{:S(2)}) collective-permute-start(bf16[2,400,384]{2,1,0:T(8,128)(2,1)S(1)} %get-tuple-element.64), channel_id=1, source_target_pairs={{0,6},{1,3},{2,0},{3,5},{4,2},{5,7},{6,4},{7,1},{8,14},{9,11},{10,... | collective-permute-start | bytes 1843208 | tf_op jit(solution)/shard_map/ppermute | solution.py:274
  88.8 24.8 %collective-permute-start.22 = (bf16[2,400,384]{2,1,0:T(8,128)(2,1)S(1)}, bf16[2,400,384]{2,1,0:T(8,128)(2,1)S(1)}, u32[]{:S(2)}, u32[]{:S(2)}) collective-permute-start(bf16[2,400,384]{2,1,0:T(8,128)(2,1)S(1)} %get-tuple-element.84), channel_id=1, source_target_pairs={{0,8},{1,33},{2,10},{3,35},{4,12},{5,37},{6,14},{7,39},{8,16},{9,4... | collective-permute-start | bytes 1843208 | tf_op jit(solution)/shard_map/ppermute | solution.py:274
  88.8 24.7 %collective-permute-start.23 = (bf16[2,400,384]{2,1,0:T(8,128)(2,1)S(1)}, bf16[2,400,384]{2,1,0:T(8,128)(2,1)S(1)}, u32[]{:S(2)}, u32[]{:S(2)}) collective-permute-start(bf16[2,400,384]{2,1,0:T(8,128)(2,1)S(1)} %get-tuple-element.78), channel_id=1, source_target_pairs={{0,24},{1,97},{2,26},{3,99},{4,28},{5,101},{6,30},{7,103},{8,0},{9... | collective-permute-start | bytes 1843208 | tf_op jit(solution)/shard_map/ppermute | solution.py:274
  91.5 12.7 %copy-start.2 = (s32[8]{0:T(128)S(1)}, s32[8]{0:T(128)}, u32[]{:S(2)}) copy-start(s32[8]{0:T(128)} %partner_ref) | copy-start | bytes 100
  91.5 22.1 %collective-permute-start.24 = (bf16[2,400,384]{2,1,0:T(8,128)(2,1)S(1)}, bf16[2,400,384]{2,1,0:T(8,128)(2,1)S(1)}, u32[]{:S(2)}, u32[]{:S(2)}) collective-permute-start(bf16[2,400,384]{2,1,0:T(8,128)(2,1)S(1)} %get-tuple-element.79), channel_id=1, source_target_pairs={{0,16},{1,65},{2,18},{3,67},{4,20},{5,69},{6,22},{7,71},{8,24},{9,... | collective-permute-start | bytes 1843208 | tf_op jit(solution)/shard_map/ppermute | solution.py:274
  104.2 9.4 %copy-start.1 = (bf16[1,384,400]{1,2,0:T(8,128)(2,1)S(1)}, bf16[1,384,400]{1,2,0:T(8,128)(2,1)}, u32[]{:S(2)}) copy-start(bf16[1,384,400]{1,2,0:T(8,128)(2,1)} %param.4) | copy-start | bytes 921604

commit v9 on v8

--- a/solution.py
+++ b/solution.py
@@ -331,7 +331,7 @@
     low, high = second(near[:2], -1), second(far[2:], 1)
     opposite = turn(w3, 1)
     low, high, opposite, across, ring_other, w = barrier((low, high, opposite, across, ring_other, w))
-    z_last, back = turn(rounded(w[1], opposite), 1), turn(w[2], -1)
+    z_last = turn(rounded(w[1], opposite), 1)
 
     v = [
         rounded(here[0], end_down[0], last_up[0]),
@@ -339,10 +339,12 @@
         rounded(here[2], end_up[0], last_down[0]),
         rounded(here[3], end_up[1], last_down[1]),
     ]
+    v, w2 = barrier((v, w[2]))
+    back = turn(w2, -1)
     ends = [second(v[1], 1), second(v[3], -1), second(v[2], 2)]
 
     sources = [kept, near, far, low, high, ring_mine, ring_other, across]
-    pair_blocks = pair_products(left, sources, after(partner, *v, z_last, back))
+    pair_blocks = pair_products(left, sources, after(partner, *v, z_last))
     pair_blocks, ends = barrier((pair_blocks, ends))
     partner_blocks = partner_products(own, added(v[0], w[0], back, z_last), ends)
     return (pair_blocks, partner_blocks[None])

time: 116 us -> 110 us (0.948)
  the two profiles are of different devices: /device:TPU:1 before, /device:TPU:0 now
where the time goes in v9:
time: 110 us; the launch traced here: 109 us
  starting transfers between devices  42.6 us (39%)
  waiting for transfers between devices  40.9 us (37%)
  Pallas kernels  19.4 us (18%)
  other arithmetic  3.98 us (4%)
    ppermute x25, starting transfers between devices, permuted(): return lax.ppermute(value, ('sx', 'sy'), pairs)  42.6 us
    ppermute x25, waiting for transfers between devices, permuted(): return lax.ppermute(value, ('sx', 'sy'), pairs)  40.9 us
    pallas_call x1, Pallas kernels, pair_products(): pl.pallas_call(pair_kernel, in_specs=[smem, pl.BlockSpec(memory_space=plt...  9.33 us
    pallas_call x1, Pallas kernels, left_products(): pl.pallas_call(left_kernel, in_specs=[pl.BlockSpec(memory_space=pltpu.HBM...  8.04 us
    convert_element_type x5, other arithmetic, rounded(): return added(*terms).astype(jnp.bfloat16)  2.27 us
  transfers between devices with their start and end apart: 25, of which 10 were waited for; matrix products, arithmetic and copies ran while one was open for 4% of the time, Pallas kernels for 16%

profile of v9, /device:TPU:0, one launch (start us, length us, event | category | flops | bytes accessed | tf_op | source)
XLA Modules:
  0.0 108.5 jit_solution(7380496983824092745)
XLA Ops:
  0.6 1.6 %collective-permute-start.2 = (bf16[400,384]{1,0:T(8,128)(2,1)}, bf16[400,384]{1,0:T(8,128)(2,1)S(1)}, u32[]{:S(2)}, u32[]{:S(2)}) collective-permute-start(bf16[400,384]{1,0:T(8,128)(2,1)} %bitcast.27), channel_id=1, source_target_pairs={{0,32},{1,9},{2,34},{3,11},{4,36},{5,13},{6,38},{7,15},{8,40},{9,1... | collective-permute-start | bytes 921608 | tf_op jit(solution)/shard_map/ppermute | solution.py:274
  2.3 2.7 %collective-permute-start.1 = (bf16[400,384]{1,0:T(8,128)(2,1)}, bf16[400,384]{1,0:T(8,128)(2,1)S(1)}, u32[]{:S(2)}, u32[]{:S(2)}) collective-permute-start(bf16[400,384]{1,0:T(8,128)(2,1)} %bitcast.28), channel_id=1, source_target_pairs={{0,64},{1,17},{2,66},{3,19},{4,68},{5,21},{6,70},{7,23},{8,72},{9,... | collective-permute-start | bytes 921608 | tf_op jit(solution)/shard_map/ppermute | solution.py:274
  5.0 1.4 %collective-permute-start = (bf16[400,384]{1,0:T(8,128)(2,1)}, bf16[400,384]{1,0:T(8,128)(2,1)S(1)}, u32[]{:S(2)}, u32[]{:S(2)}) collective-permute-start(bf16[400,384]{1,0:T(8,128)(2,1)} %bitcast.29), channel_id=1, source_target_pairs={{0,96},{1,25},{2,98},{3,27},{4,100},{5,29},{6,102},{7,31},{8,104},... | collective-permute-start | bytes 921608 | tf_op jit(solution)/shard_map/ppermute | solution.py:274
  6.4 4.0 %collective-permute-start.15 = (bf16[400,384]{1,0:T(8,128)(2,1)}, bf16[400,384]{1,0:T(8,128)(2,1)S(1)}, u32[]{:S(2)}, u32[]{:S(2)}) collective-permute-start(bf16[400,384]{1,0:T(8,128)(2,1)} %bitcast.30), channel_id=1, source_target_pairs={{0,6},{1,3},{2,0},{3,5},{4,2},{5,7},{6,4},{7,1},{8,14},{9,11},{10,... | collective-permute-start | bytes 921608 | tf_op jit(solution)/shard_map/ppermute | solution.py:274
  10.5 2.9 %collective-permute-done.1 = bf16[400,384]{1,0:T(8,128)(2,1)S(1)} collective-permute-done((bf16[400,384]{1,0:T(8,128)(2,1)}, bf16[400,384]{1,0:T(8,128)(2,1)S(1)}, u32[]{:S(2)}, u32[]{:S(2)}) %collective-permute-start.1) | collective-permute-done | bytes 307232 | tf_op jit(solution)/shard_map/ppermute | solution.py:274
  13.3 1.2 %pad_maximum_fusion.rest_0_ = bf16[4,400,384]{2,1,0:T(8,128)(2,1)S(1)} fusion(bf16[1,400,384]{2,1,0:T(8,128)(2,1)S(1)} %bitcast.40, bf16[1,400,384]{2,1,0:T(8,128)(2,1)S(1)} %bitcast.41, bf16[1,400,384]{2,1,0:T(8,128)(2,1)S(1)} %bitcast.42, bf16[1,400,384]{2,1,0:T(8,128)(2,1)} %bitcast.32), kind=kLoop, calls=%fused_computation.2 | loop fusion | flops 1843200 | bytes 2457600 | tf_op jit(solution)/shard_map/stack | solution.py:311
  14.6 3.1 %collective-permute-start.3 = (bf16[4,400,384]{2,1,0:T(8,128)(2,1)S(1)}, bf16[4,400,384]{2,1,0:T(8,128)(2,1)S(1)}, u32[]{:S(2)}, u32[]{:S(2)}) collective-permute-start(bf16[4,400,384]{2,1,0:T(8,128)(2,1)S(1)} %pad_maximum_fusion.rest_0_), channel_id=1, source_target_pairs={{0,24},{1,97},{2,26},{3,99},{4,28},{5,101},{6,30},{7,103},{8,0},{9... | collective-permute-start | bytes 3686408 | tf_op jit(solution)/shard_map/ppermute | solution.py:274
  17.7 1.1 %collective-permute-done.16 = bf16[400,384]{1,0:T(8,128)(2,1)S(1)} collective-permute-done((bf16[400,384]{1,0:T(8,128)(2,1)}, bf16[400,384]{1,0:T(8,128)(2,1)S(1)}, u32[]{:S(2)}, u32[]{:S(2)}) %collective-permute-start.16) | collective-permute-done | bytes 307232 | tf_op jit(solution)/shard_map/ppermute | solution.py:274
  18.8 0.1 pad_maximum_fusion.1.rest_5_
  18.9 8.0 %shard_map.59 = (bf16[8,2,400,384]{3,2,1,0:T(8,128)(2,1)S(1)}, bf16[2,2,400,384]{3,2,1,0:T(8,128)(2,1)}, bf16[2,2,400,384]{3,2,1,0:T(8,128)(2,1)}, bf16[2,2,400,...) custom-call(s32[8]{0:T(128)} %partner_ref, ...), custom_call_target="tpu_custom_call" | custom-call | flops 1887436800 | bytes 25000000 | tf_op jit(solution)/shard_map/pallas_call | solution.py:152
  26.9 0.1 collective-permute-start.17
  27.0 1.5 %collective-permute-start.10 = (bf16[2,2,400,384]{3,2,1,0:T(8,128)(2,1)}, bf16[2,2,400,384]{3,2,1,0:T(8,128)(2,1)S(1)}, u32[]{:S(2)}, u32[]{:S(2)}) collective-permute-start(bf16[2,2,400,384]{3,2,1,0:T(8,128)(2,1)} %get-tuple-element.60), channel_id=1, source_target_pairs={{0,96},{1,25},{2,98},{3,27},{4,100},{5,29},{6,102},{7,31},{8,104},... | collective-permute-start | bytes 3686408 | tf_op jit(solution)/shard_map/ppermute | solution.py:274
  28.5 1.2 %collective-permute-start.8 = (bf16[2,2,400,384]{3,2,1,0:T(8,128)(2,1)}, bf16[2,2,400,384]{3,2,1,0:T(8,128)(2,1)S(1)}, u32[]{:S(2)}, u32[]{:S(2)}) collective-permute-start(bf16[2,2,400,384]{3,2,1,0:T(8,128)(2,1)} %get-tuple-element.57), channel_id=1, source_target_pairs={{0,32},{1,9},{2,34},{3,11},{4,36},{5,13},{6,38},{7,15},{8,40},{9,1... | collective-permute-start | bytes 3686408 | tf_op jit(solution)/shard_map/ppermute | solution.py:274
  29.7 0.5 collective-permute-start.19
  30.3 2.6 %collective-permute-done.3.rest_1_ = bf16[4,400,384]{2,1,0:T(8,128)(2,1)S(1)} collective-permute-done((bf16[4,400,384]{2,1,0:T(8,128)(2,1)S(1)}, bf16[4,400,384]{2,1,0:T(8,128)(2,1)S(1)}, u32[]{:S(2)}, u32[]{:S(2)}) %collective-permute-start.3) | collective-permute-done | bytes 1228832 | tf_op jit(solution)/shard_map/ppermute | solution.py:274
  32.9 4.0 %collective-permute-done.4.rest_2_ = bf16[4,400,384]{2,1,0:T(8,128)(2,1)S(1)} collective-permute-done((bf16[4,400,384]{2,1,0:T(8,128)(2,1)S(1)}, bf16[4,400,384]{2,1,0:T(8,128)(2,1)S(1)}, u32[]{:S(2)}, u32[]{:S(2)}) %collective-permute-start.4) | collective-permute-done | bytes 1228832 | tf_op jit(solution)/shard_map/ppermute | solution.py:274
  36.9 2.1 %collective-permute-start.6 = (bf16[2,2,400,384]{3,2,1,0:T(8,128)(2,1)}, bf16[2,2,400,384]{3,2,1,0:T(8,128)(2,1)S(1)}, u32[]{:S(2)}, u32[]{:S(2)}) collective-permute-start(bf16[2,2,400,384]{3,2,1,0:T(8,128)(2,1)} %get-tuple-element.53), channel_id=1, source_target_pairs={{0,32},{1,9},{2,34},{3,11},{4,36},{5,13},{6,38},{7,15},{8,40},{9,1... | collective-permute-start | bytes 3686408 | tf_op jit(solution)/shard_map/ppermute | solution.py:274
  39.0 5.6 %collective-permute-done.10 = bf16[2,2,400,384]{3,2,1,0:T(8,128)(2,1)S(1)} collective-permute-done((bf16[2,2,400,384]{3,2,1,0:T(8,128)(2,1)}, bf16[2,2,400,384]{3,2,1,0:T(8,128)(2,1)S(1)}, u32[]{:S(2)}, u32[]{:S(2)}) %collective-permute-start.10) | collective-permute-done | bytes 1228832 | tf_op jit(solution)/shard_map/ppermute | solution.py:274
  44.6 2.1 %collective-permute-start.7 = (bf16[2,2,400,384]{3,2,1,0:T(8,128)(2,1)}, bf16[2,2,400,384]{3,2,1,0:T(8,128)(2,1)S(1)}, u32[]{:S(2)}, u32[]{:S(2)}) collective-permute-start(bf16[2,2,400,384]{3,2,1,0:T(8,128)(2,1)} %get-tuple-element.54), channel_id=1, source_target_pairs={{0,96},{1,25},{2,98},{3,27},{4,100},{5,29},{6,102},{7,31},{8,104},... | collective-permute-start | bytes 3686408 | tf_op jit(solution)/shard_map/ppermute | solution.py:274
  46.7 0.1 pad_maximum_fusion.2
  46.7 0.3 add_convert_fusion
  47.1 4.9 %collective-permute-start.18 = (bf16[2,400,384]{2,1,0:T(8,128)(2,1)S(1)}, bf16[2,400,384]{2,1,0:T(8,128)(2,1)S(1)}, u32[]{:S(2)}, u32[]{:S(2)}) collective-permute-start(bf16[2,400,384]{2,1,0:T(8,128)(2,1)S(1)} %pad_maximum_fusion.2), channel_id=1, source_target_pairs={{0,6},{1,3},{2,0},{3,5},{4,2},{5,7},{6,4},{7,1},{8,14},{9,11},{10,... | collective-permute-start | bytes 1843208 | tf_op jit(solution)/shard_map/ppermute | solution.py:274
  52.0 0.3 add_convert_fusion.1
  52.3 0.1 collective-permute-start.11
  52.4 2.0 %collective-permute-start.9 = (bf16[2,2,400,384]{3,2,1,0:T(8,128)(2,1)S(1)}, bf16[2,2,400,384]{3,2,1,0:T(8,128)(2,1)S(1)}, u32[]{:S(2)}, u32[]{:S(2)}) collective-permute-start(bf16[2,2,400,384]{3,2,1,0:T(8,128)(2,1)S(1)} %add_convert_fusion.1), channel_id=1, source_target_pairs={{0,32},{1,9},{2,34},{3,11},{4,36},{5,13},{6,38},{7,15},{8,40},{9,1... | collective-permute-start | bytes 3686408 | tf_op jit(solution)/shard_map/ppermute | solution.py:274
  54.4 0.6 fusion.7
  55.0 4.8 %collective-permute-done.6 = bf16[2,2,400,384]{3,2,1,0:T(8,128)(2,1)S(1)} collective-permute-done((bf16[2,2,400,384]{3,2,1,0:T(8,128)(2,1)}, bf16[2,2,400,384]{3,2,1,0:T(8,128)(2,1)S(1)}, u32[]{:S(2)}, u32[]{:S(2)}) %collective-permute-start.6) | collective-permute-done | bytes 1228832 | tf_op jit(solution)/shard_map/ppermute | solution.py:274
  59.8 1.7 %collective-permute-done.7 = bf16[2,2,400,384]{3,2,1,0:T(8,128)(2,1)S(1)} collective-permute-done((bf16[2,2,400,384]{3,2,1,0:T(8,128)(2,1)}, bf16[2,2,400,384]{3,2,1,0:T(8,128)(2,1)S(1)}, u32[]{:S(2)}, u32[]{:S(2)}) %collective-permute-start.7) | collective-permute-done | bytes 1228832 | tf_op jit(solution)/shard_map/ppermute | solution.py:274
  61.5 0.1 slice.83
  61.6 3.0 %collective-permute-start.12 = (bf16[2,400,384]{2,1,0:T(8,128)(2,1)S(1)}, bf16[2,400,384]{2,1,0:T(8,128)(2,1)S(1)}, u32[]{:S(2)}, u32[]{:S(2)}) collective-permute-start(bf16[2,400,384]{2,1,0:T(8,128)(2,1)S(1)} %slice.83), channel_id=1, source_target_pairs={{0,24},{1,97},{2,26},{3,99},{4,28},{5,101},{6,30},{7,103},{8,0},{9... | collective-permute-start | bytes 1843208 | tf_op jit(solution)/shard_map/ppermute | solution.py:274
  64.6 0.1 slice.84
  64.6 0.1 collective-permute-start.13
  64.7 2.7 %collective-permute-start.14 = (bf16[2,400,384]{2,1,0:T(8,128)(2,1)S(1)}, bf16[2,400,384]{2,1,0:T(8,128)(2,1)S(1)}, u32[]{:S(2)}, u32[]{:S(2)}) collective-permute-start(bf16[2,400,384]{2,1,0:T(8,128)(2,1)S(1)} %get-tuple-element.63), channel_id=1, source_target_pairs={{0,2},{1,7},{2,4},{3,1},{4,6},{5,3},{6,0},{7,5},{8,10},{9,15},{10,... | collective-permute-start | bytes 1843208 | tf_op jit(solution)/shard_map/ppermute | solution.py:274
  67.4 11.5 %collective-permute-done.12.rest_3_ = bf16[2,400,384]{2,1,0:T(8,128)(2,1)S(1)} collective-permute-done((bf16[2,400,384]{2,1,0:T(8,128)(2,1)S(1)}, bf16[2,400,384]{2,1,0:T(8,128)(2,1)S(1)}, u32[]{:S(2)}, u32[]{:S(2)}) %collective-permute-start.12) | collective-permute-done | bytes 614432 | tf_op jit(solution)/shard_map/ppermute | solution.py:274
  78.9 2.8 %collective-permute-done.13.rest_4_ = bf16[2,400,384]{2,1,0:T(8,128)(2,1)S(1)} collective-permute-done((bf16[2,400,384]{2,1,0:T(8,128)(2,1)S(1)}, bf16[2,400,384]{2,1,0:T(8,128)(2,1)S(1)}, u32[]{:S(2)}, u32[]{:S(2)}) %collective-permute-start.13) | collective-permute-done | bytes 614432 | tf_op jit(solution)/shard_map/ppermute | solution.py:274
  81.7 0.2 add_convert_fusion.2
  81.8 2.0 %collective-permute-start.20 = (bf16[2,400,384]{2,1,0:T(8,128)(2,1)S(1)}, bf16[2,400,384]{2,1,0:T(8,128)(2,1)S(1)}, u32[]{:S(2)}, u32[]{:S(2)}) collective-permute-start(bf16[2,400,384]{2,1,0:T(8,128)(2,1)S(1)} %add_convert_fusion.2), channel_id=1, source_target_pairs={{0,2},{1,7},{2,4},{3,1},{4,6},{5,3},{6,0},{7,5},{8,10},{9,15},{10,... | collective-permute-start | bytes 1843208 | tf_op jit(solution)/shard_map/ppermute | solution.py:274
  83.8 0.0 copy-start.2
  83.9 0.9 fusion.4
  84.8 0.1 collective-permute-start.21
  84.9 3.2 %collective-permute-start.22 = (bf16[2,400,384]{2,1,0:T(8,128)(2,1)S(1)}, bf16[2,400,384]{2,1,0:T(8,128)(2,1)S(1)}, u32[]{:S(2)}, u32[]{:S(2)}) collective-permute-start(bf16[2,400,384]{2,1,0:T(8,128)(2,1)S(1)} %get-tuple-element.71), channel_id=1, source_target_pairs={{0,24},{1,97},{2,26},{3,99},{4,28},{5,101},{6,30},{7,103},{8,0},{9... | collective-permute-start | bytes 1843208 | tf_op jit(solution)/shard_map/ppermute | solution.py:274
  88.1 4.1 %collective-permute-start.24 = (bf16[2,400,384]{2,1,0:T(8,128)(2,1)S(1)}, bf16[2,400,384]{2,1,0:T(8,128)(2,1)S(1)}, u32[]{:S(2)}, u32[]{:S(2)}) collective-permute-start(bf16[2,400,384]{2,1,0:T(8,128)(2,1)S(1)} %get-tuple-element.82), channel_id=1, source_target_pairs={{0,6},{1,3},{2,0},{3,5},{4,2},{5,7},{6,4},{7,1},{8,14},{9,11},{10,... | collective-permute-start | bytes 1843208 | tf_op jit(solution)/shard_map/ppermute | solution.py:274
  92.2 4.0 %collective-permute-done.20 = bf16[2,400,384]{2,1,0:T(8,128)(2,1)S(1)} collective-permute-done((bf16[2,400,384]{2,1,0:T(8,128)(2,1)S(1)}, bf16[2,400,384]{2,1,0:T(8,128)(2,1)S(1)}, u32[]{:S(2)}, u32[]{:S(2)}) %collective-permute-start.20) | collective-permute-done | bytes 614432 | tf_op jit(solution)/shard_map/ppermute | solution.py:274
  96.2 9.3 %shard_map.60 = bf16[8,2,400,400]{3,2,1,0:T(8,128)(2,1)} custom-call(s32[8]{0:T(128)S(1)} %copy-done.2, bf16[8,2,400,384]{3,2,1,0:T(8,128)(2,1)S(1)} %get-tuple-element.75.left_ref, bf16[4,400,384]{2,1,0:T(8,128)(2,1)S(1)} %pad_maximum_fusion.rest_0_, bf16[4,400,384]{2,1,0:T(8,128)(2,1)S(1)} %collective-permute-done.3.rest_1_, ...), custom_call_target="tpu_custom_call" | custom-call | flops 1966080000 | bytes 15000000 | tf_op jit(solution)/shard_map/pallas_call | solution.py:230
  105.5 0.0 copy-start.1
  105.6 0.3 convert_add_fusion.sum_ref
  105.8 0.6 copy-done.1
  106.5 2.1 %shard_map.61 = f32[2,400,400]{2,1,0:T(8,128)} custom-call(bf16[400,384]{1,0:T(8,128)(2,1)S(1)} %bitcast.35, f32[2,400,384]{2,1,0:T(8,128)S(1)} %convert_add_fusion.sum_ref, bf16[2,400,384]{2,1,0:T(8,128)(2,1)S(1)} %collective-permute-done.21.rest_0_, bf16[2,400,384]{2,1,0:T(8,128)(2,1)S(1)} %collective-permute-done.22.rest_1_, ...), custom_call_target="tpu_custom_call" | custom-call | tf_op jit(solution)/shard_map/pallas_call | solution.py:261
  (27 shorter events, 0.1 us)
Async XLA Ops:
  0.6 9.9 %collective-permute-start.2 = (bf16[400,384]{1,0:T(8,128)(2,1)}, bf16[400,384]{1,0:T(8,128)(2,1)S(1)}, u32[]{:S(2)}, u32[]{:S(2)}) collective-permute-start(bf16[400,384]{1,0:T(8,128)(2,1)} %bitcast.27), channel_id=1, source_target_pairs={{0,32},{1,9},{2,34},{3,11},{4,36},{5,13},{6,38},{7,15},{8,40},{9,1... | collective-permute-start | bytes 921608 | tf_op jit(solution)/shard_map/ppermute | solution.py:274
  2.3 11.1 %collective-permute-start.1 = (bf16[400,384]{1,0:T(8,128)(2,1)}, bf16[400,384]{1,0:T(8,128)(2,1)S(1)}, u32[]{:S(2)}, u32[]{:S(2)}) collective-permute-start(bf16[400,384]{1,0:T(8,128)(2,1)} %bitcast.28), channel_id=1, source_target_pairs={{0,64},{1,17},{2,66},{3,19},{4,68},{5,21},{6,70},{7,23},{8,72},{9,... | collective-permute-start | bytes 921608 | tf_op jit(solution)/shard_map/ppermute | solution.py:274
  5.0 8.3 %collective-permute-start = (bf16[400,384]{1,0:T(8,128)(2,1)}, bf16[400,384]{1,0:T(8,128)(2,1)S(1)}, u32[]{:S(2)}, u32[]{:S(2)}) collective-permute-start(bf16[400,384]{1,0:T(8,128)(2,1)} %bitcast.29), channel_id=1, source_target_pairs={{0,96},{1,25},{2,98},{3,27},{4,100},{5,29},{6,102},{7,31},{8,104},... | collective-permute-start | bytes 921608 | tf_op jit(solution)/shard_map/ppermute | solution.py:274
  6.4 11.2 %collective-permute-start.15 = (bf16[400,384]{1,0:T(8,128)(2,1)}, bf16[400,384]{1,0:T(8,128)(2,1)S(1)}, u32[]{:S(2)}, u32[]{:S(2)}) collective-permute-start(bf16[400,384]{1,0:T(8,128)(2,1)} %bitcast.30), channel_id=1, source_target_pairs={{0,6},{1,3},{2,0},{3,5},{4,2},{5,7},{6,4},{7,1},{8,14},{9,11},{10,... | collective-permute-start | bytes 921608 | tf_op jit(solution)/shard_map/ppermute | solution.py:274
  10.5 8.3 %collective-permute-start.16 = (bf16[400,384]{1,0:T(8,128)(2,1)}, bf16[400,384]{1,0:T(8,128)(2,1)S(1)}, u32[]{:S(2)}, u32[]{:S(2)}) collective-permute-start(bf16[400,384]{1,0:T(8,128)(2,1)} %bitcast.31), channel_id=1, source_target_pairs={{0,2},{1,7},{2,4},{3,1},{4,6},{5,3},{6,0},{7,5},{8,10},{9,15},{10,... | collective-permute-start | bytes 921608 | tf_op jit(solution)/shard_map/ppermute | solution.py:274
  13.3 5.4 %copy-start = (bf16[1,384,400]{1,2,0:T(8,128)(2,1)S(1)}, bf16[1,384,400]{1,2,0:T(8,128)(2,1)}, u32[]{:S(2)}) copy-start(bf16[1,384,400]{1,2,0:T(8,128)(2,1)} %param.4) | copy-start | bytes 921604
  14.6 18.3 %collective-permute-start.3 = (bf16[4,400,384]{2,1,0:T(8,128)(2,1)S(1)}, bf16[4,400,384]{2,1,0:T(8,128)(2,1)S(1)}, u32[]{:S(2)}, u32[]{:S(2)}) collective-permute-start(bf16[4,400,384]{2,1,0:T(8,128)(2,1)S(1)} %pad_maximum_fusion.rest_0_), channel_id=1, source_target_pairs={{0,24},{1,97},{2,26},{3,99},{4,28},{5,101},{6,30},{7,103},{8,0},{9... | collective-permute-start | bytes 3686408 | tf_op jit(solution)/shard_map/ppermute | solution.py:274
  17.7 19.2 %collective-permute-start.4 = (bf16[4,400,384]{2,1,0:T(8,128)(2,1)S(1)}, bf16[4,400,384]{2,1,0:T(8,128)(2,1)S(1)}, u32[]{:S(2)}, u32[]{:S(2)}) collective-permute-start(bf16[4,400,384]{2,1,0:T(8,128)(2,1)S(1)} %pad_maximum_fusion.rest_0_), channel_id=1, source_target_pairs={{0,8},{1,33},{2,10},{3,35},{4,12},{5,37},{6,14},{7,39},{8,16},{9,4... | collective-permute-start | bytes 3686408 | tf_op jit(solution)/shard_map/ppermute | solution.py:274
  26.9 2.8 %collective-permute-start.17 = (bf16[3,400,384]{2,1,0:T(8,128)(2,1)S(1)}, bf16[3,400,384]{2,1,0:T(8,128)(2,1)S(1)}, u32[]{:S(2)}, u32[]{:S(2)}) collective-permute-start(bf16[3,400,384]{2,1,0:T(8,128)(2,1)S(1)} %pad_maximum_fusion.1.rest_5_), channel_id=1, source_target_pairs={{0,1},{1,0},{2,3},{3,2},{4,5},{5,4},{6,7},{7,6},{8,9},{9,8},{10,11... | collective-permute-start | bytes 2764808 | tf_op jit(solution)/shard_map/ppermute | solution.py:274
  27.0 17.5 %collective-permute-start.10 = (bf16[2,2,400,384]{3,2,1,0:T(8,128)(2,1)}, bf16[2,2,400,384]{3,2,1,0:T(8,128)(2,1)S(1)}, u32[]{:S(2)}, u32[]{:S(2)}) collective-permute-start(bf16[2,2,400,384]{3,2,1,0:T(8,128)(2,1)} %get-tuple-element.60), channel_id=1, source_target_pairs={{0,96},{1,25},{2,98},{3,27},{4,100},{5,29},{6,102},{7,31},{8,104},... | collective-permute-start | bytes 3686408 | tf_op jit(solution)/shard_map/ppermute | solution.py:274
  28.5 18.6 %collective-permute-start.8 = (bf16[2,2,400,384]{3,2,1,0:T(8,128)(2,1)}, bf16[2,2,400,384]{3,2,1,0:T(8,128)(2,1)S(1)}, u32[]{:S(2)}, u32[]{:S(2)}) collective-permute-start(bf16[2,2,400,384]{3,2,1,0:T(8,128)(2,1)} %get-tuple-element.57), channel_id=1, source_target_pairs={{0,32},{1,9},{2,34},{3,11},{4,36},{5,13},{6,38},{7,15},{8,40},{9,1... | collective-permute-start | bytes 3686408 | tf_op jit(solution)/shard_map/ppermute | solution.py:274
  29.7 22.5 %collective-permute-start.19 = (bf16[2,2,400,384]{3,2,1,0:T(8,128)(2,1)}, bf16[2,2,400,384]{3,2,1,0:T(8,128)(2,1)S(1)}, u32[]{:S(2)}, u32[]{:S(2)}) collective-permute-start(bf16[2,2,400,384]{3,2,1,0:T(8,128)(2,1)} %get-tuple-element.66), channel_id=1, source_target_pairs={{0,1},{1,0},{2,3},{3,2},{4,5},{5,4},{6,7},{7,6},{8,9},{9,8},{10,11... | collective-permute-start | bytes 3686408 | tf_op jit(solution)/shard_map/ppermute | solution.py:274
  36.9 15.5 %collective-permute-start.5 = (bf16[2,2,400,384]{3,2,1,0:T(8,128)(2,1)}, bf16[2,2,400,384]{3,2,1,0:T(8,128)(2,1)S(1)}, u32[]{:S(2)}, u32[]{:S(2)}) collective-permute-start(bf16[2,2,400,384]{3,2,1,0:T(8,128)(2,1)} %get-tuple-element.52), channel_id=1, source_target_pairs={{0,1},{1,0},{2,3},{3,2},{4,5},{5,4},{6,7},{7,6},{8,9},{9,8},{10,11... | collective-permute-start | bytes 3686408 | tf_op jit(solution)/shard_map/ppermute | solution.py:274
  36.9 22.9 %collective-permute-start.6 = (bf16[2,2,400,384]{3,2,1,0:T(8,128)(2,1)}, bf16[2,2,400,384]{3,2,1,0:T(8,128)(2,1)S(1)}, u32[]{:S(2)}, u32[]{:S(2)}) collective-permute-start(bf16[2,2,400,384]{3,2,1,0:T(8,128)(2,1)} %get-tuple-element.53), channel_id=1, source_target_pairs={{0,32},{1,9},{2,34},{3,11},{4,36},{5,13},{6,38},{7,15},{8,40},{9,1... | collective-permute-start | bytes 3686408 | tf_op jit(solution)/shard_map/ppermute | solution.py:274
  44.6 16.9 %collective-permute-start.7 = (bf16[2,2,400,384]{3,2,1,0:T(8,128)(2,1)}, bf16[2,2,400,384]{3,2,1,0:T(8,128)(2,1)S(1)}, u32[]{:S(2)}, u32[]{:S(2)}) collective-permute-start(bf16[2,2,400,384]{3,2,1,0:T(8,128)(2,1)} %get-tuple-element.54), channel_id=1, source_target_pairs={{0,96},{1,25},{2,98},{3,27},{4,100},{5,29},{6,102},{7,31},{8,104},... | collective-permute-start | bytes 3686408 | tf_op jit(solution)/shard_map/ppermute | solution.py:274
  47.1 17.6 %collective-permute-start.18 = (bf16[2,400,384]{2,1,0:T(8,128)(2,1)S(1)}, bf16[2,400,384]{2,1,0:T(8,128)(2,1)S(1)}, u32[]{:S(2)}, u32[]{:S(2)}) collective-permute-start(bf16[2,400,384]{2,1,0:T(8,128)(2,1)S(1)} %pad_maximum_fusion.2), channel_id=1, source_target_pairs={{0,6},{1,3},{2,0},{3,5},{4,2},{5,7},{6,4},{7,1},{8,14},{9,11},{10,... | collective-permute-start | bytes 1843208 | tf_op jit(solution)/shard_map/ppermute | solution.py:274
  52.0 2.4 %copy-start.3 = (bf16[4,2,400,384]{3,2,1,0:T(8,128)(2,1)S(1)}, bf16[4,2,400,384]{3,2,1,0:T(8,128)(2,1)}, u32[]{:S(2)}) copy-start(bf16[4,2,400,384]{3,2,1,0:T(8,128)(2,1)} %get-tuple-element.51) | copy-start | bytes 7372804
  52.3 31.6 %collective-permute-start.11 = (bf16[2,2,400,384]{3,2,1,0:T(8,128)(2,1)S(1)}, bf16[2,2,400,384]{3,2,1,0:T(8,128)(2,1)S(1)}, u32[]{:S(2)}, u32[]{:S(2)}) collective-permute-start(bf16[2,2,400,384]{3,2,1,0:T(8,128)(2,1)S(1)} %add_convert_fusion), channel_id=1, source_target_pairs={{0,96},{1,25},{2,98},{3,27},{4,100},{5,29},{6,102},{7,31},{8,104},... | collective-permute-start | bytes 3686408 | tf_op jit(solution)/shard_map/ppermute | solution.py:274
  52.4 31.5 %collective-permute-start.9 = (bf16[2,2,400,384]{3,2,1,0:T(8,128)(2,1)S(1)}, bf16[2,2,400,384]{3,2,1,0:T(8,128)(2,1)S(1)}, u32[]{:S(2)}, u32[]{:S(2)}) collective-permute-start(bf16[2,2,400,384]{3,2,1,0:T(8,128)(2,1)S(1)} %add_convert_fusion.1), channel_id=1, source_target_pairs={{0,32},{1,9},{2,34},{3,11},{4,36},{5,13},{6,38},{7,15},{8,40},{9,1... | collective-permute-start | bytes 3686408 | tf_op jit(solution)/shard_map/ppermute | solution.py:274
  61.6 17.3 %collective-permute-start.12 = (bf16[2,400,384]{2,1,0:T(8,128)(2,1)S(1)}, bf16[2,400,384]{2,1,0:T(8,128)(2,1)S(1)}, u32[]{:S(2)}, u32[]{:S(2)}) collective-permute-start(bf16[2,400,384]{2,1,0:T(8,128)(2,1)S(1)} %slice.83), channel_id=1, source_target_pairs={{0,24},{1,97},{2,26},{3,99},{4,28},{5,101},{6,30},{7,103},{8,0},{9... | collective-permute-start | bytes 1843208 | tf_op jit(solution)/shard_map/ppermute | solution.py:274
  64.6 19.3 %copy-start.4 = (bf16[4,2,400,384]{3,2,1,0:T(8,128)(2,1)S(1)}, bf16[4,2,400,384]{3,2,1,0:T(8,128)(2,1)}, u32[]{:S(2)}) copy-start(bf16[4,2,400,384]{3,2,1,0:T(8,128)(2,1)} %get-tuple-element.45) | copy-start | bytes 7372804
  64.6 17.0 %collective-permute-start.13 = (bf16[2,400,384]{2,1,0:T(8,128)(2,1)S(1)}, bf16[2,400,384]{2,1,0:T(8,128)(2,1)S(1)}, u32[]{:S(2)}, u32[]{:S(2)}) collective-permute-start(bf16[2,400,384]{2,1,0:T(8,128)(2,1)S(1)} %slice.84), channel_id=1, source_target_pairs={{0,8},{1,33},{2,10},{3,35},{4,12},{5,37},{6,14},{7,39},{8,16},{9,4... | collective-permute-start | bytes 1843208 | tf_op jit(solution)/shard_map/ppermute | solution.py:274
  64.7 16.9 %collective-permute-start.14 = (bf16[2,400,384]{2,1,0:T(8,128)(2,1)S(1)}, bf16[2,400,384]{2,1,0:T(8,128)(2,1)S(1)}, u32[]{:S(2)}, u32[]{:S(2)}) collective-permute-start(bf16[2,400,384]{2,1,0:T(8,128)(2,1)S(1)} %get-tuple-element.63), channel_id=1, source_target_pairs={{0,2},{1,7},{2,4},{3,1},{4,6},{5,3},{6,0},{7,5},{8,10},{9,15},{10,... | collective-permute-start | bytes 1843208 | tf_op jit(solution)/shard_map/ppermute | solution.py:274
  81.8 14.3 %collective-permute-start.20 = (bf16[2,400,384]{2,1,0:T(8,128)(2,1)S(1)}, bf16[2,400,384]{2,1,0:T(8,128)(2,1)S(1)}, u32[]{:S(2)}, u32[]{:S(2)}) collective-permute-start(bf16[2,400,384]{2,1,0:T(8,128)(2,1)S(1)} %add_convert_fusion.2), channel_id=1, source_target_pairs={{0,2},{1,7},{2,4},{3,1},{4,6},{5,3},{6,0},{7,5},{8,10},{9,15},{10,... | collective-permute-start | bytes 1843208 | tf_op jit(solution)/shard_map/ppermute | solution.py:274
  83.8 12.3 %copy-start.2 = (s32[8]{0:T(128)S(1)}, s32[8]{0:T(128)}, u32[]{:S(2)}) copy-start(s32[8]{0:T(128)} %partner_ref) | copy-start | bytes 100
  84.8 20.8 %collective-permute-start.21 = (bf16[2,400,384]{2,1,0:T(8,128)(2,1)S(1)}, bf16[2,400,384]{2,1,0:T(8,128)(2,1)S(1)}, u32[]{:S(2)}, u32[]{:S(2)}) collective-permute-start(bf16[2,400,384]{2,1,0:T(8,128)(2,1)S(1)} %get-tuple-element.69), channel_id=1, source_target_pairs={{0,8},{1,33},{2,10},{3,35},{4,12},{5,37},{6,14},{7,39},{8,16},{9,4... | collective-permute-start | bytes 1843208 | tf_op jit(solution)/shard_map/ppermute | solution.py:274
  84.9 20.7 %collective-permute-start.22 = (bf16[2,400,384]{2,1,0:T(8,128)(2,1)S(1)}, bf16[2,400,384]{2,1,0:T(8,128)(2,1)S(1)}, u32[]{:S(2)}, u32[]{:S(2)}) collective-permute-start(bf16[2,400,384]{2,1,0:T(8,128)(2,1)S(1)} %get-tuple-element.71), channel_id=1, source_target_pairs={{0,24},{1,97},{2,26},{3,99},{4,28},{5,101},{6,30},{7,103},{8,0},{9... | collective-permute-start | bytes 1843208 | tf_op jit(solution)/shard_map/ppermute | solution.py:274
  88.1 17.5 %collective-permute-start.23 = (bf16[2,400,384]{2,1,0:T(8,128)(2,1)S(1)}, bf16[2,400,384]{2,1,0:T(8,128)(2,1)S(1)}, u32[]{:S(2)}, u32[]{:S(2)}) collective-permute-start(bf16[2,400,384]{2,1,0:T(8,128)(2,1)S(1)} %get-tuple-element.70), channel_id=1, source_target_pairs={{0,16},{1,65},{2,18},{3,67},{4,20},{5,69},{6,22},{7,71},{8,24},{9,... | collective-permute-start | bytes 1843208 | tf_op jit(solution)/shard_map/ppermute | solution.py:274
  88.1 17.5 %collective-permute-start.24 = (bf16[2,400,384]{2,1,0:T(8,128)(2,1)S(1)}, bf16[2,400,384]{2,1,0:T(8,128)(2,1)S(1)}, u32[]{:S(2)}, u32[]{:S(2)}) collective-permute-start(bf16[2,400,384]{2,1,0:T(8,128)(2,1)S(1)} %get-tuple-element.82), channel_id=1, source_target_pairs={{0,6},{1,3},{2,0},{3,5},{4,2},{5,7},{6,4},{7,1},{8,14},{9,11},{10,... | collective-permute-start | bytes 1843208 | tf_op jit(solution)/shard_map/ppermute | solution.py:274
  105.5 1.0 copy-start.1

commit v10 on v9

--- a/solution.py
+++ b/solution.py
@@ -208,16 +208,14 @@
             def _():
                 pltpu.make_async_copy(ref.at[index], panels.at[q], panel_sem.at[q]).start()
 
-    @pl.loop(0, count)
-    def _(i):
-        p = i // 2
-
-        @pl.when(i % 2 == 0)
-        def _():
-            pltpu.make_async_copy(kept.at[0], panels.at[p], panel_sem.at[p]).wait()
-
-        outs[i] = nt(left_ref[p, i % 2], panels[p]).astype(jnp.bfloat16)
-        save(i).start()
+    @pl.loop(0, pairs)
+    def _(p):
+        pltpu.make_async_copy(kept.at[0], panels.at[p], panel_sem.at[p]).wait()
+        modes, width = panels.shape[1:]
+        product = nt(left_ref[p].reshape(2 * modes, width), panels[p])
+        for t in range(2):
+            outs[2 * p + t] = product[t * modes:(t + 1) * modes].astype(jnp.bfloat16)
+            save(2 * p + t).start()
 
     @pl.loop(0, count)
     def _(i):

time: 110 us -> 108 us (0.982)
  starting transfers between devices: 42.6 us -> 40 us
  waiting for transfers between devices: 40.9 us -> 42.1 us
    ppermute x25, starting transfers between devices: 42.6 us -> 40 us  [permuted(): return lax.ppermute(value, ('sx', 'sy'), pairs)]
    pallas_call x1, Pallas kernels: 9.33 us -> 7.83 us  [pair_products(): pl.pallas_call(pair_kernel, in_specs=[smem, pl.BlockSpec(memory_space=plt...]
    ppermute x25, waiting for transfers between devices: 40.9 us -> 42.1 us  [permuted(): return lax.ppermute(value, ('sx', 'sy'), pairs)]
  transfers between devices with their start and end apart: 25 -> 25, of which waited for: 10 -> 11; matrix products, arithmetic and copies ran while one was open for 4% -> 4% of each run, Pallas kernels for 16% -> 16%
where the time goes in v10:
time: 108 us; the launch traced here: 106 us
  waiting for transfers between devices  42.1 us (39%)
  starting transfers between devices  40 us (37%)
  Pallas kernels  18.6 us (17%)
  other arithmetic  3.98 us (4%)
    ppermute x25, waiting for transfers between devices, permuted(): return lax.ppermute(value, ('sx', 'sy'), pairs)  42.1 us
    ppermute x25, starting transfers between devices, permuted(): return lax.ppermute(value, ('sx', 'sy'), pairs)  40 us
    pallas_call x1, Pallas kernels, left_products(): pl.pallas_call(left_kernel, in_specs=[pl.BlockSpec(memory_space=pltpu.HBM...  8.71 us
    pallas_call x1, Pallas kernels, pair_products(): pl.pallas_call(pair_kernel, in_specs=[smem, pl.BlockSpec(memory_space=plt...  7.83 us
    convert_element_type x5, other arithmetic, rounded(): return added(*terms).astype(jnp.bfloat16)  2.27 us
  transfers between devices with their start and end apart: 25, of which 11 were waited for; matrix products, arithmetic and copies ran while one was open for 4% of the time, Pallas kernels for 16%

profile of v10, /device:TPU:0, one launch (start us, length us, event | category | flops | bytes accessed | tf_op | source)
XLA Modules:
  0.0 106.4 jit_solution(11268670858693179006)
XLA Ops:
  0.6 1.6 %collective-permute-start.2 = (bf16[400,384]{1,0:T(8,128)(2,1)}, bf16[400,384]{1,0:T(8,128)(2,1)S(1)}, u32[]{:S(2)}, u32[]{:S(2)}) collective-permute-start(bf16[400,384]{1,0:T(8,128)(2,1)} %bitcast.27), channel_id=1, source_target_pairs={{0,32},{1,9},{2,34},{3,11},{4,36},{5,13},{6,38},{7,15},{8,40},{9,1... | collective-permute-start | bytes 921608 | tf_op jit(solution)/shard_map/ppermute | solution.py:272
  2.3 2.7 %collective-permute-start.1 = (bf16[400,384]{1,0:T(8,128)(2,1)}, bf16[400,384]{1,0:T(8,128)(2,1)S(1)}, u32[]{:S(2)}, u32[]{:S(2)}) collective-permute-start(bf16[400,384]{1,0:T(8,128)(2,1)} %bitcast.28), channel_id=1, source_target_pairs={{0,64},{1,17},{2,66},{3,19},{4,68},{5,21},{6,70},{7,23},{8,72},{9,... | collective-permute-start | bytes 921608 | tf_op jit(solution)/shard_map/ppermute | solution.py:272
  5.0 1.4 %collective-permute-start = (bf16[400,384]{1,0:T(8,128)(2,1)}, bf16[400,384]{1,0:T(8,128)(2,1)S(1)}, u32[]{:S(2)}, u32[]{:S(2)}) collective-permute-start(bf16[400,384]{1,0:T(8,128)(2,1)} %bitcast.29), channel_id=1, source_target_pairs={{0,96},{1,25},{2,98},{3,27},{4,100},{5,29},{6,102},{7,31},{8,104},... | collective-permute-start | bytes 921608 | tf_op jit(solution)/shard_map/ppermute | solution.py:272
  6.4 4.0 %collective-permute-start.15 = (bf16[400,384]{1,0:T(8,128)(2,1)}, bf16[400,384]{1,0:T(8,128)(2,1)S(1)}, u32[]{:S(2)}, u32[]{:S(2)}) collective-permute-start(bf16[400,384]{1,0:T(8,128)(2,1)} %bitcast.30), channel_id=1, source_target_pairs={{0,6},{1,3},{2,0},{3,5},{4,2},{5,7},{6,4},{7,1},{8,14},{9,11},{10,... | collective-permute-start | bytes 921608 | tf_op jit(solution)/shard_map/ppermute | solution.py:272
  10.5 2.9 %collective-permute-done.1 = bf16[400,384]{1,0:T(8,128)(2,1)S(1)} collective-permute-done((bf16[400,384]{1,0:T(8,128)(2,1)}, bf16[400,384]{1,0:T(8,128)(2,1)S(1)}, u32[]{:S(2)}, u32[]{:S(2)}) %collective-permute-start.1) | collective-permute-done | bytes 307232 | tf_op jit(solution)/shard_map/ppermute | solution.py:272
  13.3 1.2 %pad_maximum_fusion.rest_0_ = bf16[4,400,384]{2,1,0:T(8,128)(2,1)S(1)} fusion(bf16[1,400,384]{2,1,0:T(8,128)(2,1)S(1)} %bitcast.40, bf16[1,400,384]{2,1,0:T(8,128)(2,1)S(1)} %bitcast.41, bf16[1,400,384]{2,1,0:T(8,128)(2,1)S(1)} %bitcast.42, bf16[1,400,384]{2,1,0:T(8,128)(2,1)} %bitcast.32), kind=kLoop, calls=%fused_computation.2 | loop fusion | flops 1843200 | bytes 2457600 | tf_op jit(solution)/shard_map/stack | solution.py:309
  14.6 3.1 %collective-permute-start.3 = (bf16[4,400,384]{2,1,0:T(8,128)(2,1)S(1)}, bf16[4,400,384]{2,1,0:T(8,128)(2,1)S(1)}, u32[]{:S(2)}, u32[]{:S(2)}) collective-permute-start(bf16[4,400,384]{2,1,0:T(8,128)(2,1)S(1)} %pad_maximum_fusion.rest_0_), channel_id=1, source_target_pairs={{0,24},{1,97},{2,26},{3,99},{4,28},{5,101},{6,30},{7,103},{8,0},{9... | collective-permute-start | bytes 3686408 | tf_op jit(solution)/shard_map/ppermute | solution.py:272
  17.7 1.1 %collective-permute-done.16 = bf16[400,384]{1,0:T(8,128)(2,1)S(1)} collective-permute-done((bf16[400,384]{1,0:T(8,128)(2,1)}, bf16[400,384]{1,0:T(8,128)(2,1)S(1)}, u32[]{:S(2)}, u32[]{:S(2)}) %collective-permute-start.16) | collective-permute-done | bytes 307232 | tf_op jit(solution)/shard_map/ppermute | solution.py:272
  18.8 0.1 pad_maximum_fusion.1.rest_5_
  18.9 8.7 %shard_map.59 = (bf16[8,2,400,384]{3,2,1,0:T(8,128)(2,1)S(1)}, bf16[2,2,400,384]{3,2,1,0:T(8,128)(2,1)}, bf16[2,2,400,384]{3,2,1,0:T(8,128)(2,1)}, bf16[2,2,400,...) custom-call(s32[8]{0:T(128)} %partner_ref, ...), custom_call_target="tpu_custom_call" | custom-call | flops 1887436800 | bytes 25000000 | tf_op jit(solution)/shard_map/pallas_call | solution.py:152
  27.6 0.1 collective-permute-start.17
  27.7 1.5 %collective-permute-start.10 = (bf16[2,2,400,384]{3,2,1,0:T(8,128)(2,1)}, bf16[2,2,400,384]{3,2,1,0:T(8,128)(2,1)S(1)}, u32[]{:S(2)}, u32[]{:S(2)}) collective-permute-start(bf16[2,2,400,384]{3,2,1,0:T(8,128)(2,1)} %get-tuple-element.60), channel_id=1, source_target_pairs={{0,96},{1,25},{2,98},{3,27},{4,100},{5,29},{6,102},{7,31},{8,104},... | collective-permute-start | bytes 3686408 | tf_op jit(solution)/shard_map/ppermute | solution.py:272
  29.2 0.6 collective-permute-start.8
  29.8 0.4 collective-permute-done.17.rest_6_
  30.2 0.1 collective-permute-start.19
  30.3 3.3 %collective-permute-done.3.rest_1_ = bf16[4,400,384]{2,1,0:T(8,128)(2,1)S(1)} collective-permute-done((bf16[4,400,384]{2,1,0:T(8,128)(2,1)S(1)}, bf16[4,400,384]{2,1,0:T(8,128)(2,1)S(1)}, u32[]{:S(2)}, u32[]{:S(2)}) %collective-permute-start.3) | collective-permute-done | bytes 1228832 | tf_op jit(solution)/shard_map/ppermute | solution.py:272
  33.6 4.0 %collective-permute-done.4.rest_2_ = bf16[4,400,384]{2,1,0:T(8,128)(2,1)S(1)} collective-permute-done((bf16[4,400,384]{2,1,0:T(8,128)(2,1)S(1)}, bf16[4,400,384]{2,1,0:T(8,128)(2,1)S(1)}, u32[]{:S(2)}, u32[]{:S(2)}) %collective-permute-start.4) | collective-permute-done | bytes 1228832 | tf_op jit(solution)/shard_map/ppermute | solution.py:272
  37.6 1.3 %collective-permute-start.6 = (bf16[2,2,400,384]{3,2,1,0:T(8,128)(2,1)}, bf16[2,2,400,384]{3,2,1,0:T(8,128)(2,1)S(1)}, u32[]{:S(2)}, u32[]{:S(2)}) collective-permute-start(bf16[2,2,400,384]{3,2,1,0:T(8,128)(2,1)} %get-tuple-element.53), channel_id=1, source_target_pairs={{0,32},{1,9},{2,34},{3,11},{4,36},{5,13},{6,38},{7,15},{8,40},{9,1... | collective-permute-start | bytes 3686408 | tf_op jit(solution)/shard_map/ppermute | solution.py:272
  38.9 5.8 %collective-permute-done.10 = bf16[2,2,400,384]{3,2,1,0:T(8,128)(2,1)S(1)} collective-permute-done((bf16[2,2,400,384]{3,2,1,0:T(8,128)(2,1)}, bf16[2,2,400,384]{3,2,1,0:T(8,128)(2,1)S(1)}, u32[]{:S(2)}, u32[]{:S(2)}) %collective-permute-start.10) | collective-permute-done | bytes 1228832 | tf_op jit(solution)/shard_map/ppermute | solution.py:272
  44.7 2.7 %collective-permute-start.7 = (bf16[2,2,400,384]{3,2,1,0:T(8,128)(2,1)}, bf16[2,2,400,384]{3,2,1,0:T(8,128)(2,1)S(1)}, u32[]{:S(2)}, u32[]{:S(2)}) collective-permute-start(bf16[2,2,400,384]{3,2,1,0:T(8,128)(2,1)} %get-tuple-element.54), channel_id=1, source_target_pairs={{0,96},{1,25},{2,98},{3,27},{4,100},{5,29},{6,102},{7,31},{8,104},... | collective-permute-start | bytes 3686408 | tf_op jit(solution)/shard_map/ppermute | solution.py:272
  47.4 0.1 pad_maximum_fusion.2
  47.5 0.3 add_convert_fusion
  47.8 4.8 %collective-permute-start.18 = (bf16[2,400,384]{2,1,0:T(8,128)(2,1)S(1)}, bf16[2,400,384]{2,1,0:T(8,128)(2,1)S(1)}, u32[]{:S(2)}, u32[]{:S(2)}) collective-permute-start(bf16[2,400,384]{2,1,0:T(8,128)(2,1)S(1)} %pad_maximum_fusion.2), channel_id=1, source_target_pairs={{0,6},{1,3},{2,0},{3,5},{4,2},{5,7},{6,4},{7,1},{8,14},{9,11},{10,... | collective-permute-start | bytes 1843208 | tf_op jit(solution)/shard_map/ppermute | solution.py:272
  52.6 0.3 add_convert_fusion.1
  53.0 0.1 collective-permute-start.11
  53.1 2.0 %collective-permute-start.9 = (bf16[2,2,400,384]{3,2,1,0:T(8,128)(2,1)S(1)}, bf16[2,2,400,384]{3,2,1,0:T(8,128)(2,1)S(1)}, u32[]{:S(2)}, u32[]{:S(2)}) collective-permute-start(bf16[2,2,400,384]{3,2,1,0:T(8,128)(2,1)S(1)} %add_convert_fusion.1), channel_id=1, source_target_pairs={{0,32},{1,9},{2,34},{3,11},{4,36},{5,13},{6,38},{7,15},{8,40},{9,1... | collective-permute-start | bytes 3686408 | tf_op jit(solution)/shard_map/ppermute | solution.py:272
  55.1 0.6 fusion.7
  55.7 4.9 %collective-permute-done.6 = bf16[2,2,400,384]{3,2,1,0:T(8,128)(2,1)S(1)} collective-permute-done((bf16[2,2,400,384]{3,2,1,0:T(8,128)(2,1)}, bf16[2,2,400,384]{3,2,1,0:T(8,128)(2,1)S(1)}, u32[]{:S(2)}, u32[]{:S(2)}) %collective-permute-start.6) | collective-permute-done | bytes 1228832 | tf_op jit(solution)/shard_map/ppermute | solution.py:272
  60.5 1.4 %collective-permute-done.7 = bf16[2,2,400,384]{3,2,1,0:T(8,128)(2,1)S(1)} collective-permute-done((bf16[2,2,400,384]{3,2,1,0:T(8,128)(2,1)}, bf16[2,2,400,384]{3,2,1,0:T(8,128)(2,1)S(1)}, u32[]{:S(2)}, u32[]{:S(2)}) %collective-permute-start.7) | collective-permute-done | bytes 1228832 | tf_op jit(solution)/shard_map/ppermute | solution.py:272
  61.9 0.1 slice.83
  62.0 3.3 %collective-permute-start.12 = (bf16[2,400,384]{2,1,0:T(8,128)(2,1)S(1)}, bf16[2,400,384]{2,1,0:T(8,128)(2,1)S(1)}, u32[]{:S(2)}, u32[]{:S(2)}) collective-permute-start(bf16[2,400,384]{2,1,0:T(8,128)(2,1)S(1)} %slice.83), channel_id=1, source_target_pairs={{0,24},{1,97},{2,26},{3,99},{4,28},{5,101},{6,30},{7,103},{8,0},{9... | collective-permute-start | bytes 1843208 | tf_op jit(solution)/shard_map/ppermute | solution.py:272
  65.3 0.1 slice.84
  65.4 0.1 collective-permute-start.13
  65.5 2.0 %collective-permute-start.14 = (bf16[2,400,384]{2,1,0:T(8,128)(2,1)S(1)}, bf16[2,400,384]{2,1,0:T(8,128)(2,1)S(1)}, u32[]{:S(2)}, u32[]{:S(2)}) collective-permute-start(bf16[2,400,384]{2,1,0:T(8,128)(2,1)S(1)} %get-tuple-element.63), channel_id=1, source_target_pairs={{0,2},{1,7},{2,4},{3,1},{4,6},{5,3},{6,0},{7,5},{8,10},{9,15},{10,... | collective-permute-start | bytes 1843208 | tf_op jit(solution)/shard_map/ppermute | solution.py:272
  67.5 12.1 %collective-permute-done.12.rest_3_ = bf16[2,400,384]{2,1,0:T(8,128)(2,1)S(1)} collective-permute-done((bf16[2,400,384]{2,1,0:T(8,128)(2,1)S(1)}, bf16[2,400,384]{2,1,0:T(8,128)(2,1)S(1)}, u32[]{:S(2)}, u32[]{:S(2)}) %collective-permute-start.12) | collective-permute-done | bytes 614432 | tf_op jit(solution)/shard_map/ppermute | solution.py:272
  79.6 2.1 %collective-permute-done.13.rest_4_ = bf16[2,400,384]{2,1,0:T(8,128)(2,1)S(1)} collective-permute-done((bf16[2,400,384]{2,1,0:T(8,128)(2,1)S(1)}, bf16[2,400,384]{2,1,0:T(8,128)(2,1)S(1)}, u32[]{:S(2)}, u32[]{:S(2)}) %collective-permute-start.13) | collective-permute-done | bytes 614432 | tf_op jit(solution)/shard_map/ppermute | solution.py:272
  81.7 0.2 add_convert_fusion.2
  81.8 2.0 %collective-permute-start.20 = (bf16[2,400,384]{2,1,0:T(8,128)(2,1)S(1)}, bf16[2,400,384]{2,1,0:T(8,128)(2,1)S(1)}, u32[]{:S(2)}, u32[]{:S(2)}) collective-permute-start(bf16[2,400,384]{2,1,0:T(8,128)(2,1)S(1)} %add_convert_fusion.2), channel_id=1, source_target_pairs={{0,2},{1,7},{2,4},{3,1},{4,6},{5,3},{6,0},{7,5},{8,10},{9,15},{10,... | collective-permute-start | bytes 1843208 | tf_op jit(solution)/shard_map/ppermute | solution.py:272
  83.9 0.9 fusion.4
  84.8 0.1 collective-permute-start.21
  84.9 3.2 %collective-permute-start.22 = (bf16[2,400,384]{2,1,0:T(8,128)(2,1)S(1)}, bf16[2,400,384]{2,1,0:T(8,128)(2,1)S(1)}, u32[]{:S(2)}, u32[]{:S(2)}) collective-permute-start(bf16[2,400,384]{2,1,0:T(8,128)(2,1)S(1)} %get-tuple-element.71), channel_id=1, source_target_pairs={{0,24},{1,97},{2,26},{3,99},{4,28},{5,101},{6,30},{7,103},{8,0},{9... | collective-permute-start | bytes 1843208 | tf_op jit(solution)/shard_map/ppermute | solution.py:272
  88.1 0.2 collective-permute-start.23
  88.3 3.0 %collective-permute-start.24 = (bf16[2,400,384]{2,1,0:T(8,128)(2,1)S(1)}, bf16[2,400,384]{2,1,0:T(8,128)(2,1)S(1)}, u32[]{:S(2)}, u32[]{:S(2)}) collective-permute-start(bf16[2,400,384]{2,1,0:T(8,128)(2,1)S(1)} %get-tuple-element.82), channel_id=1, source_target_pairs={{0,6},{1,3},{2,0},{3,5},{4,2},{5,7},{6,4},{7,1},{8,14},{9,11},{10,... | collective-permute-start | bytes 1843208 | tf_op jit(solution)/shard_map/ppermute | solution.py:272
  91.2 4.2 %collective-permute-done.20 = bf16[2,400,384]{2,1,0:T(8,128)(2,1)S(1)} collective-permute-done((bf16[2,400,384]{2,1,0:T(8,128)(2,1)S(1)}, bf16[2,400,384]{2,1,0:T(8,128)(2,1)S(1)}, u32[]{:S(2)}, u32[]{:S(2)}) %collective-permute-start.20) | collective-permute-done | bytes 614432 | tf_op jit(solution)/shard_map/ppermute | solution.py:272
  95.5 7.8 %shard_map.60 = bf16[8,2,400,400]{3,2,1,0:T(8,128)(2,1)} custom-call(s32[8]{0:T(128)S(1)} %copy-done.2, bf16[8,2,400,384]{3,2,1,0:T(8,128)(2,1)S(1)} %get-tuple-element.75.left_ref, bf16[4,400,384]{2,1,0:T(8,128)(2,1)S(1)} %pad_maximum_fusion.rest_0_, bf16[4,400,384]{2,1,0:T(8,128)(2,1)S(1)} %collective-permute-done.3.rest_1_, ...), custom_call_target="tpu_custom_call" | custom-call | flops 1966080000 | bytes 15000000 | tf_op jit(solution)/shard_map/pallas_call | solution.py:228
  103.4 0.3 convert_add_fusion.sum_ref
  103.7 0.6 copy-done.1
  104.3 2.1 %shard_map.61 = f32[2,400,400]{2,1,0:T(8,128)} custom-call(bf16[400,384]{1,0:T(8,128)(2,1)S(1)} %bitcast.35, f32[2,400,384]{2,1,0:T(8,128)S(1)} %convert_add_fusion.sum_ref, bf16[2,400,384]{2,1,0:T(8,128)(2,1)S(1)} %collective-permute-done.21.rest_0_, bf16[2,400,384]{2,1,0:T(8,128)(2,1)S(1)} %collective-permute-done.22.rest_1_, ...), custom_call_target="tpu_custom_call" | custom-call | tf_op jit(solution)/shard_map/pallas_call | solution.py:259
  (27 shorter events, 0.1 us)
Async XLA Ops:
  0.6 9.9 %collective-permute-start.2 = (bf16[400,384]{1,0:T(8,128)(2,1)}, bf16[400,384]{1,0:T(8,128)(2,1)S(1)}, u32[]{:S(2)}, u32[]{:S(2)}) collective-permute-start(bf16[400,384]{1,0:T(8,128)(2,1)} %bitcast.27), channel_id=1, source_target_pairs={{0,32},{1,9},{2,34},{3,11},{4,36},{5,13},{6,38},{7,15},{8,40},{9,1... | collective-permute-start | bytes 921608 | tf_op jit(solution)/shard_map/ppermute | solution.py:272
  2.3 11.1 %collective-permute-start.1 = (bf16[400,384]{1,0:T(8,128)(2,1)}, bf16[400,384]{1,0:T(8,128)(2,1)S(1)}, u32[]{:S(2)}, u32[]{:S(2)}) collective-permute-start(bf16[400,384]{1,0:T(8,128)(2,1)} %bitcast.28), channel_id=1, source_target_pairs={{0,64},{1,17},{2,66},{3,19},{4,68},{5,21},{6,70},{7,23},{8,72},{9,... | collective-permute-start | bytes 921608 | tf_op jit(solution)/shard_map/ppermute | solution.py:272
  5.0 8.3 %collective-permute-start = (bf16[400,384]{1,0:T(8,128)(2,1)}, bf16[400,384]{1,0:T(8,128)(2,1)S(1)}, u32[]{:S(2)}, u32[]{:S(2)}) collective-permute-start(bf16[400,384]{1,0:T(8,128)(2,1)} %bitcast.29), channel_id=1, source_target_pairs={{0,96},{1,25},{2,98},{3,27},{4,100},{5,29},{6,102},{7,31},{8,104},... | collective-permute-start | bytes 921608 | tf_op jit(solution)/shard_map/ppermute | solution.py:272
  6.4 11.2 %collective-permute-start.15 = (bf16[400,384]{1,0:T(8,128)(2,1)}, bf16[400,384]{1,0:T(8,128)(2,1)S(1)}, u32[]{:S(2)}, u32[]{:S(2)}) collective-permute-start(bf16[400,384]{1,0:T(8,128)(2,1)} %bitcast.30), channel_id=1, source_target_pairs={{0,6},{1,3},{2,0},{3,5},{4,2},{5,7},{6,4},{7,1},{8,14},{9,11},{10,... | collective-permute-start | bytes 921608 | tf_op jit(solution)/shard_map/ppermute | solution.py:272
  10.5 8.3 %collective-permute-start.16 = (bf16[400,384]{1,0:T(8,128)(2,1)}, bf16[400,384]{1,0:T(8,128)(2,1)S(1)}, u32[]{:S(2)}, u32[]{:S(2)}) collective-permute-start(bf16[400,384]{1,0:T(8,128)(2,1)} %bitcast.31), channel_id=1, source_target_pairs={{0,2},{1,7},{2,4},{3,1},{4,6},{5,3},{6,0},{7,5},{8,10},{9,15},{10,... | collective-permute-start | bytes 921608 | tf_op jit(solution)/shard_map/ppermute | solution.py:272
  13.3 5.4 %copy-start = (bf16[1,384,400]{1,2,0:T(8,128)(2,1)S(1)}, bf16[1,384,400]{1,2,0:T(8,128)(2,1)}, u32[]{:S(2)}) copy-start(bf16[1,384,400]{1,2,0:T(8,128)(2,1)} %param.4) | copy-start | bytes 921604
  14.6 19.0 %collective-permute-start.3 = (bf16[4,400,384]{2,1,0:T(8,128)(2,1)S(1)}, bf16[4,400,384]{2,1,0:T(8,128)(2,1)S(1)}, u32[]{:S(2)}, u32[]{:S(2)}) collective-permute-start(bf16[4,400,384]{2,1,0:T(8,128)(2,1)S(1)} %pad_maximum_fusion.rest_0_), channel_id=1, source_target_pairs={{0,24},{1,97},{2,26},{3,99},{4,28},{5,101},{6,30},{7,103},{8,0},{9... | collective-permute-start | bytes 3686408 | tf_op jit(solution)/shard_map/ppermute | solution.py:272
  17.7 19.9 %collective-permute-start.4 = (bf16[4,400,384]{2,1,0:T(8,128)(2,1)S(1)}, bf16[4,400,384]{2,1,0:T(8,128)(2,1)S(1)}, u32[]{:S(2)}, u32[]{:S(2)}) collective-permute-start(bf16[4,400,384]{2,1,0:T(8,128)(2,1)S(1)} %pad_maximum_fusion.rest_0_), channel_id=1, source_target_pairs={{0,8},{1,33},{2,10},{3,35},{4,12},{5,37},{6,14},{7,39},{8,16},{9,4... | collective-permute-start | bytes 3686408 | tf_op jit(solution)/shard_map/ppermute | solution.py:272
  27.6 2.6 %collective-permute-start.17 = (bf16[3,400,384]{2,1,0:T(8,128)(2,1)S(1)}, bf16[3,400,384]{2,1,0:T(8,128)(2,1)S(1)}, u32[]{:S(2)}, u32[]{:S(2)}) collective-permute-start(bf16[3,400,384]{2,1,0:T(8,128)(2,1)S(1)} %pad_maximum_fusion.1.rest_5_), channel_id=1, source_target_pairs={{0,1},{1,0},{2,3},{3,2},{4,5},{5,4},{6,7},{7,6},{8,9},{9,8},{10,11... | collective-permute-start | bytes 2764808 | tf_op jit(solution)/shard_map/ppermute | solution.py:272
  27.7 17.0 %collective-permute-start.10 = (bf16[2,2,400,384]{3,2,1,0:T(8,128)(2,1)}, bf16[2,2,400,384]{3,2,1,0:T(8,128)(2,1)S(1)}, u32[]{:S(2)}, u32[]{:S(2)}) collective-permute-start(bf16[2,2,400,384]{3,2,1,0:T(8,128)(2,1)} %get-tuple-element.60), channel_id=1, source_target_pairs={{0,96},{1,25},{2,98},{3,27},{4,100},{5,29},{6,102},{7,31},{8,104},... | collective-permute-start | bytes 3686408 | tf_op jit(solution)/shard_map/ppermute | solution.py:272
  29.2 18.6 %collective-permute-start.8 = (bf16[2,2,400,384]{3,2,1,0:T(8,128)(2,1)}, bf16[2,2,400,384]{3,2,1,0:T(8,128)(2,1)S(1)}, u32[]{:S(2)}, u32[]{:S(2)}) collective-permute-start(bf16[2,2,400,384]{3,2,1,0:T(8,128)(2,1)} %get-tuple-element.57), channel_id=1, source_target_pairs={{0,32},{1,9},{2,34},{3,11},{4,36},{5,13},{6,38},{7,15},{8,40},{9,1... | collective-permute-start | bytes 3686408 | tf_op jit(solution)/shard_map/ppermute | solution.py:272
  30.2 22.8 %collective-permute-start.19 = (bf16[2,2,400,384]{3,2,1,0:T(8,128)(2,1)}, bf16[2,2,400,384]{3,2,1,0:T(8,128)(2,1)S(1)}, u32[]{:S(2)}, u32[]{:S(2)}) collective-permute-start(bf16[2,2,400,384]{3,2,1,0:T(8,128)(2,1)} %get-tuple-element.66), channel_id=1, source_target_pairs={{0,1},{1,0},{2,3},{3,2},{4,5},{5,4},{6,7},{7,6},{8,9},{9,8},{10,11... | collective-permute-start | bytes 3686408 | tf_op jit(solution)/shard_map/ppermute | solution.py:272
  37.6 15.5 %collective-permute-start.5 = (bf16[2,2,400,384]{3,2,1,0:T(8,128)(2,1)}, bf16[2,2,400,384]{3,2,1,0:T(8,128)(2,1)S(1)}, u32[]{:S(2)}, u32[]{:S(2)}) collective-permute-start(bf16[2,2,400,384]{3,2,1,0:T(8,128)(2,1)} %get-tuple-element.52), channel_id=1, source_target_pairs={{0,1},{1,0},{2,3},{3,2},{4,5},{5,4},{6,7},{7,6},{8,9},{9,8},{10,11... | collective-permute-start | bytes 3686408 | tf_op jit(solution)/shard_map/ppermute | solution.py:272
  37.6 22.9 %collective-permute-start.6 = (bf16[2,2,400,384]{3,2,1,0:T(8,128)(2,1)}, bf16[2,2,400,384]{3,2,1,0:T(8,128)(2,1)S(1)}, u32[]{:S(2)}, u32[]{:S(2)}) collective-permute-start(bf16[2,2,400,384]{3,2,1,0:T(8,128)(2,1)} %get-tuple-element.53), channel_id=1, source_target_pairs={{0,32},{1,9},{2,34},{3,11},{4,36},{5,13},{6,38},{7,15},{8,40},{9,1... | collective-permute-start | bytes 3686408 | tf_op jit(solution)/shard_map/ppermute | solution.py:272
  44.7 17.2 %collective-permute-start.7 = (bf16[2,2,400,384]{3,2,1,0:T(8,128)(2,1)}, bf16[2,2,400,384]{3,2,1,0:T(8,128)(2,1)S(1)}, u32[]{:S(2)}, u32[]{:S(2)}) collective-permute-start(bf16[2,2,400,384]{3,2,1,0:T(8,128)(2,1)} %get-tuple-element.54), channel_id=1, source_target_pairs={{0,96},{1,25},{2,98},{3,27},{4,100},{5,29},{6,102},{7,31},{8,104},... | collective-permute-start | bytes 3686408 | tf_op jit(solution)/shard_map/ppermute | solution.py:272
  47.8 17.6 %collective-permute-start.18 = (bf16[2,400,384]{2,1,0:T(8,128)(2,1)S(1)}, bf16[2,400,384]{2,1,0:T(8,128)(2,1)S(1)}, u32[]{:S(2)}, u32[]{:S(2)}) collective-permute-start(bf16[2,400,384]{2,1,0:T(8,128)(2,1)S(1)} %pad_maximum_fusion.2), channel_id=1, source_target_pairs={{0,6},{1,3},{2,0},{3,5},{4,2},{5,7},{6,4},{7,1},{8,14},{9,11},{10,... | collective-permute-start | bytes 1843208 | tf_op jit(solution)/shard_map/ppermute | solution.py:272
  52.6 2.4 %copy-start.3 = (bf16[4,2,400,384]{3,2,1,0:T(8,128)(2,1)S(1)}, bf16[4,2,400,384]{3,2,1,0:T(8,128)(2,1)}, u32[]{:S(2)}) copy-start(bf16[4,2,400,384]{3,2,1,0:T(8,128)(2,1)} %get-tuple-element.51) | copy-start | bytes 7372804
  53.0 30.9 %collective-permute-start.11 = (bf16[2,2,400,384]{3,2,1,0:T(8,128)(2,1)S(1)}, bf16[2,2,400,384]{3,2,1,0:T(8,128)(2,1)S(1)}, u32[]{:S(2)}, u32[]{:S(2)}) collective-permute-start(bf16[2,2,400,384]{3,2,1,0:T(8,128)(2,1)S(1)} %add_convert_fusion), channel_id=1, source_target_pairs={{0,96},{1,25},{2,98},{3,27},{4,100},{5,29},{6,102},{7,31},{8,104},... | collective-permute-start | bytes 3686408 | tf_op jit(solution)/shard_map/ppermute | solution.py:272
  53.1 30.8 %collective-permute-start.9 = (bf16[2,2,400,384]{3,2,1,0:T(8,128)(2,1)S(1)}, bf16[2,2,400,384]{3,2,1,0:T(8,128)(2,1)S(1)}, u32[]{:S(2)}, u32[]{:S(2)}) collective-permute-start(bf16[2,2,400,384]{3,2,1,0:T(8,128)(2,1)S(1)} %add_convert_fusion.1), channel_id=1, source_target_pairs={{0,32},{1,9},{2,34},{3,11},{4,36},{5,13},{6,38},{7,15},{8,40},{9,1... | collective-permute-start | bytes 3686408 | tf_op jit(solution)/shard_map/ppermute | solution.py:272
  62.0 17.6 %collective-permute-start.12 = (bf16[2,400,384]{2,1,0:T(8,128)(2,1)S(1)}, bf16[2,400,384]{2,1,0:T(8,128)(2,1)S(1)}, u32[]{:S(2)}, u32[]{:S(2)}) collective-permute-start(bf16[2,400,384]{2,1,0:T(8,128)(2,1)S(1)} %slice.83), channel_id=1, source_target_pairs={{0,24},{1,97},{2,26},{3,99},{4,28},{5,101},{6,30},{7,103},{8,0},{9... | collective-permute-start | bytes 1843208 | tf_op jit(solution)/shard_map/ppermute | solution.py:272
  65.3 18.5 %copy-start.4 = (bf16[4,2,400,384]{3,2,1,0:T(8,128)(2,1)S(1)}, bf16[4,2,400,384]{3,2,1,0:T(8,128)(2,1)}, u32[]{:S(2)}) copy-start(bf16[4,2,400,384]{3,2,1,0:T(8,128)(2,1)} %get-tuple-element.45) | copy-start | bytes 7372804
  65.4 16.3 %collective-permute-start.13 = (bf16[2,400,384]{2,1,0:T(8,128)(2,1)S(1)}, bf16[2,400,384]{2,1,0:T(8,128)(2,1)S(1)}, u32[]{:S(2)}, u32[]{:S(2)}) collective-permute-start(bf16[2,400,384]{2,1,0:T(8,128)(2,1)S(1)} %slice.84), channel_id=1, source_target_pairs={{0,8},{1,33},{2,10},{3,35},{4,12},{5,37},{6,14},{7,39},{8,16},{9,4... | collective-permute-start | bytes 1843208 | tf_op jit(solution)/shard_map/ppermute | solution.py:272
  65.5 16.2 %collective-permute-start.14 = (bf16[2,400,384]{2,1,0:T(8,128)(2,1)S(1)}, bf16[2,400,384]{2,1,0:T(8,128)(2,1)S(1)}, u32[]{:S(2)}, u32[]{:S(2)}) collective-permute-start(bf16[2,400,384]{2,1,0:T(8,128)(2,1)S(1)} %get-tuple-element.63), channel_id=1, source_target_pairs={{0,2},{1,7},{2,4},{3,1},{4,6},{5,3},{6,0},{7,5},{8,10},{9,15},{10,... | collective-permute-start | bytes 1843208 | tf_op jit(solution)/shard_map/ppermute | solution.py:272
  81.8 13.6 %collective-permute-start.20 = (bf16[2,400,384]{2,1,0:T(8,128)(2,1)S(1)}, bf16[2,400,384]{2,1,0:T(8,128)(2,1)S(1)}, u32[]{:S(2)}, u32[]{:S(2)}) collective-permute-start(bf16[2,400,384]{2,1,0:T(8,128)(2,1)S(1)} %add_convert_fusion.2), channel_id=1, source_target_pairs={{0,2},{1,7},{2,4},{3,1},{4,6},{5,3},{6,0},{7,5},{8,10},{9,15},{10,... | collective-permute-start | bytes 1843208 | tf_op jit(solution)/shard_map/ppermute | solution.py:272
  83.8 11.6 %copy-start.2 = (s32[8]{0:T(128)S(1)}, s32[8]{0:T(128)}, u32[]{:S(2)}) copy-start(s32[8]{0:T(128)} %partner_ref) | copy-start | bytes 100
  84.8 18.6 %collective-permute-start.21 = (bf16[2,400,384]{2,1,0:T(8,128)(2,1)S(1)}, bf16[2,400,384]{2,1,0:T(8,128)(2,1)S(1)}, u32[]{:S(2)}, u32[]{:S(2)}) collective-permute-start(bf16[2,400,384]{2,1,0:T(8,128)(2,1)S(1)} %get-tuple-element.69), channel_id=1, source_target_pairs={{0,8},{1,33},{2,10},{3,35},{4,12},{5,37},{6,14},{7,39},{8,16},{9,4... | collective-permute-start | bytes 1843208 | tf_op jit(solution)/shard_map/ppermute | solution.py:272
  84.9 18.5 %collective-permute-start.22 = (bf16[2,400,384]{2,1,0:T(8,128)(2,1)S(1)}, bf16[2,400,384]{2,1,0:T(8,128)(2,1)S(1)}, u32[]{:S(2)}, u32[]{:S(2)}) collective-permute-start(bf16[2,400,384]{2,1,0:T(8,128)(2,1)S(1)} %get-tuple-element.71), channel_id=1, source_target_pairs={{0,24},{1,97},{2,26},{3,99},{4,28},{5,101},{6,30},{7,103},{8,0},{9... | collective-permute-start | bytes 1843208 | tf_op jit(solution)/shard_map/ppermute | solution.py:272
  88.1 15.3 %collective-permute-start.23 = (bf16[2,400,384]{2,1,0:T(8,128)(2,1)S(1)}, bf16[2,400,384]{2,1,0:T(8,128)(2,1)S(1)}, u32[]{:S(2)}, u32[]{:S(2)}) collective-permute-start(bf16[2,400,384]{2,1,0:T(8,128)(2,1)S(1)} %get-tuple-element.70), channel_id=1, source_target_pairs={{0,16},{1,65},{2,18},{3,67},{4,20},{5,69},{6,22},{7,71},{8,24},{9,... | collective-permute-start | bytes 1843208 | tf_op jit(solution)/shard_map/ppermute | solution.py:272
  88.3 15.1 %collective-permute-start.24 = (bf16[2,400,384]{2,1,0:T(8,128)(2,1)S(1)}, bf16[2,400,384]{2,1,0:T(8,128)(2,1)S(1)}, u32[]{:S(2)}, u32[]{:S(2)}) collective-permute-start(bf16[2,400,384]{2,1,0:T(8,128)(2,1)S(1)} %get-tuple-element.82), channel_id=1, source_target_pairs={{0,6},{1,3},{2,0},{3,5},{4,2},{5,7},{6,4},{7,1},{8,14},{9,11},{10,... | collective-permute-start | bytes 1843208 | tf_op jit(solution)/shard_map/ppermute | solution.py:272
  103.3 1.0 copy-start.1

commit v11 on v10

--- a/solution.py
+++ b/solution.py
@@ -338,7 +338,7 @@
         rounded(here[3], end_up[1], last_down[1]),
     ]
     v, w2 = barrier((v, w[2]))
-    back = turn(w2, -1)
+    back = turn(after(w2, z_last), -1)
     ends = [second(v[1], 1), second(v[3], -1), second(v[2], 2)]
 
     sources = [kept, near, far, low, high, ring_mine, ring_other, across]

time: 108 us -> 108 us (level)
  waiting for transfers between devices: 42.1 us -> 43.6 us
    ppermute x25, waiting for transfers between devices: 42.1 us -> 43.6 us  [permuted(): return lax.ppermute(value, ('sx', 'sy'), pairs)]
  transfers between devices with their start and end apart: 25 -> 25, of which waited for: 11 -> 12; matrix products, arithmetic and copies ran while one was open for 4% -> 4% of each run, Pallas kernels for 16% -> 15%
where the time goes in v11:
time: 108 us; the launch traced here: 107 us
  waiting for transfers between devices  43.6 us (40%)
  starting transfers between devices  39.4 us (36%)
  Pallas kernels  18.6 us (17%)
  other arithmetic  3.98 us (4%)
    ppermute x25, waiting for transfers between devices, permuted(): return lax.ppermute(value, ('sx', 'sy'), pairs)  43.6 us
    ppermute x25, starting transfers between devices, permuted(): return lax.ppermute(value, ('sx', 'sy'), pairs)  39.4 us
    pallas_call x1, Pallas kernels, left_products(): pl.pallas_call(left_kernel, in_specs=[pl.BlockSpec(memory_space=pltpu.HBM...  8.71 us
    pallas_call x1, Pallas kernels, pair_products(): pl.pallas_call(pair_kernel, in_specs=[smem, pl.BlockSpec(memory_space=plt...  7.82 us
    convert_element_type x5, other arithmetic, rounded(): return added(*terms).astype(jnp.bfloat16)  2.27 us
  transfers between devices with their start and end apart: 25, of which 12 were waited for; matrix products, arithmetic and copies ran while one was open for 4% of the time, Pallas kernels for 15%

profile of v11, /device:TPU:0, one launch (start us, length us, event | category | flops | bytes accessed | tf_op | source)
XLA Modules:
  0.0 107.0 jit_solution(14301038850736065269)
XLA Ops:
  0.6 1.6 %collective-permute-start.2 = (bf16[400,384]{1,0:T(8,128)(2,1)}, bf16[400,384]{1,0:T(8,128)(2,1)S(1)}, u32[]{:S(2)}, u32[]{:S(2)}) collective-permute-start(bf16[400,384]{1,0:T(8,128)(2,1)} %bitcast.27), channel_id=1, source_target_pairs={{0,32},{1,9},{2,34},{3,11},{4,36},{5,13},{6,38},{7,15},{8,40},{9,1... | collective-permute-start | bytes 921608 | tf_op jit(solution)/shard_map/ppermute | solution.py:272
  2.3 2.7 %collective-permute-start.1 = (bf16[400,384]{1,0:T(8,128)(2,1)}, bf16[400,384]{1,0:T(8,128)(2,1)S(1)}, u32[]{:S(2)}, u32[]{:S(2)}) collective-permute-start(bf16[400,384]{1,0:T(8,128)(2,1)} %bitcast.28), channel_id=1, source_target_pairs={{0,64},{1,17},{2,66},{3,19},{4,68},{5,21},{6,70},{7,23},{8,72},{9,... | collective-permute-start | bytes 921608 | tf_op jit(solution)/shard_map/ppermute | solution.py:272
  5.0 1.4 %collective-permute-start = (bf16[400,384]{1,0:T(8,128)(2,1)}, bf16[400,384]{1,0:T(8,128)(2,1)S(1)}, u32[]{:S(2)}, u32[]{:S(2)}) collective-permute-start(bf16[400,384]{1,0:T(8,128)(2,1)} %bitcast.29), channel_id=1, source_target_pairs={{0,96},{1,25},{2,98},{3,27},{4,100},{5,29},{6,102},{7,31},{8,104},... | collective-permute-start | bytes 921608 | tf_op jit(solution)/shard_map/ppermute | solution.py:272
  6.4 4.0 %collective-permute-start.15 = (bf16[400,384]{1,0:T(8,128)(2,1)}, bf16[400,384]{1,0:T(8,128)(2,1)S(1)}, u32[]{:S(2)}, u32[]{:S(2)}) collective-permute-start(bf16[400,384]{1,0:T(8,128)(2,1)} %bitcast.30), channel_id=1, source_target_pairs={{0,6},{1,3},{2,0},{3,5},{4,2},{5,7},{6,4},{7,1},{8,14},{9,11},{10,... | collective-permute-start | bytes 921608 | tf_op jit(solution)/shard_map/ppermute | solution.py:272
  10.5 2.9 %collective-permute-done.1 = bf16[400,384]{1,0:T(8,128)(2,1)S(1)} collective-permute-done((bf16[400,384]{1,0:T(8,128)(2,1)}, bf16[400,384]{1,0:T(8,128)(2,1)S(1)}, u32[]{:S(2)}, u32[]{:S(2)}) %collective-permute-start.1) | collective-permute-done | bytes 307232 | tf_op jit(solution)/shard_map/ppermute | solution.py:272
  13.3 1.2 %pad_maximum_fusion.rest_0_ = bf16[4,400,384]{2,1,0:T(8,128)(2,1)S(1)} fusion(bf16[1,400,384]{2,1,0:T(8,128)(2,1)S(1)} %bitcast.40, bf16[1,400,384]{2,1,0:T(8,128)(2,1)S(1)} %bitcast.41, bf16[1,400,384]{2,1,0:T(8,128)(2,1)S(1)} %bitcast.42, bf16[1,400,384]{2,1,0:T(8,128)(2,1)} %bitcast.32), kind=kLoop, calls=%fused_computation.2 | loop fusion | flops 1843200 | bytes 2457600 | tf_op jit(solution)/shard_map/stack | solution.py:309
  14.6 3.1 %collective-permute-start.3 = (bf16[4,400,384]{2,1,0:T(8,128)(2,1)S(1)}, bf16[4,400,384]{2,1,0:T(8,128)(2,1)S(1)}, u32[]{:S(2)}, u32[]{:S(2)}) collective-permute-start(bf16[4,400,384]{2,1,0:T(8,128)(2,1)S(1)} %pad_maximum_fusion.rest_0_), channel_id=1, source_target_pairs={{0,24},{1,97},{2,26},{3,99},{4,28},{5,101},{6,30},{7,103},{8,0},{9... | collective-permute-start | bytes 3686408 | tf_op jit(solution)/shard_map/ppermute | solution.py:272
  17.7 1.1 %collective-permute-done.16 = bf16[400,384]{1,0:T(8,128)(2,1)S(1)} collective-permute-done((bf16[400,384]{1,0:T(8,128)(2,1)}, bf16[400,384]{1,0:T(8,128)(2,1)S(1)}, u32[]{:S(2)}, u32[]{:S(2)}) %collective-permute-start.16) | collective-permute-done | bytes 307232 | tf_op jit(solution)/shard_map/ppermute | solution.py:272
  18.8 0.1 pad_maximum_fusion.1.rest_5_
  18.9 8.7 %shard_map.59 = (bf16[8,2,400,384]{3,2,1,0:T(8,128)(2,1)S(1)}, bf16[2,2,400,384]{3,2,1,0:T(8,128)(2,1)}, bf16[2,2,400,384]{3,2,1,0:T(8,128)(2,1)}, bf16[2,2,400,...) custom-call(s32[8]{0:T(128)} %partner_ref, ...), custom_call_target="tpu_custom_call" | custom-call | flops 1887436800 | bytes 25000000 | tf_op jit(solution)/shard_map/pallas_call | solution.py:152
  27.6 0.1 collective-permute-start.17
  27.7 0.9 collective-permute-start.10
  28.6 1.2 %collective-permute-start.8 = (bf16[2,2,400,384]{3,2,1,0:T(8,128)(2,1)}, bf16[2,2,400,384]{3,2,1,0:T(8,128)(2,1)S(1)}, u32[]{:S(2)}, u32[]{:S(2)}) collective-permute-start(bf16[2,2,400,384]{3,2,1,0:T(8,128)(2,1)} %get-tuple-element.58), channel_id=1, source_target_pairs={{0,32},{1,9},{2,34},{3,11},{4,36},{5,13},{6,38},{7,15},{8,40},{9,1... | collective-permute-start | bytes 3686408 | tf_op jit(solution)/shard_map/ppermute | solution.py:272
  29.8 0.4 collective-permute-done.17.rest_6_
  30.2 0.8 collective-permute-start.19
  30.9 1.3 %collective-permute-done.3.rest_1_ = bf16[4,400,384]{2,1,0:T(8,128)(2,1)S(1)} collective-permute-done((bf16[4,400,384]{2,1,0:T(8,128)(2,1)S(1)}, bf16[4,400,384]{2,1,0:T(8,128)(2,1)S(1)}, u32[]{:S(2)}, u32[]{:S(2)}) %collective-permute-start.3) | collective-permute-done | bytes 1228832 | tf_op jit(solution)/shard_map/ppermute | solution.py:272
  32.2 4.0 %collective-permute-done.4.rest_2_ = bf16[4,400,384]{2,1,0:T(8,128)(2,1)S(1)} collective-permute-done((bf16[4,400,384]{2,1,0:T(8,128)(2,1)S(1)}, bf16[4,400,384]{2,1,0:T(8,128)(2,1)S(1)}, u32[]{:S(2)}, u32[]{:S(2)}) %collective-permute-start.4) | collective-permute-done | bytes 1228832 | tf_op jit(solution)/shard_map/ppermute | solution.py:272
  36.2 2.7 %collective-permute-start.6 = (bf16[2,2,400,384]{3,2,1,0:T(8,128)(2,1)}, bf16[2,2,400,384]{3,2,1,0:T(8,128)(2,1)S(1)}, u32[]{:S(2)}, u32[]{:S(2)}) collective-permute-start(bf16[2,2,400,384]{3,2,1,0:T(8,128)(2,1)} %get-tuple-element.54), channel_id=1, source_target_pairs={{0,32},{1,9},{2,34},{3,11},{4,36},{5,13},{6,38},{7,15},{8,40},{9,1... | collective-permute-start | bytes 3686408 | tf_op jit(solution)/shard_map/ppermute | solution.py:272
  38.9 5.8 %collective-permute-done.10 = bf16[2,2,400,384]{3,2,1,0:T(8,128)(2,1)S(1)} collective-permute-done((bf16[2,2,400,384]{3,2,1,0:T(8,128)(2,1)}, bf16[2,2,400,384]{3,2,1,0:T(8,128)(2,1)S(1)}, u32[]{:S(2)}, u32[]{:S(2)}) %collective-permute-start.10) | collective-permute-done | bytes 1228832 | tf_op jit(solution)/shard_map/ppermute | solution.py:272
  44.7 2.1 %collective-permute-start.7 = (bf16[2,2,400,384]{3,2,1,0:T(8,128)(2,1)}, bf16[2,2,400,384]{3,2,1,0:T(8,128)(2,1)S(1)}, u32[]{:S(2)}, u32[]{:S(2)}) collective-permute-start(bf16[2,2,400,384]{3,2,1,0:T(8,128)(2,1)} %get-tuple-element.55), channel_id=1, source_target_pairs={{0,96},{1,25},{2,98},{3,27},{4,100},{5,29},{6,102},{7,31},{8,104},... | collective-permute-start | bytes 3686408 | tf_op jit(solution)/shard_map/ppermute | solution.py:272
  46.8 0.1 pad_maximum_fusion.2
  46.9 0.3 add_convert_fusion
  47.2 4.1 %collective-permute-start.18 = (bf16[2,400,384]{2,1,0:T(8,128)(2,1)S(1)}, bf16[2,400,384]{2,1,0:T(8,128)(2,1)S(1)}, u32[]{:S(2)}, u32[]{:S(2)}) collective-permute-start(bf16[2,400,384]{2,1,0:T(8,128)(2,1)S(1)} %pad_maximum_fusion.2), channel_id=1, source_target_pairs={{0,6},{1,3},{2,0},{3,5},{4,2},{5,7},{6,4},{7,1},{8,14},{9,11},{10,... | collective-permute-start | bytes 1843208 | tf_op jit(solution)/shard_map/ppermute | solution.py:272
  51.3 0.3 add_convert_fusion.1
  51.6 0.1 collective-permute-start.11
  51.7 2.0 %collective-permute-start.9 = (bf16[2,2,400,384]{3,2,1,0:T(8,128)(2,1)S(1)}, bf16[2,2,400,384]{3,2,1,0:T(8,128)(2,1)S(1)}, u32[]{:S(2)}, u32[]{:S(2)}) collective-permute-start(bf16[2,2,400,384]{3,2,1,0:T(8,128)(2,1)S(1)} %add_convert_fusion.1), channel_id=1, source_target_pairs={{0,32},{1,9},{2,34},{3,11},{4,36},{5,13},{6,38},{7,15},{8,40},{9,1... | collective-permute-start | bytes 3686408 | tf_op jit(solution)/shard_map/ppermute | solution.py:272
  53.7 0.6 fusion.7
  54.3 5.6 %collective-permute-done.6 = bf16[2,2,400,384]{3,2,1,0:T(8,128)(2,1)S(1)} collective-permute-done((bf16[2,2,400,384]{3,2,1,0:T(8,128)(2,1)}, bf16[2,2,400,384]{3,2,1,0:T(8,128)(2,1)S(1)}, u32[]{:S(2)}, u32[]{:S(2)}) %collective-permute-start.6) | collective-permute-done | bytes 1228832 | tf_op jit(solution)/shard_map/ppermute | solution.py:272
  59.9 1.7 %collective-permute-done.7 = bf16[2,2,400,384]{3,2,1,0:T(8,128)(2,1)S(1)} collective-permute-done((bf16[2,2,400,384]{3,2,1,0:T(8,128)(2,1)}, bf16[2,2,400,384]{3,2,1,0:T(8,128)(2,1)S(1)}, u32[]{:S(2)}, u32[]{:S(2)}) %collective-permute-start.7) | collective-permute-done | bytes 1228832 | tf_op jit(solution)/shard_map/ppermute | solution.py:272
  61.6 0.1 slice.83
  61.7 4.0 %collective-permute-start.12 = (bf16[2,400,384]{2,1,0:T(8,128)(2,1)S(1)}, bf16[2,400,384]{2,1,0:T(8,128)(2,1)S(1)}, u32[]{:S(2)}, u32[]{:S(2)}) collective-permute-start(bf16[2,400,384]{2,1,0:T(8,128)(2,1)S(1)} %slice.83), channel_id=1, source_target_pairs={{0,24},{1,97},{2,26},{3,99},{4,28},{5,101},{6,30},{7,103},{8,0},{9... | collective-permute-start | bytes 1843208 | tf_op jit(solution)/shard_map/ppermute | solution.py:272
  65.7 0.1 slice.84
  65.7 0.1 collective-permute-start.13
  65.8 1.2 %collective-permute-start.14 = (bf16[2,400,384]{2,1,0:T(8,128)(2,1)S(1)}, bf16[2,400,384]{2,1,0:T(8,128)(2,1)S(1)}, u32[]{:S(2)}, u32[]{:S(2)}) collective-permute-start(bf16[2,400,384]{2,1,0:T(8,128)(2,1)S(1)} %get-tuple-element.64), channel_id=1, source_target_pairs={{0,2},{1,7},{2,4},{3,1},{4,6},{5,3},{6,0},{7,5},{8,10},{9,15},{10,... | collective-permute-start | bytes 1843208 | tf_op jit(solution)/shard_map/ppermute | solution.py:272
  67.1 12.9 %collective-permute-done.12.rest_3_ = bf16[2,400,384]{2,1,0:T(8,128)(2,1)S(1)} collective-permute-done((bf16[2,400,384]{2,1,0:T(8,128)(2,1)S(1)}, bf16[2,400,384]{2,1,0:T(8,128)(2,1)S(1)}, u32[]{:S(2)}, u32[]{:S(2)}) %collective-permute-start.12) | collective-permute-done | bytes 614432 | tf_op jit(solution)/shard_map/ppermute | solution.py:272
  80.0 1.7 %collective-permute-done.13.rest_4_ = bf16[2,400,384]{2,1,0:T(8,128)(2,1)S(1)} collective-permute-done((bf16[2,400,384]{2,1,0:T(8,128)(2,1)S(1)}, bf16[2,400,384]{2,1,0:T(8,128)(2,1)S(1)}, u32[]{:S(2)}, u32[]{:S(2)}) %collective-permute-start.13) | collective-permute-done | bytes 614432 | tf_op jit(solution)/shard_map/ppermute | solution.py:272
  81.7 0.2 add_convert_fusion.2
  81.8 2.0 %collective-permute-start.20 = (bf16[2,400,384]{2,1,0:T(8,128)(2,1)S(1)}, bf16[2,400,384]{2,1,0:T(8,128)(2,1)S(1)}, u32[]{:S(2)}, u32[]{:S(2)}) collective-permute-start(bf16[2,400,384]{2,1,0:T(8,128)(2,1)S(1)} %add_convert_fusion.2), channel_id=1, source_target_pairs={{0,2},{1,7},{2,4},{3,1},{4,6},{5,3},{6,0},{7,5},{8,10},{9,15},{10,... | collective-permute-start | bytes 1843208 | tf_op jit(solution)/shard_map/ppermute | solution.py:272
  83.9 0.9 fusion.4
  84.8 0.1 collective-permute-start.21
  84.9 3.2 %collective-permute-start.22 = (bf16[2,400,384]{2,1,0:T(8,128)(2,1)S(1)}, bf16[2,400,384]{2,1,0:T(8,128)(2,1)S(1)}, u32[]{:S(2)}, u32[]{:S(2)}) collective-permute-start(bf16[2,400,384]{2,1,0:T(8,128)(2,1)S(1)} %get-tuple-element.72), channel_id=1, source_target_pairs={{0,24},{1,97},{2,26},{3,99},{4,28},{5,101},{6,30},{7,103},{8,0},{9... | collective-permute-start | bytes 1843208 | tf_op jit(solution)/shard_map/ppermute | solution.py:272
  88.1 6.0 %collective-permute-done.20 = bf16[2,400,384]{2,1,0:T(8,128)(2,1)S(1)} collective-permute-done((bf16[2,400,384]{2,1,0:T(8,128)(2,1)S(1)}, bf16[2,400,384]{2,1,0:T(8,128)(2,1)S(1)}, u32[]{:S(2)}, u32[]{:S(2)}) %collective-permute-start.20) | collective-permute-done | bytes 614432 | tf_op jit(solution)/shard_map/ppermute | solution.py:272
  94.1 2.0 %collective-permute-start.24 = (bf16[2,400,384]{2,1,0:T(8,128)(2,1)S(1)}, bf16[2,400,384]{2,1,0:T(8,128)(2,1)S(1)}, u32[]{:S(2)}, u32[]{:S(2)}) collective-permute-start(bf16[2,400,384]{2,1,0:T(8,128)(2,1)S(1)} %get-tuple-element.84), channel_id=1, source_target_pairs={{0,6},{1,3},{2,0},{3,5},{4,2},{5,7},{6,4},{7,1},{8,14},{9,11},{10,... | collective-permute-start | bytes 1843208 | tf_op jit(solution)/shard_map/ppermute | solution.py:272
  96.1 7.8 %shard_map.60 = bf16[8,2,400,400]{3,2,1,0:T(8,128)(2,1)} custom-call(s32[8]{0:T(128)S(1)} %copy-done.2, bf16[8,2,400,384]{3,2,1,0:T(8,128)(2,1)S(1)} %get-tuple-element.76.left_ref, bf16[4,400,384]{2,1,0:T(8,128)(2,1)S(1)} %pad_maximum_fusion.rest_0_, bf16[4,400,384]{2,1,0:T(8,128)(2,1)S(1)} %collective-permute-done.3.rest_1_, ...), custom_call_target="tpu_custom_call" | custom-call | flops 1966080000 | bytes 15000000 | tf_op jit(solution)/shard_map/pallas_call | solution.py:228
  104.0 0.3 collective-permute-done.24
  104.2 0.3 convert_add_fusion.sum_ref
  104.5 0.4 copy-done.1
  104.9 2.1 %shard_map.61 = f32[2,400,400]{2,1,0:T(8,128)} custom-call(bf16[400,384]{1,0:T(8,128)(2,1)S(1)} %bitcast.35, f32[2,400,384]{2,1,0:T(8,128)S(1)} %convert_add_fusion.sum_ref, bf16[2,400,384]{2,1,0:T(8,128)(2,1)S(1)} %collective-permute-done.21.rest_0_, bf16[2,400,384]{2,1,0:T(8,128)(2,1)S(1)} %collective-permute-done.22.rest_1_, ...), custom_call_target="tpu_custom_call" | custom-call | tf_op jit(solution)/shard_map/pallas_call | solution.py:259
  (27 shorter events, 0.1 us)
Async XLA Ops:
  0.6 9.9 %collective-permute-start.2 = (bf16[400,384]{1,0:T(8,128)(2,1)}, bf16[400,384]{1,0:T(8,128)(2,1)S(1)}, u32[]{:S(2)}, u32[]{:S(2)}) collective-permute-start(bf16[400,384]{1,0:T(8,128)(2,1)} %bitcast.27), channel_id=1, source_target_pairs={{0,32},{1,9},{2,34},{3,11},{4,36},{5,13},{6,38},{7,15},{8,40},{9,1... | collective-permute-start | bytes 921608 | tf_op jit(solution)/shard_map/ppermute | solution.py:272
  2.3 11.1 %collective-permute-start.1 = (bf16[400,384]{1,0:T(8,128)(2,1)}, bf16[400,384]{1,0:T(8,128)(2,1)S(1)}, u32[]{:S(2)}, u32[]{:S(2)}) collective-permute-start(bf16[400,384]{1,0:T(8,128)(2,1)} %bitcast.28), channel_id=1, source_target_pairs={{0,64},{1,17},{2,66},{3,19},{4,68},{5,21},{6,70},{7,23},{8,72},{9,... | collective-permute-start | bytes 921608 | tf_op jit(solution)/shard_map/ppermute | solution.py:272
  5.0 8.3 %collective-permute-start = (bf16[400,384]{1,0:T(8,128)(2,1)}, bf16[400,384]{1,0:T(8,128)(2,1)S(1)}, u32[]{:S(2)}, u32[]{:S(2)}) collective-permute-start(bf16[400,384]{1,0:T(8,128)(2,1)} %bitcast.29), channel_id=1, source_target_pairs={{0,96},{1,25},{2,98},{3,27},{4,100},{5,29},{6,102},{7,31},{8,104},... | collective-permute-start | bytes 921608 | tf_op jit(solution)/shard_map/ppermute | solution.py:272
  6.4 11.2 %collective-permute-start.15 = (bf16[400,384]{1,0:T(8,128)(2,1)}, bf16[400,384]{1,0:T(8,128)(2,1)S(1)}, u32[]{:S(2)}, u32[]{:S(2)}) collective-permute-start(bf16[400,384]{1,0:T(8,128)(2,1)} %bitcast.30), channel_id=1, source_target_pairs={{0,6},{1,3},{2,0},{3,5},{4,2},{5,7},{6,4},{7,1},{8,14},{9,11},{10,... | collective-permute-start | bytes 921608 | tf_op jit(solution)/shard_map/ppermute | solution.py:272
  10.5 8.3 %collective-permute-start.16 = (bf16[400,384]{1,0:T(8,128)(2,1)}, bf16[400,384]{1,0:T(8,128)(2,1)S(1)}, u32[]{:S(2)}, u32[]{:S(2)}) collective-permute-start(bf16[400,384]{1,0:T(8,128)(2,1)} %bitcast.31), channel_id=1, source_target_pairs={{0,2},{1,7},{2,4},{3,1},{4,6},{5,3},{6,0},{7,5},{8,10},{9,15},{10,... | collective-permute-start | bytes 921608 | tf_op jit(solution)/shard_map/ppermute | solution.py:272
  13.3 5.4 %copy-start = (bf16[1,384,400]{1,2,0:T(8,128)(2,1)S(1)}, bf16[1,384,400]{1,2,0:T(8,128)(2,1)}, u32[]{:S(2)}) copy-start(bf16[1,384,400]{1,2,0:T(8,128)(2,1)} %param.4) | copy-start | bytes 921604
  14.6 17.6 %collective-permute-start.3 = (bf16[4,400,384]{2,1,0:T(8,128)(2,1)S(1)}, bf16[4,400,384]{2,1,0:T(8,128)(2,1)S(1)}, u32[]{:S(2)}, u32[]{:S(2)}) collective-permute-start(bf16[4,400,384]{2,1,0:T(8,128)(2,1)S(1)} %pad_maximum_fusion.rest_0_), channel_id=1, source_target_pairs={{0,24},{1,97},{2,26},{3,99},{4,28},{5,101},{6,30},{7,103},{8,0},{9... | collective-permute-start | bytes 3686408 | tf_op jit(solution)/shard_map/ppermute | solution.py:272
  17.7 18.5 %collective-permute-start.4 = (bf16[4,400,384]{2,1,0:T(8,128)(2,1)S(1)}, bf16[4,400,384]{2,1,0:T(8,128)(2,1)S(1)}, u32[]{:S(2)}, u32[]{:S(2)}) collective-permute-start(bf16[4,400,384]{2,1,0:T(8,128)(2,1)S(1)} %pad_maximum_fusion.rest_0_), channel_id=1, source_target_pairs={{0,8},{1,33},{2,10},{3,35},{4,12},{5,37},{6,14},{7,39},{8,16},{9,4... | collective-permute-start | bytes 3686408 | tf_op jit(solution)/shard_map/ppermute | solution.py:272
  27.6 2.6 %collective-permute-start.17 = (bf16[3,400,384]{2,1,0:T(8,128)(2,1)S(1)}, bf16[3,400,384]{2,1,0:T(8,128)(2,1)S(1)}, u32[]{:S(2)}, u32[]{:S(2)}) collective-permute-start(bf16[3,400,384]{2,1,0:T(8,128)(2,1)S(1)} %pad_maximum_fusion.1.rest_5_), channel_id=1, source_target_pairs={{0,1},{1,0},{2,3},{3,2},{4,5},{5,4},{6,7},{7,6},{8,9},{9,8},{10,11... | collective-permute-start | bytes 2764808 | tf_op jit(solution)/shard_map/ppermute | solution.py:272
  27.7 17.0 %collective-permute-start.10 = (bf16[2,2,400,384]{3,2,1,0:T(8,128)(2,1)}, bf16[2,2,400,384]{3,2,1,0:T(8,128)(2,1)S(1)}, u32[]{:S(2)}, u32[]{:S(2)}) collective-permute-start(bf16[2,2,400,384]{3,2,1,0:T(8,128)(2,1)} %get-tuple-element.61), channel_id=1, source_target_pairs={{0,96},{1,25},{2,98},{3,27},{4,100},{5,29},{6,102},{7,31},{8,104},... | collective-permute-start | bytes 3686408 | tf_op jit(solution)/shard_map/ppermute | solution.py:272
  28.6 18.6 %collective-permute-start.8 = (bf16[2,2,400,384]{3,2,1,0:T(8,128)(2,1)}, bf16[2,2,400,384]{3,2,1,0:T(8,128)(2,1)S(1)}, u32[]{:S(2)}, u32[]{:S(2)}) collective-permute-start(bf16[2,2,400,384]{3,2,1,0:T(8,128)(2,1)} %get-tuple-element.58), channel_id=1, source_target_pairs={{0,32},{1,9},{2,34},{3,11},{4,36},{5,13},{6,38},{7,15},{8,40},{9,1... | collective-permute-start | bytes 3686408 | tf_op jit(solution)/shard_map/ppermute | solution.py:272
  30.2 21.4 %collective-permute-start.19 = (bf16[2,2,400,384]{3,2,1,0:T(8,128)(2,1)}, bf16[2,2,400,384]{3,2,1,0:T(8,128)(2,1)S(1)}, u32[]{:S(2)}, u32[]{:S(2)}) collective-permute-start(bf16[2,2,400,384]{3,2,1,0:T(8,128)(2,1)} %get-tuple-element.67), channel_id=1, source_target_pairs={{0,1},{1,0},{2,3},{3,2},{4,5},{5,4},{6,7},{7,6},{8,9},{9,8},{10,11... | collective-permute-start | bytes 3686408 | tf_op jit(solution)/shard_map/ppermute | solution.py:272
  36.2 15.5 %collective-permute-start.5 = (bf16[2,2,400,384]{3,2,1,0:T(8,128)(2,1)}, bf16[2,2,400,384]{3,2,1,0:T(8,128)(2,1)S(1)}, u32[]{:S(2)}, u32[]{:S(2)}) collective-permute-start(bf16[2,2,400,384]{3,2,1,0:T(8,128)(2,1)} %get-tuple-element.53), channel_id=1, source_target_pairs={{0,1},{1,0},{2,3},{3,2},{4,5},{5,4},{6,7},{7,6},{8,9},{9,8},{10,11... | collective-permute-start | bytes 3686408 | tf_op jit(solution)/shard_map/ppermute | solution.py:272
  36.2 23.7 %collective-permute-start.6 = (bf16[2,2,400,384]{3,2,1,0:T(8,128)(2,1)}, bf16[2,2,400,384]{3,2,1,0:T(8,128)(2,1)S(1)}, u32[]{:S(2)}, u32[]{:S(2)}) collective-permute-start(bf16[2,2,400,384]{3,2,1,0:T(8,128)(2,1)} %get-tuple-element.54), channel_id=1, source_target_pairs={{0,32},{1,9},{2,34},{3,11},{4,36},{5,13},{6,38},{7,15},{8,40},{9,1... | collective-permute-start | bytes 3686408 | tf_op jit(solution)/shard_map/ppermute | solution.py:272
  44.7 16.9 %collective-permute-start.7 = (bf16[2,2,400,384]{3,2,1,0:T(8,128)(2,1)}, bf16[2,2,400,384]{3,2,1,0:T(8,128)(2,1)S(1)}, u32[]{:S(2)}, u32[]{:S(2)}) collective-permute-start(bf16[2,2,400,384]{3,2,1,0:T(8,128)(2,1)} %get-tuple-element.55), channel_id=1, source_target_pairs={{0,96},{1,25},{2,98},{3,27},{4,100},{5,29},{6,102},{7,31},{8,104},... | collective-permute-start | bytes 3686408 | tf_op jit(solution)/shard_map/ppermute | solution.py:272
  47.2 18.6 %collective-permute-start.18 = (bf16[2,400,384]{2,1,0:T(8,128)(2,1)S(1)}, bf16[2,400,384]{2,1,0:T(8,128)(2,1)S(1)}, u32[]{:S(2)}, u32[]{:S(2)}) collective-permute-start(bf16[2,400,384]{2,1,0:T(8,128)(2,1)S(1)} %pad_maximum_fusion.2), channel_id=1, source_target_pairs={{0,6},{1,3},{2,0},{3,5},{4,2},{5,7},{6,4},{7,1},{8,14},{9,11},{10,... | collective-permute-start | bytes 1843208 | tf_op jit(solution)/shard_map/ppermute | solution.py:272
  51.3 2.4 %copy-start.3 = (bf16[4,2,400,384]{3,2,1,0:T(8,128)(2,1)S(1)}, bf16[4,2,400,384]{3,2,1,0:T(8,128)(2,1)}, u32[]{:S(2)}) copy-start(bf16[4,2,400,384]{3,2,1,0:T(8,128)(2,1)} %get-tuple-element.52) | copy-start | bytes 7372804
  51.6 32.3 %collective-permute-start.11 = (bf16[2,2,400,384]{3,2,1,0:T(8,128)(2,1)S(1)}, bf16[2,2,400,384]{3,2,1,0:T(8,128)(2,1)S(1)}, u32[]{:S(2)}, u32[]{:S(2)}) collective-permute-start(bf16[2,2,400,384]{3,2,1,0:T(8,128)(2,1)S(1)} %add_convert_fusion), channel_id=1, source_target_pairs={{0,96},{1,25},{2,98},{3,27},{4,100},{5,29},{6,102},{7,31},{8,104},... | collective-permute-start | bytes 3686408 | tf_op jit(solution)/shard_map/ppermute | solution.py:272
  51.7 32.2 %collective-permute-start.9 = (bf16[2,2,400,384]{3,2,1,0:T(8,128)(2,1)S(1)}, bf16[2,2,400,384]{3,2,1,0:T(8,128)(2,1)S(1)}, u32[]{:S(2)}, u32[]{:S(2)}) collective-permute-start(bf16[2,2,400,384]{3,2,1,0:T(8,128)(2,1)S(1)} %add_convert_fusion.1), channel_id=1, source_target_pairs={{0,32},{1,9},{2,34},{3,11},{4,36},{5,13},{6,38},{7,15},{8,40},{9,1... | collective-permute-start | bytes 3686408 | tf_op jit(solution)/shard_map/ppermute | solution.py:272
  61.7 18.3 %collective-permute-start.12 = (bf16[2,400,384]{2,1,0:T(8,128)(2,1)S(1)}, bf16[2,400,384]{2,1,0:T(8,128)(2,1)S(1)}, u32[]{:S(2)}, u32[]{:S(2)}) collective-permute-start(bf16[2,400,384]{2,1,0:T(8,128)(2,1)S(1)} %slice.83), channel_id=1, source_target_pairs={{0,24},{1,97},{2,26},{3,99},{4,28},{5,101},{6,30},{7,103},{8,0},{9... | collective-permute-start | bytes 1843208 | tf_op jit(solution)/shard_map/ppermute | solution.py:272
  65.7 18.2 %copy-start.4 = (bf16[4,2,400,384]{3,2,1,0:T(8,128)(2,1)S(1)}, bf16[4,2,400,384]{3,2,1,0:T(8,128)(2,1)}, u32[]{:S(2)}) copy-start(bf16[4,2,400,384]{3,2,1,0:T(8,128)(2,1)} %get-tuple-element.46) | copy-start | bytes 7372804
  65.7 15.9 %collective-permute-start.13 = (bf16[2,400,384]{2,1,0:T(8,128)(2,1)S(1)}, bf16[2,400,384]{2,1,0:T(8,128)(2,1)S(1)}, u32[]{:S(2)}, u32[]{:S(2)}) collective-permute-start(bf16[2,400,384]{2,1,0:T(8,128)(2,1)S(1)} %slice.84), channel_id=1, source_target_pairs={{0,8},{1,33},{2,10},{3,35},{4,12},{5,37},{6,14},{7,39},{8,16},{9,4... | collective-permute-start | bytes 1843208 | tf_op jit(solution)/shard_map/ppermute | solution.py:272
  65.8 15.8 %collective-permute-start.14 = (bf16[2,400,384]{2,1,0:T(8,128)(2,1)S(1)}, bf16[2,400,384]{2,1,0:T(8,128)(2,1)S(1)}, u32[]{:S(2)}, u32[]{:S(2)}) collective-permute-start(bf16[2,400,384]{2,1,0:T(8,128)(2,1)S(1)} %get-tuple-element.64), channel_id=1, source_target_pairs={{0,2},{1,7},{2,4},{3,1},{4,6},{5,3},{6,0},{7,5},{8,10},{9,15},{10,... | collective-permute-start | bytes 1843208 | tf_op jit(solution)/shard_map/ppermute | solution.py:272
  81.8 12.2 %collective-permute-start.20 = (bf16[2,400,384]{2,1,0:T(8,128)(2,1)S(1)}, bf16[2,400,384]{2,1,0:T(8,128)(2,1)S(1)}, u32[]{:S(2)}, u32[]{:S(2)}) collective-permute-start(bf16[2,400,384]{2,1,0:T(8,128)(2,1)S(1)} %add_convert_fusion.2), channel_id=1, source_target_pairs={{0,2},{1,7},{2,4},{3,1},{4,6},{5,3},{6,0},{7,5},{8,10},{9,15},{10,... | collective-permute-start | bytes 1843208 | tf_op jit(solution)/shard_map/ppermute | solution.py:272
  83.8 12.3 %copy-start.2 = (s32[8]{0:T(128)S(1)}, s32[8]{0:T(128)}, u32[]{:S(2)}) copy-start(s32[8]{0:T(128)} %partner_ref) | copy-start | bytes 100
  84.8 19.2 %collective-permute-start.21 = (bf16[2,400,384]{2,1,0:T(8,128)(2,1)S(1)}, bf16[2,400,384]{2,1,0:T(8,128)(2,1)S(1)}, u32[]{:S(2)}, u32[]{:S(2)}) collective-permute-start(bf16[2,400,384]{2,1,0:T(8,128)(2,1)S(1)} %get-tuple-element.70), channel_id=1, source_target_pairs={{0,8},{1,33},{2,10},{3,35},{4,12},{5,37},{6,14},{7,39},{8,16},{9,4... | collective-permute-start | bytes 1843208 | tf_op jit(solution)/shard_map/ppermute | solution.py:272
  84.9 19.1 %collective-permute-start.22 = (bf16[2,400,384]{2,1,0:T(8,128)(2,1)S(1)}, bf16[2,400,384]{2,1,0:T(8,128)(2,1)S(1)}, u32[]{:S(2)}, u32[]{:S(2)}) collective-permute-start(bf16[2,400,384]{2,1,0:T(8,128)(2,1)S(1)} %get-tuple-element.72), channel_id=1, source_target_pairs={{0,24},{1,97},{2,26},{3,99},{4,28},{5,101},{6,30},{7,103},{8,0},{9... | collective-permute-start | bytes 1843208 | tf_op jit(solution)/shard_map/ppermute | solution.py:272
  88.1 15.9 %collective-permute-start.23 = (bf16[2,400,384]{2,1,0:T(8,128)(2,1)S(1)}, bf16[2,400,384]{2,1,0:T(8,128)(2,1)S(1)}, u32[]{:S(2)}, u32[]{:S(2)}) collective-permute-start(bf16[2,400,384]{2,1,0:T(8,128)(2,1)S(1)} %get-tuple-element.71), channel_id=1, source_target_pairs={{0,16},{1,65},{2,18},{3,67},{4,20},{5,69},{6,22},{7,71},{8,24},{9,... | collective-permute-start | bytes 1843208 | tf_op jit(solution)/shard_map/ppermute | solution.py:272
  94.1 10.1 %collective-permute-start.24 = (bf16[2,400,384]{2,1,0:T(8,128)(2,1)S(1)}, bf16[2,400,384]{2,1,0:T(8,128)(2,1)S(1)}, u32[]{:S(2)}, u32[]{:S(2)}) collective-permute-start(bf16[2,400,384]{2,1,0:T(8,128)(2,1)S(1)} %get-tuple-element.84), channel_id=1, source_target_pairs={{0,6},{1,3},{2,0},{3,5},{4,2},{5,7},{6,4},{7,1},{8,14},{9,11},{10,... | collective-permute-start | bytes 1843208 | tf_op jit(solution)/shard_map/ppermute | solution.py:272
  103.9 1.0 copy-start.1
